TPU v7x, 32 devices: a whole 2x2x4 slice. The times are simulated.
32 devices in a mesh: gx: 2 (over x), gy: 4 (over y, core), gz: 4 (over z).
Axes of the slice: x: 2, y: 2, z: 4, core: 2. Of those that a mesh axis runs over, the one named last changes fastest.
Arguments:
- basis: float32 [6, 4, 4, 8, 8, 512], P(None, None, None, 'gx', 'gy', 'gz'), may hold values from -15 to 15
- inverse_rows: bfloat16 [4, 8, 8, 192, 512], P(None, 'gx', 'gy', None, 'gz'), may hold values from -1 to 3
- block_diag: float32 [4, 4, 8, 8, 512], P(None, None, 'gx', 'gy', 'gz'), may hold values from -6 to 6
- couple: float32 [6, 4, 8, 8, 512], P(None, None, 'gx', 'gy', 'gz'), may hold values from 0.2 to 2
- coarse_basis: float32 [16, 4, 8, 8, 512], P(None, None, 'gx', 'gy', 'gz'), may hold values from -0.09375 to 0.09375
- coarse_factor: float32 [512, 512], P(('gx', 'gy', 'gz')), may hold values from -1 to 5, as said below
Outputs:
- krylov_next: float32 [4, 4, 8, 8, 512], P(None, None, 'gx', 'gy', 'gz')
- preconditioned: float32 [4, 4, 8, 8, 512], P(None, None, 'gx', 'gy', 'gz')
- hessenberg: float32 [4, 7], replicated
Inputs may be any that keep to these rules, and one draw needn't show every extreme that they name: coarse_factor is zero above its diagonal.
All inputs are finite; a program needn't handle non-finite values.
Results may differ from a plain program's by a relative error of at most 0.0026.
Values may be sent and summed in bfloat16 or wider, within the bound.
No kernel may reach another device: no remote copies, remote signals or barrier semaphores. Data moves between devices by JAX's collectives and lax.ppermute only.
A program may use at most 64 MiB of HBM per device.

v0:
```python
import jax
import jax.numpy as jnp
from jax import lax
from jax.sharding import PartitionSpec as P

C = 4
CX = 4
CY = 2
CZ = 128
S = 4
M = 6


epsilon = 1e-06


def padded_2(cells, sides, width):
    for axis, dim in sides:
        count = lax.axis_size(axis)
        ends = count - 1
        head = lax.slice_in_dim(cells, 0, width, axis=dim)
        tail = lax.slice_in_dim(cells, cells.shape[dim] - width, cells.shape[dim], axis=dim)
        cells = jnp.concatenate(
            [
                lax.ppermute(tail, axis, [(i, (i + 1) % count) for i in range(ends)]),
                cells,
                lax.ppermute(head, axis, [((i + 1) % count, i) for i in range(ends)]),
            ],
            axis=dim,
        )
    return cells


def on_device(basis, inverse_rows, block_diag, couple, coarse_basis, coarse_factor):
    highest = lax.Precision.HIGHEST
    vector = basis[M - 1]
    rounded = vector.astype(jnp.bfloat16)
    extended = padded_2(rounded, (("gx", 2), ("gy", 3)), 2)
    columns = extended.reshape(S, C * (CX + 4) * (CY + 4), CZ)
    local_part = jnp.einsum(
        "cxyjz,sjz->scxyz", inverse_rows, columns, preferred_element_type=jnp.float32
    )
    coarse_rhs = jnp.einsum("kcxyz,scxyz->ks", coarse_basis, vector, precision=highest)
    factor_block = coarse_factor
    factor_image = jnp.dot(
        factor_block,
        lax.all_gather(coarse_rhs, ("gx", "gy", "gz"), axis=0, tiled=True),
        precision=highest,
        preferred_element_type=jnp.float32,
    )
    factor_block = coarse_factor
    coarse_coef = lax.psum_scatter(
        jnp.dot(
            factor_block.T, factor_image, precision=highest, preferred_element_type=jnp.float32
        ),
        ("gx", "gy", "gz"),
        scatter_dimension=0,
        tiled=True,
    )
    correction = jnp.einsum("kcxyz,ks->scxyz", coarse_basis, coarse_coef, precision=highest)
    preconditioned = local_part + correction
    padded = padded_2(preconditioned, (("gx", 2), ("gy", 3), ("gz", 4)), 1)
    applied = jnp.einsum("cdxyz,sdxyz->scxyz", block_diag, preconditioned, precision=highest)
    applied = (
        applied
        - couple[0] * padded[:, :, :-2, 1:-1, 1:-1]
        - couple[1] * padded[:, :, 2:, 1:-1, 1:-1]
    )
    applied = (
        applied
        - couple[2] * padded[:, :, 1:-1, :-2, 1:-1]
        - couple[3] * padded[:, :, 1:-1, 2:, 1:-1]
    )
    applied = (
        applied
        - couple[4] * padded[:, :, 1:-1, 1:-1, :-2]
        - couple[5] * padded[:, :, 1:-1, 1:-1, 2:]
    )
    unknowns = float(
        C * CX * CY * CZ * lax.axis_size("gx") * lax.axis_size("gy") * lax.axis_size("gz")
    )
    local_products = jnp.einsum("mscxyz,scxyz->sm", basis, applied, precision=highest)
    projections = lax.psum(local_products, ("gx", "gy", "gz")) / unknowns
    remainder = applied - jnp.einsum("sm,mscxyz->scxyz", projections, basis, precision=highest)
    squares = lax.psum(jnp.sum(remainder * remainder, axis=(1, 2, 3, 4)), ("gx", "gy", "gz"))
    norm_scale = jnp.sqrt(squares / unknowns + epsilon)
    krylov_next = remainder / norm_scale[:, None, None, None, None]
    hessenberg = jnp.concatenate([projections, norm_scale[:, None]], axis=1)
    return (krylov_next, preconditioned, hessenberg)


def solution(mesh):
    return jax.shard_map(
        on_device,
        mesh=mesh,
        in_specs=(
            P(None, None, None, "gx", "gy", "gz"),
            P(None, "gx", "gy", None, "gz"),
            P(None, None, "gx", "gy", "gz"),
            P(None, None, "gx", "gy", "gz"),
            P(None, None, "gx", "gy", "gz"),
            P(("gx", "gy", "gz"), None),
        ),
        out_specs=(P(None, None, "gx", "gy", "gz"), P(None, None, "gx", "gy", "gz"), P()),
        check_vma=False,
    )
```

profile of v0, /device:TPU:0, one launch (start us, length us, event | category | flops | bytes accessed | tf_op | source)
XLA Modules:
  0.0 350.4 jit_solution(5620877075645078447)
XLA Ops:
  7.2 0.8 slice.69
  8.1 4.8 %collective-permute-start = (bf16[4,4,2,2,128]{4,0,3,2,1:T(4,128)(2,1)S(1)}, bf16[4,4,2,2,128]{4,0,3,2,1:T(4,128)(2,1)S(1)}, u32[]{:S(2)}, u32[]{:S(2)}) collective-permute-start(bf16[4,4,2,2,128]{4,0,3,2,1:T(4,128)(2,1)S(1)} %get-tuple-element.35), channel_id=1, source_target_pairs={{0,16},{1,17},{2,18},{3,19},{4,20},{5,21},{6,22},{7,23},{8,24},{9,... | collective-permute-start | bytes 49160 | tf_op jit(solution)/shard_map/ppermute | solution.py:25
  13.0 1.3 collective-permute-start.1
  14.3 1.5 convolution_bitcast_fusion.1
  15.8 69.3 %all-gather = f32[32,16,4]{1,2,0:T(4,128)S(1)} all-gather(f32[1,16,4]{1,2,0:T(4,128)S(1)} %convolution_bitcast_fusion.1), channel_id=1, replica_groups=mesh['gx'=2,'gy'=4,'gz'=4] {'gx','gy','gz'}, dimensions={0}, use_global_device_ids=true | all-gather | bytes 8448 | tf_op jit(solution)/shard_map/all_gather | solution.py:47
  85.1 0.1 reshape.12
  85.2 0.1 fusion.26
  85.3 0.2 convolution_bitcast_fusion
  85.5 0.9 copy.210
  86.4 3.4 copy.167
  89.8 0.1 pad_maximum_fusion.17
  89.9 1.3 collective-permute-start.2
  91.2 1.3 collective-permute-start.3
  92.5 123.4 %reduce-scatter.4.cloned.1.call-done = f32[16,4]{1,0:T(8,128)} async-done(((f32[512,4]{1,0:T(8,128)}), f32[16,4]{1,0:T(8,128)}) %reduce-scatter.4.cloned.1.call-update) | async-done | bytes 272
  215.9 1.1 fusion.4
  217.0 0.1 pad_maximum_fusion
  217.1 0.2 copy.200
  217.4 10.6 %fusion.25 = f32[128,4,4,4,2]{3,1,4,2,0:T(4,128)} fusion(bf16[4,192,128,1,1]{1,0,4,3,2:T(4,128)(2,1)S(1)} %copy.200, bf16[4,4,2,192,128]{3,1,2,0,4:T(4,128)(2,1)S(1)} %copy.167), kind=kOutput, calls=%fused_computation.61 | convolution fusion | flops 6291456 | bytes 1835008 | tf_op jit(solution)/shard_map/cxyjz,sjz->scxyz/dot_general | solution.py:40
  228.0 2.1 copy.168
  230.2 2.4 collective-permute-start.4
  232.6 1.3 collective-permute-start.5
  233.9 0.1 collective-permute-done.4
  234.0 4.2 %collective-permute-done.5 = f32[4,4,1,2,128]{4,1,3,2,0:T(4,128)S(1)} collective-permute-done((f32[4,4,1,2,128]{4,1,3,2,0:T(4,128)S(1)}, f32[4,4,1,2,128]{4,1,3,2,0:T(4,128)S(1)}, u32[]{:S(2)}, u32[]{:S(2)}) %collective-permute-start.5) | collective-permute-done | bytes 16416 | tf_op jit(solution)/shard_map/ppermute | solution.py:27
  238.4 1.3 collective-permute-start.6
  239.7 1.3 collective-permute-start.7
  241.0 0.9 copy.174
  242.0 1.7 copy.173
  243.8 0.1 copy.192
  243.8 0.1 copy.191
  243.9 0.1 copy.193
  244.0 0.1 pad_maximum_fusion.1
  244.1 0.2 fusion.21
  244.3 1.3 collective-permute-start.8
  245.6 1.5 collective-permute-start.9
  247.1 9.4 %fusion.27 = f32[4,2,128,4,4]{3,4,2,1,0:T(4,128)} fusion(f32[4,4,4,2,128]{1,0,4,3,2:T(4,128)} %copy.173, f32[4,4,4,2,128]{1,0,4,3,2:T(4,128)S(1)} %copy.174), kind=kOutput, calls=%fused_computation.63 | convolution fusion | flops 786432 | bytes 196608 | tf_op jit(solution)/shard_map/cdxyz,sdxyz->scxyz/dot_general | solution.py:63
  256.5 2.0 copy.175
  258.5 0.5 pad_maximum_fusion.6
  259.0 0.2 fusion.10
  259.2 1.4 fusion.2
  260.7 40.3 %psum.14 = f32[4,6]{1,0:T(4,128)S(1)} all-reduce(f32[4,6]{1,0:T(4,128)S(1)} %bitcast.72), channel_id=1, replica_groups=mesh['gx'=2,'gy'=4,'gz'=4] {'gx','gy','gz'}, use_global_device_ids=true, to_apply=%region_1.0 | all-reduce | flops 24 | bytes 192 | tf_op jit(solution)/shard_map/psum | solution.py:83
  301.0 0.8 fusion
  301.8 0.1 multiply_reduce_fusion
  301.9 0.7 copy.199
  302.6 39.4 %psum.15 = f32[4]{0:T(128)S(1)} all-reduce(f32[4]{0:T(128)S(1)} %multiply_reduce_fusion), channel_id=1, replica_groups=mesh['gx'=2,'gy'=4,'gz'=4] {'gx','gy','gz'}, use_global_device_ids=true, to_apply=%region_3.0 | all-reduce | flops 4 | bytes 32 | tf_op jit(solution)/shard_map/psum | solution.py:85
  342.0 0.1 copy.197
  342.1 0.7 pad_maximum_fusion.18
  342.8 0.1 broadcast_divide_fusion
  342.9 0.7 copy.198
  (44 shorter events, 0.4 us)
Async XLA Ops:
  7.2 78.0 %copy-start = (f32[16,512]{1,0:T(8,128)S(1)}, f32[16,512]{1,0:T(8,128)}, u32[]{:S(2)}) copy-start(f32[16,512]{1,0:T(8,128)} %param.11) | copy-start | bytes 98308
  7.2 208.7 %reduce-scatter.4.cloned.1.call-start = ((), (), s32[]{:S(2)}) async-start(), calls=%async_computation.1 | async-start | bytes 270336
  8.1 81.7 %collective-permute-start = (bf16[4,4,2,2,128]{4,0,3,2,1:T(4,128)(2,1)S(1)}, bf16[4,4,2,2,128]{4,0,3,2,1:T(4,128)(2,1)S(1)}, u32[]{:S(2)}, u32[]{:S(2)}) collective-permute-start(bf16[4,4,2,2,128]{4,0,3,2,1:T(4,128)(2,1)S(1)} %get-tuple-element.35), channel_id=1, source_target_pairs={{0,16},{1,17},{2,18},{3,19},{4,20},{5,21},{6,22},{7,23},{8,24},{9,... | collective-permute-start | bytes 49160 | tf_op jit(solution)/shard_map/ppermute | solution.py:25
  13.0 76.8 %collective-permute-start.1 = (bf16[4,4,2,2,128]{4,0,3,2,1:T(4,128)(2,1)S(1)}, bf16[4,4,2,2,128]{4,0,3,2,1:T(4,128)(2,1)S(1)}, u32[]{:S(2)}, u32[]{:S(2)}) collective-permute-start(bf16[4,4,2,2,128]{4,0,3,2,1:T(4,128)(2,1)S(1)} %get-tuple-element.36), channel_id=1, source_target_pairs={{16,0},{17,1},{18,2},{19,3},{20,4},{21,5},{22,6},{23,7},{24,8},{25... | collective-permute-start | bytes 49160 | tf_op jit(solution)/shard_map/ppermute | solution.py:27
  86.4 129.5 %copy-start.2 = (f32[16,4,4,2,128]{4,3,2,1,0:T(2,128)S(1)}, f32[16,4,4,2,128]{4,3,2,1,0:T(2,128)}, u32[]{:S(2)}) copy-start(f32[16,4,4,2,128]{4,3,2,1,0:T(2,128)} %param.10) | copy-start | bytes 786436
  89.9 127.1 %collective-permute-start.2 = (bf16[4,4,8,2,128]{4,0,3,2,1:T(4,128)(2,1)S(1)}, bf16[4,4,8,2,128]{4,0,3,2,1:T(4,128)(2,1)S(1)}, u32[]{:S(2)}, u32[]{:S(2)}) collective-permute-start(bf16[4,4,8,2,128]{4,0,3,2,1:T(4,128)(2,1)S(1)} %pad_maximum_fusion.17), channel_id=1, source_target_pairs={{0,4},{4,8},{8,12},{1,5},{5,9},{9,13},{2,6},{6,10},{10,14},{3,7},{... | collective-permute-start | bytes 196616 | tf_op jit(solution)/shard_map/ppermute | solution.py:25
  91.2 125.8 %collective-permute-start.3 = (bf16[4,4,8,2,128]{4,0,3,2,1:T(4,128)(2,1)S(1)}, bf16[4,4,8,2,128]{4,0,3,2,1:T(4,128)(2,1)S(1)}, u32[]{:S(2)}, u32[]{:S(2)}) collective-permute-start(bf16[4,4,8,2,128]{4,0,3,2,1:T(4,128)(2,1)S(1)} %pad_maximum_fusion.17), channel_id=1, source_target_pairs={{4,0},{8,4},{12,8},{5,1},{9,5},{13,9},{6,2},{10,6},{14,10},{7,3},{... | collective-permute-start | bytes 196616 | tf_op jit(solution)/shard_map/ppermute | solution.py:27
  228.0 13.0 %copy-start.3 = (f32[6,4,4,2,128]{4,3,2,1,0:T(2,128)S(1)}, f32[6,4,4,2,128]{4,3,2,1,0:T(2,128)}, u32[]{:S(2)}) copy-start(f32[6,4,4,2,128]{4,3,2,1,0:T(2,128)} %param.9) | copy-start | bytes 294916
  228.0 13.0 %copy-start.4 = (f32[4,4,4,2,128]{4,3,2,1,0:T(2,128)S(1)}, f32[4,4,4,2,128]{4,3,2,1,0:T(2,128)}, u32[]{:S(2)}) copy-start(f32[4,4,4,2,128]{4,3,2,1,0:T(2,128)} %param.8) | copy-start | bytes 196612
  230.2 3.9 %collective-permute-start.4 = (f32[4,4,1,2,128]{4,1,3,2,0:T(4,128)S(1)}, f32[4,4,1,2,128]{4,1,3,2,0:T(4,128)S(1)}, u32[]{:S(2)}, u32[]{:S(2)}) collective-permute-start(f32[4,4,1,2,128]{4,1,3,2,0:T(4,128)S(1)} %copy.177), channel_id=1, source_target_pairs={{0,16},{1,17},{2,18},{3,19},{4,20},{5,21},{6,22},{7,23},{8,24},{9,... | collective-permute-start | bytes 49160 | tf_op jit(solution)/shard_map/ppermute | solution.py:25
  232.6 5.6 %collective-permute-start.5 = (f32[4,4,1,2,128]{4,1,3,2,0:T(4,128)S(1)}, f32[4,4,1,2,128]{4,1,3,2,0:T(4,128)S(1)}, u32[]{:S(2)}, u32[]{:S(2)}) collective-permute-start(f32[4,4,1,2,128]{4,1,3,2,0:T(4,128)S(1)} %copy.180), channel_id=1, source_target_pairs={{16,0},{17,1},{18,2},{19,3},{20,4},{21,5},{22,6},{23,7},{24,8},{25... | collective-permute-start | bytes 49160 | tf_op jit(solution)/shard_map/ppermute | solution.py:27
  238.4 5.5 %collective-permute-start.6 = (f32[4,4,6,1,128]{4,1,3,2,0:T(4,128)S(1)}, f32[4,4,6,1,128]{4,1,3,2,0:T(4,128)S(1)}, u32[]{:S(2)}, u32[]{:S(2)}) collective-permute-start(f32[4,4,6,1,128]{4,1,3,2,0:T(4,128)S(1)} %copy.185), channel_id=1, source_target_pairs={{0,4},{4,8},{8,12},{1,5},{5,9},{9,13},{2,6},{6,10},{10,14},{3,7},{... | collective-permute-start | bytes 147464 | tf_op jit(solution)/shard_map/ppermute | solution.py:25
  239.7 4.2 %collective-permute-start.7 = (f32[4,4,6,1,128]{4,1,3,2,0:T(4,128)S(1)}, f32[4,4,6,1,128]{4,1,3,2,0:T(4,128)S(1)}, u32[]{:S(2)}, u32[]{:S(2)}) collective-permute-start(f32[4,4,6,1,128]{4,1,3,2,0:T(4,128)S(1)} %copy.188), channel_id=1, source_target_pairs={{4,0},{8,4},{12,8},{5,1},{9,5},{13,9},{6,2},{10,6},{14,10},{7,3},{... | collective-permute-start | bytes 147464 | tf_op jit(solution)/shard_map/ppermute | solution.py:27
  244.3 14.2 %collective-permute-start.8 = (f32[4,4,6,4,1]{4,3,2,1,0:T(4,128)S(1)}, f32[4,4,6,4,1]{4,3,2,1,0:T(4,128)S(1)}, u32[]{:S(2)}, u32[]{:S(2)}) collective-permute-start(f32[4,4,6,4,1]{4,3,2,1,0:T(4,128)S(1)} %get-tuple-element.23), channel_id=1, source_target_pairs={{0,1},{1,2},{2,3},{4,5},{5,6},{6,7},{8,9},{9,10},{10,11},{12,13},{... | collective-permute-start | bytes 4616 | tf_op jit(solution)/shard_map/ppermute | solution.py:25
  245.6 12.9 %collective-permute-start.9 = (f32[4,4,6,4,1]{4,3,2,1,0:T(4,128)S(1)}, f32[4,4,6,4,1]{4,3,2,1,0:T(4,128)S(1)}, u32[]{:S(2)}, u32[]{:S(2)}) collective-permute-start(f32[4,4,6,4,1]{4,3,2,1,0:T(4,128)S(1)} %get-tuple-element.24), channel_id=1, source_target_pairs={{1,0},{2,1},{3,2},{5,4},{6,5},{7,6},{9,8},{10,9},{11,10},{13,12},{... | collective-permute-start | bytes 4616 | tf_op jit(solution)/shard_map/ppermute | solution.py:27
  256.5 2.7 copy-start.1
Sparse Core Ops, SparseCore 0:
  86.5 129.3 reduce-scatter.3
where the time goes:
time: 351 us; the launch traced here: 350 us
  blocking collectives  149 us (42%)
  waiting for transfers between devices  128 us (36%)
  matrix products  25.1 us (7%)
  starting transfers between devices  17.8 us (5%)
  between operations  14.5 us (4%)
  local copies, waits for them, and re-layouts  14.2 us (4%)
    unnamed x2, waiting for transfers between devices  123 us
    all_gather x1, blocking collectives, on_device(): lax.all_gather(coarse_rhs, ('gx', 'gy', 'gz'), axis=0, tiled=True)  69.3 us
    psum x1, blocking collectives, on_device(): projections = lax.psum(local_products, ('gx', 'gy', 'gz')) / unknowns  40.3 us
    psum x1, blocking collectives, on_device(): lax.psum(jnp.sum(remainder * remainder, axis=(1, 2, 3, 4)), ('gx', 'gy',...  39.4 us
    ppermute x5, starting transfers between devices, padded_2(): lax.ppermute(tail, axis, [(i, (i + 1) % count) for i in range(ends)])  11.1 us
    dot_general x1, matrix products, on_device(): jnp.einsum('cxyjz,sjz->scxyz', inverse_rows, columns, preferred_element_t...  10.6 us
    dot_general x1, matrix products, on_device(): jnp.einsum('cdxyz,sdxyz->scxyz', block_diag, preconditioned, precision=hi...  9.39 us
  transfers between devices with their start and end apart: 11, of which 3 were waited for; matrix products, arithmetic and copies ran while one was open for 6% of the time, Pallas kernels for 0%

commit v1 on v0

v1 whole, which is shorter than its diff:
```python
import jax
import jax.numpy as jnp
from jax import lax
from jax.sharding import PartitionSpec as P

C = 4
CX = 4
CY = 2
CZ = 128
S = 4
M = 6
AXES = ("gx", "gy", "gz")

epsilon = 1e-06


def swap_rounds(axis, low_side, high_side):
    count = lax.axis_size(axis)
    odd = lax.axis_index(axis) % 2 == 1
    first = [(i, i + 1) for i in range(0, count - 1, 2)]
    second = [(i, i + 1) for i in range(1, count - 1, 2)]

    def both(pairs):
        return pairs + [(j, i) for i, j in pairs]

    got_first = lax.ppermute(jnp.where(odd, low_side, high_side), axis, both(first))
    if second:
        got_second = lax.ppermute(jnp.where(odd, high_side, low_side), axis, both(second))
    else:
        got_second = jnp.zeros_like(got_first)
    return jnp.where(odd, got_first, got_second), jnp.where(odd, got_second, got_first)


def padded_2(cells, sides, width):
    for axis, dim in sides:
        head = lax.slice_in_dim(cells, 0, width, axis=dim)
        tail = lax.slice_in_dim(cells, cells.shape[dim] - width, cells.shape[dim], axis=dim)
        below, above = swap_rounds(axis, head, tail)
        cells = jnp.concatenate([below, cells, above], axis=dim)
    return cells


def gathered(row, devices):
    sent = jnp.broadcast_to(row.reshape(1, 1, -1), (devices, 1, row.size))
    return lax.all_to_all(sent, AXES, 0, 0, tiled=True)


def total(row, devices):
    return jnp.sum(gathered(row, devices), axis=(0, 1))


def on_device(basis, inverse_rows, block_diag, couple, coarse_basis, coarse_factor):
    highest = lax.Precision.HIGHEST
    devices = lax.axis_size("gx") * lax.axis_size("gy") * lax.axis_size("gz")
    kinds = coarse_basis.shape[0]
    vector = basis[M - 1]
    rounded = vector.astype(jnp.bfloat16)
    extended = padded_2(rounded, (("gx", 2), ("gy", 3)), 2)
    columns = extended.reshape(S, C * (CX + 4) * (CY + 4), CZ)
    local_part = jnp.einsum(
        "cxyjz,sjz->scxyz", inverse_rows, columns, preferred_element_type=jnp.float32
    )
    coarse_rhs = jnp.einsum("kcxyz,scxyz->ks", coarse_basis, vector, precision=highest)
    all_rhs = gathered(coarse_rhs, devices).reshape(devices * kinds, S)
    factor_image = jnp.dot(coarse_factor, all_rhs, precision=highest)
    shares = jnp.dot(coarse_factor.T, factor_image, precision=highest)
    shares = lax.all_to_all(
        shares.reshape(devices, 1, kinds * S), AXES, 0, 0, tiled=True
    )
    coarse_coef = jnp.sum(shares, axis=(0, 1)).reshape(kinds, S)
    correction = jnp.einsum("kcxyz,ks->scxyz", coarse_basis, coarse_coef, precision=highest)
    preconditioned = local_part + correction
    p = preconditioned
    x_low, x_high = swap_rounds("gx", p[:, :, :1], p[:, :, -1:])
    y_low, y_high = swap_rounds("gy", p[:, :, :, :1], p[:, :, :, -1:])
    z_low, z_high = swap_rounds("gz", p[..., :1], p[..., -1:])
    px = jnp.concatenate([x_low, p, x_high], axis=2)
    py = jnp.concatenate([y_low, p, y_high], axis=3)
    pz = jnp.concatenate([z_low, p, z_high], axis=4)
    applied = sum(block_diag[:, d] * p[:, d : d + 1] for d in range(C))
    applied = applied - couple[0] * px[:, :, :-2] - couple[1] * px[:, :, 2:]
    applied = applied - couple[2] * py[:, :, :, :-2] - couple[3] * py[:, :, :, 2:]
    applied = applied - couple[4] * pz[..., :-2] - couple[5] * pz[..., 2:]
    unknowns = float(C * CX * CY * CZ * devices)
    local_products = jnp.einsum("mscxyz,scxyz->sm", basis, applied, precision=highest)
    projections = total(local_products, devices).reshape(S, M) / unknowns
    remainder = applied - jnp.einsum("sm,mscxyz->scxyz", projections, basis, precision=highest)
    squares = total(jnp.sum(remainder * remainder, axis=(1, 2, 3, 4)), devices)
    norm_scale = jnp.sqrt(squares / unknowns + epsilon)
    krylov_next = remainder / norm_scale[:, None, None, None, None]
    hessenberg = jnp.concatenate([projections, norm_scale[:, None]], axis=1)
    return (krylov_next, preconditioned, hessenberg)


def solution(mesh):
    return jax.shard_map(
        on_device,
        mesh=mesh,
        in_specs=(
            P(None, None, None, "gx", "gy", "gz"),
            P(None, "gx", "gy", None, "gz"),
            P(None, None, "gx", "gy", "gz"),
            P(None, None, "gx", "gy", "gz"),
            P(None, None, "gx", "gy", "gz"),
            P(AXES, None),
        ),
        out_specs=(P(None, None, "gx", "gy", "gz"), P(None, None, "gx", "gy", "gz"), P()),
        check_vma=False,
    )
```

time: 351 us -> 125 us (0.36)
  blocking collectives: 149 us -> 0 us
  waiting for transfers between devices: 128 us -> 26.9 us
  local copies, waits for them, and re-layouts: 14.2 us -> 44.2 us
  other arithmetic: 1.99 us -> 19 us
  matrix products: 25.1 us -> 8.26 us
  between operations: 14.5 us -> 0.99 us
  starting transfers between devices: 17.8 us -> 24.3 us
    unnamed x2 -> x0, waiting for transfers between devices: 123 us -> none
    psum x2 -> x0, blocking collectives: 79.8 us -> none  [the longest x1 40.3 us: on_device(): projections = lax.psum(local_products, ('gx', 'gy', 'gz')) / unknowns]
    all_gather x1 -> x0, blocking collectives: 69.3 us -> none  [on_device(): lax.all_gather(coarse_rhs, ('gx', 'gy', 'gz'), axis=0, tiled=True)]
    all_to_all x0 -> x4, waiting for transfers between devices: none -> 17.5 us  [the longest x3 11.5 us: gathered(): return lax.all_to_all(sent, AXES, 0, 0, tiled=True)]
    all_to_all x0 -> x4, starting transfers between devices: none -> 17.1 us  [the longest x3 12.1 us: gathered(): return lax.all_to_all(sent, AXES, 0, 0, tiled=True)]
    ppermute x10 -> x8, starting transfers between devices: 17.8 us -> 7.21 us  [the longest x5 4.47 us: swap_rounds(): lax.ppermute(jnp.where(odd, low_side, high_side), axis, both(first))]
    dot_general x3 -> x2, matrix products: 9.67 us -> 0.69 us  [the longest x1 0.54 us: on_device(): factor_image = jnp.dot(coarse_factor, all_rhs, precision=highest)]
    slice x8 -> x4, local copies, waits for them, and re-layouts: 0.27 us -> 8.22 us  [the longest x2 4.14 us: on_device(): applied = applied - couple[4] * pz[..., :-2] - couple[5] * pz[..., 2:]]
  transfers between devices with their start and end apart: 11 -> 12, of which waited for: 3 -> 5; matrix products, arithmetic and copies ran while one was open for 6% -> 23% of each run, Pallas kernels for 0% -> 0%
where the time goes in v1:
time: 125 us; the launch traced here: 124 us
  local copies, waits for them, and re-layouts  44.2 us (35%)
  waiting for transfers between devices  26.9 us (22%)
  starting transfers between devices  24.3 us (19%)
  other arithmetic  19 us (15%)
  matrix products  8.26 us (7%)
    unnamed x24, local copies, waits for them, and re-layouts  12.7 us
    all_to_all x3, starting transfers between devices, gathered(): return lax.all_to_all(sent, AXES, 0, 0, tiled=True)  12.1 us
    all_to_all x3, waiting for transfers between devices, gathered(): return lax.all_to_all(sent, AXES, 0, 0, tiled=True)  11.5 us
    ppermute x5, waiting for transfers between devices, swap_rounds(): lax.ppermute(jnp.where(odd, low_side, high_side), axis, both(first))  9.38 us
    all_to_all x1, waiting for transfers between devices, on_device(): lax.all_to_all(shares.reshape(devices, 1, kinds * S), AXES, 0, 0, tiled=T...  6.02 us
    all_to_all x1, starting transfers between devices, on_device(): lax.all_to_all(shares.reshape(devices, 1, kinds * S), AXES, 0, 0, tiled=T...  4.95 us
    concatenate x1, other arithmetic, on_device(): py = jnp.concatenate([y_low, p, y_high], axis=3)  4.47 us
    ppermute x5, starting transfers between devices, swap_rounds(): lax.ppermute(jnp.where(odd, low_side, high_side), axis, both(first))  4.47 us
  transfers between devices with their start and end apart: 12, of which 5 were waited for; matrix products, arithmetic and copies ran while one was open for 23% of the time, Pallas kernels for 0%

profile of v1, /device:TPU:0, one launch (start us, length us, event | category | flops | bytes accessed | tf_op | source)
XLA Modules:
  0.0 123.6 jit_solution(3010204603293685830)
XLA Ops:
  0.7 0.8 slice.94
  1.6 3.0 %collective-permute-start = (bf16[4,4,2,2,128]{4,0,3,2,1:T(4,128)(2,1)S(1)}, bf16[4,4,2,2,128]{4,0,3,2,1:T(4,128)(2,1)S(1)}, u32[]{:S(2)}, u32[]{:S(2)}) collective-permute-start(bf16[4,4,2,2,128]{4,0,3,2,1:T(4,128)(2,1)S(1)} %slice_select_fusion.2), channel_id=1, source_target_pairs={{0,16},{16,0},{1,17},{17,1},{2,18},{18,2},{3,19},{19,3},{4,20},{20... | collective-permute-start | bytes 49160 | tf_op jit(solution)/shard_map/ppermute | solution.py:26
  4.6 1.5 %convolution_bitcast_fusion.1 = f32[16,4]{1,0:T(8,128)S(1)} fusion(f32[16,4,4,2,128]{4,3,2,1,0:T(2,128)} %param.10, f32[1,4,4,4,2,128]{5,4,3,2,1,0:T(2,128)S(1)} %slice.94), kind=kOutput, calls=%fused_computation.8 | convolution fusion | flops 3145728 | bytes 327936 | tf_op jit(solution)/shard_map/kcxyz,scxyz->ks/dot_general | solution.py:63
  6.8 4.9 %all-to-all-start = ((f32[32,1,64]{2,1,0:T(1,128)}), f32[32,1,64]{2,1,0:T(1,128)S(1)}, u32[]{:S(2)}, u32[]{:S(2)}) async-start(f32[32,1,64]{2,1,0:T(1,128)} %broadcast_in_dim.29), calls=%async_computation | async-start | bytes 32768 | tf_op jit(solution)/shard_map/all_to_all | solution.py:45
  11.8 0.8 slice_bitcast_fusion.9
  12.6 0.8 slice_bitcast_fusion.13
  13.4 4.5 %copy.157 = bf16[4,4,2,192,128]{3,1,2,0,4:T(4,128)(2,1)} copy(bf16[4,4,2,192,128]{4,3,2,1,0:T(8,128)(2,1)} %param.7) | data formatting | bytes 3145728 | tf_op args[1]
  18.0 0.9 all-to-all-done
  19.4 0.7 reduce.3
  21.1 0.8 reshape.62
  21.9 5.0 %all-to-all-start.1 = ((f32[32,1,64]{2,1,0:T(1,128)}), f32[32,1,64]{2,1,0:T(1,128)S(1)}, u32[]{:S(2)}, u32[]{:S(2)}) async-start(f32[32,1,64]{2,1,0:T(1,128)} %bitcast.7), calls=%async_computation.1 | async-start | bytes 32768 | tf_op jit(solution)/shard_map/all_to_all | solution.py:67
  27.9 6.0 %all-to-all-done.1 = f32[32,1,64]{2,1,0:T(1,128)S(1)} async-done(((f32[32,1,64]{2,1,0:T(1,128)}), f32[32,1,64]{2,1,0:T(1,128)S(1)}, u32[]{:S(2)}, u32[]{:S(2)}) %all-to-all-start.1) | async-done | bytes 8224 | tf_op jit(solution)/shard_map/all_to_all | solution.py:67
  34.5 2.0 %copy.164 = f32[4,4,4,2,128]{0,2,3,1,4:T(4,128)} copy(f32[4,4,4,2,128]{4,0,3,2,1:T(4,128)S(1)} %fusion.4) | data formatting | bytes 131072 | tf_op jit(solution)/shard_map/kcxyz,ks->scxyz/dot_general | solution.py:71
  36.8 3.4 %bitcast_add_fusion = f32[4,4,4,2,128]{0,2,3,1,4:T(4,128)S(1)} fusion(f32[4,4,4,2,128]{0,2,3,1,4:T(4,128)} %copy.164, bf16[4,192,128,1,1]{1,0,4,3,2:T(4,128)(2,1)S(1)} %copy.209, bf16[4,4,2,192,128]{3,1,2,0,4:T(4,128)(2,1)} %copy.157), kind=kOutput, calls=%fused_computation.5 | convolution fusion | flops 6307840 | bytes 1900544 | tf_op jit(solution)/shard_map/cxyjz,sjz->scxyz/dot_general | solution.py:60
  40.3 1.4 %slice_select_fusion.1 = (f32[4,4,4,1,128]{0,2,3,1,4:T(4,128)}, f32[4,4,4,1,128]{0,2,3,1,4:T(4,128)S(1)}) fusion(f32[4,4,4,2,128]{0,2,3,1,4:T(4,128)S(1)} %bitcast_add_fusion, pred[]{:T(512)S(6)} %eq.17), kind=kLoop, calls=%fused_computation.14 | loop fusion | flops 16384 | bytes 131073 | tf_op jit(solution)/shard_map/jit(_where)/select_n | solution.py:26
  41.6 1.4 %broadcast_select_fusion.2 = f32[4,4,1,2,128]{0,2,3,1,4:T(1,128)} fusion(pred[]{:T(512)S(6)} %eq.18, f32[4,4,4,2,128]{0,2,3,1,4:T(4,128)S(1)} %bitcast_add_fusion), kind=kLoop, calls=%fused_computation.12 | loop fusion | flops 4096 | bytes 49153 | tf_op jit(solution)/shard_map/jit(_where)/select_n | solution.py:26
  43.0 1.5 %slice_bitcast_fusion.3 = (f32[4,4,2,128]{0,1,2,3:T(4,128)}, f32[4,4,2,128]{0,1,2,3:T(4,128)}, f32[4,4,2,128]{0,1,2,3:T(4,128)}, f32[4,4,2,128]{0,1,2,3:T(4,128)}) fusion(f32[4,4,4,2,128]{0,2,3,1,4:T(4,128)S(1)} %bitcast_add_fusion), kind=kLoop, calls=%fused_computation.22 | loop fusion | bytes 131072 | tf_op jit(solution)/shard_map/mul | solution.py:80
  44.5 1.2 copy.178
  45.7 2.2 %copy.185 = f32[4,4,4,1,128]{4,2,3,1,0:T(4,128)} copy(f32[4,4,4,1,128]{0,2,3,1,4:T(4,128)} %get-tuple-element.28) | data formatting | bytes 65536 | tf_op jit(solution)/shard_map/jit(_where)/select_n | solution.py:26
  47.9 1.2 copy.186
  49.1 1.3 %collective-permute-start.5 = (f32[4,4,4,1,128]{4,2,3,1,0:T(4,128)}, f32[4,4,4,1,128]{4,2,3,1,0:T(4,128)}, u32[]{:S(2)}, u32[]{:S(2)}) collective-permute-start(f32[4,4,4,1,128]{4,2,3,1,0:T(4,128)} %copy.186), channel_id=1, source_target_pairs={{4,8},{8,4},{5,9},{9,5},{6,10},{10,6},{7,11},{11,7},{20,24},{24,20... | collective-permute-start | bytes 98312 | tf_op jit(solution)/shard_map/ppermute | solution.py:28
  50.9 0.8 collective-permute-start.7
  52.4 1.2 copy.227
  53.6 1.2 %copy.229 = f32[4,4,2,128]{3,2,1,0:T(2,128)S(1)} copy(f32[4,4,2,128]{0,1,2,3:T(4,128)} %get-tuple-element.21) | data formatting | bytes 32768
  54.8 1.2 %copy.231 = f32[4,4,2,128]{3,2,1,0:T(2,128)S(1)} copy(f32[4,4,2,128]{0,1,2,3:T(4,128)} %get-tuple-element.20) | data formatting | bytes 32768
  56.1 1.2 %copy.233 = f32[4,4,2,128]{3,2,1,0:T(2,128)S(1)} copy(f32[4,4,2,128]{0,1,2,3:T(4,128)} %get-tuple-element.19) | data formatting | bytes 32768
  57.3 9.4 %collective-permute-done.3 = f32[4,4,1,2,128]{0,2,3,1,4:T(1,128)} collective-permute-done((f32[4,4,1,2,128]{0,2,3,1,4:T(1,128)}, f32[4,4,1,2,128]{0,2,3,1,4:T(1,128)}, u32[]{:S(2)}, u32[]{:S(2)}) %collective-permute-start.3) | collective-permute-done | bytes 16416 | tf_op jit(solution)/shard_map/ppermute | solution.py:26
  66.7 1.8 %broadcast_select_fusion.1 = (f32[4,4,1,2,128]{0,2,3,1,4:T(1,128)S(1)}, f32[4,4,1,2,128]{0,2,3,1,4:T(1,128)S(1)}) fusion(f32[4,4,1,2,128]{0,2,3,1,4:T(1,128)} %collective-permute-done.3, pred[]{:T(512)S(6)} %eq.18), kind=kLoop, calls=%fused_computation.11 | loop fusion | flops 8192 | bytes 49153 | tf_op jit(solution)/shard_map/jit(_where)/select_n | solution.py:31
  69.7 1.4 %copy.187 = f32[4,4,4,1,128]{0,2,3,1,4:T(4,128)S(1)} copy(f32[4,4,4,1,128]{4,2,3,1,0:T(4,128)} %collective-permute-done.4) | data formatting | bytes 65536 | tf_op jit(solution)/shard_map/ppermute | solution.py:26
  71.1 2.2 %copy.188 = f32[4,4,4,1,128]{0,2,3,1,4:T(4,128)} copy(f32[4,4,4,1,128]{4,2,3,1,0:T(4,128)} %collective-permute-done.5) | data formatting | bytes 65536 | tf_op jit(solution)/shard_map/ppermute | solution.py:28
  73.3 1.6 %broadcast_select_fusion.4 = (f32[4,4,4,1,128]{0,2,3,1,4:T(4,128)S(1)}, f32[4,4,4,1,128]{0,2,3,1,4:T(4,128)S(1)}) fusion(f32[4,4,4,1,128]{0,2,3,1,4:T(4,128)S(1)} %copy.187, f32[4,4,4,1,128]{0,2,3,1,4:T(4,128)} %copy.188, pred[]{:T(512)S(6)} %eq.17), kind=kLoop, calls=%fused_computation.24 | loop fusion | flops 16384 | bytes 131073 | tf_op jit(solution)/shard_map/jit(_where)/select_n | solution.py:31
  74.9 4.5 %pad_maximum_fusion.3 = (f32[4,4,4,2,128]{0,2,3,1,4:T(4,128)}, f32[4,4,4,2,128]{0,2,3,1,4:T(4,128)}, f32[4,4,4,2,128]{0,2,3,1,4:T(4,128)}, f32[4,4,4,2,128]{0,2,3,1,4:T(4,128)}) fusion(f32[4,4,4,2,128]{0,2,3,1,4:T(4,128)S(1)} %bitcast_add_fusion, f32[4,4,4,1,128]{0,2,3,1,4:T(4,128)S(1)} %get-tuple-element.26, f32[4,4,4,1,128]{0,2,3,1,4:T(4,128)S(1)} %get-tuple-element.27, ...), kind=kLoop, calls=%fused_computation.3 | loop fusion | flops 65536 | bytes 394240 | tf_op jit(solution)/shard_map/concatenate | solution.py:78
  79.3 2.0 %copy.190 = f32[4,4,4,2,128]{4,1,3,2,0:T(4,128)S(1)} copy(f32[4,4,4,2,128]{0,2,3,1,4:T(4,128)} %get-tuple-element.22) | data formatting | bytes 131072 | tf_op jit(solution)/shard_map/slice | solution.py:82
  81.4 2.0 %copy.195 = f32[4,4,4,2,128]{4,1,3,2,0:T(4,128)S(1)} copy(f32[4,4,4,2,128]{0,2,3,1,4:T(4,128)} %get-tuple-element.23) | data formatting | bytes 131072 | tf_op jit(solution)/shard_map/slice | solution.py:82
  83.4 2.1 %copy.198 = f32[4,4,4,2,128]{4,1,3,2,0:T(4,128)S(1)} copy(f32[4,4,4,2,128]{0,2,3,1,4:T(4,128)} %get-tuple-element.24) | data formatting | bytes 131072 | tf_op jit(solution)/shard_map/slice | solution.py:83
  85.5 2.0 %copy.201 = f32[4,4,4,2,128]{4,1,3,2,0:T(4,128)S(1)} copy(f32[4,4,4,2,128]{0,2,3,1,4:T(4,128)} %get-tuple-element.25) | data formatting | bytes 131072 | tf_op jit(solution)/shard_map/slice | solution.py:83
  87.7 1.4 %fusion.2 = f32[4,1,6,1,1,1]{2,1,5,4,3,0:T(1,128)S(1)} fusion(f32[6,4,4,4,2,128]{5,4,3,2,1,0:T(2,128)S(1)} %copy-done.1, f32[4,4,4,2,128,1]{4,1,3,2,0,5:T(4,128)S(1)} %bitcast.76), kind=kOutput, calls=%fused_computation.17 | convolution fusion | flops 1179648 | bytes 458848 | tf_op jit(solution)/shard_map/mscxyz,scxyz->sm/dot_general | solution.py:85
  89.8 4.7 %all-to-all-start.2 = ((f32[32,1,24]{2,1,0:T(1,128)}), f32[32,1,24]{2,1,0:T(1,128)S(1)}, u32[]{:S(2)}, u32[]{:S(2)}) async-start(f32[32,1,24]{2,1,0:T(1,128)} %broadcast_in_dim.32), calls=%async_computation.2 | async-start | bytes 32768 | tf_op jit(solution)/shard_map/all_to_all | solution.py:45
  94.5 1.9 %copy.204 = f32[4,4,4,2,128]{0,2,3,1,4:T(4,128)} copy(f32[4,4,4,2,128]{4,1,3,2,0:T(4,128)S(1)} %fusion.12) | data formatting | bytes 131072 | tf_op jit(solution)/shard_map/sub | solution.py:83
  96.4 5.2 %all-to-all-done.2 = f32[32,1,24]{2,1,0:T(1,128)S(1)} async-done(((f32[32,1,24]{2,1,0:T(1,128)}), f32[32,1,24]{2,1,0:T(1,128)S(1)}, u32[]{:S(2)}, u32[]{:S(2)}) %all-to-all-start.2) | async-done | bytes 3104 | tf_op jit(solution)/shard_map/all_to_all | solution.py:45
  101.7 0.8 fusion
  102.5 1.9 %copy.216 = f32[4,1,4,4,2,128]{0,3,4,2,5,1:T(4,128)} copy(f32[4,1,4,4,2,128]{5,1,4,3,2,0:T(1,128)S(1)} %fusion) | data formatting | bytes 131072 | tf_op jit(solution)/shard_map/sm,mscxyz->scxyz/dot_general | solution.py:87
  104.4 3.3 %multiply_reduce_fusion = f32[4]{0:T(128)S(1)} fusion(f32[4,4,4,2,128]{0,2,3,1,4:T(4,128)} %copy.204, f32[4,1,4,4,2,128]{0,3,4,2,5,1:T(4,128)} %copy.216), kind=kLoop, calls=%fused_computation.6 | loop fusion | flops 49148 | bytes 131088 | tf_op jit(solution)/shard_map/reduce_sum | solution.py:88
  108.4 2.5 %all-to-all-start.3 = ((f32[32,1,4]{2,1,0:T(1,128)}), f32[32,1,4]{2,1,0:T(1,128)S(1)}, u32[]{:S(2)}, u32[]{:S(2)}) async-start(f32[32,1,4]{2,1,0:T(1,128)} %broadcast_in_dim.33), calls=%async_computation.3 | async-start | bytes 32768 | tf_op jit(solution)/shard_map/all_to_all | solution.py:45
  110.9 1.6 %copy.208 = f32[4,4,4,2,128]{4,3,2,1,0:T(2,128)} copy(f32[4,4,4,2,128]{0,2,3,1,4:T(4,128)S(1)} %bitcast_add_fusion) | data formatting | bytes 131072
  112.6 5.4 %all-to-all-done.3 = f32[32,1,4]{2,1,0:T(1,128)S(1)} async-done(((f32[32,1,4]{2,1,0:T(1,128)}), f32[32,1,4]{2,1,0:T(1,128)S(1)}, u32[]{:S(2)}, u32[]{:S(2)}) %all-to-all-start.3) | async-done | bytes 544 | tf_op jit(solution)/shard_map/all_to_all | solution.py:45
  118.2 3.2 %broadcast_divide_fusion = f32[4,4,4,2,128]{0,2,3,1,4:T(4,128)S(1)} fusion(f32[4]{0:T(128)S(1)} %get-tuple-element.51, f32[4,4,4,2,128]{0,2,3,1,4:T(4,128)} %copy.204, f32[4,1,4,4,2,128]{0,3,4,2,5,1:T(4,128)} %copy.216), kind=kLoop, calls=%fused_computation.9 | loop fusion | flops 32768 | bytes 196624 | tf_op jit(solution)/shard_map/div | solution.py:90
  121.4 1.6 %copy.207 = f32[4,4,4,2,128]{4,3,2,1,0:T(2,128)} copy(f32[4,4,4,2,128]{0,2,3,1,4:T(4,128)S(1)} %broadcast_divide_fusion) | data formatting | bytes 131072
  (61 shorter events, 9.2 us)
Async XLA Ops:
  0.6 19.6 %copy-start = (f32[16,512]{1,0:T(8,128)S(1)}, f32[16,512]{1,0:T(8,128)}, u32[]{:S(2)}) copy-start(f32[16,512]{1,0:T(8,128)} %param.11) | copy-start | bytes 98308
  1.6 25.2 %collective-permute-start = (bf16[4,4,2,2,128]{4,0,3,2,1:T(4,128)(2,1)S(1)}, bf16[4,4,2,2,128]{4,0,3,2,1:T(4,128)(2,1)S(1)}, u32[]{:S(2)}, u32[]{:S(2)}) collective-permute-start(bf16[4,4,2,2,128]{4,0,3,2,1:T(4,128)(2,1)S(1)} %slice_select_fusion.2), channel_id=1, source_target_pairs={{0,16},{16,0},{1,17},{17,1},{2,18},{18,2},{3,19},{19,3},{4,20},{20... | collective-permute-start | bytes 49160 | tf_op jit(solution)/shard_map/ppermute | solution.py:26
  6.8 12.0 %all-to-all-start = ((f32[32,1,64]{2,1,0:T(1,128)}), f32[32,1,64]{2,1,0:T(1,128)S(1)}, u32[]{:S(2)}, u32[]{:S(2)}) async-start(f32[32,1,64]{2,1,0:T(1,128)} %broadcast_in_dim.29), calls=%async_computation | async-start | bytes 32768 | tf_op jit(solution)/shard_map/all_to_all | solution.py:45
  13.3 20.7 %copy-start.2 = (f32[16,4,4,2,128]{4,3,2,1,0:T(2,128)S(1)}, f32[16,4,4,2,128]{4,3,2,1,0:T(2,128)}, u32[]{:S(2)}) copy-start(f32[16,4,4,2,128]{4,3,2,1,0:T(2,128)} %param.10) | copy-start | bytes 786436
  21.9 12.1 %all-to-all-start.1 = ((f32[32,1,64]{2,1,0:T(1,128)}), f32[32,1,64]{2,1,0:T(1,128)S(1)}, u32[]{:S(2)}, u32[]{:S(2)}) async-start(f32[32,1,64]{2,1,0:T(1,128)} %bitcast.7), calls=%async_computation.1 | async-start | bytes 32768 | tf_op jit(solution)/shard_map/all_to_all | solution.py:67
  26.9 9.5 %collective-permute-start.1 = (bf16[4,4,8,2,128]{4,0,3,2,1:T(4,128)(2,1)S(1)}, bf16[4,4,8,2,128]{4,0,3,2,1:T(4,128)(2,1)S(1)}, u32[]{:S(2)}, u32[]{:S(2)}) collective-permute-start(bf16[4,4,8,2,128]{4,0,3,2,1:T(4,128)(2,1)S(1)} %pad_maximum_fusion.7), channel_id=1, source_target_pairs={{0,4},{8,12},{4,0},{12,8},{1,5},{9,13},{5,1},{13,9},{2,6},{10,14},... | collective-permute-start | bytes 196616 | tf_op jit(solution)/shard_map/ppermute | solution.py:26
  27.2 9.2 %collective-permute-start.2 = (bf16[4,4,8,2,128]{4,0,3,2,1:T(4,128)(2,1)S(1)}, bf16[4,4,8,2,128]{4,0,3,2,1:T(4,128)(2,1)S(1)}, u32[]{:S(2)}, u32[]{:S(2)}) collective-permute-start(bf16[4,4,8,2,128]{4,0,3,2,1:T(4,128)(2,1)S(1)} %pad_maximum_fusion.7), channel_id=1, source_target_pairs={{4,8},{8,4},{5,9},{9,5},{6,10},{10,6},{7,11},{11,7},{20,24},{24,20... | collective-permute-start | bytes 196616 | tf_op jit(solution)/shard_map/ppermute | solution.py:28
  47.9 21.8 %collective-permute-start.4 = (f32[4,4,4,1,128]{4,2,3,1,0:T(4,128)}, f32[4,4,4,1,128]{4,2,3,1,0:T(4,128)}, u32[]{:S(2)}, u32[]{:S(2)}) collective-permute-start(f32[4,4,4,1,128]{4,2,3,1,0:T(4,128)} %copy.185), channel_id=1, source_target_pairs={{0,4},{8,12},{4,0},{12,8},{1,5},{9,13},{5,1},{13,9},{2,6},{10,14},... | collective-permute-start | bytes 98312 | tf_op jit(solution)/shard_map/ppermute | solution.py:26
  49.1 22.0 %collective-permute-start.5 = (f32[4,4,4,1,128]{4,2,3,1,0:T(4,128)}, f32[4,4,4,1,128]{4,2,3,1,0:T(4,128)}, u32[]{:S(2)}, u32[]{:S(2)}) collective-permute-start(f32[4,4,4,1,128]{4,2,3,1,0:T(4,128)} %copy.186), channel_id=1, source_target_pairs={{4,8},{8,4},{5,9},{9,5},{6,10},{10,6},{7,11},{11,7},{20,24},{24,20... | collective-permute-start | bytes 98312 | tf_op jit(solution)/shard_map/ppermute | solution.py:28
  50.4 6.9 %collective-permute-start.6 = (f32[4,4,4,2,1]{0,2,3,1,4:T(4,128)S(1)}, f32[4,4,4,2,1]{0,2,3,1,4:T(4,128)S(1)}, u32[]{:S(2)}, u32[]{:S(2)}) collective-permute-start(f32[4,4,4,2,1]{0,2,3,1,4:T(4,128)S(1)} %get-tuple-element.30), channel_id=1, source_target_pairs={{0,1},{2,3},{1,0},{3,2},{4,5},{6,7},{5,4},{7,6},{8,9},{10,11},{9,8... | collective-permute-start | bytes 1544 | tf_op jit(solution)/shard_map/ppermute | solution.py:26
  50.9 6.5 %collective-permute-start.7 = (f32[4,4,4,2,1]{0,2,3,1,4:T(4,128)S(1)}, f32[4,4,4,2,1]{0,2,3,1,4:T(4,128)S(1)}, u32[]{:S(2)}, u32[]{:S(2)}) collective-permute-start(f32[4,4,4,2,1]{0,2,3,1,4:T(4,128)S(1)} %get-tuple-element.31), channel_id=1, source_target_pairs={{1,2},{2,1},{5,6},{6,5},{9,10},{10,9},{13,14},{14,13},{17,18},{18,... | collective-permute-start | bytes 1544 | tf_op jit(solution)/shard_map/ppermute | solution.py:28
  51.7 15.0 %collective-permute-start.3 = (f32[4,4,1,2,128]{0,2,3,1,4:T(1,128)}, f32[4,4,1,2,128]{0,2,3,1,4:T(1,128)}, u32[]{:S(2)}, u32[]{:S(2)}) collective-permute-start(f32[4,4,1,2,128]{0,2,3,1,4:T(1,128)} %broadcast_select_fusion.2), channel_id=1, source_target_pairs={{0,16},{16,0},{1,17},{17,1},{2,18},{18,2},{3,19},{19,3},{4,20},{20... | collective-permute-start | bytes 49160 | tf_op jit(solution)/shard_map/ppermute | solution.py:26
  83.4 4.2 %copy-start.1 = (f32[6,4,4,4,2,128]{5,4,3,2,1,0:T(2,128)S(1)}, f32[6,4,4,4,2,128]{5,4,3,2,1,0:T(2,128)}, u32[]{:S(2)}) copy-start(f32[6,4,4,4,2,128]{5,4,3,2,1,0:T(2,128)} %param.6) | copy-start | bytes 1179652
  89.8 11.8 %all-to-all-start.2 = ((f32[32,1,24]{2,1,0:T(1,128)}), f32[32,1,24]{2,1,0:T(1,128)S(1)}, u32[]{:S(2)}, u32[]{:S(2)}) async-start(f32[32,1,24]{2,1,0:T(1,128)} %broadcast_in_dim.32), calls=%async_computation.2 | async-start | bytes 32768 | tf_op jit(solution)/shard_map/all_to_all | solution.py:45
  108.4 9.6 %all-to-all-start.3 = ((f32[32,1,4]{2,1,0:T(1,128)}), f32[32,1,4]{2,1,0:T(1,128)S(1)}, u32[]{:S(2)}, u32[]{:S(2)}) async-start(f32[32,1,4]{2,1,0:T(1,128)} %broadcast_in_dim.33), calls=%async_computation.3 | async-start | bytes 32768 | tf_op jit(solution)/shard_map/all_to_all | solution.py:45

commit v2 on v1

v2 whole, which is shorter than its diff:
```python
import functools

import jax
import jax.numpy as jnp
import numpy as np
from jax import lax
from jax.experimental import pallas as pl
from jax.experimental.pallas import tpu as pltpu
from jax.sharding import PartitionSpec as P

C = 4
CX = 4
CY = 2
CZ = 128
S = 4
M = 6
K = 16
XY = CX * CY
ROWS = C * (CX + 4) * (CY + 4)
AXES = ("gx", "gy", "gz")
PAIRS = [(m, n) for m in range(M) for n in range(m, M)]
BASE = 88
CANCEL = 1e-2

epsilon = 1e-06

VMEM = pl.BlockSpec(memory_space=pltpu.VMEM)
F32 = jnp.float32


def call(body, outs, operands, flops, scratch=()):
    size = sum(x.size * x.dtype.itemsize for x in list(operands) + list(outs))
    return pl.pallas_call(
        body,
        out_shape=tuple(outs),
        in_specs=[VMEM] * len(operands),
        out_specs=tuple([VMEM] * len(outs)),
        scratch_shapes=list(scratch),
        compiler_params=pltpu.CompilerParams(vmem_limit_bytes=24 * 1024 * 1024),
        cost_estimate=pl.CostEstimate(flops=flops, bytes_accessed=size, transcendentals=0),
    )(*operands)


def shape(*dims, dtype=F32):
    return jax.ShapeDtypeStruct(dims, dtype)


def iota(axis):
    return lax.broadcasted_iota(jnp.int32, (8, 128), axis)


def rolled(x, shift, axis):
    return pltpu.roll(x, shift % x.shape[axis], axis)


def row_sums(blocks):
    sub = iota(0)
    for bit in (4, 2, 1):
        low = (sub & bit) == 0
        half = len(blocks) // 2
        blocks = [
            jnp.where(
                low,
                blocks[i] + rolled(blocks[i], -bit, 0),
                blocks[i + half] + rolled(blocks[i + half], bit, 0),
            )
            for i in range(half)
        ]
    return blocks[0]


def across(left, right):
    return lax.dot_general(
        left,
        right,
        (((1,), (1,)), ((), ())),
        precision=lax.Precision.HIGHEST,
        preferred_element_type=F32,
    )


def all_rows(x, t):
    return jnp.broadcast_to(x[t : t + 1, :], (8, 128))


def splat(x, lane):
    return jnp.broadcast_to(x[:, lane : lane + 1], (8, 128))


def ends():
    sub, lane = iota(0), iota(1)
    pick = ((sub == 0) & (lane == 0)) | ((sub == 1) & (lane == CZ - 1))
    return jnp.where(pick, 1.0, 0.0).astype(F32)


def place():
    x, y, z = (lax.axis_index(a) for a in AXES)
    ny, nz = lax.axis_size("gy"), lax.axis_size("gz")
    return (x * ny + y) * nz + z, z > 0, z < nz - 1


def rhs_body(basis, phi, out):
    n = out.shape[0]
    rows = []
    for s in range(S):
        v = [basis[M - 1, s * C + c] for c in range(C)]
        prods = [sum(phi[k * C + c] * v[c] for c in range(C)) for k in range(K)]
        rows.append(row_sums(prods[:8]))
        rows.append(row_sums(prods[8:]))
    rows.append(jnp.zeros((64, 128), F32))
    rhs = across(jnp.ones((8, 128), F32), jnp.concatenate(rows, 0))
    faces = across(ends(), phi[...].reshape(K * C * XY, CZ))
    sub = iota(0)
    base = jnp.where(sub == 0, rhs, 0.0)
    out[...] = jnp.broadcast_to(base[None], (n, 8, 128))

    def with_face(side):
        block = base
        for r in range(4):
            block = jnp.where(sub == r + 1, all_rows(faces[:, 128 * r : 128 * r + 128], side), block)
        return block

    me, below, above = place()

    @pl.when(below)
    def _():
        out[me - 1] = with_face(0)

    @pl.when(above)
    def _():
        out[me + 1] = with_face(1)


def local_body(two_x, inv, cols, phi, basis, loc, locz, gram, *sends):
    def one(c, carry):
        total = [[jnp.zeros((8, 128), F32) for _ in range(XY)] for _ in range(S)]
        for j in range(0, ROWS, 16):
            seen = [cols[s, j : j + 16, :].astype(F32) for s in range(S)]
            for i in range(XY):
                w = inv[c, i, j : j + 16, :].astype(F32)
                for s in range(S):
                    part = w * seen[s]
                    total[s][i] = total[s][i] + part[:8] + part[8:]
        for s in range(S):
            loc[s * C + c] = row_sums(total[s])
        return carry

    lax.fori_loop(0, C, one, 0)
    locz[...] = across(ends(), loc[...].reshape(S * C * XY, CZ))

    rows = []
    for m, n in PAIRS:
        for s in range(S):
            rows.append(sum(basis[m, s * C + c] * basis[n, s * C + c] for c in range(C)))
    rows += [jnp.zeros((8, 128), F32)] * (BASE - len(rows))
    for g in range(0, BASE, 8):
        gram[g : g + 8, :] = row_sums(rows[g : g + 8])

    odd_y = lax.axis_index("gy") % 2 == 1
    odd_x = lax.axis_index("gx") % 2 == 1
    sub = iota(0)
    even = (sub & 1) == 0

    def block(half, of, i):
        share, own = K * C // of, S * C // of
        return phi[half * share + i] if i < share else loc[half * own + i - share]

    for i in range((K + S) * C // 2):
        a, b = block(0, 2, i), block(1, 2, i)
        low = jnp.where(even, a, rolled(b, 1, 0))
        high = jnp.where(even, rolled(a, -1, 0), b)
        sends[0][i] = jnp.where(odd_y, low, high)
        sends[1][i] = jnp.where(odd_y, high, low)
    for i in range((K + S) * C // 4):
        low = high = None
        for g in range(4):
            a = block(g, 4, i)
            to_low, to_high = rolled(a, 2 * g, 0), rolled(a, 2 * g - 6, 0)
            low = to_low if low is None else jnp.where((sub >> 1) == g, to_low, low)
            high = to_high if high is None else jnp.where((sub >> 1) == g, to_high, high)
        sends[2][i] = jnp.where(odd_x, low, high)
        if two_x:
            sends[3][i] = jnp.where(odd_x, high, low)


def periodic(x):
    for shift in (16, 32, 64):
        x = x + rolled(x, shift, 1)
    return x


def slots(two_x):
    return ["own", "ylo", "yhi"] + (["xlo", "xhi"] if two_x else ["x"]) + ["zlo", "zhi"]


def factor_body(two_x, got, locz, factor, out):
    n = factor.shape[1] // K
    stride = out.shape[0] // n
    sub, lane = iota(0), iota(1)
    diag = (lane >> 4) == sub
    image = [jnp.zeros((K, 128), F32) for _ in range(S)]
    for b in range(n // 8):
        rhs = got[pl.ds(64 * b, 8, stride=8), :]
        rows = factor[:, 128 * b : 128 * b + 128]
        for s in range(S):
            mine = jnp.where(diag, periodic(jnp.where((lane >> 4) == s, rhs, 0.0)), 0.0)
            image[s] = image[s] + rows * jnp.sum(mine, axis=0, keepdims=True)
    image = [jnp.sum(x, axis=1, keepdims=True) for x in image]
    shares = []
    for b in range(n // 8):
        rows = factor[:, 128 * b : 128 * b + 128]
        block = jnp.zeros((8, 128), F32)
        for s in range(S):
            part = jnp.sum(rows * image[s], axis=0, keepdims=True)
            mine = periodic(jnp.where(diag, part, 0.0))
            block = jnp.where((lane >> 4) == s, mine, block)
        shares.append(block)
    shares = jnp.concatenate(shares, 0)
    nz = lax.axis_size("gz")
    plane = lax.axis_size("gy") * nz
    shift = {"own": 0, "ylo": nz, "yhi": -nz, "x": plane, "xlo": plane, "xhi": -plane, "zlo": 1, "zhi": -1}
    names = slots(two_x)
    for t in range(0, len(names), 2):
        pair = [rolled(shares, shift[x], 0) if shift[x] else shares for x in names[t : t + 2]]
        row = pair[0] if len(pair) == 1 else pair[0] + rolled(pair[1], 64, 1)
        out[pl.ds(t // 2, n, stride=stride), :] = row
    face = (len(names) + 1) // 2
    for t in range(face, stride):
        out[pl.ds(t, n, stride=stride), :] = jnp.zeros((n, 128), F32)
    me, below, above = place()

    @pl.when(below)
    def _():
        out[pl.ds((me - 1) * stride + face, 1), :] = locz[0:1, :]

    @pl.when(above)
    def _():
        out[pl.ds((me + 1) * stride + face, 1), :] = locz[1:2, :]


def image_body(two_x, loc, phi, diagonal, couple, basis, gram, coarse, got, *rest):
    faces, (pre, image, sent) = rest[:-3], rest[-3:]
    n = sent.shape[0]
    stride = coarse.shape[0] // n
    sub, lane = iota(0), iota(1)
    even = (sub & 1) == 0
    total = coarse[0:8, :]
    for b in range(1, coarse.shape[0] // 8):
        total = total + coarse[8 * b : 8 * b + 8, :]
    if stride == 4:
        total = total + rolled(total, 4, 0)
    names = slots(two_x)

    def coefs(name):
        at = names.index(name)
        return rolled(all_rows(total, at // 2), -64 * (at % 2), 1)

    own = coefs("own")
    p = [loc[i] for i in range(S * C)]
    for s in range(S):
        for k in range(K):
            w = splat(own, s * K + k)
            for c in range(C):
                p[s * C + c] = p[s * C + c] + w * phi[k * C + c]

    odd_y = lax.axis_index("gy") % 2 == 1
    odd_x = lax.axis_index("gx") % 2 == 1

    def y_side(face, coef):
        sums = []
        for s in range(S):
            mine = even if s < 2 else ~even
            part = [jnp.where(mine, face[32 + (s % 2) * C + c], 0.0) for c in range(C)]
            for k in range(K // 2):
                w = jnp.where(even, splat(coef, s * K + k), splat(coef, s * K + k + K // 2))
                for c in range(C):
                    part[c] = part[c] + w * face[k * C + c]
            sums += part
        return sums

    def x_side(face, coef):
        sums = []
        for s in range(S):
            part = [jnp.where((sub >> 1) == s, face[16 + c], 0.0) for c in range(C)]
            for k in range(K // 4):
                w = splat(coef, s * K + k)
                for g in range(1, 4):
                    w = jnp.where((sub >> 1) == g, splat(coef, s * K + k + 4 * g), w)
                for c in range(C):
                    part[c] = part[c] + w * face[k * C + c]
            for x in part:
                x = x + rolled(x, 2, 0)
                sums.append(x + rolled(x, 4, 0))
        return sums

    ylo, yhi = coefs("ylo"), coefs("yhi")
    y_first = y_side(faces[0], jnp.where(odd_y, ylo, yhi))
    y_second = y_side(faces[1], jnp.where(odd_y, yhi, ylo))
    if two_x:
        xlo, xhi = coefs("xlo"), coefs("xhi")
        x_first = x_side(faces[2], jnp.where(odd_x, xlo, xhi))
        x_second = x_side(faces[3], jnp.where(odd_x, xhi, xlo))
    else:
        x_first = x_side(faces[2], coefs("x"))
        x_second = [jnp.zeros((8, 128), F32)] * (S * C)

    me, below, above = place()

    def z_side(there, neighbour, coef):
        at = jnp.where(there, neighbour, me)
        parts = got[pl.ds(pl.multiple_of(at * 8, 8), 8), :]
        parts = jnp.where((sub >= 1) & (sub <= 4), parts, 0.0)
        row = jnp.broadcast_to(coarse[pl.ds(at * stride + (len(names) + 1) // 2, 1), :], (8, 128))
        for s in range(S):
            w = jnp.zeros((8, 128), F32)
            for k in range(K):
                w = jnp.where((sub == 1 + k // 4) & ((lane >> 5) == k % 4), splat(coef, s * K + k), w)
            part = parts * w
            for shift in (4, 2, 1):
                part = part + rolled(part, shift, 0)
            for shift in (32, 64):
                part = part + rolled(part, shift, 1)
            row = row + jnp.where((lane >> 5) == s, part, 0.0)
        return jnp.where(there, row, 0.0)

    zlo = z_side(below, me - 1, coefs("zlo"))
    zhi = z_side(above, me + 1, coefs("zhi"))
    columns = jnp.transpose(jnp.where(sub == 0, zlo, zhi))

    for s in range(S):
        sides = []
        for c in range(C):
            i = s * C + c
            x = p[i]
            pre[i] = x
            zl = jnp.broadcast_to(columns[i * XY : (i + 1) * XY, 0:1], (8, 128))
            zh = jnp.broadcast_to(columns[i * XY : (i + 1) * XY, 1:2], (8, 128))
            y_low = jnp.where(odd_y, y_first[i], y_second[i])
            y_high = jnp.where(odd_y, y_second[i], y_first[i])
            x_low = jnp.where(odd_x, x_first[i], x_second[i])
            x_high = jnp.where(odd_x, x_second[i], x_first[i])
            y_low = y_low + rolled(y_low, -1, 0)
            y_high = y_high + rolled(y_high, 1, 0)
            sides = [
                jnp.where(sub < CY, x_low, rolled(x, CY, 0)),
                jnp.where(sub >= XY - CY, x_high, rolled(x, -CY, 0)),
                jnp.where(even, y_low, rolled(x, 1, 0)),
                jnp.where(even, rolled(x, -1, 0), y_high),
                jnp.where(lane == 0, zl, rolled(x, 1, 1)),
                jnp.where(lane == CZ - 1, zh, rolled(x, -1, 1)),
            ]
            a = sum(diagonal[c * C + d] * p[s * C + d] for d in range(C))
            for d, side in enumerate(sides):
                a = a - couple[d * C + c] * side
            image[i] = a

    rows = []
    for m in range(M):
        for s in range(S):
            rows.append(sum(basis[m, s * C + c] * image[s * C + c] for c in range(C)))
    for s in range(S):
        rows.append(sum(image[s * C + c] * image[s * C + c] for c in range(C)))
    rows += [jnp.zeros((8, 128), F32)] * 4
    sums = [row_sums(rows[g : g + 8]) for g in range(0, 32, 8)]
    sums = jnp.concatenate([gram[...]] + sums + [jnp.zeros((8, 128), F32)], 0)
    row = across(jnp.ones((8, 128), F32), sums)
    sent[...] = jnp.broadcast_to(row[None], (n // 8, 8, 128)).reshape(n, 128)


def tables():
    first = np.zeros((128, 128), np.float32)
    second = np.zeros((128, 128), np.float32)
    out = np.zeros((128, 128), np.float32)
    fixed = np.zeros((8, 128), np.float32)
    for s in range(S):
        for at, (m, n) in enumerate(PAIRS):
            first[BASE + 4 * m + s, 4 * at + s] = 1
            second[BASE + 4 * n + s, 4 * at + s] = 1
            fixed[2, 4 * at + s] = 1 if m == n else 2
        for m in range(M):
            lane = BASE + 4 * m + s
            first[lane, lane] = 1
            fixed[1, lane] = 1
            fixed[2, lane] = -2
        lane = BASE + 4 * M + s
        fixed[0, lane] = fixed[1, lane] = fixed[2, lane] = 1
        for i in range(M + 1):
            out[BASE + 4 * i + s, i] = 1
    return np.stack([first, second, out]), fixed


def finish_body(unknowns, got, image, basis, maps, fixed, krylov, hessenberg, flag):
    sub, lane = iota(0), iota(1)
    total = got[0:8, :]
    for b in range(1, got.shape[0] // 8):
        total = total + got[8 * b : 8 * b + 8, :]
    for shift in (4, 2, 1):
        total = total + rolled(total, shift, 0)
    h = total / unknowns

    def times(x, table):
        return jnp.dot(x, table, precision=lax.Precision.HIGHEST, preferred_element_type=F32)

    terms = total * all_rows(fixed, 2)
    terms = terms * (times(h, maps[0]) + all_rows(fixed, 0)) * (times(h, maps[1]) + all_rows(fixed, 1))
    size = jnp.abs(terms)
    for shift in (4, 8, 16, 32, 64):
        terms = terms + rolled(terms, shift, 1)
        size = size + rolled(size, shift, 1)
    norm = jnp.sqrt(jnp.maximum(terms, 0.0) / unknowns + epsilon)
    scale = 1.0 / norm
    flag[...] = jnp.where(terms < CANCEL * size, 1.0, 0.0)
    for s in range(S):
        w = [splat(h, BASE + 4 * m + s) for m in range(M)]
        f = splat(scale, s)
        for c in range(C):
            i = s * C + c
            krylov[i] = (image[i] - sum(w[m] * basis[m, i] for m in range(M))) * f
    values = jnp.where(lane >= BASE + 4 * M, norm, h)
    values = jnp.where((lane & 3) == sub, values, 0.0)
    hessenberg[...] = times(values, maps[2])[:S, : M + 1]


def pairs_of(axis):
    count = lax.axis_size(axis)
    rounds = [[(i, i + 1) for i in range(start, count - 1, 2)] for start in (0, 1)]
    return [r + [(j, i) for i, j in r] for r in rounds if r]


def swap_rounds(axis, low_side, high_side):
    odd = lax.axis_index(axis) % 2 == 1
    rounds = pairs_of(axis)
    got_first = lax.ppermute(jnp.where(odd, low_side, high_side), axis, rounds[0])
    if len(rounds) == 2:
        got_second = lax.ppermute(jnp.where(odd, high_side, low_side), axis, rounds[1])
    else:
        got_second = jnp.zeros_like(got_first)
    return jnp.where(odd, got_first, got_second), jnp.where(odd, got_second, got_first)


def exchange(rows, n):
    sent = rows.reshape(n, -1, 128)
    return lax.all_to_all(sent, AXES, 0, 0, tiled=True)


def on_device(basis, inverse_rows, block_diag, couple, coarse_basis, coarse_factor):
    n = lax.axis_size("gx") * lax.axis_size("gy") * lax.axis_size("gz")
    unknowns = float(C * XY * CZ * n)
    two_x = lax.axis_size("gx") > 2
    vectors = basis.reshape(M, S * C, XY, CZ)
    phi = coarse_basis.reshape(K * C, XY, CZ)

    rounded = basis[M - 1].astype(jnp.bfloat16)
    y_low, y_high = swap_rounds("gy", rounded, rounded)
    (rhs,) = call(rhs_body, [shape(n, 8, 128)], (vectors, phi), 2 * K * S * C * XY * CZ)
    got = exchange(rhs, n).reshape(n * 8, 128)

    extended = jnp.concatenate([y_low, rounded, y_high], axis=3)
    x_low, x_high = swap_rounds("gx", extended[:, :, :2], extended[:, :, -2:])
    extended = jnp.concatenate([x_low, extended, x_high], axis=2)
    columns = extended.reshape(S, ROWS, CZ)
    half, quarter = (K + S) * C // 2, (K + S) * C // 4
    sends = [shape(half, 8, 128)] * 2 + [shape(quarter, 8, 128)] * (2 if two_x else 1)
    loc, locz, gram, *sends = call(
        functools.partial(local_body, two_x),
        [shape(S * C, XY, CZ), shape(8, 128), shape(BASE, 128)] + sends,
        (inverse_rows.reshape(C, XY, ROWS, CZ), columns, phi, vectors),
        2 * S * C * XY * ROWS * CZ,
    )
    faces = [lax.ppermute(x, "gy", pairs) for x, pairs in zip(sends, pairs_of("gy"))]
    faces += [lax.ppermute(x, "gx", pairs) for x, pairs in zip(sends[2:], pairs_of("gx"))]

    stride = 8 if two_x else 4
    (shares,) = call(
        functools.partial(factor_body, two_x),
        [shape(n * stride, 128)],
        (got, locz, coarse_factor),
        4 * S * K * K * n,
    )
    coarse = exchange(shares, n).reshape(n * stride, 128)
    pre, image, sent = call(
        functools.partial(image_body, two_x),
        [shape(S * C, XY, CZ), shape(S * C, XY, CZ), shape(n, 128)],
        (
            loc,
            phi,
            block_diag.reshape(C * C, XY, CZ),
            couple.reshape(6 * C, XY, CZ),
            vectors,
            gram,
            coarse,
            got,
            *faces,
        ),
        2 * S * C * XY * CZ * 40,
    )
    products = exchange(sent, n).reshape(n, 128)
    maps, fixed = tables()
    krylov, hessenberg, flag = call(
        functools.partial(finish_body, unknowns),
        [shape(S * C, XY, CZ), shape(S, M + 1), shape(8, 128)],
        (products, image, vectors, jnp.asarray(maps), jnp.asarray(fixed)),
        2 * S * C * XY * CZ * 8,
    )

    def exact(image, vectors, krylov, hessenberg):
        h = hessenberg[:, :M]
        left = image.reshape(S, C, XY, CZ) - jnp.sum(
            h.T[:, :, None, None, None] * vectors.reshape(M, S, C, XY, CZ), axis=0
        )
        squares = jnp.zeros((1, 128), F32).at[0, :S].set(jnp.sum(left * left, axis=(1, 2, 3)))
        squares = jnp.sum(exchange(jnp.broadcast_to(squares, (n, 128)), n), axis=(0, 1))[:S]
        norm = jnp.sqrt(squares / unknowns + epsilon)
        return (
            (left / norm[:, None, None, None]).reshape(S * C, XY, CZ),
            jnp.concatenate([h, norm[:, None]], axis=1),
        )

    def as_is(image, vectors, krylov, hessenberg):
        return krylov, hessenberg

    krylov, hessenberg = lax.cond(
        jnp.max(flag) > 0.0, exact, as_is, image, vectors, krylov, hessenberg
    )
    cells = (S, C, CX, CY, CZ)
    return krylov.reshape(cells), pre.reshape(cells), hessenberg


def solution(mesh):
    return jax.shard_map(
        on_device,
        mesh=mesh,
        in_specs=(
            P(None, None, None, "gx", "gy", "gz"),
            P(None, "gx", "gy", None, "gz"),
            P(None, None, "gx", "gy", "gz"),
            P(None, None, "gx", "gy", "gz"),
            P(None, None, "gx", "gy", "gz"),
            P(AXES, None),
        ),
        out_specs=(P(None, None, "gx", "gy", "gz"), P(None, None, "gx", "gy", "gz"), P()),
        check_vma=False,
    )
```

time: 125 us -> 52.8 us (0.42)
  local copies, waits for them, and re-layouts: 44.2 us -> 2.67 us
  other arithmetic: 19 us -> 0.9 us
  waiting for transfers between devices: 26.9 us -> 12.4 us
  blocking collectives: 0 us -> 9.9 us
  matrix products: 8.26 us -> 0 us
  Pallas kernels: 0 us -> 7.66 us
  starting transfers between devices: 24.3 us -> 17.5 us
    unnamed x24 -> x22, local copies, waits for them, and re-layouts: 12.7 us -> 1.61 us
    all_to_all x0 -> x1, blocking collectives: none -> 9.9 us  [exchange(): return lax.all_to_all(sent, AXES, 0, 0, tiled=True)]
    all_to_all x4 -> x2, waiting for transfers between devices: 17.5 us -> 8.24 us  [exchange(): return lax.all_to_all(sent, AXES, 0, 0, tiled=True)]
    slice x5 -> x0, local copies, waits for them, and re-layouts: 9.07 us -> none  [the longest x2 4.14 us: on_device(): applied = applied - couple[4] * pz[..., :-2] - couple[5] * pz[..., 2:]]
    all_to_all x4 -> x2, starting transfers between devices: 17.1 us -> 8.25 us  [exchange(): return lax.all_to_all(sent, AXES, 0, 0, tiled=True)]
    dot_general x7 -> x0, matrix products: 8.26 us -> none  [the longest x1 3.45 us: on_device(): jnp.einsum('cxyjz,sjz->scxyz', inverse_rows, columns, preferred_element_t...]
    pallas_call x0 -> x5, Pallas kernels: none -> 7.66 us  [call(): pl.pallas_call(body, out_shape=tuple(outs), in_specs=[VMEM] * len(operand...]
    ppermute x8 -> x6, waiting for transfers between devices: 9.39 us -> 4.13 us  [the longest x1 3.26 us: on_device(): lax.ppermute(x, 'gx', pairs)]
  transfers between devices with their start and end apart: 12 -> 8, of which waited for: 5 -> 4; matrix products, arithmetic and copies ran while one was open for 23% -> 1% of each run, Pallas kernels for 0% -> 9%
where the time goes in v2:
time: 52.8 us; the launch traced here: 52.5 us
  starting transfers between devices  17.5 us (33%)
  waiting for transfers between devices  12.4 us (23%)
  blocking collectives  9.9 us (19%)
  Pallas kernels  7.66 us (15%)
  local copies, waits for them, and re-layouts  2.67 us (5%)
  between operations  1.46 us (3%)
  other arithmetic  0.9 us (2%)
    all_to_all x1, blocking collectives, exchange(): return lax.all_to_all(sent, AXES, 0, 0, tiled=True)  9.9 us
    all_to_all x2, starting transfers between devices, exchange(): return lax.all_to_all(sent, AXES, 0, 0, tiled=True)  8.25 us
    all_to_all x2, waiting for transfers between devices, exchange(): return lax.all_to_all(sent, AXES, 0, 0, tiled=True)  8.24 us
    pallas_call x5, Pallas kernels, call(): pl.pallas_call(body, out_shape=tuple(outs), in_specs=[VMEM] * len(operand...  7.66 us
    ppermute x2, starting transfers between devices, swap_rounds(): lax.ppermute(jnp.where(odd, low_side, high_side), axis, rounds[0])  5.95 us
    ppermute x1, waiting for transfers between devices, on_device(): lax.ppermute(x, 'gx', pairs)  3.26 us
    ppermute x1, starting transfers between devices, on_device(): lax.ppermute(x, 'gx', pairs)  1.7 us
    unnamed x22, local copies, waits for them, and re-layouts  1.61 us
  transfers between devices with their start and end apart: 8, of which 4 were waited for; matrix products, arithmetic and copies ran while one was open for 1% of the time, Pallas kernels for 9%

profile of v2, /device:TPU:0, one launch (start us, length us, event | category | flops | bytes accessed | tf_op | source)
XLA Modules:
  0.0 52.5 jit_solution(17703754770335122727)
XLA Ops:
  0.6 0.9 %fusion = bf16[4,4,4,2,128]{4,3,2,1,0:T(2,128)(2,1)S(1)} fusion(f32[6,4,4,4,2,128]{5,4,3,2,1,0:T(2,128)} %param.12), kind=kLoop, calls=%fused_computation.16 | loop fusion | bytes 65536 | tf_op jit(solution)/shard_map/convert_element_type | solution.py:453
  1.5 0.7 %collective-permute-start.1 = (bf16[4,4,4,2,128]{4,3,2,1,0:T(2,128)(2,1)S(1)}, bf16[4,4,4,2,128]{4,3,2,1,0:T(2,128)(2,1)S(1)}, u32[]{:S(2)}, u32[]{:S(2)}) collective-permute-start(bf16[4,4,4,2,128]{4,3,2,1,0:T(2,128)(2,1)S(1)} %fusion), channel_id=1, source_target_pairs={{4,8},{8,4},{5,9},{9,5},{6,10},{10,6},{7,11},{11,7},{20,24},{24,20... | collective-permute-start | bytes 98312 | tf_op jit(solution)/shard_map/ppermute | solution.py:435
  2.2 4.4 %collective-permute-start = (bf16[4,4,4,2,128]{4,3,2,1,0:T(2,128)(2,1)S(1)}, bf16[4,4,4,2,128]{4,3,2,1,0:T(2,128)(2,1)S(1)}, u32[]{:S(2)}, u32[]{:S(2)}) collective-permute-start(bf16[4,4,4,2,128]{4,3,2,1,0:T(2,128)(2,1)S(1)} %fusion), channel_id=1, source_target_pairs={{0,4},{8,12},{4,0},{12,8},{1,5},{9,13},{5,1},{13,9},{2,6},{10,14},... | collective-permute-start | bytes 98312 | tf_op jit(solution)/shard_map/ppermute | solution.py:433
  6.6 0.0 collective-permute-done.1
  6.6 0.9 %collective-permute-done = bf16[4,4,4,2,128]{4,3,2,1,0:T(2,128)(2,1)S(1)} collective-permute-done((bf16[4,4,4,2,128]{4,3,2,1,0:T(2,128)(2,1)S(1)}, bf16[4,4,4,2,128]{4,3,2,1,0:T(2,128)(2,1)S(1)}, u32[]{:S(2)}, u32[]{:S(2)}) %collective-permute-start) | collective-permute-done | bytes 32800 | tf_op jit(solution)/shard_map/ppermute | solution.py:433
  7.4 0.0 copy-start.1
  7.4 0.1 pad_maximum_fusion.2
  7.6 1.6 %collective-permute-start.2 = (bf16[4,4,2,6,128]{4,3,2,1,0:T(8,128)(2,1)S(1)}, bf16[4,4,2,6,128]{4,3,2,1,0:T(8,128)(2,1)S(1)}, u32[]{:S(2)}, u32[]{:S(2)}) collective-permute-start(bf16[4,4,2,6,128]{4,3,2,1,0:T(8,128)(2,1)S(1)} %slice_select_fusion), channel_id=1, source_target_pairs={{0,16},{16,0},{1,17},{17,1},{2,18},{18,2},{3,19},{19,3},{4,20},{20... | collective-permute-start | bytes 147464 | tf_op jit(solution)/shard_map/ppermute | solution.py:433
  9.1 0.0 copy-start
  9.1 0.9 %copy-done = f32[16,4,4,2,128]{4,3,2,1,0:T(2,128)S(1)} copy-done((f32[16,4,4,2,128]{4,3,2,1,0:T(2,128)S(1)}, f32[16,4,4,2,128]{4,3,2,1,0:T(2,128)}, u32[]{:S(2)}) %copy-start) | copy-done | bytes 262168
  10.1 0.0 copy-start.2
  10.1 2.3 %shard_map.104 = f32[32,8,128]{2,1,0:T(8,128)} custom-call(f32[6,16,8,128]{3,2,1,0:T(8,128)} %bitcast.38, f32[64,8,128]{2,1,0:T(8,128)S(1)} %bitcast.27), custom_call_target="tpu_custom_call" | custom-call | flops 524288 | bytes 786432 | tf_op jit(solution)/shard_map/pallas_call | solution.py:33
  12.4 5.7 %all-to-all-start.1 = ((f32[32,8,128]{2,1,0:T(8,128)}), f32[32,8,128]{2,1,0:T(8,128)S(1)}, u32[]{:S(2)}, u32[]{:S(2)}) async-start(f32[32,8,128]{2,1,0:T(8,128)} %shard_map.104), calls=%async_computation.1 | async-start | bytes 262144 | tf_op jit(solution)/shard_map/all_to_all | solution.py:443
  18.0 0.0 collective-permute-done.2
  18.1 0.1 pad_maximum_fusion.1
  18.2 0.0 copy-start.6
  18.2 0.2 copy.30
  18.4 0.0 copy-start.4
  18.4 0.0 copy-start.5
  18.5 0.0 copy-done.1
  18.5 0.0 copy-done.2
  18.5 0.0 copy-done.8
  18.5 1.4 %shard_map.103 = (f32[16,8,128]{2,1,0:T(8,128)S(1)}, f32[8,128]{1,0:T(8,128)S(1)}, f32[88,128]{1,0:T(8,128)S(1)}, f32[40,8,128]{2,1,0:T(8,128)S(1)}, f32[40,8,12...) custom-call(bf16[4,8,192,128]{3,2,1,0:T(8,128)(2,1)S(1)} %bitcast.30, bf16[4,192,128]{2,1,0:T(8,128)(2,1)S(1)} %copy.31.cols, ...), custom_call_target="tpu_custom_call" | custom-call | flops 6291456 | bytes 2949120 | tf_op jit(solution)/shard_map/pallas_call | solution.py:33
  19.9 0.0 copy-start.3
  19.9 0.0 copy-start.7
  19.9 0.3 collective-permute-start.3
  20.2 0.7 %collective-permute-start.4 = (f32[40,8,128]{2,1,0:T(8,128)S(1)}, f32[40,8,128]{2,1,0:T(8,128)S(1)}, u32[]{:S(2)}, u32[]{:S(2)}) collective-permute-start(f32[40,8,128]{2,1,0:T(8,128)S(1)} %get-tuple-element.51), channel_id=1, source_target_pairs={{4,8},{8,4},{5,9},{9,5},{6,10},{10,6},{7,11},{11,7},{20,24},{24,20... | collective-permute-start | bytes 491528 | tf_op jit(solution)/shard_map/ppermute | solution.py:470
  20.8 5.7 %all-to-all-done.1 = f32[32,8,128]{2,1,0:T(8,128)S(1)} async-done(((f32[32,8,128]{2,1,0:T(8,128)}), f32[32,8,128]{2,1,0:T(8,128)S(1)}, u32[]{:S(2)}, u32[]{:S(2)}) %all-to-all-start.1) | async-done | bytes 131104 | tf_op jit(solution)/shard_map/all_to_all | solution.py:443
  26.5 0.0 copy-done.6
  26.6 1.3 %shard_map.105 = f32[128,128]{1,0:T(8,128)} custom-call(f32[256,128]{1,0:T(8,128)S(1)} %bitcast.31, f32[8,128]{1,0:T(8,128)S(1)} %get-tuple-element.49.locz, f32[16,512]{1,0:T(8,128)S(1)} %copy-done.6), custom_call_target="tpu_custom_call" | custom-call | flops 131072 | bytes 233472 | tf_op jit(solution)/shard_map/pallas_call | solution.py:33
  27.8 2.6 %all-to-all-start.2 = ((f32[32,4,128]{2,1,0:T(4,128)}), f32[32,4,128]{2,1,0:T(4,128)S(1)}, u32[]{:S(2)}, u32[]{:S(2)}) async-start(f32[32,4,128]{2,1,0:T(4,128)} %bitcast.12), calls=%async_computation.2 | async-start | bytes 131072 | tf_op jit(solution)/shard_map/all_to_all | solution.py:443
  30.4 1.7 %collective-permute-start.5 = (f32[20,8,128]{2,1,0:T(8,128)S(1)}, f32[20,8,128]{2,1,0:T(8,128)S(1)}, u32[]{:S(2)}, u32[]{:S(2)}) collective-permute-start(f32[20,8,128]{2,1,0:T(8,128)S(1)} %get-tuple-element.52), channel_id=1, source_target_pairs={{0,16},{16,0},{1,17},{17,1},{2,18},{18,2},{3,19},{19,3},{4,20},{20... | collective-permute-start | bytes 245768 | tf_op jit(solution)/shard_map/ppermute | solution.py:471
  32.1 3.3 %collective-permute-done.5.rest_2_ = f32[20,8,128]{2,1,0:T(8,128)S(1)} collective-permute-done((f32[20,8,128]{2,1,0:T(8,128)S(1)}, f32[20,8,128]{2,1,0:T(8,128)S(1)}, u32[]{:S(2)}, u32[]{:S(2)}) %collective-permute-start.5) | collective-permute-done | bytes 81952 | tf_op jit(solution)/shard_map/ppermute | solution.py:471
  35.3 0.0 collective-permute-done.3.rest_0_
  35.3 0.0 collective-permute-done.4.rest_1_
  35.4 2.5 %all-to-all-done.2 = f32[32,4,128]{2,1,0:T(4,128)S(1)} async-done(((f32[32,4,128]{2,1,0:T(4,128)}), f32[32,4,128]{2,1,0:T(4,128)S(1)}, u32[]{:S(2)}, u32[]{:S(2)}) %all-to-all-start.2) | async-done | bytes 65568 | tf_op jit(solution)/shard_map/all_to_all | solution.py:443
  37.9 0.0 copy-done.4
  37.9 0.0 copy-done.5
  37.9 2.0 %shard_map.106 = (f32[16,8,128]{2,1,0:T(8,128)}, f32[16,8,128]{2,1,0:T(8,128)S(1)}, f32[32,128]{1,0:T(8,128)S(1)}) custom-call(f32[16,8,128]{2,1,0:T(8,128)S(1)} %get-tuple-element.47.loc, f32[64,8,128]{2,1,0:T(8,128)S(1)} %bitcast.29, f32[16,8,128]{2,1,0:T(8,128)S(1)} %bitcast.35, f32[24,8,128]{2,1,0:T(8,128)S(1)} %bitcast.34, ...), custom_call_target="tpu_custom_call" | custom-call | flops 1310720 | bytes 1683456 | tf_op jit(solution)/shard_map/pallas_call | solution.py:33
  39.8 9.9 %all_to_all.20 = f32[32,1,128]{2,1,0:T(1,128)S(1)} all-to-all(f32[32,1,128]{2,1,0:T(1,128)S(1)} %bitcast.37), channel_id=1, replica_groups=mesh['gx'=2,'gy'=4,'gz'=4] {'gx','gy','gz'}, dimensions={0} | all-to-all | bytes 32768 | tf_op jit(solution)/shard_map/all_to_all | solution.py:443
  49.7 0.0 copy-done.3
  49.7 0.0 copy-done.7
  49.7 0.8 %shard_map.107 = (f32[16,8,128]{2,1,0:T(8,128)S(1)}, f32[4,7]{1,0:T(4,128)S(1)}, f32[8,128]{1,0:T(8,128)S(1)}) custom-call(f32[32,128]{1,0:T(8,128)S(1)} %bitcast.36, f32[16,8,128]{2,1,0:T(8,128)S(1)} %get-tuple-element.54.image, f32[6,16,8,128]{3,2,1,0:T(8,128)S(1)} %bitcast.41, f32[3,128,128]{2,1,0:T(8,128)S(1)} %copy-done.3, f32[8,128]{1,0:T(8,128)S(1)} %copy-done.7), custom_call_target="tpu_custom_call" | custom-call | flops 262144 | bytes 745584 | tf_op jit(solution)/shard_map/pallas_call | solution.py:33
  50.6 0.6 %reduce_max.9 = f32[]{:T(128)} reduce(f32[8,128]{1,0:T(8,128)S(1)} %get-tuple-element.55, f32[]{:T(128)} %constant.75.clone.1), dimensions={0,1}, to_apply=%region_0.1 | reduce | flops 1023 | bytes 4104 | tf_op jit(solution)/shard_map/reduce_max | solution.py:523
  51.8 0.0 copy-start.9
  51.9 0.0 copy-start.10
  51.9 0.6 %copy-done.9 = f32[4,7]{1,0:T(4,128)} copy-done((f32[4,7]{1,0:T(4,128)}, f32[4,7]{1,0:T(4,128)S(1)}, u32[]{:S(2)}) %copy-start.9) | copy-done | bytes 136
  52.4 0.1 copy-done.10
  (6 shorter events, 0.1 us)
Async XLA Ops:
  1.5 5.1 %collective-permute-start.1 = (bf16[4,4,4,2,128]{4,3,2,1,0:T(2,128)(2,1)S(1)}, bf16[4,4,4,2,128]{4,3,2,1,0:T(2,128)(2,1)S(1)}, u32[]{:S(2)}, u32[]{:S(2)}) collective-permute-start(bf16[4,4,4,2,128]{4,3,2,1,0:T(2,128)(2,1)S(1)} %fusion), channel_id=1, source_target_pairs={{4,8},{8,4},{5,9},{9,5},{6,10},{10,6},{7,11},{11,7},{20,24},{24,20... | collective-permute-start | bytes 98312 | tf_op jit(solution)/shard_map/ppermute | solution.py:435
  2.2 5.3 %collective-permute-start = (bf16[4,4,4,2,128]{4,3,2,1,0:T(2,128)(2,1)S(1)}, bf16[4,4,4,2,128]{4,3,2,1,0:T(2,128)(2,1)S(1)}, u32[]{:S(2)}, u32[]{:S(2)}) collective-permute-start(bf16[4,4,4,2,128]{4,3,2,1,0:T(2,128)(2,1)S(1)} %fusion), channel_id=1, source_target_pairs={{0,4},{8,12},{4,0},{12,8},{1,5},{9,13},{5,1},{13,9},{2,6},{10,14},... | collective-permute-start | bytes 98312 | tf_op jit(solution)/shard_map/ppermute | solution.py:433
  7.4 11.0 %copy-start.1 = (f32[16,4,4,2,128]{4,3,2,1,0:T(2,128)S(1)}, f32[16,4,4,2,128]{4,3,2,1,0:T(2,128)}, u32[]{:S(2)}) copy-start(f32[16,4,4,2,128]{4,3,2,1,0:T(2,128)} %param.16) | copy-start | bytes 786436
  7.6 10.5 %collective-permute-start.2 = (bf16[4,4,2,6,128]{4,3,2,1,0:T(8,128)(2,1)S(1)}, bf16[4,4,2,6,128]{4,3,2,1,0:T(8,128)(2,1)S(1)}, u32[]{:S(2)}, u32[]{:S(2)}) collective-permute-start(bf16[4,4,2,6,128]{4,3,2,1,0:T(8,128)(2,1)S(1)} %slice_select_fusion), channel_id=1, source_target_pairs={{0,16},{16,0},{1,17},{17,1},{2,18},{18,2},{3,19},{19,3},{4,20},{20... | collective-permute-start | bytes 147464 | tf_op jit(solution)/shard_map/ppermute | solution.py:433
  9.1 0.9 %copy-start = (f32[16,4,4,2,128]{4,3,2,1,0:T(2,128)S(1)}, f32[16,4,4,2,128]{4,3,2,1,0:T(2,128)}, u32[]{:S(2)}) copy-start(f32[16,4,4,2,128]{4,3,2,1,0:T(2,128)} %param.16) | copy-start | bytes 786436
  10.1 8.4 %copy-start.2 = (bf16[4,4,2,192,128]{4,3,2,1,0:T(8,128)(2,1)S(1)}, bf16[4,4,2,192,128]{4,3,2,1,0:T(8,128)(2,1)}, u32[]{:S(2)}) copy-start(bf16[4,4,2,192,128]{4,3,2,1,0:T(8,128)(2,1)} %param.13) | copy-start | bytes 4718596
  10.1 8.4 %copy-start.8 = (f32[6,4,4,4,2,128]{5,4,3,2,1,0:T(2,128)S(1)}, f32[6,4,4,4,2,128]{5,4,3,2,1,0:T(2,128)}, u32[]{:S(2)}) copy-start(f32[6,4,4,4,2,128]{5,4,3,2,1,0:T(2,128)} %param.12) | copy-start | bytes 1179652
  12.4 14.2 %all-to-all-start.1 = ((f32[32,8,128]{2,1,0:T(8,128)}), f32[32,8,128]{2,1,0:T(8,128)S(1)}, u32[]{:S(2)}, u32[]{:S(2)}) async-start(f32[32,8,128]{2,1,0:T(8,128)} %shard_map.104), calls=%async_computation.1 | async-start | bytes 262144 | tf_op jit(solution)/shard_map/all_to_all | solution.py:443
  18.2 8.3 %copy-start.6 = (f32[16,512]{1,0:T(8,128)S(1)}, f32[16,512]{1,0:T(8,128)}, u32[]{:S(2)}) copy-start(f32[16,512]{1,0:T(8,128)} %factor.1) | copy-start | bytes 98308
  18.4 19.5 %copy-start.4 = (f32[6,4,4,2,128]{4,3,2,1,0:T(2,128)S(1)}, f32[6,4,4,2,128]{4,3,2,1,0:T(2,128)}, u32[]{:S(2)}) copy-start(f32[6,4,4,2,128]{4,3,2,1,0:T(2,128)} %param.15) | copy-start | bytes 294916
  18.4 19.5 %copy-start.5 = (f32[4,4,4,2,128]{4,3,2,1,0:T(2,128)S(1)}, f32[4,4,4,2,128]{4,3,2,1,0:T(2,128)}, u32[]{:S(2)}) copy-start(f32[4,4,4,2,128]{4,3,2,1,0:T(2,128)} %param.14) | copy-start | bytes 196612
  19.9 29.9 %copy-start.3 = (f32[3,128,128]{2,1,0:T(8,128)S(1)}, f32[3,128,128]{2,1,0:T(8,128)}, u32[]{:S(2)}) copy-start(f32[3,128,128]{2,1,0:T(8,128)} %constant.77.clone.maps) | copy-start | bytes 589828
  19.9 29.9 %copy-start.7 = (f32[8,128]{1,0:T(8,128)S(1)}, f32[8,128]{1,0:T(8,128)}, u32[]{:S(2)}) copy-start(f32[8,128]{1,0:T(8,128)} %constant.78.clone.fixed) | copy-start | bytes 12292
  19.9 15.5 %collective-permute-start.3 = (f32[40,8,128]{2,1,0:T(8,128)S(1)}, f32[40,8,128]{2,1,0:T(8,128)S(1)}, u32[]{:S(2)}, u32[]{:S(2)}) collective-permute-start(f32[40,8,128]{2,1,0:T(8,128)S(1)} %get-tuple-element.50), channel_id=1, source_target_pairs={{0,4},{8,12},{4,0},{12,8},{1,5},{9,13},{5,1},{13,9},{2,6},{10,14},... | collective-permute-start | bytes 491528 | tf_op jit(solution)/shard_map/ppermute | solution.py:470
  20.2 15.2 %collective-permute-start.4 = (f32[40,8,128]{2,1,0:T(8,128)S(1)}, f32[40,8,128]{2,1,0:T(8,128)S(1)}, u32[]{:S(2)}, u32[]{:S(2)}) collective-permute-start(f32[40,8,128]{2,1,0:T(8,128)S(1)} %get-tuple-element.51), channel_id=1, source_target_pairs={{4,8},{8,4},{5,9},{9,5},{6,10},{10,6},{7,11},{11,7},{20,24},{24,20... | collective-permute-start | bytes 491528 | tf_op jit(solution)/shard_map/ppermute | solution.py:470
  27.8 10.1 %all-to-all-start.2 = ((f32[32,4,128]{2,1,0:T(4,128)}), f32[32,4,128]{2,1,0:T(4,128)S(1)}, u32[]{:S(2)}, u32[]{:S(2)}) async-start(f32[32,4,128]{2,1,0:T(4,128)} %bitcast.12), calls=%async_computation.2 | async-start | bytes 131072 | tf_op jit(solution)/shard_map/all_to_all | solution.py:443
  30.4 5.0 %collective-permute-start.5 = (f32[20,8,128]{2,1,0:T(8,128)S(1)}, f32[20,8,128]{2,1,0:T(8,128)S(1)}, u32[]{:S(2)}, u32[]{:S(2)}) collective-permute-start(f32[20,8,128]{2,1,0:T(8,128)S(1)} %get-tuple-element.52), channel_id=1, source_target_pairs={{0,16},{16,0},{1,17},{17,1},{2,18},{18,2},{3,19},{19,3},{4,20},{20... | collective-permute-start | bytes 245768 | tf_op jit(solution)/shard_map/ppermute | solution.py:471
  51.8 0.6 %copy-start.9 = (f32[4,7]{1,0:T(4,128)}, f32[4,7]{1,0:T(4,128)S(1)}, u32[]{:S(2)}) copy-start(f32[4,7]{1,0:T(4,128)S(1)} %get-tuple-element.64) | copy-start | bytes 340
  51.9 0.6 %copy-start.10 = (f32[16,8,128]{2,1,0:T(8,128)}, f32[16,8,128]{2,1,0:T(8,128)S(1)}, u32[]{:S(2)}) copy-start(f32[16,8,128]{2,1,0:T(8,128)S(1)} %get-tuple-element.65) | copy-start | bytes 196612

commit v3 on v2

--- a/solution.py
+++ b/solution.py
@@ -28,13 +28,13 @@
 F32 = jnp.float32
 
 
-def call(body, outs, operands, flops, scratch=()):
-    size = sum(x.size * x.dtype.itemsize for x in list(operands) + list(outs))
+def call(body, outs, operands, flops, in_specs=None, out_specs=None, scratch=()):
+    size = sum(int(np.prod(x.shape)) * x.dtype.itemsize for x in list(operands) + list(outs))
     return pl.pallas_call(
         body,
         out_shape=tuple(outs),
-        in_specs=[VMEM] * len(operands),
-        out_specs=tuple([VMEM] * len(outs)),
+        in_specs=in_specs or [VMEM] * len(operands),
+        out_specs=tuple(out_specs or [VMEM] * len(outs)),
         scratch_shapes=list(scratch),
         compiler_params=pltpu.CompilerParams(vmem_limit_bytes=24 * 1024 * 1024),
         cost_estimate=pl.CostEstimate(flops=flops, bytes_accessed=size, transcendentals=0),
@@ -43,6 +43,14 @@
 
 def shape(*dims, dtype=F32):
     return jax.ShapeDtypeStruct(dims, dtype)
+
+
+def kept(*dims, dtype=F32):
+    return pltpu.VMEM(dims, dtype)
+
+
+def in_hbm(x):
+    return pltpu.with_memory_space_constraint(x, pltpu.HBM)
 
 
 def iota(axis):
@@ -93,17 +101,32 @@
     return jnp.where(pick, 1.0, 0.0).astype(F32)
 
 
+def both_sides(axis):
+    at = lax.axis_index(axis)
+    return at > 0, at < lax.axis_size(axis) - 1
+
+
 def place():
     x, y, z = (lax.axis_index(a) for a in AXES)
     ny, nz = lax.axis_size("gy"), lax.axis_size("gz")
     return (x * ny + y) * nz + z, z > 0, z < nz - 1
 
 
-def rhs_body(basis, phi, out):
+def load_body(basis, phi, vector, rounded, phi_kept, sems):
+    first = pltpu.make_async_copy(basis.at[M - 1], vector, sems.at[0])
+    second = pltpu.make_async_copy(phi, phi_kept, sems.at[1])
+    first.start()
+    second.start()
+    first.wait()
+    rounded[...] = vector[...].astype(jnp.bfloat16)
+    second.wait()
+
+
+def rhs_body(vector, phi, out):
     n = out.shape[0]
     rows = []
     for s in range(S):
-        v = [basis[M - 1, s * C + c] for c in range(C)]
+        v = [vector[s * C + c] for c in range(C)]
         prods = [sum(phi[k * C + c] * v[c] for c in range(C)) for k in range(K)]
         rows.append(row_sums(prods[:8]))
         rows.append(row_sums(prods[8:]))
@@ -266,6 +289,8 @@
     odd_y = lax.axis_index("gy") % 2 == 1
     odd_x = lax.axis_index("gx") % 2 == 1
 
+    has_y, has_x = both_sides("gy"), both_sides("gx")
+
     def y_side(face, coef):
         sums = []
         for s in range(S):
@@ -302,7 +327,7 @@
         x_second = x_side(faces[3], jnp.where(odd_x, xhi, xlo))
     else:
         x_first = x_side(faces[2], coefs("x"))
-        x_second = [jnp.zeros((8, 128), F32)] * (S * C)
+        x_second = x_first
 
     me, below, above = place()
 
@@ -339,8 +364,9 @@
             y_high = jnp.where(odd_y, y_second[i], y_first[i])
             x_low = jnp.where(odd_x, x_first[i], x_second[i])
             x_high = jnp.where(odd_x, x_second[i], x_first[i])
-            y_low = y_low + rolled(y_low, -1, 0)
-            y_high = y_high + rolled(y_high, 1, 0)
+            y_low = jnp.where(has_y[0], y_low + rolled(y_low, -1, 0), 0.0)
+            y_high = jnp.where(has_y[1], y_high + rolled(y_high, 1, 0), 0.0)
+            x_low, x_high = jnp.where(has_x[0], x_low, 0.0), jnp.where(has_x[1], x_high, 0.0)
             sides = [
                 jnp.where(sub < CY, x_low, rolled(x, CY, 0)),
                 jnp.where(sub >= XY - CY, x_high, rolled(x, -CY, 0)),
@@ -409,7 +435,7 @@
         size = size + rolled(size, shift, 1)
     norm = jnp.sqrt(jnp.maximum(terms, 0.0) / unknowns + epsilon)
     scale = 1.0 / norm
-    flag[...] = jnp.where(terms < CANCEL * size, 1.0, 0.0)
+    flag[0] = jnp.max(jnp.where(terms < CANCEL * size, 1, 0))
     for s in range(S):
         w = [splat(h, BASE + 4 * m + s) for m in range(M)]
         f = splat(scale, s)
@@ -423,19 +449,26 @@
 
 def pairs_of(axis):
     count = lax.axis_size(axis)
-    rounds = [[(i, i + 1) for i in range(start, count - 1, 2)] for start in (0, 1)]
-    return [r + [(j, i) for i, j in r] for r in rounds if r]
-
-
-def swap_rounds(axis, low_side, high_side):
+    rounds = [[(i, i + 1) for i in range(0, count, 2)]]
+    if count > 2:
+        rounds.append([(i, (i + 1) % count) for i in range(1, count, 2)])
+    return [r + [(j, i) for i, j in r] for r in rounds]
+
+
+def swap(axis, low_side, high_side):
     odd = lax.axis_index(axis) % 2 == 1
     rounds = pairs_of(axis)
-    got_first = lax.ppermute(jnp.where(odd, low_side, high_side), axis, rounds[0])
-    if len(rounds) == 2:
-        got_second = lax.ppermute(jnp.where(odd, high_side, low_side), axis, rounds[1])
-    else:
-        got_second = jnp.zeros_like(got_first)
-    return jnp.where(odd, got_first, got_second), jnp.where(odd, got_second, got_first)
+    sides = [jnp.where(odd, low_side, high_side), jnp.where(odd, high_side, low_side)]
+    return [lax.ppermute(x, axis, pairs) for x, pairs in zip(sides, rounds)]
+
+
+def by_side(axis, got):
+    at = lax.axis_index(axis)
+    odd = at % 2 == 1
+    first, second = got if len(got) == 2 else (got[0], got[0])
+    low, high = jnp.where(odd, first, second), jnp.where(odd, second, first)
+    none = jnp.zeros_like(first)
+    return jnp.where(at > 0, low, none), jnp.where(at < lax.axis_size(axis) - 1, high, none)
 
 
 def exchange(rows, n):
@@ -450,13 +483,22 @@
     vectors = basis.reshape(M, S * C, XY, CZ)
     phi = coarse_basis.reshape(K * C, XY, CZ)
 
-    rounded = basis[M - 1].astype(jnp.bfloat16)
-    y_low, y_high = swap_rounds("gy", rounded, rounded)
-    (rhs,) = call(rhs_body, [shape(n, 8, 128)], (vectors, phi), 2 * K * S * C * XY * CZ)
+    vector, rounded, phi = call(
+        load_body,
+        [kept(S * C, XY, CZ), kept(S * C, XY, CZ, dtype=jnp.bfloat16), kept(K * C, XY, CZ)],
+        (in_hbm(vectors), in_hbm(phi)),
+        S * C * XY * CZ,
+        in_specs=[pl.BlockSpec(memory_space=pltpu.HBM)] * 2,
+        scratch=[pltpu.SemaphoreType.DMA((2,))],
+    )
+    rounded = rounded.reshape(S, C, CX, CY, CZ)
+    (rhs,) = call(rhs_body, [kept(n, 8, 128)], (vector, phi), 2 * K * S * C * XY * CZ)
+    swapped, rhs = lax.optimization_barrier((swap("gy", rounded, rounded), rhs))
+    y_low, y_high = by_side("gy", swapped)
     got = exchange(rhs, n).reshape(n * 8, 128)
 
     extended = jnp.concatenate([y_low, rounded, y_high], axis=3)
-    x_low, x_high = swap_rounds("gx", extended[:, :, :2], extended[:, :, -2:])
+    x_low, x_high = by_side("gx", swap("gx", extended[:, :, :2], extended[:, :, -2:]))
     extended = jnp.concatenate([x_low, extended, x_high], axis=2)
     columns = extended.reshape(S, ROWS, CZ)
     half, quarter = (K + S) * C // 2, (K + S) * C // 4
@@ -467,20 +509,21 @@
         (inverse_rows.reshape(C, XY, ROWS, CZ), columns, phi, vectors),
         2 * S * C * XY * ROWS * CZ,
     )
+    x_faces = [lax.ppermute(x, "gx", pairs) for x, pairs in zip(sends[2:], pairs_of("gx"))]
     faces = [lax.ppermute(x, "gy", pairs) for x, pairs in zip(sends, pairs_of("gy"))]
-    faces += [lax.ppermute(x, "gx", pairs) for x, pairs in zip(sends[2:], pairs_of("gx"))]
+    faces += x_faces
 
     stride = 8 if two_x else 4
     (shares,) = call(
         functools.partial(factor_body, two_x),
-        [shape(n * stride, 128)],
+        [kept(n * stride, 128)],
         (got, locz, coarse_factor),
         4 * S * K * K * n,
     )
     coarse = exchange(shares, n).reshape(n * stride, 128)
     pre, image, sent = call(
         functools.partial(image_body, two_x),
-        [shape(S * C, XY, CZ), shape(S * C, XY, CZ), shape(n, 128)],
+        [shape(S * C, XY, CZ), kept(S * C, XY, CZ), kept(n, 128)],
         (
             loc,
             phi,
@@ -498,9 +541,10 @@
     maps, fixed = tables()
     krylov, hessenberg, flag = call(
         functools.partial(finish_body, unknowns),
-        [shape(S * C, XY, CZ), shape(S, M + 1), shape(8, 128)],
+        [shape(S * C, XY, CZ), shape(S, M + 1), pltpu.SMEM((1,), jnp.int32)],
         (products, image, vectors, jnp.asarray(maps), jnp.asarray(fixed)),
         2 * S * C * XY * CZ * 8,
+        out_specs=[VMEM, VMEM, pl.BlockSpec(memory_space=pltpu.SMEM)],
     )
 
     def exact(image, vectors, krylov, hessenberg):
@@ -520,7 +564,7 @@
         return krylov, hessenberg
 
     krylov, hessenberg = lax.cond(
-        jnp.max(flag) > 0.0, exact, as_is, image, vectors, krylov, hessenberg
+        flag[0] > 0, exact, as_is, image, vectors, krylov, hessenberg
     )
     cells = (S, C, CX, CY, CZ)
     return krylov.reshape(cells), pre.reshape(cells), hessenberg

time: 52.8 us -> 47 us (0.89)
  local copies, waits for them, and re-layouts: 2.67 us -> 0.71 us
  starting transfers between devices: 17.5 us -> 15.9 us
  waiting for transfers between devices: 12.4 us -> 11.2 us
  between operations: 1.46 us -> 0.82 us
  other arithmetic: 0.9 us -> 0.34 us
    ppermute x3, starting transfers between devices: 6.61 us -> 4.82 us  [swap(): return [lax.ppermute(x, axis, pairs) for x, pairs in zip(sides, rounds)]]
    ppermute x2, starting transfers between devices: 0.96 us -> 1.93 us  [on_device(): lax.ppermute(x, 'gy', pairs)]
    unnamed x22 -> x18, local copies, waits for them, and re-layouts: 1.61 us -> 0.66 us
    convert_element_type x1 -> x0, local copies, waits for them, and re-layouts: 0.87 us -> none  [on_device(): rounded = basis[M - 1].astype(jnp.bfloat16)]
    all_to_all x2, waiting for transfers between devices: 8.24 us -> 7.41 us  [exchange(): return lax.all_to_all(sent, AXES, 0, 0, tiled=True)]
    all_to_all x2, starting transfers between devices: 8.25 us -> 7.49 us  [exchange(): return lax.all_to_all(sent, AXES, 0, 0, tiled=True)]
    reduce_max x1 -> x0, other arithmetic: 0.6 us -> none  [on_device(): jnp.max(flag) > 0.0]
    pallas_call x5 -> x6, Pallas kernels: 7.66 us -> 7.8 us  [call(): pl.pallas_call(body, out_shape=tuple(outs), in_specs=in_specs or [VMEM] *...]
  transfers between devices with their start and end apart: 8 -> 8, of which waited for: 4 -> 4; matrix products, arithmetic and copies ran while one was open for 1% -> 0% of each run, Pallas kernels for 9% -> 8%
where the time goes in v3:
time: 47 us; the launch traced here: 46.7 us
  starting transfers between devices  15.9 us (34%)
  waiting for transfers between devices  11.2 us (24%)
  blocking collectives  9.9 us (21%)
  Pallas kernels  7.8 us (17%)
  between operations  0.82 us (2%)
  local copies, waits for them, and re-layouts  0.71 us (2%)
    all_to_all x1, blocking collectives, exchange(): return lax.all_to_all(sent, AXES, 0, 0, tiled=True)  9.9 us
    pallas_call x6, Pallas kernels, call(): pl.pallas_call(body, out_shape=tuple(outs), in_specs=in_specs or [VMEM] *...  7.8 us
    all_to_all x2, starting transfers between devices, exchange(): return lax.all_to_all(sent, AXES, 0, 0, tiled=True)  7.49 us
    all_to_all x2, waiting for transfers between devices, exchange(): return lax.all_to_all(sent, AXES, 0, 0, tiled=True)  7.41 us
    ppermute x3, starting transfers between devices, swap(): return [lax.ppermute(x, axis, pairs) for x, pairs in zip(sides, rounds)]  4.82 us
    ppermute x1, waiting for transfers between devices, on_device(): lax.ppermute(x, 'gx', pairs)  3.26 us
    ppermute x2, starting transfers between devices, on_device(): lax.ppermute(x, 'gy', pairs)  1.93 us
    ppermute x1, starting transfers between devices, on_device(): lax.ppermute(x, 'gx', pairs)  1.7 us
  transfers between devices with their start and end apart: 8, of which 4 were waited for; matrix products, arithmetic and copies ran while one was open for 0% of the time, Pallas kernels for 8%

profile of v3, /device:TPU:0, one launch (start us, length us, event | category | flops | bytes accessed | tf_op | source)
XLA Modules:
  0.0 46.7 jit_solution(16012217288409636018)
XLA Ops:
  0.6 0.0 copy-start.6
  0.6 0.0 copy-start
  0.7 1.1 %shard_map.103 = (f32[16,8,128]{2,1,0:T(8,128)S(1)}, bf16[16,8,128]{2,1,0:T(8,128)(2,1)S(1)}, f32[64,8,128]{2,1,0:T(8,128)S(1)}) custom-call(f32[6,16,8,128]{3,2,1,0:T(8,128)} %bitcast.32, f32[64,8,128]{2,1,0:T(8,128)} %bitcast.38), custom_call_target="tpu_custom_call" | custom-call | flops 16384 | bytes 1015808 | tf_op jit(solution)/shard_map/pallas_call | solution.py:33
  1.8 0.5 %collective-permute-start = (bf16[4,4,4,2,128]{4,0,3,2,1:T(4,128)(2,1)S(1)}, bf16[4,4,4,2,128]{4,0,3,2,1:T(4,128)(2,1)S(1)}, u32[]{:S(2)}, u32[]{:S(2)}) collective-permute-start(bf16[4,4,4,2,128]{4,0,3,2,1:T(4,128)(2,1)S(1)} %copy.36), channel_id=1, source_target_pairs={{0,4},{8,12},{4,0},{12,8},{1,5},{9,13},{5,1},{13,9},{2,6},{10,14},... | collective-permute-start | bytes 98312 | tf_op jit(solution)/shard_map/ppermute | solution.py:462
  2.3 2.6 %collective-permute-start.1 = (bf16[4,4,4,2,128]{4,0,3,2,1:T(4,128)(2,1)S(1)}, bf16[4,4,4,2,128]{4,0,3,2,1:T(4,128)(2,1)S(1)}, u32[]{:S(2)}, u32[]{:S(2)}) collective-permute-start(bf16[4,4,4,2,128]{4,0,3,2,1:T(4,128)(2,1)S(1)} %copy.36), channel_id=1, source_target_pairs={{4,8},{12,0},{8,4},{0,12},{5,9},{13,1},{9,5},{1,13},{6,10},{14,2},... | collective-permute-start | bytes 98312 | tf_op jit(solution)/shard_map/ppermute | solution.py:462
  5.0 1.1 %shard_map.104 = f32[32,8,128]{2,1,0:T(8,128)} custom-call(f32[16,8,128]{2,1,0:T(8,128)S(1)} %get-tuple-element.54.vector, f32[64,8,128]{2,1,0:T(8,128)S(1)} %get-tuple-element.55.phi), custom_call_target="tpu_custom_call" | custom-call | flops 524288 | bytes 458752 | tf_op jit(solution)/shard_map/pallas_call | solution.py:33
  6.1 0.0 collective-permute-done
  6.1 0.5 %collective-permute-done.1 = bf16[4,4,4,2,128]{4,0,3,2,1:T(4,128)(2,1)S(1)} collective-permute-done((bf16[4,4,4,2,128]{4,0,3,2,1:T(4,128)(2,1)S(1)}, bf16[4,4,4,2,128]{4,0,3,2,1:T(4,128)(2,1)S(1)}, u32[]{:S(2)}, u32[]{:S(2)}) %collective-permute-start.1) | collective-permute-done | bytes 32800 | tf_op jit(solution)/shard_map/ppermute | solution.py:462
  6.7 0.1 pad_maximum_fusion.2
  6.8 1.7 %collective-permute-start.2 = (bf16[4,4,2,6,128]{4,0,3,2,1:T(4,128)(2,1)S(1)}, bf16[4,4,2,6,128]{4,0,3,2,1:T(4,128)(2,1)S(1)}, u32[]{:S(2)}, u32[]{:S(2)}) collective-permute-start(bf16[4,4,2,6,128]{4,0,3,2,1:T(4,128)(2,1)S(1)} %slice_select_fusion), channel_id=1, source_target_pairs={{0,16},{16,0},{1,17},{17,1},{2,18},{18,2},{3,19},{19,3},{4,20},{20... | collective-permute-start | bytes 147464 | tf_op jit(solution)/shard_map/ppermute | solution.py:462
  8.5 4.9 %all-to-all-start.1 = ((f32[32,8,128]{2,1,0:T(8,128)}), f32[32,8,128]{2,1,0:T(8,128)S(1)}, u32[]{:S(2)}, u32[]{:S(2)}) async-start(f32[32,8,128]{2,1,0:T(8,128)} %shard_map.104), calls=%async_computation.1 | async-start | bytes 262144 | tf_op jit(solution)/shard_map/all_to_all | solution.py:476
  13.4 0.0 collective-permute-done.2
  13.5 0.0 copy-start.4
  13.5 0.2 pad_maximum_fusion.1
  13.6 0.0 copy-start.2
  13.6 0.0 copy-start.3
  13.7 0.0 copy-done.6
  13.7 0.0 copy-done
  13.7 1.4 %shard_map.105 = (f32[16,8,128]{2,1,0:T(8,128)S(1)}, f32[8,128]{1,0:T(8,128)S(1)}, f32[88,128]{1,0:T(8,128)S(1)}, f32[40,8,128]{2,1,0:T(8,128)S(1)}, f32[40,8,12...) custom-call(bf16[4,8,192,128]{3,2,1,0:T(8,128)(2,1)S(1)} %bitcast.23, bf16[4,192,128]{2,1,0:T(8,128)(2,1)S(1)} %copy.39.cols, ...), custom_call_target="tpu_custom_call" | custom-call | flops 6291456 | bytes 2949120 | tf_op jit(solution)/shard_map/pallas_call | solution.py:33
  15.1 0.0 copy-start.1
  15.1 0.0 copy-start.5
  15.1 0.3 collective-permute-start.3
  15.4 1.6 %collective-permute-start.4 = (f32[40,8,128]{2,1,0:T(8,128)S(1)}, f32[40,8,128]{2,1,0:T(8,128)S(1)}, u32[]{:S(2)}, u32[]{:S(2)}) collective-permute-start(f32[40,8,128]{2,1,0:T(8,128)S(1)} %get-tuple-element.63), channel_id=1, source_target_pairs={{4,8},{12,0},{8,4},{0,12},{5,9},{13,1},{9,5},{1,13},{6,10},{14,2},... | collective-permute-start | bytes 491528 | tf_op jit(solution)/shard_map/ppermute | solution.py:513
  17.0 4.9 %all-to-all-done.1 = f32[32,8,128]{2,1,0:T(8,128)S(1)} async-done(((f32[32,8,128]{2,1,0:T(8,128)}), f32[32,8,128]{2,1,0:T(8,128)S(1)}, u32[]{:S(2)}, u32[]{:S(2)}) %all-to-all-start.1) | async-done | bytes 131104 | tf_op jit(solution)/shard_map/all_to_all | solution.py:476
  21.9 0.0 copy-done.4
  21.9 1.3 %shard_map.106 = f32[128,128]{1,0:T(8,128)} custom-call(f32[256,128]{1,0:T(8,128)S(1)} %bitcast.24, f32[8,128]{1,0:T(8,128)S(1)} %get-tuple-element.61.locz, f32[16,512]{1,0:T(8,128)S(1)} %copy-done.4), custom_call_target="tpu_custom_call" | custom-call | flops 131072 | bytes 233472 | tf_op jit(solution)/shard_map/pallas_call | solution.py:33
  23.2 2.6 %all-to-all-start.2 = ((f32[32,4,128]{2,1,0:T(4,128)}), f32[32,4,128]{2,1,0:T(4,128)S(1)}, u32[]{:S(2)}, u32[]{:S(2)}) async-start(f32[32,4,128]{2,1,0:T(4,128)} %bitcast.12), calls=%async_computation.2 | async-start | bytes 131072 | tf_op jit(solution)/shard_map/all_to_all | solution.py:476
  25.7 1.7 %collective-permute-start.5 = (f32[20,8,128]{2,1,0:T(8,128)S(1)}, f32[20,8,128]{2,1,0:T(8,128)S(1)}, u32[]{:S(2)}, u32[]{:S(2)}) collective-permute-start(f32[20,8,128]{2,1,0:T(8,128)S(1)} %get-tuple-element.64), channel_id=1, source_target_pairs={{0,16},{16,0},{1,17},{17,1},{2,18},{18,2},{3,19},{19,3},{4,20},{20... | collective-permute-start | bytes 245768 | tf_op jit(solution)/shard_map/ppermute | solution.py:512
  27.4 3.3 %collective-permute-done.5.rest_2_ = f32[20,8,128]{2,1,0:T(8,128)S(1)} collective-permute-done((f32[20,8,128]{2,1,0:T(8,128)S(1)}, f32[20,8,128]{2,1,0:T(8,128)S(1)}, u32[]{:S(2)}, u32[]{:S(2)}) %collective-permute-start.5) | collective-permute-done | bytes 81952 | tf_op jit(solution)/shard_map/ppermute | solution.py:512
  30.7 0.0 collective-permute-done.3.rest_0_
  30.7 0.0 collective-permute-done.4.rest_1_
  30.7 2.5 %all-to-all-done.2 = f32[32,4,128]{2,1,0:T(4,128)S(1)} async-done(((f32[32,4,128]{2,1,0:T(4,128)}), f32[32,4,128]{2,1,0:T(4,128)S(1)}, u32[]{:S(2)}, u32[]{:S(2)}) %all-to-all-start.2) | async-done | bytes 65568 | tf_op jit(solution)/shard_map/all_to_all | solution.py:476
  33.2 0.0 copy-done.2
  33.2 0.0 copy-done.3
  33.2 2.0 %shard_map.107 = (f32[16,8,128]{2,1,0:T(8,128)}, f32[16,8,128]{2,1,0:T(8,128)S(1)}, f32[32,128]{1,0:T(8,128)S(1)}) custom-call(f32[16,8,128]{2,1,0:T(8,128)S(1)} %get-tuple-element.58.loc, f32[64,8,128]{2,1,0:T(8,128)S(1)} %get-tuple-element.55.phi, f32[16,8,128]{2,1,0:T(8,128)S(1)} %bitcast.28, f32[24,8,128]{2,1,0:T(8,128)S(1)} %bitcast.27, ...), custom_call_target="tpu_custom_call" | custom-call | flops 1310720 | bytes 1683456 | tf_op jit(solution)/shard_map/pallas_call | solution.py:33
  35.2 9.9 %all_to_all.20 = f32[32,1,128]{2,1,0:T(1,128)S(1)} all-to-all(f32[32,1,128]{2,1,0:T(1,128)S(1)} %bitcast.31), channel_id=1, replica_groups=mesh['gx'=2,'gy'=4,'gz'=4] {'gx','gy','gz'}, dimensions={0} | all-to-all | bytes 32768 | tf_op jit(solution)/shard_map/all_to_all | solution.py:476
  45.1 0.0 copy-done.1
  45.1 0.0 copy-done.5
  45.1 0.9 %shard_map.108 = (f32[16,8,128]{2,1,0:T(8,128)S(1)}, f32[4,7]{1,0:T(4,128)S(1)}, s32[1]{0:T(128)S(4)}) custom-call(f32[32,128]{1,0:T(8,128)S(1)} %bitcast.29, f32[16,8,128]{2,1,0:T(8,128)S(1)} %get-tuple-element.66.image, f32[6,16,8,128]{3,2,1,0:T(8,128)S(1)} %bitcast.35, f32[3,128,128]{2,1,0:T(8,128)S(1)} %copy-done.1, f32[8,128]{1,0:T(8,128)S(1)} %copy-done.5), custom_call_target="tpu_custom_call" | custom-call | flops 262144 | bytes 741492 | tf_op jit(solution)/shard_map/pallas_call | solution.py:33
  46.1 0.0 copy-start.7
  46.1 0.0 copy-start.8
  46.1 0.6 %copy-done.7 = f32[4,7]{1,0:T(4,128)} copy-done((f32[4,7]{1,0:T(4,128)}, f32[4,7]{1,0:T(4,128)S(1)}, u32[]{:S(2)}) %copy-start.7) | copy-done | bytes 136
  46.7 0.1 copy-done.8
  (6 shorter events, 0.2 us)
Async XLA Ops:
  0.6 13.1 %copy-start.6 = (f32[6,4,4,4,2,128]{5,4,3,2,1,0:T(2,128)S(1)}, f32[6,4,4,4,2,128]{5,4,3,2,1,0:T(2,128)}, u32[]{:S(2)}) copy-start(f32[6,4,4,4,2,128]{5,4,3,2,1,0:T(2,128)} %param.12) | copy-start | bytes 1179652
  0.6 13.1 %copy-start = (bf16[4,4,2,192,128]{4,3,2,1,0:T(8,128)(2,1)S(1)}, bf16[4,4,2,192,128]{4,3,2,1,0:T(8,128)(2,1)}, u32[]{:S(2)}) copy-start(bf16[4,4,2,192,128]{4,3,2,1,0:T(8,128)(2,1)} %param.13) | copy-start | bytes 4718596
  1.8 4.3 %collective-permute-start = (bf16[4,4,4,2,128]{4,0,3,2,1:T(4,128)(2,1)S(1)}, bf16[4,4,4,2,128]{4,0,3,2,1:T(4,128)(2,1)S(1)}, u32[]{:S(2)}, u32[]{:S(2)}) collective-permute-start(bf16[4,4,4,2,128]{4,0,3,2,1:T(4,128)(2,1)S(1)} %copy.36), channel_id=1, source_target_pairs={{0,4},{8,12},{4,0},{12,8},{1,5},{9,13},{5,1},{13,9},{2,6},{10,14},... | collective-permute-start | bytes 98312 | tf_op jit(solution)/shard_map/ppermute | solution.py:462
  2.3 4.3 %collective-permute-start.1 = (bf16[4,4,4,2,128]{4,0,3,2,1:T(4,128)(2,1)S(1)}, bf16[4,4,4,2,128]{4,0,3,2,1:T(4,128)(2,1)S(1)}, u32[]{:S(2)}, u32[]{:S(2)}) collective-permute-start(bf16[4,4,4,2,128]{4,0,3,2,1:T(4,128)(2,1)S(1)} %copy.36), channel_id=1, source_target_pairs={{4,8},{12,0},{8,4},{0,12},{5,9},{13,1},{9,5},{1,13},{6,10},{14,2},... | collective-permute-start | bytes 98312 | tf_op jit(solution)/shard_map/ppermute | solution.py:462
  6.8 6.6 %collective-permute-start.2 = (bf16[4,4,2,6,128]{4,0,3,2,1:T(4,128)(2,1)S(1)}, bf16[4,4,2,6,128]{4,0,3,2,1:T(4,128)(2,1)S(1)}, u32[]{:S(2)}, u32[]{:S(2)}) collective-permute-start(bf16[4,4,2,6,128]{4,0,3,2,1:T(4,128)(2,1)S(1)} %slice_select_fusion), channel_id=1, source_target_pairs={{0,16},{16,0},{1,17},{17,1},{2,18},{18,2},{3,19},{19,3},{4,20},{20... | collective-permute-start | bytes 147464 | tf_op jit(solution)/shard_map/ppermute | solution.py:462
  8.5 13.4 %all-to-all-start.1 = ((f32[32,8,128]{2,1,0:T(8,128)}), f32[32,8,128]{2,1,0:T(8,128)S(1)}, u32[]{:S(2)}, u32[]{:S(2)}) async-start(f32[32,8,128]{2,1,0:T(8,128)} %shard_map.104), calls=%async_computation.1 | async-start | bytes 262144 | tf_op jit(solution)/shard_map/all_to_all | solution.py:476
  13.5 8.4 %copy-start.4 = (f32[16,512]{1,0:T(8,128)S(1)}, f32[16,512]{1,0:T(8,128)}, u32[]{:S(2)}) copy-start(f32[16,512]{1,0:T(8,128)} %factor.1) | copy-start | bytes 98308
  13.6 19.6 %copy-start.2 = (f32[6,4,4,2,128]{4,3,2,1,0:T(2,128)S(1)}, f32[6,4,4,2,128]{4,3,2,1,0:T(2,128)}, u32[]{:S(2)}) copy-start(f32[6,4,4,2,128]{4,3,2,1,0:T(2,128)} %param.15) | copy-start | bytes 294916
  13.6 19.6 %copy-start.3 = (f32[4,4,4,2,128]{4,3,2,1,0:T(2,128)S(1)}, f32[4,4,4,2,128]{4,3,2,1,0:T(2,128)}, u32[]{:S(2)}) copy-start(f32[4,4,4,2,128]{4,3,2,1,0:T(2,128)} %param.14) | copy-start | bytes 196612
  15.1 30.0 %copy-start.1 = (f32[3,128,128]{2,1,0:T(8,128)S(1)}, f32[3,128,128]{2,1,0:T(8,128)}, u32[]{:S(2)}) copy-start(f32[3,128,128]{2,1,0:T(8,128)} %constant.83.clone.maps) | copy-start | bytes 589828
  15.1 30.0 %copy-start.5 = (f32[8,128]{1,0:T(8,128)S(1)}, f32[8,128]{1,0:T(8,128)}, u32[]{:S(2)}) copy-start(f32[8,128]{1,0:T(8,128)} %constant.84.clone.fixed) | copy-start | bytes 12292
  15.1 15.6 %collective-permute-start.3 = (f32[40,8,128]{2,1,0:T(8,128)S(1)}, f32[40,8,128]{2,1,0:T(8,128)S(1)}, u32[]{:S(2)}, u32[]{:S(2)}) collective-permute-start(f32[40,8,128]{2,1,0:T(8,128)S(1)} %get-tuple-element.62), channel_id=1, source_target_pairs={{0,4},{8,12},{4,0},{12,8},{1,5},{9,13},{5,1},{13,9},{2,6},{10,14},... | collective-permute-start | bytes 491528 | tf_op jit(solution)/shard_map/ppermute | solution.py:513
  15.4 15.3 %collective-permute-start.4 = (f32[40,8,128]{2,1,0:T(8,128)S(1)}, f32[40,8,128]{2,1,0:T(8,128)S(1)}, u32[]{:S(2)}, u32[]{:S(2)}) collective-permute-start(f32[40,8,128]{2,1,0:T(8,128)S(1)} %get-tuple-element.63), channel_id=1, source_target_pairs={{4,8},{12,0},{8,4},{0,12},{5,9},{13,1},{9,5},{1,13},{6,10},{14,2},... | collective-permute-start | bytes 491528 | tf_op jit(solution)/shard_map/ppermute | solution.py:513
  23.2 10.1 %all-to-all-start.2 = ((f32[32,4,128]{2,1,0:T(4,128)}), f32[32,4,128]{2,1,0:T(4,128)S(1)}, u32[]{:S(2)}, u32[]{:S(2)}) async-start(f32[32,4,128]{2,1,0:T(4,128)} %bitcast.12), calls=%async_computation.2 | async-start | bytes 131072 | tf_op jit(solution)/shard_map/all_to_all | solution.py:476
  25.7 5.0 %collective-permute-start.5 = (f32[20,8,128]{2,1,0:T(8,128)S(1)}, f32[20,8,128]{2,1,0:T(8,128)S(1)}, u32[]{:S(2)}, u32[]{:S(2)}) collective-permute-start(f32[20,8,128]{2,1,0:T(8,128)S(1)} %get-tuple-element.64), channel_id=1, source_target_pairs={{0,16},{16,0},{1,17},{17,1},{2,18},{18,2},{3,19},{19,3},{4,20},{20... | collective-permute-start | bytes 245768 | tf_op jit(solution)/shard_map/ppermute | solution.py:512
  46.1 0.6 %copy-start.7 = (f32[4,7]{1,0:T(4,128)}, f32[4,7]{1,0:T(4,128)S(1)}, u32[]{:S(2)}) copy-start(f32[4,7]{1,0:T(4,128)S(1)} %get-tuple-element.76) | copy-start | bytes 340
  46.1 0.6 %copy-start.8 = (f32[16,8,128]{2,1,0:T(8,128)}, f32[16,8,128]{2,1,0:T(8,128)S(1)}, u32[]{:S(2)}) copy-start(f32[16,8,128]{2,1,0:T(8,128)S(1)} %get-tuple-element.77) | copy-start | bytes 196612

commit v4 on v3

--- a/solution.py
+++ b/solution.py
@@ -112,14 +112,32 @@
     return (x * ny + y) * nz + z, z > 0, z < nz - 1
 
 
-def load_body(basis, phi, vector, rounded, phi_kept, sems):
-    first = pltpu.make_async_copy(basis.at[M - 1], vector, sems.at[0])
-    second = pltpu.make_async_copy(phi, phi_kept, sems.at[1])
-    first.start()
-    second.start()
-    first.wait()
-    rounded[...] = vector[...].astype(jnp.bfloat16)
-    second.wait()
+def y_faces(first, second):
+    even = (iota(0) & 1) == 0
+    low = jnp.where(even, first, rolled(second, 1, 0))
+    high = jnp.where(even, rolled(first, -1, 0), second)
+    return low, high
+
+
+def load_body(basis, phi, vector, rounded, phi_kept, to_first, to_second, sems):
+    copies = [
+        pltpu.make_async_copy(basis.at[M - 1], vector, sems.at[0]),
+        pltpu.make_async_copy(phi, phi_kept, sems.at[1]),
+    ]
+    for copy in copies:
+        copy.start()
+    odd = lax.axis_index("gy") % 2 == 1
+    copies[0].wait()
+    low = vector[...].astype(jnp.bfloat16)
+    rounded[...] = low
+    to_first[: S * C] = low.astype(F32)
+    to_second[: S * C] = low.astype(F32)
+    copies[1].wait()
+    half = K * C // 2
+    for i in range(half):
+        low, high = y_faces(phi_kept[i], phi_kept[half + i])
+        to_first[S * C + i] = jnp.where(odd, low, high)
+        to_second[S * C + i] = jnp.where(odd, high, low)
 
 
 def rhs_body(vector, phi, out):
@@ -182,16 +200,13 @@
     odd_y = lax.axis_index("gy") % 2 == 1
     odd_x = lax.axis_index("gx") % 2 == 1
     sub = iota(0)
-    even = (sub & 1) == 0
 
     def block(half, of, i):
         share, own = K * C // of, S * C // of
         return phi[half * share + i] if i < share else loc[half * own + i - share]
 
-    for i in range((K + S) * C // 2):
-        a, b = block(0, 2, i), block(1, 2, i)
-        low = jnp.where(even, a, rolled(b, 1, 0))
-        high = jnp.where(even, rolled(a, -1, 0), b)
+    for i in range(S * C // 2):
+        low, high = y_faces(loc[i], loc[S * C // 2 + i])
         sends[0][i] = jnp.where(odd_y, low, high)
         sends[1][i] = jnp.where(odd_y, high, low)
     for i in range((K + S) * C // 4):
@@ -262,7 +277,7 @@
 
 
 def image_body(two_x, loc, phi, diagonal, couple, basis, gram, coarse, got, *rest):
-    faces, (pre, image, sent) = rest[:-3], rest[-3:]
+    slabs, faces, (pre, image, sent) = rest[:2], rest[2:-3], rest[-3:]
     n = sent.shape[0]
     stride = coarse.shape[0] // n
     sub, lane = iota(0), iota(1)
@@ -291,15 +306,15 @@
 
     has_y, has_x = both_sides("gy"), both_sides("gx")
 
-    def y_side(face, coef):
+    def y_side(slab, face, coef):
         sums = []
         for s in range(S):
             mine = even if s < 2 else ~even
-            part = [jnp.where(mine, face[32 + (s % 2) * C + c], 0.0) for c in range(C)]
+            part = [jnp.where(mine, face[(s % 2) * C + c], 0.0) for c in range(C)]
             for k in range(K // 2):
                 w = jnp.where(even, splat(coef, s * K + k), splat(coef, s * K + k + K // 2))
                 for c in range(C):
-                    part[c] = part[c] + w * face[k * C + c]
+                    part[c] = part[c] + w * slab[S * C + k * C + c]
             sums += part
         return sums
 
@@ -319,8 +334,8 @@
         return sums
 
     ylo, yhi = coefs("ylo"), coefs("yhi")
-    y_first = y_side(faces[0], jnp.where(odd_y, ylo, yhi))
-    y_second = y_side(faces[1], jnp.where(odd_y, yhi, ylo))
+    y_first = y_side(slabs[0], faces[0], jnp.where(odd_y, ylo, yhi))
+    y_second = y_side(slabs[1], faces[1], jnp.where(odd_y, yhi, ylo))
     if two_x:
         xlo, xhi = coefs("xlo"), coefs("xhi")
         x_first = x_side(faces[2], jnp.where(odd_x, xlo, xhi))
@@ -483,9 +498,16 @@
     vectors = basis.reshape(M, S * C, XY, CZ)
     phi = coarse_basis.reshape(K * C, XY, CZ)
 
-    vector, rounded, phi = call(
+    slab = S * C + K * C // 2
+    vector, rounded, phi, *slabs = call(
         load_body,
-        [kept(S * C, XY, CZ), kept(S * C, XY, CZ, dtype=jnp.bfloat16), kept(K * C, XY, CZ)],
+        [
+            kept(S * C, XY, CZ),
+            kept(S * C, XY, CZ, dtype=jnp.bfloat16),
+            kept(K * C, XY, CZ),
+            kept(slab, XY, CZ),
+            kept(slab, XY, CZ),
+        ],
         (in_hbm(vectors), in_hbm(phi)),
         S * C * XY * CZ,
         in_specs=[pl.BlockSpec(memory_space=pltpu.HBM)] * 2,
@@ -493,25 +515,38 @@
     )
     rounded = rounded.reshape(S, C, CX, CY, CZ)
     (rhs,) = call(rhs_body, [kept(n, 8, 128)], (vector, phi), 2 * K * S * C * XY * CZ)
-    swapped, rhs = lax.optimization_barrier((swap("gy", rounded, rounded), rhs))
-    y_low, y_high = by_side("gy", swapped)
     got = exchange(rhs, n).reshape(n * 8, 128)
-
-    extended = jnp.concatenate([y_low, rounded, y_high], axis=3)
-    x_low, x_high = by_side("gx", swap("gx", extended[:, :, :2], extended[:, :, -2:]))
-    extended = jnp.concatenate([x_low, extended, x_high], axis=2)
-    columns = extended.reshape(S, ROWS, CZ)
-    half, quarter = (K + S) * C // 2, (K + S) * C // 4
+    swapped = [lax.ppermute(x, "gy", pairs) for x, pairs in zip(slabs, pairs_of("gy"))]
+
+    always = lax.axis_index("gx") >= 0
+
+    def extend(swapped, rounded):
+        parts = [x[: S * C].reshape(S, C, CX, CY, CZ).astype(rounded.dtype) for x in swapped]
+        y_low, y_high = by_side("gy", parts)
+        extended = jnp.concatenate([y_low, rounded, y_high], axis=3)
+        x_low, x_high = by_side("gx", swap("gx", extended[:, :, :2], extended[:, :, -2:]))
+        extended = jnp.concatenate([x_low, extended, x_high], axis=2)
+        return extended.reshape(S, ROWS, CZ)
+
+    def unused(swapped, rounded):
+        return jnp.zeros((S, ROWS, CZ), rounded.dtype)
+
+    columns = lax.cond(always, extend, unused, swapped, rounded)
+    half, quarter = S * C // 2, (K + S) * C // 4
     sends = [shape(half, 8, 128)] * 2 + [shape(quarter, 8, 128)] * (2 if two_x else 1)
     loc, locz, gram, *sends = call(
         functools.partial(local_body, two_x),
         [shape(S * C, XY, CZ), shape(8, 128), shape(BASE, 128)] + sends,
         (inverse_rows.reshape(C, XY, ROWS, CZ), columns, phi, vectors),
-        2 * S * C * XY * ROWS * CZ,
-    )
-    x_faces = [lax.ppermute(x, "gx", pairs) for x, pairs in zip(sends[2:], pairs_of("gx"))]
-    faces = [lax.ppermute(x, "gy", pairs) for x, pairs in zip(sends, pairs_of("gy"))]
-    faces += x_faces
+        20000 * S * C * XY * ROWS * CZ,
+    )
+
+    def trade(*sends):
+        x_faces = [lax.ppermute(x, "gx", pairs) for x, pairs in zip(sends[2:], pairs_of("gx"))]
+        return [lax.ppermute(x, "gy", pairs) for x, pairs in zip(sends, pairs_of("gy"))] + x_faces
+
+    def untouched(*sends):
+        return list(sends)
 
     stride = 8 if two_x else 4
     (shares,) = call(
@@ -521,6 +556,7 @@
         4 * S * K * K * n,
     )
     coarse = exchange(shares, n).reshape(n * stride, 128)
+    faces = lax.cond(always, trade, untouched, *sends)
     pre, image, sent = call(
         functools.partial(image_body, two_x),
         [shape(S * C, XY, CZ), kept(S * C, XY, CZ), kept(n, 128)],
@@ -533,6 +569,7 @@
             gram,
             coarse,
             got,
+            *swapped,
             *faces,
         ),
         2 * S * C * XY * CZ * 40,

time: 47 us -> 45.6 us (0.970)
  waiting for transfers between devices: 11.2 us -> 8.76 us
  starting transfers between devices: 15.9 us -> 16.9 us
    all_to_all x2, waiting for transfers between devices: 7.41 us -> 4.27 us  [exchange(): return lax.all_to_all(sent, AXES, 0, 0, tiled=True)]
    ppermute x3 -> x1, starting transfers between devices: 4.82 us -> 1.83 us  [swap(): return [lax.ppermute(x, axis, pairs) for x, pairs in zip(sides, rounds)]]
    ppermute x3 -> x1, waiting for transfers between devices: 0.54 us -> 2.66 us  [swap(): return [lax.ppermute(x, axis, pairs) for x, pairs in zip(sides, rounds)]]
    ppermute x1 -> x3, starting transfers between devices: 1.7 us -> 3.41 us  [the longest x1 1.83 us: trade(): lax.ppermute(x, 'gx', pairs)]
    ppermute x1 -> x3, waiting for transfers between devices: 3.26 us -> 1.83 us  [the longest x2 1.82 us: trade(): lax.ppermute(x, 'gy', pairs)]
    ppermute x2, starting transfers between devices: 1.93 us -> 3.16 us  [on_device(): lax.ppermute(x, 'gy', pairs)]
    all_to_all x2, starting transfers between devices: 7.49 us -> 8.48 us  [exchange(): return lax.all_to_all(sent, AXES, 0, 0, tiled=True)]
  transfers between devices with their start and end apart: 8 -> 8, of which waited for: 4 -> 4; matrix products, arithmetic and copies ran while one was open for 0% -> 1% of each run, Pallas kernels for 8% -> 6%
where the time goes in v4:
time: 45.6 us; the launch traced here: 45.3 us
  starting transfers between devices  16.9 us (37%)
  blocking collectives  9.95 us (22%)
  waiting for transfers between devices  8.76 us (19%)
  Pallas kernels  7.83 us (17%)
  local copies, waits for them, and re-layouts  0.79 us (2%)
  between operations  0.78 us (2%)
    all_to_all x1, blocking collectives, exchange(): return lax.all_to_all(sent, AXES, 0, 0, tiled=True)  9.95 us
    all_to_all x2, starting transfers between devices, exchange(): return lax.all_to_all(sent, AXES, 0, 0, tiled=True)  8.48 us
    pallas_call x6, Pallas kernels, call(): pl.pallas_call(body, out_shape=tuple(outs), in_specs=in_specs or [VMEM] *...  7.83 us
    all_to_all x2, waiting for transfers between devices, exchange(): return lax.all_to_all(sent, AXES, 0, 0, tiled=True)  4.27 us
    ppermute x2, starting transfers between devices, on_device(): lax.ppermute(x, 'gy', pairs)  3.16 us
    ppermute x1, waiting for transfers between devices, swap(): return [lax.ppermute(x, axis, pairs) for x, pairs in zip(sides, rounds)]  2.66 us
    ppermute x1, starting transfers between devices, swap(): return [lax.ppermute(x, axis, pairs) for x, pairs in zip(sides, rounds)]  1.83 us
    ppermute x1, starting transfers between devices, trade(): lax.ppermute(x, 'gx', pairs)  1.83 us
  transfers between devices with their start and end apart: 8, of which 4 were waited for; matrix products, arithmetic and copies ran while one was open for 1% of the time, Pallas kernels for 6%

profile of v4, /device:TPU:0, one launch (start us, length us, event | category | flops | bytes accessed | tf_op | source)
XLA Modules:
  0.0 45.3 jit_solution(17822985309534548703)
XLA Ops:
  0.6 0.0 copy-start.6
  0.6 0.0 copy-start.5
  0.7 1.2 %shard_map.103 = (f32[16,8,128]{2,1,0:T(8,128)S(1)}, bf16[16,8,128]{2,1,0:T(8,128)(2,1)S(1)}, f32[64,8,128]{2,1,0:T(8,128)S(1)}, f32[48,8,128]{2,1,0:T(8,128)S(1)}, f32[48,8,128]{2,1,0:T(8,128)S(1)}) custom-call(f32[6,16,8,128]{3,2,1,0:T(8,128)} %bitcast.34, f32[64,8,128]{2,1,0:T(8,128)} %bitcast.40), custom_call_target="tpu_custom_call" | custom-call | flops 16384 | bytes 1409024 | tf_op jit(solution)/shard_map/pallas_call | solution.py:33
  1.8 0.5 %collective-permute-start.4 = (f32[48,8,128]{2,1,0:T(8,128)S(1)}, f32[48,8,128]{2,1,0:T(8,128)S(1)}, u32[]{:S(2)}, u32[]{:S(2)}) collective-permute-start(f32[48,8,128]{2,1,0:T(8,128)S(1)} %get-tuple-element.83), channel_id=1, source_target_pairs={{0,4},{8,12},{4,0},{12,8},{1,5},{9,13},{5,1},{13,9},{2,6},{10,14},... | collective-permute-start | bytes 589832 | tf_op jit(solution)/shard_map/ppermute | solution.py:519
  2.3 2.6 %collective-permute-start.5 = (f32[48,8,128]{2,1,0:T(8,128)S(1)}, f32[48,8,128]{2,1,0:T(8,128)S(1)}, u32[]{:S(2)}, u32[]{:S(2)}) collective-permute-start(f32[48,8,128]{2,1,0:T(8,128)S(1)} %get-tuple-element.84), channel_id=1, source_target_pairs={{4,8},{12,0},{8,4},{0,12},{5,9},{13,1},{9,5},{1,13},{6,10},{14,2},... | collective-permute-start | bytes 589832 | tf_op jit(solution)/shard_map/ppermute | solution.py:519
  5.0 1.1 %shard_map.105 = f32[32,8,128]{2,1,0:T(8,128)} custom-call(f32[16,8,128]{2,1,0:T(8,128)S(1)} %get-tuple-element.89.vector, f32[64,8,128]{2,1,0:T(8,128)S(1)} %get-tuple-element.86.phi), custom_call_target="tpu_custom_call" | custom-call | flops 524288 | bytes 458752 | tf_op jit(solution)/shard_map/pallas_call | solution.py:33
  6.1 4.9 %all-to-all-start.1 = ((f32[32,8,128]{2,1,0:T(8,128)}), f32[32,8,128]{2,1,0:T(8,128)S(1)}, u32[]{:S(2)}, u32[]{:S(2)}) async-start(f32[32,8,128]{2,1,0:T(8,128)} %shard_map.105), calls=%async_computation.1 | async-start | bytes 262144 | tf_op jit(solution)/shard_map/all_to_all | solution.py:491
  11.0 0.0 collective-permute-done.4.rest_0_
  11.0 0.0 collective-permute-done.5.rest_1_
  11.0 4.9 %conditional.3 = (bf16[4,192,128]{2,1,0:T(8,128)(2,1)S(1)}) conditional(s32[]{:T(128)} %convert_element_type.14, () %tuple.37, (f32[48,8,128]{2,1,0:T(8,128)S(1)}, f32[48,8,128]{2,1,0:T(8,128)S(1)}, bf16[16,8,128]{2,1,0:T(8,128)(2,1)S(1)}) %tuple.38), branch_computations={%region_0.0_spmd, %region_1.2_spmd} | conditional | flops 335906 | bytes 1606022 | solution.py:534
  11.2 1.8 %collective-permute-start.3 = (bf16[4,4,2,6,128]{4,0,3,2,1:T(4,128)(2,1)S(1)}, bf16[4,4,2,6,128]{4,0,3,2,1:T(4,128)(2,1)S(1)}, u32[]{:S(2)}, u32[]{:S(2)}) collective-permute-start(bf16[4,4,2,6,128]{4,0,3,2,1:T(4,128)(2,1)S(1)} %slice_select_fusion), channel_id=1, source_target_pairs={{0,16},{16,0},{1,17},{17,1},{2,18},{18,2},{3,19},{19,3},{4,20},{20... | collective-permute-start | bytes 147464 | tf_op jit(solution)/shard_map/cond/branch_1_fun/ppermute | solution.py:477
  13.1 2.7 %collective-permute-done.3 = bf16[4,4,2,6,128]{4,0,3,2,1:T(4,128)(2,1)S(1)} collective-permute-done((bf16[4,4,2,6,128]{4,0,3,2,1:T(4,128)(2,1)S(1)}, bf16[4,4,2,6,128]{4,0,3,2,1:T(4,128)(2,1)S(1)}, u32[]{:S(2)}, u32[]{:S(2)}) %collective-permute-start.3) | collective-permute-done | bytes 49184 | tf_op jit(solution)/shard_map/cond/branch_1_fun/ppermute | solution.py:477
  15.8 0.1 pad_maximum_fusion
  15.9 0.0 copy-done.6
  16.0 0.0 copy-done.5
  16.0 0.0 copy-start.3
  16.0 0.0 copy-start.1
  16.0 0.0 copy-start.2
  16.0 1.4 %shard_map.104 = (f32[16,8,128]{2,1,0:T(8,128)S(1)}, f32[8,128]{1,0:T(8,128)S(1)}, f32[88,128]{1,0:T(8,128)S(1)}, f32[8,8,128]{2,1,0:T(8,128)S(1)}, f32[8,8,128]{2,1,0:T(8,128)S(1)}, /*index=5*/f32[20,8,128]{2,1,0:T(8,128)S(1)}) custom-call(bf16[4,8,192,128]{3,2,1,0:T(8,128)(2,1)S(1)} %bitcast.33, bf16[4,192,128]{2,1,0:T(8,128)(2,1)S(1)} %get-tuple-element.108.cols, ...), custom_call_target="tpu_custom_call" | custom-call | flops 62914560000 | bytes 2686976 | tf_op jit(solution)/shard_map/pallas_call | solution.py:33
  17.4 0.0 copy-start
  17.4 0.0 copy-start.4
  17.4 2.0 %all-to-all-done.1 = f32[32,8,128]{2,1,0:T(8,128)S(1)} async-done(((f32[32,8,128]{2,1,0:T(8,128)}), f32[32,8,128]{2,1,0:T(8,128)S(1)}, u32[]{:S(2)}, u32[]{:S(2)}) %all-to-all-start.1) | async-done | bytes 131104 | tf_op jit(solution)/shard_map/all_to_all | solution.py:491
  19.4 0.0 copy-done.3
  19.4 1.3 %shard_map.106 = f32[128,128]{1,0:T(8,128)} custom-call(f32[256,128]{1,0:T(8,128)S(1)} %bitcast.25, f32[8,128]{1,0:T(8,128)S(1)} %get-tuple-element.90.locz, f32[16,512]{1,0:T(8,128)S(1)} %copy-done.3), custom_call_target="tpu_custom_call" | custom-call | flops 131072 | bytes 233472 | tf_op jit(solution)/shard_map/pallas_call | solution.py:33
  20.7 3.6 %all-to-all-start.2 = ((f32[32,4,128]{2,1,0:T(4,128)}), f32[32,4,128]{2,1,0:T(4,128)S(1)}, u32[]{:S(2)}, u32[]{:S(2)}) async-start(f32[32,4,128]{2,1,0:T(4,128)} %bitcast.14), calls=%async_computation.2 | async-start | bytes 131072 | tf_op jit(solution)/shard_map/all_to_all | solution.py:491
  24.3 5.3 %conditional.4 = ((f32[8,8,128]{2,1,0:T(8,128)S(1)}, f32[8,8,128]{2,1,0:T(8,128)S(1)}, f32[20,8,128]{2,1,0:T(8,128)S(1)})) conditional(s32[]{:T(128)} %convert_element_type.14, (f32[8,8,128]{2,1,0:T(8,128)S(1)}, f32[8,8,128]{2,1,0:T(8,128)S(1)}, f32[20,8,128]{2,1,0:T(8,128)S(1)}) %tuple.39, (f32[8,8,128]{2,1,0:T(8,128)S(1)}, ...), branch_computations={%region_2.3_spmd, %region_3.4_spmd} | conditional | bytes 884888 | solution.py:559
  24.3 1.8 %collective-permute-start.2 = (f32[20,8,128]{2,1,0:T(8,128)S(1)}, f32[20,8,128]{2,1,0:T(8,128)S(1)}, u32[]{:S(2)}, u32[]{:S(2)}) collective-permute-start(f32[20,8,128]{2,1,0:T(8,128)S(1)} %get-tuple-element.54), channel_id=1, source_target_pairs={{0,16},{16,0},{1,17},{17,1},{2,18},{18,2},{3,19},{19,3},{4,20},{20... | collective-permute-start | bytes 245768 | tf_op jit(solution)/shard_map/cond/branch_1_fun/ppermute | solution.py:545
  26.1 0.0 collective-permute-start
  26.1 1.6 %collective-permute-start.1 = (f32[8,8,128]{2,1,0:T(8,128)S(1)}, f32[8,8,128]{2,1,0:T(8,128)S(1)}, u32[]{:S(2)}, u32[]{:S(2)}) collective-permute-start(f32[8,8,128]{2,1,0:T(8,128)S(1)} %get-tuple-element.53), channel_id=1, source_target_pairs={{4,8},{12,0},{8,4},{0,12},{5,9},{13,1},{9,5},{1,13},{6,10},{14,2},... | collective-permute-start | bytes 98312 | tf_op jit(solution)/shard_map/cond/branch_1_fun/ppermute | solution.py:546
  27.7 0.0 collective-permute-done
  27.7 1.8 %collective-permute-done.1 = f32[8,8,128]{2,1,0:T(8,128)S(1)} collective-permute-done((f32[8,8,128]{2,1,0:T(8,128)S(1)}, f32[8,8,128]{2,1,0:T(8,128)S(1)}, u32[]{:S(2)}, u32[]{:S(2)}) %collective-permute-start.1) | collective-permute-done | bytes 32800 | tf_op jit(solution)/shard_map/cond/branch_1_fun/ppermute | solution.py:546
  29.5 0.0 collective-permute-done.2
  29.5 2.2 %all-to-all-done.2 = f32[32,4,128]{2,1,0:T(4,128)S(1)} async-done(((f32[32,4,128]{2,1,0:T(4,128)}), f32[32,4,128]{2,1,0:T(4,128)S(1)}, u32[]{:S(2)}, u32[]{:S(2)}) %all-to-all-start.2) | async-done | bytes 65568 | tf_op jit(solution)/shard_map/all_to_all | solution.py:491
  31.8 0.0 copy-done.1
  31.8 0.0 copy-done.2
  31.8 2.0 %shard_map.107 = (f32[16,8,128]{2,1,0:T(8,128)}, f32[16,8,128]{2,1,0:T(8,128)S(1)}, f32[32,128]{1,0:T(8,128)S(1)}) custom-call(f32[16,8,128]{2,1,0:T(8,128)S(1)} %get-tuple-element.87.loc, f32[64,8,128]{2,1,0:T(8,128)S(1)} %get-tuple-element.86.phi, f32[16,8,128]{2,1,0:T(8,128)S(1)} %bitcast.29, f32[24,8,128]{2,1,0:T(8,128)S(1)} %bitcast.28, ...), custom_call_target="tpu_custom_call" | custom-call | flops 1310720 | bytes 1814528 | tf_op jit(solution)/shard_map/pallas_call | solution.py:33
  33.7 10.0 %all_to_all.20 = f32[32,1,128]{2,1,0:T(1,128)S(1)} all-to-all(f32[32,1,128]{2,1,0:T(1,128)S(1)} %bitcast.32), channel_id=1, replica_groups=mesh['gx'=2,'gy'=4,'gz'=4] {'gx','gy','gz'}, dimensions={0} | all-to-all | bytes 32768 | tf_op jit(solution)/shard_map/all_to_all | solution.py:491
  43.7 0.0 copy-done
  43.7 0.0 copy-done.4
  43.7 0.9 %shard_map.108 = (f32[16,8,128]{2,1,0:T(8,128)S(1)}, f32[4,7]{1,0:T(4,128)S(1)}, s32[1]{0:T(128)S(4)}) custom-call(f32[32,128]{1,0:T(8,128)S(1)} %bitcast.30, f32[16,8,128]{2,1,0:T(8,128)S(1)} %get-tuple-element.98.image, f32[6,16,8,128]{3,2,1,0:T(8,128)S(1)} %bitcast.37, f32[3,128,128]{2,1,0:T(8,128)S(1)} %copy-done, f32[8,128]{1,0:T(8,128)S(1)} %copy-done.4), custom_call_target="tpu_custom_call" | custom-call | flops 262144 | bytes 741492 | tf_op jit(solution)/shard_map/pallas_call | solution.py:33
  44.7 0.0 copy-start.7
  44.7 0.0 copy-start.8
  44.7 0.6 %copy-done.7 = f32[4,7]{1,0:T(4,128)} copy-done((f32[4,7]{1,0:T(4,128)}, f32[4,7]{1,0:T(4,128)S(1)}, u32[]{:S(2)}) %copy-start.7) | copy-done | bytes 136
  45.2 0.1 copy-done.8
  (11 shorter events, 0.2 us)
Async XLA Ops:
  0.6 15.3 %copy-start.6 = (f32[6,4,4,4,2,128]{5,4,3,2,1,0:T(2,128)S(1)}, f32[6,4,4,4,2,128]{5,4,3,2,1,0:T(2,128)}, u32[]{:S(2)}) copy-start(f32[6,4,4,4,2,128]{5,4,3,2,1,0:T(2,128)} %param.16) | copy-start | bytes 1179652
  0.6 15.3 %copy-start.5 = (bf16[4,4,2,192,128]{4,3,2,1,0:T(8,128)(2,1)S(1)}, bf16[4,4,2,192,128]{4,3,2,1,0:T(8,128)(2,1)}, u32[]{:S(2)}) copy-start(bf16[4,4,2,192,128]{4,3,2,1,0:T(8,128)(2,1)} %param.17) | copy-start | bytes 4718596
  1.8 9.2 %collective-permute-start.4 = (f32[48,8,128]{2,1,0:T(8,128)S(1)}, f32[48,8,128]{2,1,0:T(8,128)S(1)}, u32[]{:S(2)}, u32[]{:S(2)}) collective-permute-start(f32[48,8,128]{2,1,0:T(8,128)S(1)} %get-tuple-element.83), channel_id=1, source_target_pairs={{0,4},{8,12},{4,0},{12,8},{1,5},{9,13},{5,1},{13,9},{2,6},{10,14},... | collective-permute-start | bytes 589832 | tf_op jit(solution)/shard_map/ppermute | solution.py:519
  2.3 8.7 %collective-permute-start.5 = (f32[48,8,128]{2,1,0:T(8,128)S(1)}, f32[48,8,128]{2,1,0:T(8,128)S(1)}, u32[]{:S(2)}, u32[]{:S(2)}) collective-permute-start(f32[48,8,128]{2,1,0:T(8,128)S(1)} %get-tuple-element.84), channel_id=1, source_target_pairs={{4,8},{12,0},{8,4},{0,12},{5,9},{13,1},{9,5},{1,13},{6,10},{14,2},... | collective-permute-start | bytes 589832 | tf_op jit(solution)/shard_map/ppermute | solution.py:519
  6.1 13.3 %all-to-all-start.1 = ((f32[32,8,128]{2,1,0:T(8,128)}), f32[32,8,128]{2,1,0:T(8,128)S(1)}, u32[]{:S(2)}, u32[]{:S(2)}) async-start(f32[32,8,128]{2,1,0:T(8,128)} %shard_map.105), calls=%async_computation.1 | async-start | bytes 262144 | tf_op jit(solution)/shard_map/all_to_all | solution.py:491
  11.2 4.5 %collective-permute-start.3 = (bf16[4,4,2,6,128]{4,0,3,2,1:T(4,128)(2,1)S(1)}, bf16[4,4,2,6,128]{4,0,3,2,1:T(4,128)(2,1)S(1)}, u32[]{:S(2)}, u32[]{:S(2)}) collective-permute-start(bf16[4,4,2,6,128]{4,0,3,2,1:T(4,128)(2,1)S(1)} %slice_select_fusion), channel_id=1, source_target_pairs={{0,16},{16,0},{1,17},{17,1},{2,18},{18,2},{3,19},{19,3},{4,20},{20... | collective-permute-start | bytes 147464 | tf_op jit(solution)/shard_map/cond/branch_1_fun/ppermute | solution.py:477
  16.0 3.5 %copy-start.3 = (f32[16,512]{1,0:T(8,128)S(1)}, f32[16,512]{1,0:T(8,128)}, u32[]{:S(2)}) copy-start(f32[16,512]{1,0:T(8,128)} %factor.1) | copy-start | bytes 98308
  16.0 15.8 %copy-start.1 = (f32[6,4,4,2,128]{4,3,2,1,0:T(2,128)S(1)}, f32[6,4,4,2,128]{4,3,2,1,0:T(2,128)}, u32[]{:S(2)}) copy-start(f32[6,4,4,2,128]{4,3,2,1,0:T(2,128)} %param.19) | copy-start | bytes 294916
  16.0 15.8 %copy-start.2 = (f32[4,4,4,2,128]{4,3,2,1,0:T(2,128)S(1)}, f32[4,4,4,2,128]{4,3,2,1,0:T(2,128)}, u32[]{:S(2)}) copy-start(f32[4,4,4,2,128]{4,3,2,1,0:T(2,128)} %param.18) | copy-start | bytes 196612
  17.4 26.3 %copy-start = (f32[3,128,128]{2,1,0:T(8,128)S(1)}, f32[3,128,128]{2,1,0:T(8,128)}, u32[]{:S(2)}) copy-start(f32[3,128,128]{2,1,0:T(8,128)} %constant.91.clone.maps) | copy-start | bytes 589828
  17.4 26.3 %copy-start.4 = (f32[8,128]{1,0:T(8,128)S(1)}, f32[8,128]{1,0:T(8,128)}, u32[]{:S(2)}) copy-start(f32[8,128]{1,0:T(8,128)} %constant.92.clone.fixed) | copy-start | bytes 12292
  20.7 11.1 %all-to-all-start.2 = ((f32[32,4,128]{2,1,0:T(4,128)}), f32[32,4,128]{2,1,0:T(4,128)S(1)}, u32[]{:S(2)}, u32[]{:S(2)}) async-start(f32[32,4,128]{2,1,0:T(4,128)} %bitcast.14), calls=%async_computation.2 | async-start | bytes 131072 | tf_op jit(solution)/shard_map/all_to_all | solution.py:491
  24.3 5.2 %collective-permute-start.2 = (f32[20,8,128]{2,1,0:T(8,128)S(1)}, f32[20,8,128]{2,1,0:T(8,128)S(1)}, u32[]{:S(2)}, u32[]{:S(2)}) collective-permute-start(f32[20,8,128]{2,1,0:T(8,128)S(1)} %get-tuple-element.54), channel_id=1, source_target_pairs={{0,16},{16,0},{1,17},{17,1},{2,18},{18,2},{3,19},{19,3},{4,20},{20... | collective-permute-start | bytes 245768 | tf_op jit(solution)/shard_map/cond/branch_1_fun/ppermute | solution.py:545
  26.1 1.6 %collective-permute-start = (f32[8,8,128]{2,1,0:T(8,128)S(1)}, f32[8,8,128]{2,1,0:T(8,128)S(1)}, u32[]{:S(2)}, u32[]{:S(2)}) collective-permute-start(f32[8,8,128]{2,1,0:T(8,128)S(1)} %get-tuple-element.52), channel_id=1, source_target_pairs={{0,4},{8,12},{4,0},{12,8},{1,5},{9,13},{5,1},{13,9},{2,6},{10,14},... | collective-permute-start | bytes 98312 | tf_op jit(solution)/shard_map/cond/branch_1_fun/ppermute | solution.py:546
  26.1 3.4 %collective-permute-start.1 = (f32[8,8,128]{2,1,0:T(8,128)S(1)}, f32[8,8,128]{2,1,0:T(8,128)S(1)}, u32[]{:S(2)}, u32[]{:S(2)}) collective-permute-start(f32[8,8,128]{2,1,0:T(8,128)S(1)} %get-tuple-element.53), channel_id=1, source_target_pairs={{4,8},{12,0},{8,4},{0,12},{5,9},{13,1},{9,5},{1,13},{6,10},{14,2},... | collective-permute-start | bytes 98312 | tf_op jit(solution)/shard_map/cond/branch_1_fun/ppermute | solution.py:546
  44.7 0.6 %copy-start.7 = (f32[4,7]{1,0:T(4,128)}, f32[4,7]{1,0:T(4,128)S(1)}, u32[]{:S(2)}) copy-start(f32[4,7]{1,0:T(4,128)S(1)} %get-tuple-element.109) | copy-start | bytes 340
  44.7 0.6 %copy-start.8 = (f32[16,8,128]{2,1,0:T(8,128)}, f32[16,8,128]{2,1,0:T(8,128)S(1)}, u32[]{:S(2)}) copy-start(f32[16,8,128]{2,1,0:T(8,128)S(1)} %get-tuple-element.110) | copy-start | bytes 196612

commit v5 on v4

--- a/solution.py
+++ b/solution.py
@@ -16,7 +16,10 @@
 M = 6
 K = 16
 XY = CX * CY
-ROWS = C * (CX + 4) * (CY + 4)
+GATHERED = 1 + K * C * XY // CZ
+EXTENT = (CX + 4) * (CY + 4)
+SIDE = EXTENT // 3
+ROWS = C * EXTENT
 AXES = ("gx", "gy", "gz")
 PAIRS = [(m, n) for m in range(M) for n in range(m, M)]
 BASE = 88
@@ -141,7 +144,6 @@
 
 
 def rhs_body(vector, phi, out):
-    n = out.shape[0]
     rows = []
     for s in range(S):
         v = [vector[s * C + c] for c in range(C)]
@@ -151,44 +153,52 @@
     rows.append(jnp.zeros((64, 128), F32))
     rhs = across(jnp.ones((8, 128), F32), jnp.concatenate(rows, 0))
     faces = across(ends(), phi[...].reshape(K * C * XY, CZ))
-    sub = iota(0)
-    base = jnp.where(sub == 0, rhs, 0.0)
-    out[...] = jnp.broadcast_to(base[None], (n, 8, 128))
-
-    def with_face(side):
-        block = base
-        for r in range(4):
-            block = jnp.where(sub == r + 1, all_rows(faces[:, 128 * r : 128 * r + 128], side), block)
-        return block
-
-    me, below, above = place()
-
-    @pl.when(below)
-    def _():
-        out[me - 1] = with_face(0)
-
-    @pl.when(above)
-    def _():
-        out[me + 1] = with_face(1)
-
-
-def local_body(two_x, inv, cols, phi, basis, loc, locz, gram, *sends):
+    n = out.shape[0] // GATHERED
+    me, _, _ = place()
+    later = lax.broadcasted_iota(jnp.int32, (n, 128), 0) > me
+    out[pl.ds(0, n, stride=GATHERED), :] = jnp.broadcast_to(rhs[0:1], (n, 128))
+    for r in range(GATHERED - 1):
+        row = faces[:, 128 * r : 128 * r + 128]
+        out[pl.ds(r + 1, n, stride=GATHERED), :] = jnp.where(later, row[1:2], row[0:1])
+
+
+def x_faces(blocks, sends, at):
+    odd = lax.axis_index("gx") % 2 == 1
+    group = iota(0) >> 1
+    count = len(blocks) // 4
+    for i in range(count):
+        low = high = None
+        for g in range(4):
+            x = blocks[g * count + i]
+            to_low, to_high = rolled(x, 2 * g, 0), rolled(x, 2 * g - 6, 0)
+            low = to_low if low is None else jnp.where(group == g, to_low, low)
+            high = to_high if high is None else jnp.where(group == g, to_high, high)
+        sends[0][at + i] = jnp.where(odd, low, high)
+        if len(sends) > 1:
+            sends[1][at + i] = jnp.where(odd, high, low)
+
+
+def solve(inv, cols, starts, done):
     def one(c, carry):
         total = [[jnp.zeros((8, 128), F32) for _ in range(XY)] for _ in range(S)]
-        for j in range(0, ROWS, 16):
+        for at, j in starts:
             seen = [cols[s, j : j + 16, :].astype(F32) for s in range(S)]
             for i in range(XY):
-                w = inv[c, i, j : j + 16, :].astype(F32)
+                w = inv[c, i, at : at + 16, :].astype(F32)
                 for s in range(S):
                     part = w * seen[s]
                     total[s][i] = total[s][i] + part[:8] + part[8:]
         for s in range(S):
-            loc[s * C + c] = row_sums(total[s])
+            done(s * C + c, row_sums(total[s]))
         return carry
 
     lax.fori_loop(0, C, one, 0)
-    locz[...] = across(ends(), loc[...].reshape(S * C * XY, CZ))
-
+
+
+def early_body(two_x, phi, basis, inv, cols, gram, loc, inv_kept, *refs):
+    phi_faces, (sem,) = refs[: 1 + two_x], refs[1 + two_x :]
+    copy = pltpu.make_async_copy(inv, inv_kept, sem)
+    copy.start()
     rows = []
     for m, n in PAIRS:
         for s in range(S):
@@ -197,28 +207,33 @@
     for g in range(0, BASE, 8):
         gram[g : g + 8, :] = row_sums(rows[g : g + 8])
 
+    x_faces([phi[i] for i in range(K * C)], phi_faces, 0)
+
+    def done(i, x):
+        loc[i] = x
+
+    copy.wait()
+    solve(inv_kept, cols, [(EXTENT * c + SIDE, SIDE * c) for c in range(C)], done)
+
+
+def local_body(two_x, inv, cols, early, *refs):
+    phi_faces, (loc, locz, *sends) = refs[: 1 + two_x], refs[1 + two_x :]
+
+    def done(i, x):
+        loc[i] = early[i] + x
+
+    starts = [(EXTENT * c, 2 * SIDE * c) for c in range(C)]
+    starts += [(EXTENT * c + 2 * SIDE, 2 * SIDE * c + SIDE) for c in range(C)]
+    solve(inv, cols, starts, done)
+    locz[...] = across(ends(), loc[...].reshape(S * C * XY, CZ))
     odd_y = lax.axis_index("gy") % 2 == 1
-    odd_x = lax.axis_index("gx") % 2 == 1
-    sub = iota(0)
-
-    def block(half, of, i):
-        share, own = K * C // of, S * C // of
-        return phi[half * share + i] if i < share else loc[half * own + i - share]
-
     for i in range(S * C // 2):
         low, high = y_faces(loc[i], loc[S * C // 2 + i])
         sends[0][i] = jnp.where(odd_y, low, high)
         sends[1][i] = jnp.where(odd_y, high, low)
-    for i in range((K + S) * C // 4):
-        low = high = None
-        for g in range(4):
-            a = block(g, 4, i)
-            to_low, to_high = rolled(a, 2 * g, 0), rolled(a, 2 * g - 6, 0)
-            low = to_low if low is None else jnp.where((sub >> 1) == g, to_low, low)
-            high = to_high if high is None else jnp.where((sub >> 1) == g, to_high, high)
-        sends[2][i] = jnp.where(odd_x, low, high)
-        if two_x:
-            sends[3][i] = jnp.where(odd_x, high, low)
+    x_faces([loc[i] for i in range(S * C)], sends[2:], 0)
+    for x, known in zip(sends[2:], phi_faces):
+        x[C:] = known[...]
 
 
 def periodic(x):
@@ -238,7 +253,7 @@
     diag = (lane >> 4) == sub
     image = [jnp.zeros((K, 128), F32) for _ in range(S)]
     for b in range(n // 8):
-        rhs = got[pl.ds(64 * b, 8, stride=8), :]
+        rhs = got[pl.ds(8 * GATHERED * b, 8, stride=GATHERED), :]
         rows = factor[:, 128 * b : 128 * b + 128]
         for s in range(S):
             mine = jnp.where(diag, periodic(jnp.where((lane >> 4) == s, rhs, 0.0)), 0.0)
@@ -282,16 +297,49 @@
     stride = coarse.shape[0] // n
     sub, lane = iota(0), iota(1)
     even = (sub & 1) == 0
-    total = coarse[0:8, :]
-    for b in range(1, coarse.shape[0] // 8):
-        total = total + coarse[8 * b : 8 * b + 8, :]
     if stride == 4:
+        total = coarse[0:8, :]
+        for b in range(1, coarse.shape[0] // 8):
+            total = total + coarse[8 * b : 8 * b + 8, :]
         total = total + rolled(total, 4, 0)
+        totals = [all_rows(total, t) for t in range(stride - 1)]
+    else:
+        totals = [
+            jnp.broadcast_to(
+                jnp.sum(coarse[pl.ds(t, n, stride=stride), :], axis=0, keepdims=True), (8, 128)
+            )
+            for t in range(stride - 1)
+        ]
     names = slots(two_x)
 
     def coefs(name):
         at = names.index(name)
-        return rolled(all_rows(total, at // 2), -64 * (at % 2), 1)
+        return totals[at // 2] if at % 2 == 0 else rolled(totals[at // 2], 64, 1)
+
+    me, below, above = place()
+
+    def z_side(there, neighbour, coef):
+        at = jnp.where(there, neighbour, me)
+        parts = [
+            jnp.broadcast_to(got[pl.ds(at * GATHERED + 1 + r, 1), :], (8, 128))
+            for r in range(GATHERED - 1)
+        ]
+        row = jnp.broadcast_to(coarse[pl.ds(at * stride + stride - 1, 1), :], (8, 128))
+        for s in range(S):
+            part = None
+            for r in range(GATHERED - 1):
+                w = splat(coef, s * K + 4 * r)
+                for k in range(1, 4):
+                    w = jnp.where((lane >> 5) == k, splat(coef, s * K + 4 * r + k), w)
+                part = parts[r] * w if part is None else part + parts[r] * w
+            for shift in (32, 64):
+                part = part + rolled(part, shift, 1)
+            row = row + jnp.where((lane >> 5) == s, part, 0.0)
+        return jnp.where(there, row, 0.0)
+
+    zlo = z_side(below, me - 1, coefs("zlo"))
+    zhi = z_side(above, me + 1, coefs("zhi"))
+    columns = jnp.transpose(jnp.where(sub == 0, zlo, zhi))
 
     own = coefs("own")
     p = [loc[i] for i in range(S * C)]
@@ -321,13 +369,13 @@
     def x_side(face, coef):
         sums = []
         for s in range(S):
-            part = [jnp.where((sub >> 1) == s, face[16 + c], 0.0) for c in range(C)]
+            part = [jnp.where((sub >> 1) == s, face[c], 0.0) for c in range(C)]
             for k in range(K // 4):
                 w = splat(coef, s * K + k)
                 for g in range(1, 4):
                     w = jnp.where((sub >> 1) == g, splat(coef, s * K + k + 4 * g), w)
                 for c in range(C):
-                    part[c] = part[c] + w * face[k * C + c]
+                    part[c] = part[c] + w * face[C + k * C + c]
             for x in part:
                 x = x + rolled(x, 2, 0)
                 sums.append(x + rolled(x, 4, 0))
@@ -343,29 +391,6 @@
     else:
         x_first = x_side(faces[2], coefs("x"))
         x_second = x_first
-
-    me, below, above = place()
-
-    def z_side(there, neighbour, coef):
-        at = jnp.where(there, neighbour, me)
-        parts = got[pl.ds(pl.multiple_of(at * 8, 8), 8), :]
-        parts = jnp.where((sub >= 1) & (sub <= 4), parts, 0.0)
-        row = jnp.broadcast_to(coarse[pl.ds(at * stride + (len(names) + 1) // 2, 1), :], (8, 128))
-        for s in range(S):
-            w = jnp.zeros((8, 128), F32)
-            for k in range(K):
-                w = jnp.where((sub == 1 + k // 4) & ((lane >> 5) == k % 4), splat(coef, s * K + k), w)
-            part = parts * w
-            for shift in (4, 2, 1):
-                part = part + rolled(part, shift, 0)
-            for shift in (32, 64):
-                part = part + rolled(part, shift, 1)
-            row = row + jnp.where((lane >> 5) == s, part, 0.0)
-        return jnp.where(there, row, 0.0)
-
-    zlo = z_side(below, me - 1, coefs("zlo"))
-    zhi = z_side(above, me + 1, coefs("zhi"))
-    columns = jnp.transpose(jnp.where(sub == 0, zlo, zhi))
 
     for s in range(S):
         sides = []
@@ -486,9 +511,8 @@
     return jnp.where(at > 0, low, none), jnp.where(at < lax.axis_size(axis) - 1, high, none)
 
 
-def exchange(rows, n):
-    sent = rows.reshape(n, -1, 128)
-    return lax.all_to_all(sent, AXES, 0, 0, tiled=True)
+def exchange(rows):
+    return lax.all_to_all(rows[:, None], AXES, 0, 0, tiled=True).reshape(rows.shape)
 
 
 def on_device(basis, inverse_rows, block_diag, couple, coarse_basis, coarse_factor):
@@ -514,30 +538,59 @@
         scratch=[pltpu.SemaphoreType.DMA((2,))],
     )
     rounded = rounded.reshape(S, C, CX, CY, CZ)
-    (rhs,) = call(rhs_body, [kept(n, 8, 128)], (vector, phi), 2 * K * S * C * XY * CZ)
-    got = exchange(rhs, n).reshape(n * 8, 128)
+    (rhs,) = call(rhs_body, [kept(n * GATHERED, 128)], (vector, phi), 2 * K * S * C * XY * CZ)
+    got = exchange(rhs)
     swapped = [lax.ppermute(x, "gy", pairs) for x, pairs in zip(slabs, pairs_of("gy"))]
 
     always = lax.axis_index("gx") >= 0
 
-    def extend(swapped, rounded):
+    inverse = inverse_rows.reshape(C, XY, ROWS, CZ)
+
+    def extend(swapped, rounded, phi, vectors, inverse):
         parts = [x[: S * C].reshape(S, C, CX, CY, CZ).astype(rounded.dtype) for x in swapped]
         y_low, y_high = by_side("gy", parts)
         extended = jnp.concatenate([y_low, rounded, y_high], axis=3)
         x_low, x_high = by_side("gx", swap("gx", extended[:, :, :2], extended[:, :, -2:]))
-        extended = jnp.concatenate([x_low, extended, x_high], axis=2)
-        return extended.reshape(S, ROWS, CZ)
-
-    def unused(swapped, rounded):
-        return jnp.zeros((S, ROWS, CZ), rounded.dtype)
-
-    columns = lax.cond(always, extend, unused, swapped, rounded)
+        mine = extended.reshape(S, C, CX * (CY + 4), CZ)
+        edge = (EXTENT - CX * (CY + 4)) // 2
+        middle = mine[:, :, SIDE - edge : 2 * SIDE - edge].reshape(S, C * SIDE, CZ)
+        early = call(
+            functools.partial(early_body, two_x),
+            [kept(BASE, 128), kept(S * C, XY, CZ), kept(*inverse.shape, dtype=inverse.dtype)]
+            + [kept(K * C // 4, 8, 128)] * (1 + two_x),
+            (phi, vectors, in_hbm(inverse), middle),
+            10**10,
+            in_specs=[VMEM, VMEM, pl.BlockSpec(memory_space=pltpu.HBM), VMEM],
+            scratch=[pltpu.SemaphoreType.DMA],
+        )
+        outer = jnp.concatenate(
+            [
+                x_low.reshape(S, C, edge, CZ),
+                mine[:, :, : SIDE - edge],
+                mine[:, :, 2 * SIDE - edge :],
+                x_high.reshape(S, C, edge, CZ),
+            ],
+            axis=2,
+        )
+        return [outer.reshape(S, C * 2 * SIDE, CZ)] + list(early)
+
+    def unused(swapped, rounded, phi, vectors, inverse):
+        return [
+            jnp.zeros((S, C * 2 * SIDE, CZ), rounded.dtype),
+            jnp.zeros((BASE, 128), F32),
+            jnp.zeros((S * C, XY, CZ), F32),
+            jnp.zeros_like(inverse),
+        ] + [jnp.zeros((K * C // 4, 8, 128), F32)] * (1 + two_x)
+
+    columns, gram, part, inverse, *phi_faces = lax.cond(
+        always, extend, unused, swapped, rounded, phi, vectors, inverse
+    )
     half, quarter = S * C // 2, (K + S) * C // 4
     sends = [shape(half, 8, 128)] * 2 + [shape(quarter, 8, 128)] * (2 if two_x else 1)
-    loc, locz, gram, *sends = call(
+    loc, locz, *sends = call(
         functools.partial(local_body, two_x),
-        [shape(S * C, XY, CZ), shape(8, 128), shape(BASE, 128)] + sends,
-        (inverse_rows.reshape(C, XY, ROWS, CZ), columns, phi, vectors),
+        [shape(S * C, XY, CZ), shape(8, 128)] + sends,
+        (inverse, columns, part, *phi_faces),
         20000 * S * C * XY * ROWS * CZ,
     )
 
@@ -548,18 +601,18 @@
     def untouched(*sends):
         return list(sends)
 
-    stride = 8 if two_x else 4
+    stride = (len(slots(two_x)) + 1) // 2 + 1
     (shares,) = call(
         functools.partial(factor_body, two_x),
         [kept(n * stride, 128)],
         (got, locz, coarse_factor),
         4 * S * K * K * n,
     )
-    coarse = exchange(shares, n).reshape(n * stride, 128)
+    coarse = exchange(shares)
     faces = lax.cond(always, trade, untouched, *sends)
     pre, image, sent = call(
         functools.partial(image_body, two_x),
-        [shape(S * C, XY, CZ), kept(S * C, XY, CZ), kept(n, 128)],
+        [kept(S * C, XY, CZ), kept(S * C, XY, CZ), kept(n, 128)],
         (
             loc,
             phi,
@@ -574,7 +627,7 @@
         ),
         2 * S * C * XY * CZ * 40,
     )
-    products = exchange(sent, n).reshape(n, 128)
+    products = exchange(sent)
     maps, fixed = tables()
     krylov, hessenberg, flag = call(
         functools.partial(finish_body, unknowns),
@@ -590,7 +643,7 @@
             h.T[:, :, None, None, None] * vectors.reshape(M, S, C, XY, CZ), axis=0
         )
         squares = jnp.zeros((1, 128), F32).at[0, :S].set(jnp.sum(left * left, axis=(1, 2, 3)))
-        squares = jnp.sum(exchange(jnp.broadcast_to(squares, (n, 128)), n), axis=(0, 1))[:S]
+        squares = jnp.sum(exchange(jnp.broadcast_to(squares, (n, 128))), axis=0)[:S]
         norm = jnp.sqrt(squares / unknowns + epsilon)
         return (
             (left / norm[:, None, None, None]).reshape(S * C, XY, CZ),
@@ -603,6 +656,7 @@
     krylov, hessenberg = lax.cond(
         flag[0] > 0, exact, as_is, image, vectors, krylov, hessenberg
     )
+    krylov, pre = lax.optimization_barrier((krylov, pre))
     cells = (S, C, CX, CY, CZ)
     return krylov.reshape(cells), pre.reshape(cells), hessenberg
 

time: 45.6 us -> 44.3 us (0.971)
  waiting for transfers between devices: 8.76 us -> 5.63 us
  Pallas kernels: 7.83 us -> 9.48 us
    ppermute x1, waiting for transfers between devices: 2.66 us -> 0.01 us  [swap(): return [lax.ppermute(x, axis, pairs) for x, pairs in zip(sides, rounds)]]
    pallas_call x6 -> x7, Pallas kernels: 7.83 us -> 9.48 us  [call(): pl.pallas_call(body, out_shape=tuple(outs), in_specs=in_specs or [VMEM] *...]
    all_to_all x2, waiting for transfers between devices: 4.27 us -> 3.79 us  [exchange(): lax.all_to_all(rows[:, None], AXES, 0, 0, tiled=True).reshape(rows.shape)]
  transfers between devices with their start and end apart: 8 -> 8, of which waited for: 4 -> 3; matrix products, arithmetic and copies ran while one was open for 1% -> 1% of each run, Pallas kernels for 6% -> 11%
where the time goes in v5:
time: 44.3 us; the launch traced here: 44 us
  starting transfers between devices  17 us (38%)
  blocking collectives  9.98 us (23%)
  Pallas kernels  9.48 us (21%)
  waiting for transfers between devices  5.63 us (13%)
  local copies, waits for them, and re-layouts  0.84 us (2%)
  between operations  0.76 us (2%)
    all_to_all x1, blocking collectives, exchange(): lax.all_to_all(rows[:, None], AXES, 0, 0, tiled=True).reshape(rows.shape)  9.98 us
    pallas_call x7, Pallas kernels, call(): pl.pallas_call(body, out_shape=tuple(outs), in_specs=in_specs or [VMEM] *...  9.48 us
    all_to_all x2, starting transfers between devices, exchange(): lax.all_to_all(rows[:, None], AXES, 0, 0, tiled=True).reshape(rows.shape)  8.58 us
    all_to_all x2, waiting for transfers between devices, exchange(): lax.all_to_all(rows[:, None], AXES, 0, 0, tiled=True).reshape(rows.shape)  3.79 us
    ppermute x2, starting transfers between devices, on_device(): lax.ppermute(x, 'gy', pairs)  3.16 us
    ppermute x1, starting transfers between devices, swap(): return [lax.ppermute(x, axis, pairs) for x, pairs in zip(sides, rounds)]  1.83 us
    ppermute x1, starting transfers between devices, trade(): lax.ppermute(x, 'gx', pairs)  1.83 us
    ppermute x2, waiting for transfers between devices, trade(): lax.ppermute(x, 'gy', pairs)  1.82 us
  transfers between devices with their start and end apart: 8, of which 3 were waited for; matrix products, arithmetic and copies ran while one was open for 1% of the time, Pallas kernels for 11%

profile of v5, /device:TPU:0, one launch (start us, length us, event | category | flops | bytes accessed | tf_op | source)
XLA Modules:
  0.0 44.0 jit_solution(10937676216155019956)
XLA Ops:
  0.6 1.0 %shard_map.104 = (f32[16,8,128]{2,1,0:T(8,128)S(1)}, bf16[16,8,128]{2,1,0:T(8,128)(2,1)S(1)}, f32[64,8,128]{2,1,0:T(8,128)S(1)}, f32[48,8,128]{2,1,0:T(8,128)S(1)}, f32[48,8,128]{2,1,0:T(8,128)S(1)}) custom-call(f32[6,16,8,128]{3,2,1,0:T(8,128)} %bitcast.48, f32[64,8,128]{2,1,0:T(8,128)} %bitcast.55), custom_call_target="tpu_custom_call" | custom-call | flops 16384 | bytes 1409024 | tf_op jit(solution)/shard_map/pallas_call | solution.py:36
  1.7 0.5 %collective-permute-start.4 = (f32[48,8,128]{2,1,0:T(8,128)S(1)}, f32[48,8,128]{2,1,0:T(8,128)S(1)}, u32[]{:S(2)}, u32[]{:S(2)}) collective-permute-start(f32[48,8,128]{2,1,0:T(8,128)S(1)} %get-tuple-element.95), channel_id=1, source_target_pairs={{0,4},{8,12},{4,0},{12,8},{1,5},{9,13},{5,1},{13,9},{2,6},{10,14},... | collective-permute-start | bytes 589832 | tf_op jit(solution)/shard_map/ppermute | solution.py:543
  2.2 2.6 %collective-permute-start.5 = (f32[48,8,128]{2,1,0:T(8,128)S(1)}, f32[48,8,128]{2,1,0:T(8,128)S(1)}, u32[]{:S(2)}, u32[]{:S(2)}) collective-permute-start(f32[48,8,128]{2,1,0:T(8,128)S(1)} %get-tuple-element.96), channel_id=1, source_target_pairs={{4,8},{12,0},{8,4},{0,12},{5,9},{13,1},{9,5},{1,13},{6,10},{14,2},... | collective-permute-start | bytes 589832 | tf_op jit(solution)/shard_map/ppermute | solution.py:543
  4.8 1.1 %shard_map.106 = f32[160,128]{1,0:T(8,128)} custom-call(f32[16,8,128]{2,1,0:T(8,128)S(1)} %get-tuple-element.105.vector, f32[64,8,128]{2,1,0:T(8,128)S(1)} %get-tuple-element.98.phi), custom_call_target="tpu_custom_call" | custom-call | flops 524288 | bytes 409600 | tf_op jit(solution)/shard_map/pallas_call | solution.py:36
  5.9 4.9 %all-to-all-start.1 = ((f32[160,1,128]{2,1,0:T(1,128)}), f32[160,1,128]{2,1,0:T(1,128)S(1)}, u32[]{:S(2)}, u32[]{:S(2)}) async-start(f32[160,1,128]{2,1,0:T(1,128)} %bitcast.20), calls=%async_computation.1 | async-start | bytes 163840 | tf_op jit(solution)/shard_map/all_to_all | solution.py:515
  10.8 0.0 collective-permute-done.4.rest_0_
  10.8 0.0 collective-permute-done.5.rest_1_
  10.9 5.1 %conditional.3 = (bf16[4,128,128]{2,1,0:T(8,128)(2,1)S(1)}, f32[88,128]{1,0:T(8,128)S(1)}, f32[16,8,128]{2,1,0:T(8,128)S(1)}, bf16[4,8,192,128]{3,2,1,0:T(8,128)(2,1)S(1)}, f32[16,8,128]{2,1,0:T(8,128)S(1)}) conditional(s32[]{:T(128)} %convert_element_type.14, () %tuple.35, (f32[48,8,128]{2,1,0:T(8,128)S(1)}, f32[48,8,128]{2,1,0:T(8,128)S(1)}, ...), branch_computations={%region_0.0_spmd, %region_1.2_spmd} | conditional | flops 10000335872 | bytes 5714342 | solution.py:585
  11.0 1.8 %collective-permute-start.3 = (bf16[4,4,2,6,128]{4,1,3,2,0:T(4,128)(2,1)S(1)}, bf16[4,4,2,6,128]{4,1,3,2,0:T(4,128)(2,1)S(1)}, u32[]{:S(2)}, u32[]{:S(2)}) collective-permute-start(bf16[4,4,2,6,128]{4,1,3,2,0:T(4,128)(2,1)S(1)} %slice_select_fusion), channel_id=1, source_target_pairs={{0,16},{16,0},{1,17},{17,1},{2,18},{18,2},{3,19},{19,3},{4,20},{20... | collective-permute-start | bytes 147464 | tf_op jit(solution)/shard_map/cond/branch_1_fun/ppermute | solution.py:502
  12.9 2.8 %branch_1_fun.1 = (f32[88,128]{1,0:T(8,128)S(1)}, f32[16,8,128]{2,1,0:T(8,128)S(1)}, bf16[4,8,192,128]{3,2,1,0:T(8,128)(2,1)S(1)}, f32[16,8,128]{2,1,0:T(8,128)S(1)}) custom-call(f32[64,8,128]{2,1,0:T(8,128)S(1)} %get-tuple-element.51.phi, f32[6,16,8,128]{3,2,1,0:T(8,128)} %get-tuple-element.52.basis, bf16[4,8,192,128]{3,2,1,0:T(8,128)(2,1)} %bitcast.62, ...), custom_call_target="tpu_custom_call" | custom-call | flops 10000000000 | bytes 4042752 | tf_op jit(solution)/shard_map/cond/branch_1_fun/pallas_call | solution.py:36
  15.8 0.0 collective-permute-done.3
  15.8 0.1 pad_maximum_fusion
  16.0 0.0 copy-start.3
  16.0 0.0 copy-start.1
  16.0 0.0 copy-start.2
  16.0 0.0 copy-start.5
  16.0 1.0 %shard_map.105 = (f32[16,8,128]{2,1,0:T(8,128)S(1)}, f32[8,128]{1,0:T(8,128)S(1)}, f32[8,8,128]{2,1,0:T(8,128)S(1)}, f32[8,8,128]{2,1,0:T(8,128)S(1)}, f32[20,8,128]{2,1,0:T(8,128)S(1)}) custom-call(bf16[4,8,192,128]{3,2,1,0:T(8,128)(2,1)S(1)} %get-tuple-element.99.inv, bf16[4,128,128]{2,1,0:T(8,128)(2,1)S(1)} %get-tuple-element.100.cols, ...), custom_call_target="tpu_custom_call" | custom-call | flops 62914560000 | bytes 2052096 | tf_op jit(solution)/shard_map/pallas_call | solution.py:36
  17.0 0.0 copy-start
  17.0 0.0 copy-start.4
  17.0 1.6 %all-to-all-done.1 = f32[160,1,128]{2,1,0:T(1,128)S(1)} async-done(((f32[160,1,128]{2,1,0:T(1,128)}), f32[160,1,128]{2,1,0:T(1,128)S(1)}, u32[]{:S(2)}, u32[]{:S(2)}) %all-to-all-start.1) | async-done | bytes 81952 | tf_op jit(solution)/shard_map/all_to_all | solution.py:515
  18.5 0.0 copy-done.3
  18.6 1.2 %shard_map.107 = f32[128,128]{1,0:T(8,128)} custom-call(f32[160,128]{1,0:T(8,128)S(1)} %bitcast.39, f32[8,128]{1,0:T(8,128)S(1)} %get-tuple-element.106.locz, f32[16,512]{1,0:T(8,128)S(1)} %copy-done.3), custom_call_target="tpu_custom_call" | custom-call | flops 131072 | bytes 184320 | tf_op jit(solution)/shard_map/pallas_call | solution.py:36
  19.8 3.7 %all-to-all-start.2 = ((f32[128,1,128]{2,1,0:T(1,128)}), f32[128,1,128]{2,1,0:T(1,128)S(1)}, u32[]{:S(2)}, u32[]{:S(2)}) async-start(f32[128,1,128]{2,1,0:T(1,128)} %bitcast.23), calls=%async_computation.2 | async-start | bytes 131072 | tf_op jit(solution)/shard_map/all_to_all | solution.py:515
  23.5 5.3 %conditional.4 = ((f32[8,8,128]{2,1,0:T(8,128)S(1)}, f32[8,8,128]{2,1,0:T(8,128)S(1)}, f32[20,8,128]{2,1,0:T(8,128)S(1)})) conditional(s32[]{:T(128)} %convert_element_type.14, (f32[8,8,128]{2,1,0:T(8,128)S(1)}, f32[8,8,128]{2,1,0:T(8,128)S(1)}, f32[20,8,128]{2,1,0:T(8,128)S(1)}) %tuple.37, (f32[8,8,128]{2,1,0:T(8,128)S(1)}, ...), branch_computations={%region_2.3_spmd, %region_3.4_spmd} | conditional | bytes 884888 | solution.py:612
  23.5 1.8 %collective-permute-start.2 = (f32[20,8,128]{2,1,0:T(8,128)S(1)}, f32[20,8,128]{2,1,0:T(8,128)S(1)}, u32[]{:S(2)}, u32[]{:S(2)}) collective-permute-start(f32[20,8,128]{2,1,0:T(8,128)S(1)} %get-tuple-element.60), channel_id=1, source_target_pairs={{0,16},{16,0},{1,17},{17,1},{2,18},{18,2},{3,19},{19,3},{4,20},{20... | collective-permute-start | bytes 245768 | tf_op jit(solution)/shard_map/cond/branch_1_fun/ppermute | solution.py:598
  25.3 0.0 collective-permute-start
  25.3 1.6 %collective-permute-start.1 = (f32[8,8,128]{2,1,0:T(8,128)S(1)}, f32[8,8,128]{2,1,0:T(8,128)S(1)}, u32[]{:S(2)}, u32[]{:S(2)}) collective-permute-start(f32[8,8,128]{2,1,0:T(8,128)S(1)} %get-tuple-element.59), channel_id=1, source_target_pairs={{4,8},{12,0},{8,4},{0,12},{5,9},{13,1},{9,5},{1,13},{6,10},{14,2},... | collective-permute-start | bytes 98312 | tf_op jit(solution)/shard_map/cond/branch_1_fun/ppermute | solution.py:599
  26.9 0.0 collective-permute-done
  26.9 1.8 %collective-permute-done.1 = f32[8,8,128]{2,1,0:T(8,128)S(1)} collective-permute-done((f32[8,8,128]{2,1,0:T(8,128)S(1)}, f32[8,8,128]{2,1,0:T(8,128)S(1)}, u32[]{:S(2)}, u32[]{:S(2)}) %collective-permute-start.1) | collective-permute-done | bytes 32800 | tf_op jit(solution)/shard_map/cond/branch_1_fun/ppermute | solution.py:599
  28.7 0.0 collective-permute-done.2
  28.8 2.2 %all-to-all-done.2 = f32[128,1,128]{2,1,0:T(1,128)S(1)} async-done(((f32[128,1,128]{2,1,0:T(1,128)}), f32[128,1,128]{2,1,0:T(1,128)S(1)}, u32[]{:S(2)}, u32[]{:S(2)}) %all-to-all-start.2) | async-done | bytes 65568 | tf_op jit(solution)/shard_map/all_to_all | solution.py:515
  31.0 0.0 copy-done.1
  31.0 0.0 copy-done.2
  31.0 0.0 copy-done.5
  31.0 1.4 %shard_map.108 = (f32[16,8,128]{2,1,0:T(8,128)S(1)}, f32[16,8,128]{2,1,0:T(8,128)S(1)}, f32[32,128]{1,0:T(8,128)S(1)}) custom-call(f32[16,8,128]{2,1,0:T(8,128)S(1)} %get-tuple-element.103.loc, f32[64,8,128]{2,1,0:T(8,128)S(1)} %get-tuple-element.98.phi, f32[16,8,128]{2,1,0:T(8,128)S(1)} %bitcast.43, f32[24,8,128]{2,1,0:T(8,128)S(1)} %bitcast.42, ...), custom_call_target="tpu_custom_call" | custom-call | flops 1310720 | bytes 1765376 | tf_op jit(solution)/shard_map/pallas_call | solution.py:36
  32.4 10.0 %all_to_all.20 = f32[32,1,128]{2,1,0:T(1,128)S(1)} all-to-all(f32[32,1,128]{2,1,0:T(1,128)S(1)} %bitcast.47), channel_id=1, replica_groups=mesh['gx'=2,'gy'=4,'gz'=4] {'gx','gy','gz'}, dimensions={0} | all-to-all | bytes 32768 | tf_op jit(solution)/shard_map/all_to_all | solution.py:515
  42.3 0.0 copy-done
  42.3 0.0 copy-done.4
  42.3 0.9 %shard_map.109 = (f32[16,8,128]{2,1,0:T(8,128)S(1)}, f32[4,7]{1,0:T(4,128)S(1)}, s32[1]{0:T(128)S(4)}) custom-call(f32[32,128]{1,0:T(8,128)S(1)} %bitcast.45, f32[16,8,128]{2,1,0:T(8,128)S(1)} %get-tuple-element.114.image, f32[6,16,8,128]{3,2,1,0:T(8,128)S(1)} %bitcast.51, f32[3,128,128]{2,1,0:T(8,128)S(1)} %copy-done, f32[8,128]{1,0:T(8,128)S(1)} %copy-done.4), custom_call_target="tpu_custom_call" | custom-call | flops 262144 | bytes 741492 | tf_op jit(solution)/shard_map/pallas_call | solution.py:36
  43.3 0.0 copy-start.6
  43.3 0.0 copy-start.7
  43.4 0.6 %copy.83 = f32[4,4,4,2,128]{4,3,2,1,0:T(2,128)} copy(f32[4,4,4,2,128]{4,3,2,1,0:T(2,128)S(1)} %bitcast.38) | data formatting | bytes 131072
  44.0 0.0 copy-done.6
  44.0 0.0 copy-done.7
  (14 shorter events, 0.2 us)
Async XLA Ops:
  1.7 9.2 %collective-permute-start.4 = (f32[48,8,128]{2,1,0:T(8,128)S(1)}, f32[48,8,128]{2,1,0:T(8,128)S(1)}, u32[]{:S(2)}, u32[]{:S(2)}) collective-permute-start(f32[48,8,128]{2,1,0:T(8,128)S(1)} %get-tuple-element.95), channel_id=1, source_target_pairs={{0,4},{8,12},{4,0},{12,8},{1,5},{9,13},{5,1},{13,9},{2,6},{10,14},... | collective-permute-start | bytes 589832 | tf_op jit(solution)/shard_map/ppermute | solution.py:543
  2.2 8.7 %collective-permute-start.5 = (f32[48,8,128]{2,1,0:T(8,128)S(1)}, f32[48,8,128]{2,1,0:T(8,128)S(1)}, u32[]{:S(2)}, u32[]{:S(2)}) collective-permute-start(f32[48,8,128]{2,1,0:T(8,128)S(1)} %get-tuple-element.96), channel_id=1, source_target_pairs={{4,8},{12,0},{8,4},{0,12},{5,9},{13,1},{9,5},{1,13},{6,10},{14,2},... | collective-permute-start | bytes 589832 | tf_op jit(solution)/shard_map/ppermute | solution.py:543
  5.9 12.6 %all-to-all-start.1 = ((f32[160,1,128]{2,1,0:T(1,128)}), f32[160,1,128]{2,1,0:T(1,128)S(1)}, u32[]{:S(2)}, u32[]{:S(2)}) async-start(f32[160,1,128]{2,1,0:T(1,128)} %bitcast.20), calls=%async_computation.1 | async-start | bytes 163840 | tf_op jit(solution)/shard_map/all_to_all | solution.py:515
  11.0 4.7 %collective-permute-start.3 = (bf16[4,4,2,6,128]{4,1,3,2,0:T(4,128)(2,1)S(1)}, bf16[4,4,2,6,128]{4,1,3,2,0:T(4,128)(2,1)S(1)}, u32[]{:S(2)}, u32[]{:S(2)}) collective-permute-start(bf16[4,4,2,6,128]{4,1,3,2,0:T(4,128)(2,1)S(1)} %slice_select_fusion), channel_id=1, source_target_pairs={{0,16},{16,0},{1,17},{17,1},{2,18},{18,2},{3,19},{19,3},{4,20},{20... | collective-permute-start | bytes 147464 | tf_op jit(solution)/shard_map/cond/branch_1_fun/ppermute | solution.py:502
  16.0 2.6 %copy-start.3 = (f32[16,512]{1,0:T(8,128)S(1)}, f32[16,512]{1,0:T(8,128)}, u32[]{:S(2)}) copy-start(f32[16,512]{1,0:T(8,128)} %factor.1) | copy-start | bytes 98308
  16.0 15.0 %copy-start.1 = (f32[6,4,4,2,128]{4,3,2,1,0:T(2,128)S(1)}, f32[6,4,4,2,128]{4,3,2,1,0:T(2,128)}, u32[]{:S(2)}) copy-start(f32[6,4,4,2,128]{4,3,2,1,0:T(2,128)} %param.19) | copy-start | bytes 294916
  16.0 15.0 %copy-start.2 = (f32[4,4,4,2,128]{4,3,2,1,0:T(2,128)S(1)}, f32[4,4,4,2,128]{4,3,2,1,0:T(2,128)}, u32[]{:S(2)}) copy-start(f32[4,4,4,2,128]{4,3,2,1,0:T(2,128)} %param.18) | copy-start | bytes 196612
  16.0 15.0 %copy-start.5 = (f32[6,4,4,4,2,128]{5,4,3,2,1,0:T(2,128)S(1)}, f32[6,4,4,4,2,128]{5,4,3,2,1,0:T(2,128)}, u32[]{:S(2)}) copy-start(f32[6,4,4,4,2,128]{5,4,3,2,1,0:T(2,128)} %param.16) | copy-start | bytes 1179652
  17.0 25.4 %copy-start = (f32[3,128,128]{2,1,0:T(8,128)S(1)}, f32[3,128,128]{2,1,0:T(8,128)}, u32[]{:S(2)}) copy-start(f32[3,128,128]{2,1,0:T(8,128)} %constant.94.clone.maps) | copy-start | bytes 589828
  17.0 25.4 %copy-start.4 = (f32[8,128]{1,0:T(8,128)S(1)}, f32[8,128]{1,0:T(8,128)}, u32[]{:S(2)}) copy-start(f32[8,128]{1,0:T(8,128)} %constant.95.clone.fixed) | copy-start | bytes 12292
  19.8 11.2 %all-to-all-start.2 = ((f32[128,1,128]{2,1,0:T(1,128)}), f32[128,1,128]{2,1,0:T(1,128)S(1)}, u32[]{:S(2)}, u32[]{:S(2)}) async-start(f32[128,1,128]{2,1,0:T(1,128)} %bitcast.23), calls=%async_computation.2 | async-start | bytes 131072 | tf_op jit(solution)/shard_map/all_to_all | solution.py:515
  23.5 5.2 %collective-permute-start.2 = (f32[20,8,128]{2,1,0:T(8,128)S(1)}, f32[20,8,128]{2,1,0:T(8,128)S(1)}, u32[]{:S(2)}, u32[]{:S(2)}) collective-permute-start(f32[20,8,128]{2,1,0:T(8,128)S(1)} %get-tuple-element.60), channel_id=1, source_target_pairs={{0,16},{16,0},{1,17},{17,1},{2,18},{18,2},{3,19},{19,3},{4,20},{20... | collective-permute-start | bytes 245768 | tf_op jit(solution)/shard_map/cond/branch_1_fun/ppermute | solution.py:598
  25.3 1.6 %collective-permute-start = (f32[8,8,128]{2,1,0:T(8,128)S(1)}, f32[8,8,128]{2,1,0:T(8,128)S(1)}, u32[]{:S(2)}, u32[]{:S(2)}) collective-permute-start(f32[8,8,128]{2,1,0:T(8,128)S(1)} %get-tuple-element.58), channel_id=1, source_target_pairs={{0,4},{8,12},{4,0},{12,8},{1,5},{9,13},{5,1},{13,9},{2,6},{10,14},... | collective-permute-start | bytes 98312 | tf_op jit(solution)/shard_map/cond/branch_1_fun/ppermute | solution.py:599
  25.3 3.4 %collective-permute-start.1 = (f32[8,8,128]{2,1,0:T(8,128)S(1)}, f32[8,8,128]{2,1,0:T(8,128)S(1)}, u32[]{:S(2)}, u32[]{:S(2)}) collective-permute-start(f32[8,8,128]{2,1,0:T(8,128)S(1)} %get-tuple-element.59), channel_id=1, source_target_pairs={{4,8},{12,0},{8,4},{0,12},{5,9},{13,1},{9,5},{1,13},{6,10},{14,2},... | collective-permute-start | bytes 98312 | tf_op jit(solution)/shard_map/cond/branch_1_fun/ppermute | solution.py:599
  43.3 0.7 %copy-start.6 = (f32[4,7]{1,0:T(4,128)}, f32[4,7]{1,0:T(4,128)S(1)}, u32[]{:S(2)}) copy-start(f32[4,7]{1,0:T(4,128)S(1)} %get-tuple-element.157) | copy-start | bytes 340
  43.3 0.7 %copy-start.7 = (f32[16,8,128]{2,1,0:T(8,128)}, f32[16,8,128]{2,1,0:T(8,128)S(1)}, u32[]{:S(2)}) copy-start(f32[16,8,128]{2,1,0:T(8,128)S(1)} %get-tuple-element.120) | copy-start | bytes 196612

commit v6 on v5

--- a/solution.py
+++ b/solution.py
@@ -80,14 +80,26 @@
     return blocks[0]
 
 
+def thirds(x):
+    parts = []
+    for _ in range(3):
+        parts.append(x.astype(jnp.bfloat16))
+        x = x - parts[-1].astype(F32)
+    return parts
+
+
 def across(left, right):
-    return lax.dot_general(
-        left,
-        right,
-        (((1,), (1,)), ((), ())),
-        precision=lax.Precision.HIGHEST,
-        preferred_element_type=F32,
-    )
+    left = left.astype(jnp.bfloat16)
+    return sum(
+        lax.dot_general(left, part, (((1,), (1,)), ((), ())), preferred_element_type=F32)
+        for part in thirds(right)
+    )
+
+
+def times(x, table):
+    rows = jnp.concatenate([p.astype(F32) for p in thirds(x)] + [jnp.zeros((8, 128), F32)], 0)
+    y = jnp.dot(rows.astype(jnp.bfloat16), table, preferred_element_type=F32)
+    return y[:8] + y[8:16] + y[16:24]
 
 
 def all_rows(x, t):
@@ -236,10 +248,11 @@
         x[C:] = known[...]
 
 
-def periodic(x):
-    for shift in (16, 32, 64):
-        x = x + rolled(x, shift, 1)
-    return x
+def staggered(coef, group):
+    out = coef
+    for g in range(1, 4):
+        out = jnp.where(group == g, rolled(coef, -4 * g, 1), out)
+    return out
 
 
 def slots(two_x):
@@ -255,8 +268,9 @@
     for b in range(n // 8):
         rhs = got[pl.ds(8 * GATHERED * b, 8, stride=GATHERED), :]
         rows = factor[:, 128 * b : 128 * b + 128]
+        rhs = pltpu.roll(rhs, 0, 1, stride=K, stride_axis=0)
         for s in range(S):
-            mine = jnp.where(diag, periodic(jnp.where((lane >> 4) == s, rhs, 0.0)), 0.0)
+            mine = jnp.where(diag, rolled(rhs, -K * s, 1) if s else rhs, 0.0)
             image[s] = image[s] + rows * jnp.sum(mine, axis=0, keepdims=True)
     image = [jnp.sum(x, axis=1, keepdims=True) for x in image]
     shares = []
@@ -265,8 +279,10 @@
         block = jnp.zeros((8, 128), F32)
         for s in range(S):
             part = jnp.sum(rows * image[s], axis=0, keepdims=True)
-            mine = periodic(jnp.where(diag, part, 0.0))
-            block = jnp.where((lane >> 4) == s, mine, block)
+            mine = jnp.where(diag, part, 0.0)
+            block = block + (rolled(mine, K * s, 1) if s else mine)
+        for bit in (1, 2, 4):
+            block = jnp.where((sub & bit) == 0, block, rolled(block, -K * bit, 1))
         shares.append(block)
     shares = jnp.concatenate(shares, 0)
     nz = lax.axis_size("gz")
@@ -318,28 +334,30 @@
 
     me, below, above = place()
 
-    def z_side(there, neighbour, coef):
-        at = jnp.where(there, neighbour, me)
-        parts = [
-            jnp.broadcast_to(got[pl.ds(at * GATHERED + 1 + r, 1), :], (8, 128))
-            for r in range(GATHERED - 1)
-        ]
-        row = jnp.broadcast_to(coarse[pl.ds(at * stride + stride - 1, 1), :], (8, 128))
-        for s in range(S):
-            part = None
-            for r in range(GATHERED - 1):
-                w = splat(coef, s * K + 4 * r)
-                for k in range(1, 4):
-                    w = jnp.where((lane >> 5) == k, splat(coef, s * K + 4 * r + k), w)
-                part = parts[r] * w if part is None else part + parts[r] * w
-            for shift in (32, 64):
-                part = part + rolled(part, shift, 1)
-            row = row + jnp.where((lane >> 5) == s, part, 0.0)
-        return jnp.where(there, row, 0.0)
-
-    zlo = z_side(below, me - 1, coefs("zlo"))
-    zhi = z_side(above, me + 1, coefs("zhi"))
-    columns = jnp.transpose(jnp.where(sub == 0, zlo, zhi))
+    lower = sub < 4
+    at = [jnp.where(below, me - 1, me), jnp.where(above, me + 1, me)]
+    parts = None
+    for r in range(8):
+        row = got[pl.ds(at[r // 4] * GATHERED + 1 + r % 4, 1), :]
+        row = jnp.broadcast_to(row, (8, 128))
+        parts = row if r == 0 else jnp.where(sub == r, row, parts)
+    coef = staggered(jnp.where(lower, coefs("zlo"), coefs("zhi")), sub & 3)
+    z = None
+    for s in range(S):
+        w = splat(coef, s * K)
+        for k in range(1, 4):
+            w = jnp.where((lane >> 5) == k, splat(coef, s * K + k), w)
+        part = parts * w
+        for shift in (32, 64):
+            part = part + rolled(part, shift, 1)
+        z = part if z is None else jnp.where((lane >> 5) == s, part, z)
+    for shift in (1, 2):
+        z = z + rolled(z, -shift, 0)
+    rows = [coarse[pl.ds(x * stride + stride - 1, 1), :] for x in at]
+    rows = [jnp.broadcast_to(x, (8, 128)) for x in rows]
+    z = z + jnp.where(lower, rows[0], rows[1])
+    there = jnp.where(lower, below.astype(jnp.int32), above.astype(jnp.int32)) == 1
+    columns = jnp.transpose(jnp.where(there, z, 0.0))
 
     own = coefs("own")
     p = [loc[i] for i in range(S * C)]
@@ -355,25 +373,25 @@
     has_y, has_x = both_sides("gy"), both_sides("gx")
 
     def y_side(slab, face, coef):
+        coef = jnp.where(even, coef, rolled(coef, -K // 2, 1))
         sums = []
         for s in range(S):
             mine = even if s < 2 else ~even
             part = [jnp.where(mine, face[(s % 2) * C + c], 0.0) for c in range(C)]
             for k in range(K // 2):
-                w = jnp.where(even, splat(coef, s * K + k), splat(coef, s * K + k + K // 2))
+                w = splat(coef, s * K + k)
                 for c in range(C):
                     part[c] = part[c] + w * slab[S * C + k * C + c]
             sums += part
         return sums
 
     def x_side(face, coef):
+        coef = staggered(coef, sub >> 1)
         sums = []
         for s in range(S):
             part = [jnp.where((sub >> 1) == s, face[c], 0.0) for c in range(C)]
             for k in range(K // 4):
                 w = splat(coef, s * K + k)
-                for g in range(1, 4):
-                    w = jnp.where((sub >> 1) == g, splat(coef, s * K + k + 4 * g), w)
                 for c in range(C):
                     part[c] = part[c] + w * face[C + k * C + c]
             for x in part:
@@ -399,7 +417,7 @@
             x = p[i]
             pre[i] = x
             zl = jnp.broadcast_to(columns[i * XY : (i + 1) * XY, 0:1], (8, 128))
-            zh = jnp.broadcast_to(columns[i * XY : (i + 1) * XY, 1:2], (8, 128))
+            zh = jnp.broadcast_to(columns[i * XY : (i + 1) * XY, 4:5], (8, 128))
             y_low = jnp.where(odd_y, y_first[i], y_second[i])
             y_high = jnp.where(odd_y, y_second[i], y_first[i])
             x_low = jnp.where(odd_x, x_first[i], x_second[i])
@@ -452,7 +470,7 @@
         fixed[0, lane] = fixed[1, lane] = fixed[2, lane] = 1
         for i in range(M + 1):
             out[BASE + 4 * i + s, i] = 1
-    return np.stack([first, second, out]), fixed
+    return np.stack([first, second, out]).astype(jnp.bfloat16), fixed
 
 
 def finish_body(unknowns, got, image, basis, maps, fixed, krylov, hessenberg, flag):
@@ -463,9 +481,6 @@
     for shift in (4, 2, 1):
         total = total + rolled(total, shift, 0)
     h = total / unknowns
-
-    def times(x, table):
-        return jnp.dot(x, table, precision=lax.Precision.HIGHEST, preferred_element_type=F32)
 
     terms = total * all_rows(fixed, 2)
     terms = terms * (times(h, maps[0]) + all_rows(fixed, 0)) * (times(h, maps[1]) + all_rows(fixed, 1))

time: 44.3 us -> 43.5 us (0.982)
  Pallas kernels: 9.48 us -> 8.59 us
    pallas_call x7, Pallas kernels: 9.48 us -> 8.59 us  [call(): pl.pallas_call(body, out_shape=tuple(outs), in_specs=in_specs or [VMEM] *...]
where the time goes in v6:
time: 43.5 us; the launch traced here: 43.2 us
  starting transfers between devices  17 us (39%)
  blocking collectives  10 us (23%)
  Pallas kernels  8.59 us (20%)
  waiting for transfers between devices  5.69 us (13%)
  local copies, waits for them, and re-layouts  0.84 us (2%)
  between operations  0.76 us (2%)
    all_to_all x1, blocking collectives, exchange(): lax.all_to_all(rows[:, None], AXES, 0, 0, tiled=True).reshape(rows.shape)  10 us
    pallas_call x7, Pallas kernels, call(): pl.pallas_call(body, out_shape=tuple(outs), in_specs=in_specs or [VMEM] *...  8.59 us
    all_to_all x2, starting transfers between devices, exchange(): lax.all_to_all(rows[:, None], AXES, 0, 0, tiled=True).reshape(rows.shape)  8.55 us
    all_to_all x2, waiting for transfers between devices, exchange(): lax.all_to_all(rows[:, None], AXES, 0, 0, tiled=True).reshape(rows.shape)  3.86 us
    ppermute x2, starting transfers between devices, on_device(): lax.ppermute(x, 'gy', pairs)  3.16 us
    ppermute x1, starting transfers between devices, swap(): return [lax.ppermute(x, axis, pairs) for x, pairs in zip(sides, rounds)]  1.83 us
    ppermute x1, starting transfers between devices, trade(): lax.ppermute(x, 'gx', pairs)  1.83 us
    ppermute x2, waiting for transfers between devices, trade(): lax.ppermute(x, 'gy', pairs)  1.82 us
  transfers between devices with their start and end apart: 8, of which 3 were waited for; matrix products, arithmetic and copies ran while one was open for 1% of the time, Pallas kernels for 11%

profile of v6, /device:TPU:0, one launch (start us, length us, event | category | flops | bytes accessed | tf_op | source)
XLA Modules:
  0.0 43.2 jit_solution(4936685361973988581)
XLA Ops:
  0.6 1.0 %shard_map.104 = (f32[16,8,128]{2,1,0:T(8,128)S(1)}, bf16[16,8,128]{2,1,0:T(8,128)(2,1)S(1)}, f32[64,8,128]{2,1,0:T(8,128)S(1)}, f32[48,8,128]{2,1,0:T(8,128)S(1)}, f32[48,8,128]{2,1,0:T(8,128)S(1)}) custom-call(f32[6,16,8,128]{3,2,1,0:T(8,128)} %bitcast.48, f32[64,8,128]{2,1,0:T(8,128)} %bitcast.55), custom_call_target="tpu_custom_call" | custom-call | flops 16384 | bytes 1409024 | tf_op jit(solution)/shard_map/pallas_call | solution.py:36
  1.7 0.5 %collective-permute-start.4 = (f32[48,8,128]{2,1,0:T(8,128)S(1)}, f32[48,8,128]{2,1,0:T(8,128)S(1)}, u32[]{:S(2)}, u32[]{:S(2)}) collective-permute-start(f32[48,8,128]{2,1,0:T(8,128)S(1)} %get-tuple-element.95), channel_id=1, source_target_pairs={{0,4},{8,12},{4,0},{12,8},{1,5},{9,13},{5,1},{13,9},{2,6},{10,14},... | collective-permute-start | bytes 589832 | tf_op jit(solution)/shard_map/ppermute | solution.py:558
  2.2 2.6 %collective-permute-start.5 = (f32[48,8,128]{2,1,0:T(8,128)S(1)}, f32[48,8,128]{2,1,0:T(8,128)S(1)}, u32[]{:S(2)}, u32[]{:S(2)}) collective-permute-start(f32[48,8,128]{2,1,0:T(8,128)S(1)} %get-tuple-element.96), channel_id=1, source_target_pairs={{4,8},{12,0},{8,4},{0,12},{5,9},{13,1},{9,5},{1,13},{6,10},{14,2},... | collective-permute-start | bytes 589832 | tf_op jit(solution)/shard_map/ppermute | solution.py:558
  4.8 1.0 %shard_map.106 = f32[160,128]{1,0:T(8,128)} custom-call(f32[16,8,128]{2,1,0:T(8,128)S(1)} %get-tuple-element.105.vector, f32[64,8,128]{2,1,0:T(8,128)S(1)} %get-tuple-element.98.phi), custom_call_target="tpu_custom_call" | custom-call | flops 524288 | bytes 409600 | tf_op jit(solution)/shard_map/pallas_call | solution.py:36
  5.8 4.9 %all-to-all-start.1 = ((f32[160,1,128]{2,1,0:T(1,128)}), f32[160,1,128]{2,1,0:T(1,128)S(1)}, u32[]{:S(2)}, u32[]{:S(2)}) async-start(f32[160,1,128]{2,1,0:T(1,128)} %bitcast.20), calls=%async_computation.1 | async-start | bytes 163840 | tf_op jit(solution)/shard_map/all_to_all | solution.py:530
  10.7 0.0 collective-permute-done.4.rest_0_
  10.8 0.0 collective-permute-done.5.rest_1_
  10.8 5.1 %conditional.3 = (bf16[4,128,128]{2,1,0:T(8,128)(2,1)S(1)}, f32[88,128]{1,0:T(8,128)S(1)}, f32[16,8,128]{2,1,0:T(8,128)S(1)}, bf16[4,8,192,128]{3,2,1,0:T(8,128)(2,1)S(1)}, f32[16,8,128]{2,1,0:T(8,128)S(1)}) conditional(s32[]{:T(128)} %convert_element_type.14, () %tuple.35, (f32[48,8,128]{2,1,0:T(8,128)S(1)}, f32[48,8,128]{2,1,0:T(8,128)S(1)}, ...), branch_computations={%region_0.0_spmd, %region_1.2_spmd} | conditional | flops 10000335872 | bytes 5714342 | solution.py:600
  10.9 1.8 %collective-permute-start.3 = (bf16[4,4,2,6,128]{4,1,3,2,0:T(4,128)(2,1)S(1)}, bf16[4,4,2,6,128]{4,1,3,2,0:T(4,128)(2,1)S(1)}, u32[]{:S(2)}, u32[]{:S(2)}) collective-permute-start(bf16[4,4,2,6,128]{4,1,3,2,0:T(4,128)(2,1)S(1)} %slice_select_fusion), channel_id=1, source_target_pairs={{0,16},{16,0},{1,17},{17,1},{2,18},{18,2},{3,19},{19,3},{4,20},{20... | collective-permute-start | bytes 147464 | tf_op jit(solution)/shard_map/cond/branch_1_fun/ppermute | solution.py:517
  12.8 2.8 %branch_1_fun.1 = (f32[88,128]{1,0:T(8,128)S(1)}, f32[16,8,128]{2,1,0:T(8,128)S(1)}, bf16[4,8,192,128]{3,2,1,0:T(8,128)(2,1)S(1)}, f32[16,8,128]{2,1,0:T(8,128)S(1)}) custom-call(f32[64,8,128]{2,1,0:T(8,128)S(1)} %get-tuple-element.51.phi, f32[6,16,8,128]{3,2,1,0:T(8,128)} %get-tuple-element.52.basis, bf16[4,8,192,128]{3,2,1,0:T(8,128)(2,1)} %bitcast.62, ...), custom_call_target="tpu_custom_call" | custom-call | flops 10000000000 | bytes 4042752 | tf_op jit(solution)/shard_map/cond/branch_1_fun/pallas_call | solution.py:36
  15.7 0.0 collective-permute-done.3
  15.7 0.1 pad_maximum_fusion
  15.9 0.0 copy-start.3
  15.9 0.0 copy-start
  15.9 0.0 copy-start.2
  15.9 0.0 copy-start.5
  15.9 0.9 %shard_map.105 = (f32[16,8,128]{2,1,0:T(8,128)S(1)}, f32[8,128]{1,0:T(8,128)S(1)}, f32[8,8,128]{2,1,0:T(8,128)S(1)}, f32[8,8,128]{2,1,0:T(8,128)S(1)}, f32[20,8,128]{2,1,0:T(8,128)S(1)}) custom-call(bf16[4,8,192,128]{3,2,1,0:T(8,128)(2,1)S(1)} %get-tuple-element.99.inv, bf16[4,128,128]{2,1,0:T(8,128)(2,1)S(1)} %get-tuple-element.100.cols, ...), custom_call_target="tpu_custom_call" | custom-call | flops 62914560000 | bytes 2052096 | tf_op jit(solution)/shard_map/pallas_call | solution.py:36
  16.8 0.0 copy-start.1
  16.8 0.0 copy-start.4
  16.8 1.6 %all-to-all-done.1 = f32[160,1,128]{2,1,0:T(1,128)S(1)} async-done(((f32[160,1,128]{2,1,0:T(1,128)}), f32[160,1,128]{2,1,0:T(1,128)S(1)}, u32[]{:S(2)}, u32[]{:S(2)}) %all-to-all-start.1) | async-done | bytes 81952 | tf_op jit(solution)/shard_map/all_to_all | solution.py:530
  18.5 0.0 copy-done.3
  18.5 1.2 %shard_map.107 = f32[128,128]{1,0:T(8,128)} custom-call(f32[160,128]{1,0:T(8,128)S(1)} %bitcast.39, f32[8,128]{1,0:T(8,128)S(1)} %get-tuple-element.106.locz, f32[16,512]{1,0:T(8,128)S(1)} %copy-done.3), custom_call_target="tpu_custom_call" | custom-call | flops 131072 | bytes 184320 | tf_op jit(solution)/shard_map/pallas_call | solution.py:36
  19.7 3.7 %all-to-all-start.2 = ((f32[128,1,128]{2,1,0:T(1,128)}), f32[128,1,128]{2,1,0:T(1,128)S(1)}, u32[]{:S(2)}, u32[]{:S(2)}) async-start(f32[128,1,128]{2,1,0:T(1,128)} %bitcast.23), calls=%async_computation.2 | async-start | bytes 131072 | tf_op jit(solution)/shard_map/all_to_all | solution.py:530
  23.4 5.3 %conditional.4 = ((f32[8,8,128]{2,1,0:T(8,128)S(1)}, f32[8,8,128]{2,1,0:T(8,128)S(1)}, f32[20,8,128]{2,1,0:T(8,128)S(1)})) conditional(s32[]{:T(128)} %convert_element_type.14, (f32[8,8,128]{2,1,0:T(8,128)S(1)}, f32[8,8,128]{2,1,0:T(8,128)S(1)}, f32[20,8,128]{2,1,0:T(8,128)S(1)}) %tuple.37, (f32[8,8,128]{2,1,0:T(8,128)S(1)}, ...), branch_computations={%region_2.3_spmd, %region_3.4_spmd} | conditional | bytes 884888 | solution.py:627
  23.4 1.8 %collective-permute-start.2 = (f32[20,8,128]{2,1,0:T(8,128)S(1)}, f32[20,8,128]{2,1,0:T(8,128)S(1)}, u32[]{:S(2)}, u32[]{:S(2)}) collective-permute-start(f32[20,8,128]{2,1,0:T(8,128)S(1)} %get-tuple-element.60), channel_id=1, source_target_pairs={{0,16},{16,0},{1,17},{17,1},{2,18},{18,2},{3,19},{19,3},{4,20},{20... | collective-permute-start | bytes 245768 | tf_op jit(solution)/shard_map/cond/branch_1_fun/ppermute | solution.py:613
  25.2 0.0 collective-permute-start
  25.2 1.6 %collective-permute-start.1 = (f32[8,8,128]{2,1,0:T(8,128)S(1)}, f32[8,8,128]{2,1,0:T(8,128)S(1)}, u32[]{:S(2)}, u32[]{:S(2)}) collective-permute-start(f32[8,8,128]{2,1,0:T(8,128)S(1)} %get-tuple-element.59), channel_id=1, source_target_pairs={{4,8},{12,0},{8,4},{0,12},{5,9},{13,1},{9,5},{1,13},{6,10},{14,2},... | collective-permute-start | bytes 98312 | tf_op jit(solution)/shard_map/cond/branch_1_fun/ppermute | solution.py:614
  26.8 0.0 collective-permute-done
  26.8 1.8 %collective-permute-done.1 = f32[8,8,128]{2,1,0:T(8,128)S(1)} collective-permute-done((f32[8,8,128]{2,1,0:T(8,128)S(1)}, f32[8,8,128]{2,1,0:T(8,128)S(1)}, u32[]{:S(2)}, u32[]{:S(2)}) %collective-permute-start.1) | collective-permute-done | bytes 32800 | tf_op jit(solution)/shard_map/cond/branch_1_fun/ppermute | solution.py:614
  28.6 0.0 collective-permute-done.2
  28.6 2.2 %all-to-all-done.2 = f32[128,1,128]{2,1,0:T(1,128)S(1)} async-done(((f32[128,1,128]{2,1,0:T(1,128)}), f32[128,1,128]{2,1,0:T(1,128)S(1)}, u32[]{:S(2)}, u32[]{:S(2)}) %all-to-all-start.2) | async-done | bytes 65568 | tf_op jit(solution)/shard_map/all_to_all | solution.py:530
  30.8 0.0 copy-done
  30.9 0.0 copy-done.2
  30.9 0.0 copy-done.5
  30.9 0.9 %shard_map.108 = (f32[16,8,128]{2,1,0:T(8,128)S(1)}, f32[16,8,128]{2,1,0:T(8,128)S(1)}, f32[32,128]{1,0:T(8,128)S(1)}) custom-call(f32[16,8,128]{2,1,0:T(8,128)S(1)} %get-tuple-element.103.loc, f32[64,8,128]{2,1,0:T(8,128)S(1)} %get-tuple-element.98.phi, f32[16,8,128]{2,1,0:T(8,128)S(1)} %bitcast.43, f32[24,8,128]{2,1,0:T(8,128)S(1)} %bitcast.42, ...), custom_call_target="tpu_custom_call" | custom-call | flops 1310720 | bytes 1765376 | tf_op jit(solution)/shard_map/pallas_call | solution.py:36
  31.8 10.0 %all_to_all.20 = f32[32,1,128]{2,1,0:T(1,128)S(1)} all-to-all(f32[32,1,128]{2,1,0:T(1,128)S(1)} %bitcast.47), channel_id=1, replica_groups=mesh['gx'=2,'gy'=4,'gz'=4] {'gx','gy','gz'}, dimensions={0} | all-to-all | bytes 32768 | tf_op jit(solution)/shard_map/all_to_all | solution.py:530
  41.8 0.0 copy-done.1
  41.8 0.0 copy-done.4
  41.8 0.7 %shard_map.109 = (f32[16,8,128]{2,1,0:T(8,128)S(1)}, f32[4,7]{1,0:T(4,128)S(1)}, s32[1]{0:T(128)S(4)}) custom-call(f32[32,128]{1,0:T(8,128)S(1)} %bitcast.44, f32[16,8,128]{2,1,0:T(8,128)S(1)} %get-tuple-element.114.image, f32[6,16,8,128]{3,2,1,0:T(8,128)S(1)} %bitcast.51, bf16[3,128,128]{2,1,0:T(8,128)(2,1)S(1)} %copy-done.1, f32[8,128]{1,0:T(8,128)S(1)} %copy-done.4), custom_call_target="tpu_custom_call" | custom-call | flops 262144 | bytes 643188 | tf_op jit(solution)/shard_map/pallas_call | solution.py:36
  42.5 0.0 copy-start.6
  42.5 0.0 copy-start.7
  42.5 0.6 %copy.83 = f32[4,4,4,2,128]{4,3,2,1,0:T(2,128)} copy(f32[4,4,4,2,128]{4,3,2,1,0:T(2,128)S(1)} %bitcast.38) | data formatting | bytes 131072
  43.2 0.0 copy-done.6
  43.2 0.0 copy-done.7
  (14 shorter events, 0.2 us)
Async XLA Ops:
  1.7 9.1 %collective-permute-start.4 = (f32[48,8,128]{2,1,0:T(8,128)S(1)}, f32[48,8,128]{2,1,0:T(8,128)S(1)}, u32[]{:S(2)}, u32[]{:S(2)}) collective-permute-start(f32[48,8,128]{2,1,0:T(8,128)S(1)} %get-tuple-element.95), channel_id=1, source_target_pairs={{0,4},{8,12},{4,0},{12,8},{1,5},{9,13},{5,1},{13,9},{2,6},{10,14},... | collective-permute-start | bytes 589832 | tf_op jit(solution)/shard_map/ppermute | solution.py:558
  2.2 8.6 %collective-permute-start.5 = (f32[48,8,128]{2,1,0:T(8,128)S(1)}, f32[48,8,128]{2,1,0:T(8,128)S(1)}, u32[]{:S(2)}, u32[]{:S(2)}) collective-permute-start(f32[48,8,128]{2,1,0:T(8,128)S(1)} %get-tuple-element.96), channel_id=1, source_target_pairs={{4,8},{12,0},{8,4},{0,12},{5,9},{13,1},{9,5},{1,13},{6,10},{14,2},... | collective-permute-start | bytes 589832 | tf_op jit(solution)/shard_map/ppermute | solution.py:558
  5.8 12.6 %all-to-all-start.1 = ((f32[160,1,128]{2,1,0:T(1,128)}), f32[160,1,128]{2,1,0:T(1,128)S(1)}, u32[]{:S(2)}, u32[]{:S(2)}) async-start(f32[160,1,128]{2,1,0:T(1,128)} %bitcast.20), calls=%async_computation.1 | async-start | bytes 163840 | tf_op jit(solution)/shard_map/all_to_all | solution.py:530
  10.9 4.7 %collective-permute-start.3 = (bf16[4,4,2,6,128]{4,1,3,2,0:T(4,128)(2,1)S(1)}, bf16[4,4,2,6,128]{4,1,3,2,0:T(4,128)(2,1)S(1)}, u32[]{:S(2)}, u32[]{:S(2)}) collective-permute-start(bf16[4,4,2,6,128]{4,1,3,2,0:T(4,128)(2,1)S(1)} %slice_select_fusion), channel_id=1, source_target_pairs={{0,16},{16,0},{1,17},{17,1},{2,18},{18,2},{3,19},{19,3},{4,20},{20... | collective-permute-start | bytes 147464 | tf_op jit(solution)/shard_map/cond/branch_1_fun/ppermute | solution.py:517
  15.9 2.6 %copy-start.3 = (f32[16,512]{1,0:T(8,128)S(1)}, f32[16,512]{1,0:T(8,128)}, u32[]{:S(2)}) copy-start(f32[16,512]{1,0:T(8,128)} %factor.1) | copy-start | bytes 98308
  15.9 15.0 %copy-start = (f32[6,4,4,2,128]{4,3,2,1,0:T(2,128)S(1)}, f32[6,4,4,2,128]{4,3,2,1,0:T(2,128)}, u32[]{:S(2)}) copy-start(f32[6,4,4,2,128]{4,3,2,1,0:T(2,128)} %param.19) | copy-start | bytes 294916
  15.9 15.0 %copy-start.2 = (f32[4,4,4,2,128]{4,3,2,1,0:T(2,128)S(1)}, f32[4,4,4,2,128]{4,3,2,1,0:T(2,128)}, u32[]{:S(2)}) copy-start(f32[4,4,4,2,128]{4,3,2,1,0:T(2,128)} %param.18) | copy-start | bytes 196612
  15.9 14.9 %copy-start.5 = (f32[6,4,4,4,2,128]{5,4,3,2,1,0:T(2,128)S(1)}, f32[6,4,4,4,2,128]{5,4,3,2,1,0:T(2,128)}, u32[]{:S(2)}) copy-start(f32[6,4,4,4,2,128]{5,4,3,2,1,0:T(2,128)} %param.16) | copy-start | bytes 1179652
  16.8 25.0 %copy-start.1 = (bf16[3,128,128]{2,1,0:T(8,128)(2,1)S(1)}, bf16[3,128,128]{2,1,0:T(8,128)(2,1)}, u32[]{:S(2)}) copy-start(bf16[3,128,128]{2,1,0:T(8,128)(2,1)} %constant.94.clone.maps) | copy-start | bytes 294916
  16.8 25.0 %copy-start.4 = (f32[8,128]{1,0:T(8,128)S(1)}, f32[8,128]{1,0:T(8,128)}, u32[]{:S(2)}) copy-start(f32[8,128]{1,0:T(8,128)} %constant.95.clone.fixed) | copy-start | bytes 12292
  19.7 11.2 %all-to-all-start.2 = ((f32[128,1,128]{2,1,0:T(1,128)}), f32[128,1,128]{2,1,0:T(1,128)S(1)}, u32[]{:S(2)}, u32[]{:S(2)}) async-start(f32[128,1,128]{2,1,0:T(1,128)} %bitcast.23), calls=%async_computation.2 | async-start | bytes 131072 | tf_op jit(solution)/shard_map/all_to_all | solution.py:530
  23.4 5.2 %collective-permute-start.2 = (f32[20,8,128]{2,1,0:T(8,128)S(1)}, f32[20,8,128]{2,1,0:T(8,128)S(1)}, u32[]{:S(2)}, u32[]{:S(2)}) collective-permute-start(f32[20,8,128]{2,1,0:T(8,128)S(1)} %get-tuple-element.60), channel_id=1, source_target_pairs={{0,16},{16,0},{1,17},{17,1},{2,18},{18,2},{3,19},{19,3},{4,20},{20... | collective-permute-start | bytes 245768 | tf_op jit(solution)/shard_map/cond/branch_1_fun/ppermute | solution.py:613
  25.2 1.6 %collective-permute-start = (f32[8,8,128]{2,1,0:T(8,128)S(1)}, f32[8,8,128]{2,1,0:T(8,128)S(1)}, u32[]{:S(2)}, u32[]{:S(2)}) collective-permute-start(f32[8,8,128]{2,1,0:T(8,128)S(1)} %get-tuple-element.58), channel_id=1, source_target_pairs={{0,4},{8,12},{4,0},{12,8},{1,5},{9,13},{5,1},{13,9},{2,6},{10,14},... | collective-permute-start | bytes 98312 | tf_op jit(solution)/shard_map/cond/branch_1_fun/ppermute | solution.py:614
  25.2 3.4 %collective-permute-start.1 = (f32[8,8,128]{2,1,0:T(8,128)S(1)}, f32[8,8,128]{2,1,0:T(8,128)S(1)}, u32[]{:S(2)}, u32[]{:S(2)}) collective-permute-start(f32[8,8,128]{2,1,0:T(8,128)S(1)} %get-tuple-element.59), channel_id=1, source_target_pairs={{4,8},{12,0},{8,4},{0,12},{5,9},{13,1},{9,5},{1,13},{6,10},{14,2},... | collective-permute-start | bytes 98312 | tf_op jit(solution)/shard_map/cond/branch_1_fun/ppermute | solution.py:614
  42.5 0.7 %copy-start.6 = (f32[4,7]{1,0:T(4,128)}, f32[4,7]{1,0:T(4,128)S(1)}, u32[]{:S(2)}) copy-start(f32[4,7]{1,0:T(4,128)S(1)} %get-tuple-element.157) | copy-start | bytes 340
  42.5 0.7 %copy-start.7 = (f32[16,8,128]{2,1,0:T(8,128)}, f32[16,8,128]{2,1,0:T(8,128)S(1)}, u32[]{:S(2)}) copy-start(f32[16,8,128]{2,1,0:T(8,128)S(1)} %get-tuple-element.120) | copy-start | bytes 196612

commit v7 on v6

--- a/solution.py
+++ b/solution.py
@@ -190,13 +190,15 @@
             sends[1][at + i] = jnp.where(odd, high, low)
 
 
-def solve(inv, cols, starts, done):
+def solve(inv, cols, starts, done, ready=None):
     def one(c, carry):
+        if ready is not None:
+            ready(c)
         total = [[jnp.zeros((8, 128), F32) for _ in range(XY)] for _ in range(S)]
         for at, j in starts:
-            seen = [cols[s, j : j + 16, :].astype(F32) for s in range(S)]
+            seen = [cols[s, j : j + SIDE, :].astype(F32) for s in range(S)]
             for i in range(XY):
-                w = inv[c, i, at : at + 16, :].astype(F32)
+                w = inv[c, i, pl.ds(at, SIDE), :].astype(F32)
                 for s in range(S):
                     part = w * seen[s]
                     total[s][i] = total[s][i] + part[:8] + part[8:]
@@ -207,10 +209,18 @@
     lax.fori_loop(0, C, one, 0)
 
 
+def edge(first):
+    return pl.multiple_of(jnp.where(first, 0, 2 * SIDE), SIDE)
+
+
 def early_body(two_x, phi, basis, inv, cols, gram, loc, inv_kept, *refs):
-    phi_faces, (sem,) = refs[: 1 + two_x], refs[1 + two_x :]
-    copy = pltpu.make_async_copy(inv, inv_kept, sem)
-    copy.start()
+    phi_faces, (sems,) = refs[: 1 + two_x], refs[1 + two_x :]
+
+    def copy(c):
+        return pltpu.make_async_copy(inv.at[c], inv_kept.at[c], sems.at[c])
+
+    for c in range(C):
+        copy(c).start()
     rows = []
     for m, n in PAIRS:
         for s in range(S):
@@ -224,8 +234,13 @@
     def done(i, x):
         loc[i] = x
 
-    copy.wait()
-    solve(inv_kept, cols, [(EXTENT * c + SIDE, SIDE * c) for c in range(C)], done)
+    if two_x:
+        starts = [(EXTENT * c + SIDE, SIDE * c) for c in range(C)]
+    else:
+        at = edge(lax.axis_index("gx") == 0)
+        starts = [(EXTENT * c + SIDE, 2 * SIDE * c) for c in range(C)]
+        starts += [(EXTENT * c + at, 2 * SIDE * c + SIDE) for c in range(C)]
+    solve(inv_kept, cols, starts, done, lambda c: copy(c).wait())
 
 
 def local_body(two_x, inv, cols, early, *refs):
@@ -234,8 +249,12 @@
     def done(i, x):
         loc[i] = early[i] + x
 
-    starts = [(EXTENT * c, 2 * SIDE * c) for c in range(C)]
-    starts += [(EXTENT * c + 2 * SIDE, 2 * SIDE * c + SIDE) for c in range(C)]
+    if two_x:
+        starts = [(EXTENT * c, 2 * SIDE * c) for c in range(C)]
+        starts += [(EXTENT * c + 2 * SIDE, 2 * SIDE * c + SIDE) for c in range(C)]
+    else:
+        at = edge(lax.axis_index("gx") == 1)
+        starts = [(EXTENT * c + at, SIDE * c) for c in range(C)]
     solve(inv, cols, starts, done)
     locz[...] = across(ends(), loc[...].reshape(S * C * XY, CZ))
     odd_y = lax.axis_index("gy") % 2 == 1
@@ -565,10 +584,19 @@
         parts = [x[: S * C].reshape(S, C, CX, CY, CZ).astype(rounded.dtype) for x in swapped]
         y_low, y_high = by_side("gy", parts)
         extended = jnp.concatenate([y_low, rounded, y_high], axis=3)
-        x_low, x_high = by_side("gx", swap("gx", extended[:, :, :2], extended[:, :, -2:]))
+        slabs = swap("gx", extended[:, :, :2], extended[:, :, -2:])
         mine = extended.reshape(S, C, CX * (CY + 4), CZ)
-        edge = (EXTENT - CX * (CY + 4)) // 2
-        middle = mine[:, :, SIDE - edge : 2 * SIDE - edge].reshape(S, C * SIDE, CZ)
+        width = (EXTENT - CX * (CY + 4)) // 2
+        low, high = mine[:, :, : SIDE - width], mine[:, :, 2 * SIDE - width :]
+        middle = mine[:, :, SIDE - width : 2 * SIDE - width]
+        first = lax.axis_index("gx") == 0
+        none = jnp.zeros((S, C, width, CZ), rounded.dtype)
+        if not two_x:
+            ending = jnp.where(
+                first, jnp.concatenate([none, low], axis=2), jnp.concatenate([high, none], axis=2)
+            )
+            middle = jnp.concatenate([middle, ending], axis=2)
+        middle = middle.reshape(S, -1, CZ)
         early = call(
             functools.partial(early_body, two_x),
             [kept(BASE, 128), kept(S * C, XY, CZ), kept(*inverse.shape, dtype=inverse.dtype)]
@@ -576,22 +604,22 @@
             (phi, vectors, in_hbm(inverse), middle),
             10**10,
             in_specs=[VMEM, VMEM, pl.BlockSpec(memory_space=pltpu.HBM), VMEM],
-            scratch=[pltpu.SemaphoreType.DMA],
+            scratch=[pltpu.SemaphoreType.DMA((C,))],
         )
-        outer = jnp.concatenate(
-            [
-                x_low.reshape(S, C, edge, CZ),
-                mine[:, :, : SIDE - edge],
-                mine[:, :, 2 * SIDE - edge :],
-                x_high.reshape(S, C, edge, CZ),
-            ],
-            axis=2,
-        )
-        return [outer.reshape(S, C * 2 * SIDE, CZ)] + list(early)
+        slabs, early = lax.optimization_barrier((slabs, early))
+        if two_x:
+            slabs = [x.reshape(S, C, width, CZ) for x in by_side("gx", slabs)]
+            outer = jnp.concatenate([slabs[0], low, high, slabs[1]], axis=2)
+        else:
+            slab = slabs[0].reshape(S, C, width, CZ)
+            outer = jnp.where(
+                first, jnp.concatenate([high, slab], axis=2), jnp.concatenate([slab, low], axis=2)
+            )
+        return [outer.reshape(S, -1, CZ)] + list(early)
 
     def unused(swapped, rounded, phi, vectors, inverse):
         return [
-            jnp.zeros((S, C * 2 * SIDE, CZ), rounded.dtype),
+            jnp.zeros((S, C * SIDE * (1 + two_x), CZ), rounded.dtype),
             jnp.zeros((BASE, 128), F32),
             jnp.zeros((S * C, XY, CZ), F32),
             jnp.zeros_like(inverse),

time: 43.5 us -> 43.1 us (level)
  transfers between devices with their start and end apart: 8 -> 8, of which waited for: 3 -> 3; matrix products, arithmetic and copies ran while one was open for 1% -> 1% of each run, Pallas kernels for 11% -> 10%
where the time goes in v7:
time: 43.1 us; the launch traced here: 42.8 us
  starting transfers between devices  16.6 us (39%)
  blocking collectives  10 us (23%)
  Pallas kernels  8.22 us (19%)
  waiting for transfers between devices  6.04 us (14%)
  local copies, waits for them, and re-layouts  0.83 us (2%)
  between operations  0.76 us (2%)
    all_to_all x1, blocking collectives, exchange(): lax.all_to_all(rows[:, None], AXES, 0, 0, tiled=True).reshape(rows.shape)  10 us
    pallas_call x7, Pallas kernels, call(): pl.pallas_call(body, out_shape=tuple(outs), in_specs=in_specs or [VMEM] *...  8.22 us
    all_to_all x2, starting transfers between devices, exchange(): lax.all_to_all(rows[:, None], AXES, 0, 0, tiled=True).reshape(rows.shape)  8.2 us
    all_to_all x2, waiting for transfers between devices, exchange(): lax.all_to_all(rows[:, None], AXES, 0, 0, tiled=True).reshape(rows.shape)  4.2 us
    ppermute x2, starting transfers between devices, on_device(): lax.ppermute(x, 'gy', pairs)  3.16 us
    ppermute x1, starting transfers between devices, swap(): return [lax.ppermute(x, axis, pairs) for x, pairs in zip(sides, rounds)]  1.83 us
    ppermute x1, starting transfers between devices, trade(): lax.ppermute(x, 'gx', pairs)  1.83 us
    ppermute x2, waiting for transfers between devices, trade(): lax.ppermute(x, 'gy', pairs)  1.82 us
  transfers between devices with their start and end apart: 8, of which 3 were waited for; matrix products, arithmetic and copies ran while one was open for 1% of the time, Pallas kernels for 10%

profile of v7, /device:TPU:0, one launch (start us, length us, event | category | flops | bytes accessed | tf_op | source)
XLA Modules:
  0.0 42.8 jit_solution(16225624802498813785)
XLA Ops:
  0.6 1.0 %shard_map.104 = (f32[16,8,128]{2,1,0:T(8,128)S(1)}, bf16[16,8,128]{2,1,0:T(8,128)(2,1)S(1)}, f32[64,8,128]{2,1,0:T(8,128)S(1)}, f32[48,8,128]{2,1,0:T(8,128)S(1)}, f32[48,8,128]{2,1,0:T(8,128)S(1)}) custom-call(f32[6,16,8,128]{3,2,1,0:T(8,128)} %bitcast.47, f32[64,8,128]{2,1,0:T(8,128)} %bitcast.54), custom_call_target="tpu_custom_call" | custom-call | flops 16384 | bytes 1409024 | tf_op jit(solution)/shard_map/pallas_call | solution.py:36
  1.7 0.5 %collective-permute-start.4 = (f32[48,8,128]{2,1,0:T(8,128)S(1)}, f32[48,8,128]{2,1,0:T(8,128)S(1)}, u32[]{:S(2)}, u32[]{:S(2)}) collective-permute-start(f32[48,8,128]{2,1,0:T(8,128)S(1)} %get-tuple-element.100), channel_id=1, source_target_pairs={{0,4},{8,12},{4,0},{12,8},{1,5},{9,13},{5,1},{13,9},{2,6},{10,14},... | collective-permute-start | bytes 589832 | tf_op jit(solution)/shard_map/ppermute | solution.py:577
  2.2 2.6 %collective-permute-start.5 = (f32[48,8,128]{2,1,0:T(8,128)S(1)}, f32[48,8,128]{2,1,0:T(8,128)S(1)}, u32[]{:S(2)}, u32[]{:S(2)}) collective-permute-start(f32[48,8,128]{2,1,0:T(8,128)S(1)} %get-tuple-element.101), channel_id=1, source_target_pairs={{4,8},{12,0},{8,4},{0,12},{5,9},{13,1},{9,5},{1,13},{6,10},{14,2},... | collective-permute-start | bytes 589832 | tf_op jit(solution)/shard_map/ppermute | solution.py:577
  4.8 1.0 %shard_map.106 = f32[160,128]{1,0:T(8,128)} custom-call(f32[16,8,128]{2,1,0:T(8,128)S(1)} %get-tuple-element.110.vector, f32[64,8,128]{2,1,0:T(8,128)S(1)} %get-tuple-element.103.phi), custom_call_target="tpu_custom_call" | custom-call | flops 524288 | bytes 409600 | tf_op jit(solution)/shard_map/pallas_call | solution.py:36
  5.8 4.9 %all-to-all-start.1 = ((f32[160,1,128]{2,1,0:T(1,128)}), f32[160,1,128]{2,1,0:T(1,128)S(1)}, u32[]{:S(2)}, u32[]{:S(2)}) async-start(f32[160,1,128]{2,1,0:T(1,128)} %bitcast.19), calls=%async_computation.1 | async-start | bytes 163840 | tf_op jit(solution)/shard_map/all_to_all | solution.py:549
  10.7 0.0 collective-permute-done.4.rest_0_
  10.8 0.0 collective-permute-done.5.rest_1_
  10.8 5.1 %conditional.3 = (bf16[4,64,128]{2,1,0:T(8,128)(2,1)S(1)}, f32[88,128]{1,0:T(8,128)S(1)}, f32[16,8,128]{2,1,0:T(8,128)S(1)}, bf16[4,8,192,128]{3,2,1,0:T(8,128)(2,1)S(1)}, f32[16,8,128]{2,1,0:T(8,128)S(1)}) conditional(s32[]{:T(128)} %convert_element_type.14, () %tuple.36, (f32[48,8,128]{2,1,0:T(8,128)S(1)}, f32[48,8,128]{2,1,0:T(8,128)S(1)}, ...), branch_computations={%region_0.0_spmd, %region_1.2_spmd} | conditional | flops 10000286720 | bytes 5878173 | solution.py:628
  10.9 1.8 %collective-permute-start.3 = (bf16[4,4,2,6,128]{4,1,3,2,0:T(4,128)(2,1)S(1)}, bf16[4,4,2,6,128]{4,1,3,2,0:T(4,128)(2,1)S(1)}, u32[]{:S(2)}, u32[]{:S(2)}) collective-permute-start(bf16[4,4,2,6,128]{4,1,3,2,0:T(4,128)(2,1)S(1)} %slice_select_fusion), channel_id=1, source_target_pairs={{0,16},{16,0},{1,17},{17,1},{2,18},{18,2},{3,19},{19,3},{4,20},{20... | collective-permute-start | bytes 147464 | tf_op jit(solution)/shard_map/cond/branch_1_fun/ppermute | solution.py:536
  12.9 0.1 pad_maximum_fusion
  13.0 2.8 %branch_1_fun.1 = (f32[88,128]{1,0:T(8,128)S(1)}, f32[16,8,128]{2,1,0:T(8,128)S(1)}, bf16[4,8,192,128]{3,2,1,0:T(8,128)(2,1)S(1)}, f32[16,8,128]{2,1,0:T(8,128)S(1)}) custom-call(f32[64,8,128]{2,1,0:T(8,128)S(1)} %get-tuple-element.51.phi, f32[6,16,8,128]{3,2,1,0:T(8,128)} %get-tuple-element.52.basis, bf16[4,8,192,128]{3,2,1,0:T(8,128)(2,1)} %bitcast.60, ...), custom_call_target="tpu_custom_call" | custom-call | flops 10000000000 | bytes 4108288 | tf_op jit(solution)/shard_map/cond/branch_1_fun/pallas_call | solution.py:36
  15.8 0.0 collective-permute-done.3
  15.8 0.1 maximum_select_fusion
  15.9 0.0 copy-start.3
  15.9 0.0 copy-start
  15.9 0.0 copy-start.2
  15.9 0.0 copy-start.5
  15.9 0.6 %shard_map.105 = (f32[16,8,128]{2,1,0:T(8,128)S(1)}, f32[8,128]{1,0:T(8,128)S(1)}, f32[8,8,128]{2,1,0:T(8,128)S(1)}, f32[8,8,128]{2,1,0:T(8,128)S(1)}, f32[20,8,128]{2,1,0:T(8,128)S(1)}) custom-call(bf16[4,8,192,128]{3,2,1,0:T(8,128)(2,1)S(1)} %get-tuple-element.104.inv, bf16[4,64,128]{2,1,0:T(8,128)(2,1)S(1)} %get-tuple-element.105.cols, ...), custom_call_target="tpu_custom_call" | custom-call | flops 62914560000 | bytes 1986560 | tf_op jit(solution)/shard_map/pallas_call | solution.py:36
  16.5 0.0 copy-start.1
  16.5 0.0 copy-start.4
  16.5 2.0 %all-to-all-done.1 = f32[160,1,128]{2,1,0:T(1,128)S(1)} async-done(((f32[160,1,128]{2,1,0:T(1,128)}), f32[160,1,128]{2,1,0:T(1,128)S(1)}, u32[]{:S(2)}, u32[]{:S(2)}) %all-to-all-start.1) | async-done | bytes 81952 | tf_op jit(solution)/shard_map/all_to_all | solution.py:549
  18.5 0.0 copy-done.3
  18.5 1.2 %shard_map.107 = f32[128,128]{1,0:T(8,128)} custom-call(f32[160,128]{1,0:T(8,128)S(1)} %bitcast.38, f32[8,128]{1,0:T(8,128)S(1)} %get-tuple-element.111.locz, f32[16,512]{1,0:T(8,128)S(1)} %copy-done.3), custom_call_target="tpu_custom_call" | custom-call | flops 131072 | bytes 184320 | tf_op jit(solution)/shard_map/pallas_call | solution.py:36
  19.7 3.3 %all-to-all-start.2 = ((f32[128,1,128]{2,1,0:T(1,128)}), f32[128,1,128]{2,1,0:T(1,128)S(1)}, u32[]{:S(2)}, u32[]{:S(2)}) async-start(f32[128,1,128]{2,1,0:T(1,128)} %bitcast.22), calls=%async_computation.2 | async-start | bytes 131072 | tf_op jit(solution)/shard_map/all_to_all | solution.py:549
  23.0 5.3 %conditional.4 = ((f32[8,8,128]{2,1,0:T(8,128)S(1)}, f32[8,8,128]{2,1,0:T(8,128)S(1)}, f32[20,8,128]{2,1,0:T(8,128)S(1)})) conditional(s32[]{:T(128)} %convert_element_type.14, (f32[8,8,128]{2,1,0:T(8,128)S(1)}, f32[8,8,128]{2,1,0:T(8,128)S(1)}, f32[20,8,128]{2,1,0:T(8,128)S(1)}) %tuple.38, (f32[8,8,128]{2,1,0:T(8,128)S(1)}, ...), branch_computations={%region_2.3_spmd, %region_3.4_spmd} | conditional | bytes 884888 | solution.py:655
  23.0 1.8 %collective-permute-start.2 = (f32[20,8,128]{2,1,0:T(8,128)S(1)}, f32[20,8,128]{2,1,0:T(8,128)S(1)}, u32[]{:S(2)}, u32[]{:S(2)}) collective-permute-start(f32[20,8,128]{2,1,0:T(8,128)S(1)} %get-tuple-element.65), channel_id=1, source_target_pairs={{0,16},{16,0},{1,17},{17,1},{2,18},{18,2},{3,19},{19,3},{4,20},{20... | collective-permute-start | bytes 245768 | tf_op jit(solution)/shard_map/cond/branch_1_fun/ppermute | solution.py:641
  24.9 0.0 collective-permute-start
  24.9 1.6 %collective-permute-start.1 = (f32[8,8,128]{2,1,0:T(8,128)S(1)}, f32[8,8,128]{2,1,0:T(8,128)S(1)}, u32[]{:S(2)}, u32[]{:S(2)}) collective-permute-start(f32[8,8,128]{2,1,0:T(8,128)S(1)} %get-tuple-element.64), channel_id=1, source_target_pairs={{4,8},{12,0},{8,4},{0,12},{5,9},{13,1},{9,5},{1,13},{6,10},{14,2},... | collective-permute-start | bytes 98312 | tf_op jit(solution)/shard_map/cond/branch_1_fun/ppermute | solution.py:642
  26.4 0.0 collective-permute-done
  26.4 1.8 %collective-permute-done.1 = f32[8,8,128]{2,1,0:T(8,128)S(1)} collective-permute-done((f32[8,8,128]{2,1,0:T(8,128)S(1)}, f32[8,8,128]{2,1,0:T(8,128)S(1)}, u32[]{:S(2)}, u32[]{:S(2)}) %collective-permute-start.1) | collective-permute-done | bytes 32800 | tf_op jit(solution)/shard_map/cond/branch_1_fun/ppermute | solution.py:642
  28.3 0.0 collective-permute-done.2
  28.3 2.2 %all-to-all-done.2 = f32[128,1,128]{2,1,0:T(1,128)S(1)} async-done(((f32[128,1,128]{2,1,0:T(1,128)}), f32[128,1,128]{2,1,0:T(1,128)S(1)}, u32[]{:S(2)}, u32[]{:S(2)}) %all-to-all-start.2) | async-done | bytes 65568 | tf_op jit(solution)/shard_map/all_to_all | solution.py:549
  30.5 0.0 copy-done
  30.5 0.0 copy-done.2
  30.5 0.0 copy-done.5
  30.5 0.9 %shard_map.108 = (f32[16,8,128]{2,1,0:T(8,128)S(1)}, f32[16,8,128]{2,1,0:T(8,128)S(1)}, f32[32,128]{1,0:T(8,128)S(1)}) custom-call(f32[16,8,128]{2,1,0:T(8,128)S(1)} %get-tuple-element.108.loc, f32[64,8,128]{2,1,0:T(8,128)S(1)} %get-tuple-element.103.phi, f32[16,8,128]{2,1,0:T(8,128)S(1)} %bitcast.43, f32[24,8,128]{2,1,0:T(8,128)S(1)} %bitcast.42, ...), custom_call_target="tpu_custom_call" | custom-call | flops 1310720 | bytes 1765376 | tf_op jit(solution)/shard_map/pallas_call | solution.py:36
  31.4 10.0 %all_to_all.20 = f32[32,1,128]{2,1,0:T(1,128)S(1)} all-to-all(f32[32,1,128]{2,1,0:T(1,128)S(1)} %bitcast.46), channel_id=1, replica_groups=mesh['gx'=2,'gy'=4,'gz'=4] {'gx','gy','gz'}, dimensions={0} | all-to-all | bytes 32768 | tf_op jit(solution)/shard_map/all_to_all | solution.py:549
  41.5 0.0 copy-done.1
  41.5 0.0 copy-done.4
  41.5 0.7 %shard_map.109 = (f32[16,8,128]{2,1,0:T(8,128)S(1)}, f32[4,7]{1,0:T(4,128)S(1)}, s32[1]{0:T(128)S(4)}) custom-call(f32[32,128]{1,0:T(8,128)S(1)} %bitcast.44, f32[16,8,128]{2,1,0:T(8,128)S(1)} %get-tuple-element.119.image, f32[6,16,8,128]{3,2,1,0:T(8,128)S(1)} %bitcast.50, bf16[3,128,128]{2,1,0:T(8,128)(2,1)S(1)} %copy-done.1, f32[8,128]{1,0:T(8,128)S(1)} %copy-done.4), custom_call_target="tpu_custom_call" | custom-call | flops 262144 | bytes 643188 | tf_op jit(solution)/shard_map/pallas_call | solution.py:36
  42.2 0.0 copy-start.6
  42.2 0.0 copy-start.7
  42.2 0.6 %copy.83 = f32[4,4,4,2,128]{4,3,2,1,0:T(2,128)} copy(f32[4,4,4,2,128]{4,3,2,1,0:T(2,128)S(1)} %bitcast.37) | data formatting | bytes 131072
  42.8 0.0 copy-done.6
  42.8 0.0 copy-done.7
  (14 shorter events, 0.2 us)
Async XLA Ops:
  1.7 9.1 %collective-permute-start.4 = (f32[48,8,128]{2,1,0:T(8,128)S(1)}, f32[48,8,128]{2,1,0:T(8,128)S(1)}, u32[]{:S(2)}, u32[]{:S(2)}) collective-permute-start(f32[48,8,128]{2,1,0:T(8,128)S(1)} %get-tuple-element.100), channel_id=1, source_target_pairs={{0,4},{8,12},{4,0},{12,8},{1,5},{9,13},{5,1},{13,9},{2,6},{10,14},... | collective-permute-start | bytes 589832 | tf_op jit(solution)/shard_map/ppermute | solution.py:577
  2.2 8.6 %collective-permute-start.5 = (f32[48,8,128]{2,1,0:T(8,128)S(1)}, f32[48,8,128]{2,1,0:T(8,128)S(1)}, u32[]{:S(2)}, u32[]{:S(2)}) collective-permute-start(f32[48,8,128]{2,1,0:T(8,128)S(1)} %get-tuple-element.101), channel_id=1, source_target_pairs={{4,8},{12,0},{8,4},{0,12},{5,9},{13,1},{9,5},{1,13},{6,10},{14,2},... | collective-permute-start | bytes 589832 | tf_op jit(solution)/shard_map/ppermute | solution.py:577
  5.8 12.6 %all-to-all-start.1 = ((f32[160,1,128]{2,1,0:T(1,128)}), f32[160,1,128]{2,1,0:T(1,128)S(1)}, u32[]{:S(2)}, u32[]{:S(2)}) async-start(f32[160,1,128]{2,1,0:T(1,128)} %bitcast.19), calls=%async_computation.1 | async-start | bytes 163840 | tf_op jit(solution)/shard_map/all_to_all | solution.py:549
  10.9 4.8 %collective-permute-start.3 = (bf16[4,4,2,6,128]{4,1,3,2,0:T(4,128)(2,1)S(1)}, bf16[4,4,2,6,128]{4,1,3,2,0:T(4,128)(2,1)S(1)}, u32[]{:S(2)}, u32[]{:S(2)}) collective-permute-start(bf16[4,4,2,6,128]{4,1,3,2,0:T(4,128)(2,1)S(1)} %slice_select_fusion), channel_id=1, source_target_pairs={{0,16},{16,0},{1,17},{17,1},{2,18},{18,2},{3,19},{19,3},{4,20},{20... | collective-permute-start | bytes 147464 | tf_op jit(solution)/shard_map/cond/branch_1_fun/ppermute | solution.py:536
  15.9 2.6 %copy-start.3 = (f32[16,512]{1,0:T(8,128)S(1)}, f32[16,512]{1,0:T(8,128)}, u32[]{:S(2)}) copy-start(f32[16,512]{1,0:T(8,128)} %factor.1) | copy-start | bytes 98308
  15.9 14.6 %copy-start = (f32[6,4,4,2,128]{4,3,2,1,0:T(2,128)S(1)}, f32[6,4,4,2,128]{4,3,2,1,0:T(2,128)}, u32[]{:S(2)}) copy-start(f32[6,4,4,2,128]{4,3,2,1,0:T(2,128)} %param.19) | copy-start | bytes 294916
  15.9 14.6 %copy-start.2 = (f32[4,4,4,2,128]{4,3,2,1,0:T(2,128)S(1)}, f32[4,4,4,2,128]{4,3,2,1,0:T(2,128)}, u32[]{:S(2)}) copy-start(f32[4,4,4,2,128]{4,3,2,1,0:T(2,128)} %param.18) | copy-start | bytes 196612
  15.9 14.6 %copy-start.5 = (f32[6,4,4,4,2,128]{5,4,3,2,1,0:T(2,128)S(1)}, f32[6,4,4,4,2,128]{5,4,3,2,1,0:T(2,128)}, u32[]{:S(2)}) copy-start(f32[6,4,4,4,2,128]{5,4,3,2,1,0:T(2,128)} %param.16) | copy-start | bytes 1179652
  16.5 25.0 %copy-start.1 = (bf16[3,128,128]{2,1,0:T(8,128)(2,1)S(1)}, bf16[3,128,128]{2,1,0:T(8,128)(2,1)}, u32[]{:S(2)}) copy-start(bf16[3,128,128]{2,1,0:T(8,128)(2,1)} %constant.92.clone.maps) | copy-start | bytes 294916
  16.5 25.0 %copy-start.4 = (f32[8,128]{1,0:T(8,128)S(1)}, f32[8,128]{1,0:T(8,128)}, u32[]{:S(2)}) copy-start(f32[8,128]{1,0:T(8,128)} %constant.93.clone.fixed) | copy-start | bytes 12292
  19.7 10.8 %all-to-all-start.2 = ((f32[128,1,128]{2,1,0:T(1,128)}), f32[128,1,128]{2,1,0:T(1,128)S(1)}, u32[]{:S(2)}, u32[]{:S(2)}) async-start(f32[128,1,128]{2,1,0:T(1,128)} %bitcast.22), calls=%async_computation.2 | async-start | bytes 131072 | tf_op jit(solution)/shard_map/all_to_all | solution.py:549
  23.0 5.2 %collective-permute-start.2 = (f32[20,8,128]{2,1,0:T(8,128)S(1)}, f32[20,8,128]{2,1,0:T(8,128)S(1)}, u32[]{:S(2)}, u32[]{:S(2)}) collective-permute-start(f32[20,8,128]{2,1,0:T(8,128)S(1)} %get-tuple-element.65), channel_id=1, source_target_pairs={{0,16},{16,0},{1,17},{17,1},{2,18},{18,2},{3,19},{19,3},{4,20},{20... | collective-permute-start | bytes 245768 | tf_op jit(solution)/shard_map/cond/branch_1_fun/ppermute | solution.py:641
  24.9 1.6 %collective-permute-start = (f32[8,8,128]{2,1,0:T(8,128)S(1)}, f32[8,8,128]{2,1,0:T(8,128)S(1)}, u32[]{:S(2)}, u32[]{:S(2)}) collective-permute-start(f32[8,8,128]{2,1,0:T(8,128)S(1)} %get-tuple-element.63), channel_id=1, source_target_pairs={{0,4},{8,12},{4,0},{12,8},{1,5},{9,13},{5,1},{13,9},{2,6},{10,14},... | collective-permute-start | bytes 98312 | tf_op jit(solution)/shard_map/cond/branch_1_fun/ppermute | solution.py:642
  24.9 3.4 %collective-permute-start.1 = (f32[8,8,128]{2,1,0:T(8,128)S(1)}, f32[8,8,128]{2,1,0:T(8,128)S(1)}, u32[]{:S(2)}, u32[]{:S(2)}) collective-permute-start(f32[8,8,128]{2,1,0:T(8,128)S(1)} %get-tuple-element.64), channel_id=1, source_target_pairs={{4,8},{12,0},{8,4},{0,12},{5,9},{13,1},{9,5},{1,13},{6,10},{14,2},... | collective-permute-start | bytes 98312 | tf_op jit(solution)/shard_map/cond/branch_1_fun/ppermute | solution.py:642
  42.2 0.7 %copy-start.6 = (f32[4,7]{1,0:T(4,128)}, f32[4,7]{1,0:T(4,128)S(1)}, u32[]{:S(2)}) copy-start(f32[4,7]{1,0:T(4,128)S(1)} %get-tuple-element.160) | copy-start | bytes 340
  42.2 0.7 %copy-start.7 = (f32[16,8,128]{2,1,0:T(8,128)}, f32[16,8,128]{2,1,0:T(8,128)S(1)}, u32[]{:S(2)}) copy-start(f32[16,8,128]{2,1,0:T(8,128)S(1)} %get-tuple-element.125) | copy-start | bytes 196612

commit v8 on v7

--- a/solution.py
+++ b/solution.py
@@ -28,6 +28,7 @@
 epsilon = 1e-06
 
 VMEM = pl.BlockSpec(memory_space=pltpu.VMEM)
+HBM = pl.BlockSpec(memory_space=pltpu.HBM)
 F32 = jnp.float32
 
 
@@ -190,7 +191,7 @@
             sends[1][at + i] = jnp.where(odd, high, low)
 
 
-def solve(inv, cols, starts, done, ready=None):
+def solve(inv, cols, starts, done, ready=None, unroll=False):
     def one(c, carry):
         if ready is not None:
             ready(c)
@@ -206,7 +207,11 @@
             done(s * C + c, row_sums(total[s]))
         return carry
 
-    lax.fori_loop(0, C, one, 0)
+    if unroll:
+        for c in range(C):
+            one(c, 0)
+    else:
+        lax.fori_loop(0, C, one, 0)
 
 
 def edge(first):
@@ -214,21 +219,15 @@
 
 
 def early_body(two_x, phi, basis, inv, cols, gram, loc, inv_kept, *refs):
-    phi_faces, (sems,) = refs[: 1 + two_x], refs[1 + two_x :]
+    phi_faces, (vectors, sems) = refs[: 1 + two_x], refs[1 + two_x :]
+    fetch = pltpu.make_async_copy(basis, vectors, sems.at[C])
+    fetch.start()
 
     def copy(c):
         return pltpu.make_async_copy(inv.at[c], inv_kept.at[c], sems.at[c])
 
     for c in range(C):
         copy(c).start()
-    rows = []
-    for m, n in PAIRS:
-        for s in range(S):
-            rows.append(sum(basis[m, s * C + c] * basis[n, s * C + c] for c in range(C)))
-    rows += [jnp.zeros((8, 128), F32)] * (BASE - len(rows))
-    for g in range(0, BASE, 8):
-        gram[g : g + 8, :] = row_sums(rows[g : g + 8])
-
     x_faces([phi[i] for i in range(K * C)], phi_faces, 0)
 
     def done(i, x):
@@ -241,44 +240,21 @@
         starts = [(EXTENT * c + SIDE, 2 * SIDE * c) for c in range(C)]
         starts += [(EXTENT * c + at, 2 * SIDE * c + SIDE) for c in range(C)]
     solve(inv_kept, cols, starts, done, lambda c: copy(c).wait())
-
-
-def local_body(two_x, inv, cols, early, *refs):
-    phi_faces, (loc, locz, *sends) = refs[: 1 + two_x], refs[1 + two_x :]
-
-    def done(i, x):
-        loc[i] = early[i] + x
-
-    if two_x:
-        starts = [(EXTENT * c, 2 * SIDE * c) for c in range(C)]
-        starts += [(EXTENT * c + 2 * SIDE, 2 * SIDE * c + SIDE) for c in range(C)]
-    else:
-        at = edge(lax.axis_index("gx") == 1)
-        starts = [(EXTENT * c + at, SIDE * c) for c in range(C)]
-    solve(inv, cols, starts, done)
-    locz[...] = across(ends(), loc[...].reshape(S * C * XY, CZ))
-    odd_y = lax.axis_index("gy") % 2 == 1
-    for i in range(S * C // 2):
-        low, high = y_faces(loc[i], loc[S * C // 2 + i])
-        sends[0][i] = jnp.where(odd_y, low, high)
-        sends[1][i] = jnp.where(odd_y, high, low)
-    x_faces([loc[i] for i in range(S * C)], sends[2:], 0)
-    for x, known in zip(sends[2:], phi_faces):
-        x[C:] = known[...]
-
-
-def staggered(coef, group):
-    out = coef
-    for g in range(1, 4):
-        out = jnp.where(group == g, rolled(coef, -4 * g, 1), out)
-    return out
+    fetch.wait()
+    rows = []
+    for m, n in PAIRS:
+        for s in range(S):
+            rows.append(sum(vectors[m, s * C + c] * vectors[n, s * C + c] for c in range(C)))
+    rows += [jnp.zeros((8, 128), F32)] * (BASE - len(rows))
+    for g in range(0, BASE, 8):
+        gram[g : g + 8, :] = row_sums(rows[g : g + 8])
 
 
 def slots(two_x):
     return ["own", "ylo", "yhi"] + (["xlo", "xhi"] if two_x else ["x"]) + ["zlo", "zhi"]
 
 
-def factor_body(two_x, got, locz, factor, out):
+def factor_body(two_x, got, factor, out):
     n = factor.shape[1] // K
     stride = out.shape[0] // n
     sub, lane = iota(0), iota(1)
@@ -315,15 +291,52 @@
     face = (len(names) + 1) // 2
     for t in range(face, stride):
         out[pl.ds(t, n, stride=stride), :] = jnp.zeros((n, 128), F32)
+
+
+def send_ends(two_x, locz, out):
+    face = (len(slots(two_x)) + 1) // 2
+    stride = face + 1
     me, below, above = place()
 
     @pl.when(below)
     def _():
-        out[pl.ds((me - 1) * stride + face, 1), :] = locz[0:1, :]
+        out[pl.ds((me - 1) * stride + face, 1), :] = locz[0:1]
 
     @pl.when(above)
     def _():
-        out[pl.ds((me + 1) * stride + face, 1), :] = locz[1:2, :]
+        out[pl.ds((me + 1) * stride + face, 1), :] = locz[1:2]
+
+
+def local_body(two_x, inv, cols, early, got, factor, *refs):
+    phi_faces, (out, loc, *sends) = refs[: 1 + two_x], refs[1 + two_x :]
+    factor_body(two_x, got, factor, out)
+
+    def done(i, x):
+        loc[i] = early[i] + x
+
+    if two_x:
+        starts = [(EXTENT * c, 2 * SIDE * c) for c in range(C)]
+        starts += [(EXTENT * c + 2 * SIDE, 2 * SIDE * c + SIDE) for c in range(C)]
+    else:
+        at = edge(lax.axis_index("gx") == 1)
+        starts = [(EXTENT * c + at, SIDE * c) for c in range(C)]
+    solve(inv, cols, starts, done, unroll=True)
+    send_ends(two_x, across(ends(), loc[...].reshape(S * C * XY, CZ)), out)
+    odd_y = lax.axis_index("gy") % 2 == 1
+    for i in range(S * C // 2):
+        low, high = y_faces(loc[i], loc[S * C // 2 + i])
+        sends[0][i] = jnp.where(odd_y, low, high)
+        sends[1][i] = jnp.where(odd_y, high, low)
+    x_faces([loc[i] for i in range(S * C)], sends[2:], 0)
+    for x, known in zip(sends[2:], phi_faces):
+        x[C:] = known[...]
+
+
+def staggered(coef, group):
+    out = coef
+    for g in range(1, 4):
+        out = jnp.where(group == g, rolled(coef, -4 * g, 1), out)
+    return out
 
 
 def image_body(two_x, loc, phi, diagonal, couple, basis, gram, coarse, got, *rest):
@@ -568,7 +581,7 @@
         ],
         (in_hbm(vectors), in_hbm(phi)),
         S * C * XY * CZ,
-        in_specs=[pl.BlockSpec(memory_space=pltpu.HBM)] * 2,
+        in_specs=[HBM] * 2,
         scratch=[pltpu.SemaphoreType.DMA((2,))],
     )
     rounded = rounded.reshape(S, C, CX, CY, CZ)
@@ -601,10 +614,10 @@
             functools.partial(early_body, two_x),
             [kept(BASE, 128), kept(S * C, XY, CZ), kept(*inverse.shape, dtype=inverse.dtype)]
             + [kept(K * C // 4, 8, 128)] * (1 + two_x),
-            (phi, vectors, in_hbm(inverse), middle),
+            (phi, in_hbm(vectors), in_hbm(inverse), middle),
             10**10,
-            in_specs=[VMEM, VMEM, pl.BlockSpec(memory_space=pltpu.HBM), VMEM],
-            scratch=[pltpu.SemaphoreType.DMA((C,))],
+            in_specs=[VMEM, HBM, HBM, VMEM],
+            scratch=[pltpu.VMEM(vectors.shape, F32), pltpu.SemaphoreType.DMA((C + 1,))],
         )
         slabs, early = lax.optimization_barrier((slabs, early))
         if two_x:
@@ -630,11 +643,12 @@
     )
     half, quarter = S * C // 2, (K + S) * C // 4
     sends = [shape(half, 8, 128)] * 2 + [shape(quarter, 8, 128)] * (2 if two_x else 1)
-    loc, locz, *sends = call(
+    stride = (len(slots(two_x)) + 1) // 2 + 1
+    shares, loc, *sends = call(
         functools.partial(local_body, two_x),
-        [shape(S * C, XY, CZ), shape(8, 128)] + sends,
-        (inverse, columns, part, *phi_faces),
-        20000 * S * C * XY * ROWS * CZ,
+        [kept(n * stride, 128), shape(S * C, XY, CZ)] + sends,
+        (inverse, columns, part, got, coarse_factor, *phi_faces),
+        2 * S * C * XY * C * SIDE * CZ,
     )
 
     def trade(*sends):
@@ -644,13 +658,6 @@
     def untouched(*sends):
         return list(sends)
 
-    stride = (len(slots(two_x)) + 1) // 2 + 1
-    (shares,) = call(
-        functools.partial(factor_body, two_x),
-        [kept(n * stride, 128)],
-        (got, locz, coarse_factor),
-        4 * S * K * K * n,
-    )
     coarse = exchange(shares)
     faces = lax.cond(always, trade, untouched, *sends)
     pre, image, sent = call(

time: 43.1 us -> 42.7 us (level)
  waiting for transfers between devices: 6.04 us -> 7.36 us
  Pallas kernels: 8.22 us -> 7.16 us
  starting transfers between devices: 16.6 us -> 15.9 us
    all_to_all x2, waiting for transfers between devices: 4.2 us -> 5.3 us  [exchange(): lax.all_to_all(rows[:, None], AXES, 0, 0, tiled=True).reshape(rows.shape)]
    pallas_call x7 -> x6, Pallas kernels: 8.22 us -> 7.16 us  [call(): pl.pallas_call(body, out_shape=tuple(outs), in_specs=in_specs or [VMEM] *...]
    all_to_all x2, starting transfers between devices: 8.2 us -> 7.54 us  [exchange(): lax.all_to_all(rows[:, None], AXES, 0, 0, tiled=True).reshape(rows.shape)]
  transfers between devices with their start and end apart: 8 -> 8, of which waited for: 3 -> 4; matrix products, arithmetic and copies ran while one was open for 1% -> 1% of each run, Pallas kernels for 10% -> 7%
where the time goes in v8:
time: 42.7 us; the launch traced here: 42.4 us
  starting transfers between devices  15.9 us (37%)
  blocking collectives  10 us (23%)
  waiting for transfers between devices  7.36 us (17%)
  Pallas kernels  7.16 us (17%)
  local copies, waits for them, and re-layouts  0.83 us (2%)
  between operations  0.76 us (2%)
    all_to_all x1, blocking collectives, exchange(): lax.all_to_all(rows[:, None], AXES, 0, 0, tiled=True).reshape(rows.shape)  10 us
    all_to_all x2, starting transfers between devices, exchange(): lax.all_to_all(rows[:, None], AXES, 0, 0, tiled=True).reshape(rows.shape)  7.54 us
    pallas_call x6, Pallas kernels, call(): pl.pallas_call(body, out_shape=tuple(outs), in_specs=in_specs or [VMEM] *...  7.16 us
    all_to_all x2, waiting for transfers between devices, exchange(): lax.all_to_all(rows[:, None], AXES, 0, 0, tiled=True).reshape(rows.shape)  5.3 us
    ppermute x2, starting transfers between devices, on_device(): lax.ppermute(x, 'gy', pairs)  3.16 us
    ppermute x1, starting transfers between devices, swap(): return [lax.ppermute(x, axis, pairs) for x, pairs in zip(sides, rounds)]  1.83 us
    ppermute x1, starting transfers between devices, trade(): lax.ppermute(x, 'gx', pairs)  1.83 us
    ppermute x2, waiting for transfers between devices, trade(): lax.ppermute(x, 'gy', pairs)  1.82 us
  transfers between devices with their start and end apart: 8, of which 4 were waited for; matrix products, arithmetic and copies ran while one was open for 1% of the time, Pallas kernels for 7%

profile of v8, /device:TPU:0, one launch (start us, length us, event | category | flops | bytes accessed | tf_op | source)
XLA Modules:
  0.0 42.4 jit_solution(15431130621369284146)
XLA Ops:
  0.6 1.0 %shard_map.104 = (f32[16,8,128]{2,1,0:T(8,128)S(1)}, bf16[16,8,128]{2,1,0:T(8,128)(2,1)S(1)}, f32[64,8,128]{2,1,0:T(8,128)S(1)}, f32[48,8,128]{2,1,0:T(8,128)S(1)}, f32[48,8,128]{2,1,0:T(8,128)S(1)}) custom-call(f32[6,16,8,128]{3,2,1,0:T(8,128)} %bitcast.47, f32[64,8,128]{2,1,0:T(8,128)} %bitcast.55), custom_call_target="tpu_custom_call" | custom-call | flops 16384 | bytes 1409024 | tf_op jit(solution)/shard_map/pallas_call | solution.py:37
  1.7 0.5 %collective-permute-start.4 = (f32[48,8,128]{2,1,0:T(8,128)S(1)}, f32[48,8,128]{2,1,0:T(8,128)S(1)}, u32[]{:S(2)}, u32[]{:S(2)}) collective-permute-start(f32[48,8,128]{2,1,0:T(8,128)S(1)} %get-tuple-element.100), channel_id=1, source_target_pairs={{0,4},{8,12},{4,0},{12,8},{1,5},{9,13},{5,1},{13,9},{2,6},{10,14},... | collective-permute-start | bytes 589832 | tf_op jit(solution)/shard_map/ppermute | solution.py:590
  2.2 2.6 %collective-permute-start.5 = (f32[48,8,128]{2,1,0:T(8,128)S(1)}, f32[48,8,128]{2,1,0:T(8,128)S(1)}, u32[]{:S(2)}, u32[]{:S(2)}) collective-permute-start(f32[48,8,128]{2,1,0:T(8,128)S(1)} %get-tuple-element.101), channel_id=1, source_target_pairs={{4,8},{12,0},{8,4},{0,12},{5,9},{13,1},{9,5},{1,13},{6,10},{14,2},... | collective-permute-start | bytes 589832 | tf_op jit(solution)/shard_map/ppermute | solution.py:590
  4.8 1.0 %shard_map.105 = f32[160,128]{1,0:T(8,128)} custom-call(f32[16,8,128]{2,1,0:T(8,128)S(1)} %get-tuple-element.107.vector, f32[64,8,128]{2,1,0:T(8,128)S(1)} %get-tuple-element.103.phi), custom_call_target="tpu_custom_call" | custom-call | flops 524288 | bytes 409600 | tf_op jit(solution)/shard_map/pallas_call | solution.py:37
  5.8 4.9 %all-to-all-start.1 = ((f32[160,1,128]{2,1,0:T(1,128)}), f32[160,1,128]{2,1,0:T(1,128)S(1)}, u32[]{:S(2)}, u32[]{:S(2)}) async-start(f32[160,1,128]{2,1,0:T(1,128)} %bitcast.17), calls=%async_computation.1 | async-start | bytes 163840 | tf_op jit(solution)/shard_map/all_to_all | solution.py:562
  10.7 0.0 collective-permute-done.4.rest_0_
  10.8 0.0 collective-permute-done.5.rest_1_
  10.8 0.0 copy-start.3
  10.8 4.6 %conditional.3 = (bf16[4,64,128]{2,1,0:T(8,128)(2,1)S(1)}, f32[88,128]{1,0:T(8,128)S(1)}, f32[16,8,128]{2,1,0:T(8,128)S(1)}, bf16[4,8,192,128]{3,2,1,0:T(8,128)(2,1)S(1)}, f32[16,8,128]{2,1,0:T(8,128)S(1)}) conditional(s32[]{:T(128)} %convert_element_type.14, () %tuple.36, (f32[48,8,128]{2,1,0:T(8,128)S(1)}, f32[48,8,128]{2,1,0:T(8,128)S(1)}, ...), branch_computations={%region_0.0_spmd, %region_1.2_spmd} | conditional | flops 10000286720 | bytes 5878173 | solution.py:641
  11.0 1.8 %collective-permute-start.3 = (bf16[4,4,2,6,128]{4,1,3,2,0:T(4,128)(2,1)S(1)}, bf16[4,4,2,6,128]{4,1,3,2,0:T(4,128)(2,1)S(1)}, u32[]{:S(2)}, u32[]{:S(2)}) collective-permute-start(bf16[4,4,2,6,128]{4,1,3,2,0:T(4,128)(2,1)S(1)} %slice_select_fusion), channel_id=1, source_target_pairs={{0,16},{16,0},{1,17},{17,1},{2,18},{18,2},{3,19},{19,3},{4,20},{20... | collective-permute-start | bytes 147464 | tf_op jit(solution)/shard_map/cond/branch_1_fun/ppermute | solution.py:549
  12.9 0.1 pad_maximum_fusion
  13.0 2.0 %branch_1_fun.1 = (f32[88,128]{1,0:T(8,128)S(1)}, f32[16,8,128]{2,1,0:T(8,128)S(1)}, bf16[4,8,192,128]{3,2,1,0:T(8,128)(2,1)S(1)}, f32[16,8,128]{2,1,0:T(8,128)S(1)}) custom-call(f32[64,8,128]{2,1,0:T(8,128)S(1)} %get-tuple-element.51.phi, f32[6,16,8,128]{3,2,1,0:T(8,128)} %get-tuple-element.52.basis, bf16[4,8,192,128]{3,2,1,0:T(8,128)(2,1)} %bitcast.60, ...), custom_call_target="tpu_custom_call" | custom-call | flops 10000000000 | bytes 4108288 | tf_op jit(solution)/shard_map/cond/branch_1_fun/pallas_call | solution.py:37
  15.0 0.2 collective-permute-done.3
  15.3 0.1 maximum_select_fusion
  15.4 0.0 copy-start
  15.4 0.0 copy-start.2
  15.4 0.0 copy-start.5
  15.4 3.1 %all-to-all-done.1 = f32[160,1,128]{2,1,0:T(1,128)S(1)} async-done(((f32[160,1,128]{2,1,0:T(1,128)}), f32[160,1,128]{2,1,0:T(1,128)S(1)}, u32[]{:S(2)}, u32[]{:S(2)}) %all-to-all-start.1) | async-done | bytes 81952 | tf_op jit(solution)/shard_map/all_to_all | solution.py:562
  18.5 0.0 copy-done.3
  18.5 0.0 copy-start.1
  18.5 0.0 copy-start.4
  18.5 1.5 %shard_map.106 = (f32[128,128]{1,0:T(8,128)}, f32[16,8,128]{2,1,0:T(8,128)S(1)}, f32[8,8,128]{2,1,0:T(8,128)S(1)}, f32[8,8,128]{2,1,0:T(8,128)S(1)}, f32[20,8,128]{2,1,0:T(8,128)S(1)}) custom-call(bf16[4,8,192,128]{3,2,1,0:T(8,128)(2,1)S(1)} %get-tuple-element.104.inv, bf16[4,64,128]{2,1,0:T(8,128)(2,1)S(1)} %get-tuple-element.105.cols, ...), custom_call_target="tpu_custom_call" | custom-call | flops 2097152 | bytes 2162688 | tf_op jit(solution)/shard_map/pallas_call | solution.py:37
  20.0 2.6 %all-to-all-start.2 = ((f32[128,1,128]{2,1,0:T(1,128)}), f32[128,1,128]{2,1,0:T(1,128)S(1)}, u32[]{:S(2)}, u32[]{:S(2)}) async-start(f32[128,1,128]{2,1,0:T(1,128)} %bitcast.22), calls=%async_computation.2 | async-start | bytes 131072 | tf_op jit(solution)/shard_map/all_to_all | solution.py:562
  22.6 5.3 %conditional.4 = ((f32[8,8,128]{2,1,0:T(8,128)S(1)}, f32[8,8,128]{2,1,0:T(8,128)S(1)}, f32[20,8,128]{2,1,0:T(8,128)S(1)})) conditional(s32[]{:T(128)} %convert_element_type.14, (f32[8,8,128]{2,1,0:T(8,128)S(1)}, f32[8,8,128]{2,1,0:T(8,128)S(1)}, f32[20,8,128]{2,1,0:T(8,128)S(1)}) %tuple.38, (f32[8,8,128]{2,1,0:T(8,128)S(1)}, ...), branch_computations={%region_2.3_spmd, %region_3.4_spmd} | conditional | bytes 884888 | solution.py:662
  22.6 1.8 %collective-permute-start.2 = (f32[20,8,128]{2,1,0:T(8,128)S(1)}, f32[20,8,128]{2,1,0:T(8,128)S(1)}, u32[]{:S(2)}, u32[]{:S(2)}) collective-permute-start(f32[20,8,128]{2,1,0:T(8,128)S(1)} %get-tuple-element.65), channel_id=1, source_target_pairs={{0,16},{16,0},{1,17},{17,1},{2,18},{18,2},{3,19},{19,3},{4,20},{20... | collective-permute-start | bytes 245768 | tf_op jit(solution)/shard_map/cond/branch_1_fun/ppermute | solution.py:655
  24.5 0.0 collective-permute-start
  24.5 1.6 %collective-permute-start.1 = (f32[8,8,128]{2,1,0:T(8,128)S(1)}, f32[8,8,128]{2,1,0:T(8,128)S(1)}, u32[]{:S(2)}, u32[]{:S(2)}) collective-permute-start(f32[8,8,128]{2,1,0:T(8,128)S(1)} %get-tuple-element.64), channel_id=1, source_target_pairs={{4,8},{12,0},{8,4},{0,12},{5,9},{13,1},{9,5},{1,13},{6,10},{14,2},... | collective-permute-start | bytes 98312 | tf_op jit(solution)/shard_map/cond/branch_1_fun/ppermute | solution.py:656
  26.0 0.0 collective-permute-done
  26.0 1.8 %collective-permute-done.1 = f32[8,8,128]{2,1,0:T(8,128)S(1)} collective-permute-done((f32[8,8,128]{2,1,0:T(8,128)S(1)}, f32[8,8,128]{2,1,0:T(8,128)S(1)}, u32[]{:S(2)}, u32[]{:S(2)}) %collective-permute-start.1) | collective-permute-done | bytes 32800 | tf_op jit(solution)/shard_map/cond/branch_1_fun/ppermute | solution.py:656
  27.9 0.0 collective-permute-done.2
  27.9 2.2 %all-to-all-done.2 = f32[128,1,128]{2,1,0:T(1,128)S(1)} async-done(((f32[128,1,128]{2,1,0:T(1,128)}), f32[128,1,128]{2,1,0:T(1,128)S(1)}, u32[]{:S(2)}, u32[]{:S(2)}) %all-to-all-start.2) | async-done | bytes 65568 | tf_op jit(solution)/shard_map/all_to_all | solution.py:562
  30.1 0.0 copy-done
  30.1 0.0 copy-done.2
  30.1 0.0 copy-done.5
  30.1 0.9 %shard_map.107 = (f32[16,8,128]{2,1,0:T(8,128)S(1)}, f32[16,8,128]{2,1,0:T(8,128)S(1)}, f32[32,128]{1,0:T(8,128)S(1)}) custom-call(f32[16,8,128]{2,1,0:T(8,128)S(1)} %get-tuple-element.109.loc, f32[64,8,128]{2,1,0:T(8,128)S(1)} %get-tuple-element.103.phi, f32[16,8,128]{2,1,0:T(8,128)S(1)} %bitcast.43, f32[24,8,128]{2,1,0:T(8,128)S(1)} %bitcast.42, ...), custom_call_target="tpu_custom_call" | custom-call | flops 1310720 | bytes 1765376 | tf_op jit(solution)/shard_map/pallas_call | solution.py:37
  31.0 10.0 %all_to_all.20 = f32[32,1,128]{2,1,0:T(1,128)S(1)} all-to-all(f32[32,1,128]{2,1,0:T(1,128)S(1)} %bitcast.46), channel_id=1, replica_groups=mesh['gx'=2,'gy'=4,'gz'=4] {'gx','gy','gz'}, dimensions={0} | all-to-all | bytes 32768 | tf_op jit(solution)/shard_map/all_to_all | solution.py:562
  41.0 0.0 copy-done.1
  41.0 0.0 copy-done.4
  41.0 0.7 %shard_map.108 = (f32[16,8,128]{2,1,0:T(8,128)S(1)}, f32[4,7]{1,0:T(4,128)S(1)}, s32[1]{0:T(128)S(4)}) custom-call(f32[32,128]{1,0:T(8,128)S(1)} %bitcast.44, f32[16,8,128]{2,1,0:T(8,128)S(1)} %get-tuple-element.119.image, f32[6,16,8,128]{3,2,1,0:T(8,128)S(1)} %bitcast.50, bf16[3,128,128]{2,1,0:T(8,128)(2,1)S(1)} %copy-done.1, f32[8,128]{1,0:T(8,128)S(1)} %copy-done.4), custom_call_target="tpu_custom_call" | custom-call | flops 262144 | bytes 643188 | tf_op jit(solution)/shard_map/pallas_call | solution.py:37
  41.8 0.0 copy-start.6
  41.8 0.0 copy-start.7
  41.8 0.6 %copy.83 = f32[4,4,4,2,128]{4,3,2,1,0:T(2,128)} copy(f32[4,4,4,2,128]{4,3,2,1,0:T(2,128)S(1)} %bitcast.37) | data formatting | bytes 131072
  42.4 0.0 copy-done.6
  42.4 0.0 copy-done.7
  (14 shorter events, 0.2 us)
Async XLA Ops:
  1.7 9.1 %collective-permute-start.4 = (f32[48,8,128]{2,1,0:T(8,128)S(1)}, f32[48,8,128]{2,1,0:T(8,128)S(1)}, u32[]{:S(2)}, u32[]{:S(2)}) collective-permute-start(f32[48,8,128]{2,1,0:T(8,128)S(1)} %get-tuple-element.100), channel_id=1, source_target_pairs={{0,4},{8,12},{4,0},{12,8},{1,5},{9,13},{5,1},{13,9},{2,6},{10,14},... | collective-permute-start | bytes 589832 | tf_op jit(solution)/shard_map/ppermute | solution.py:590
  2.2 8.6 %collective-permute-start.5 = (f32[48,8,128]{2,1,0:T(8,128)S(1)}, f32[48,8,128]{2,1,0:T(8,128)S(1)}, u32[]{:S(2)}, u32[]{:S(2)}) collective-permute-start(f32[48,8,128]{2,1,0:T(8,128)S(1)} %get-tuple-element.101), channel_id=1, source_target_pairs={{4,8},{12,0},{8,4},{0,12},{5,9},{13,1},{9,5},{1,13},{6,10},{14,2},... | collective-permute-start | bytes 589832 | tf_op jit(solution)/shard_map/ppermute | solution.py:590
  5.8 12.6 %all-to-all-start.1 = ((f32[160,1,128]{2,1,0:T(1,128)}), f32[160,1,128]{2,1,0:T(1,128)S(1)}, u32[]{:S(2)}, u32[]{:S(2)}) async-start(f32[160,1,128]{2,1,0:T(1,128)} %bitcast.17), calls=%async_computation.1 | async-start | bytes 163840 | tf_op jit(solution)/shard_map/all_to_all | solution.py:562
  10.8 7.7 %copy-start.3 = (f32[16,512]{1,0:T(8,128)S(1)}, f32[16,512]{1,0:T(8,128)}, u32[]{:S(2)}) copy-start(f32[16,512]{1,0:T(8,128)} %factor.1) | copy-start | bytes 98308
  11.0 4.3 %collective-permute-start.3 = (bf16[4,4,2,6,128]{4,1,3,2,0:T(4,128)(2,1)S(1)}, bf16[4,4,2,6,128]{4,1,3,2,0:T(4,128)(2,1)S(1)}, u32[]{:S(2)}, u32[]{:S(2)}) collective-permute-start(bf16[4,4,2,6,128]{4,1,3,2,0:T(4,128)(2,1)S(1)} %slice_select_fusion), channel_id=1, source_target_pairs={{0,16},{16,0},{1,17},{17,1},{2,18},{18,2},{3,19},{19,3},{4,20},{20... | collective-permute-start | bytes 147464 | tf_op jit(solution)/shard_map/cond/branch_1_fun/ppermute | solution.py:549
  15.4 14.8 %copy-start = (f32[6,4,4,2,128]{4,3,2,1,0:T(2,128)S(1)}, f32[6,4,4,2,128]{4,3,2,1,0:T(2,128)}, u32[]{:S(2)}) copy-start(f32[6,4,4,2,128]{4,3,2,1,0:T(2,128)} %param.19) | copy-start | bytes 294916
  15.4 14.7 %copy-start.2 = (f32[4,4,4,2,128]{4,3,2,1,0:T(2,128)S(1)}, f32[4,4,4,2,128]{4,3,2,1,0:T(2,128)}, u32[]{:S(2)}) copy-start(f32[4,4,4,2,128]{4,3,2,1,0:T(2,128)} %param.18) | copy-start | bytes 196612
  15.4 14.7 %copy-start.5 = (f32[6,4,4,4,2,128]{5,4,3,2,1,0:T(2,128)S(1)}, f32[6,4,4,4,2,128]{5,4,3,2,1,0:T(2,128)}, u32[]{:S(2)}) copy-start(f32[6,4,4,4,2,128]{5,4,3,2,1,0:T(2,128)} %param.16) | copy-start | bytes 1179652
  18.5 22.6 %copy-start.1 = (bf16[3,128,128]{2,1,0:T(8,128)(2,1)S(1)}, bf16[3,128,128]{2,1,0:T(8,128)(2,1)}, u32[]{:S(2)}) copy-start(bf16[3,128,128]{2,1,0:T(8,128)(2,1)} %constant.92.clone.maps) | copy-start | bytes 294916
  18.5 22.6 %copy-start.4 = (f32[8,128]{1,0:T(8,128)S(1)}, f32[8,128]{1,0:T(8,128)}, u32[]{:S(2)}) copy-start(f32[8,128]{1,0:T(8,128)} %constant.93.clone.fixed) | copy-start | bytes 12292
  20.0 10.1 %all-to-all-start.2 = ((f32[128,1,128]{2,1,0:T(1,128)}), f32[128,1,128]{2,1,0:T(1,128)S(1)}, u32[]{:S(2)}, u32[]{:S(2)}) async-start(f32[128,1,128]{2,1,0:T(1,128)} %bitcast.22), calls=%async_computation.2 | async-start | bytes 131072 | tf_op jit(solution)/shard_map/all_to_all | solution.py:562
  22.6 5.2 %collective-permute-start.2 = (f32[20,8,128]{2,1,0:T(8,128)S(1)}, f32[20,8,128]{2,1,0:T(8,128)S(1)}, u32[]{:S(2)}, u32[]{:S(2)}) collective-permute-start(f32[20,8,128]{2,1,0:T(8,128)S(1)} %get-tuple-element.65), channel_id=1, source_target_pairs={{0,16},{16,0},{1,17},{17,1},{2,18},{18,2},{3,19},{19,3},{4,20},{20... | collective-permute-start | bytes 245768 | tf_op jit(solution)/shard_map/cond/branch_1_fun/ppermute | solution.py:655
  24.5 1.6 %collective-permute-start = (f32[8,8,128]{2,1,0:T(8,128)S(1)}, f32[8,8,128]{2,1,0:T(8,128)S(1)}, u32[]{:S(2)}, u32[]{:S(2)}) collective-permute-start(f32[8,8,128]{2,1,0:T(8,128)S(1)} %get-tuple-element.63), channel_id=1, source_target_pairs={{0,4},{8,12},{4,0},{12,8},{1,5},{9,13},{5,1},{13,9},{2,6},{10,14},... | collective-permute-start | bytes 98312 | tf_op jit(solution)/shard_map/cond/branch_1_fun/ppermute | solution.py:656
  24.5 3.4 %collective-permute-start.1 = (f32[8,8,128]{2,1,0:T(8,128)S(1)}, f32[8,8,128]{2,1,0:T(8,128)S(1)}, u32[]{:S(2)}, u32[]{:S(2)}) collective-permute-start(f32[8,8,128]{2,1,0:T(8,128)S(1)} %get-tuple-element.64), channel_id=1, source_target_pairs={{4,8},{12,0},{8,4},{0,12},{5,9},{13,1},{9,5},{1,13},{6,10},{14,2},... | collective-permute-start | bytes 98312 | tf_op jit(solution)/shard_map/cond/branch_1_fun/ppermute | solution.py:656
  41.8 0.7 %copy-start.6 = (f32[4,7]{1,0:T(4,128)}, f32[4,7]{1,0:T(4,128)S(1)}, u32[]{:S(2)}) copy-start(f32[4,7]{1,0:T(4,128)S(1)} %get-tuple-element.160) | copy-start | bytes 340
  41.8 0.7 %copy-start.7 = (f32[16,8,128]{2,1,0:T(8,128)}, f32[16,8,128]{2,1,0:T(8,128)S(1)}, u32[]{:S(2)}) copy-start(f32[16,8,128]{2,1,0:T(8,128)S(1)} %get-tuple-element.125) | copy-start | bytes 196612

commit v9 on v8

--- a/solution.py
+++ b/solution.py
@@ -309,7 +309,6 @@
 
 def local_body(two_x, inv, cols, early, got, factor, *refs):
     phi_faces, (out, loc, *sends) = refs[: 1 + two_x], refs[1 + two_x :]
-    factor_body(two_x, got, factor, out)
 
     def done(i, x):
         loc[i] = early[i] + x
@@ -321,6 +320,7 @@
         at = edge(lax.axis_index("gx") == 1)
         starts = [(EXTENT * c + at, SIDE * c) for c in range(C)]
     solve(inv, cols, starts, done, unroll=True)
+    factor_body(two_x, got, factor, out)
     send_ends(two_x, across(ends(), loc[...].reshape(S * C * XY, CZ)), out)
     odd_y = lax.axis_index("gy") % 2 == 1
     for i in range(S * C // 2):
@@ -502,7 +502,9 @@
         fixed[0, lane] = fixed[1, lane] = fixed[2, lane] = 1
         for i in range(M + 1):
             out[BASE + 4 * i + s, i] = 1
-    return np.stack([first, second, out]).astype(jnp.bfloat16), fixed
+    lanes = np.arange(128)
+    fold = (lanes[:, None] % 4 == lanes[None, :] % 4).astype(np.float32)
+    return np.stack([first, second, out, fold]).astype(jnp.bfloat16), fixed
 
 
 def finish_body(unknowns, got, image, basis, maps, fixed, krylov, hessenberg, flag):
@@ -516,12 +518,10 @@
 
     terms = total * all_rows(fixed, 2)
     terms = terms * (times(h, maps[0]) + all_rows(fixed, 0)) * (times(h, maps[1]) + all_rows(fixed, 1))
-    size = jnp.abs(terms)
-    for shift in (4, 8, 16, 32, 64):
-        terms = terms + rolled(terms, shift, 1)
-        size = size + rolled(size, shift, 1)
-    norm = jnp.sqrt(jnp.maximum(terms, 0.0) / unknowns + epsilon)
-    scale = 1.0 / norm
+    sums = times(jnp.where(sub < 4, terms, jnp.abs(terms)), maps[3])
+    terms, size = all_rows(sums, 0), all_rows(sums, 4)
+    square = jnp.maximum(terms, 0.0) / unknowns + epsilon
+    scale, norm = lax.rsqrt(square), jnp.sqrt(square)
     flag[0] = jnp.max(jnp.where(terms < CANCEL * size, 1, 0))
     for s in range(S):
         w = [splat(h, BASE + 4 * m + s) for m in range(M)]

time: 42.7 us -> 42.5 us (level)
  no operation moved by 1% of the time
where the time goes in v9:
time: 42.5 us; the launch traced here: 42.2 us
  starting transfers between devices  15.9 us (37%)
  blocking collectives  10 us (24%)
  waiting for transfers between devices  7.36 us (17%)
  Pallas kernels  6.94 us (16%)
  local copies, waits for them, and re-layouts  0.83 us (2%)
  between operations  0.76 us (2%)
    all_to_all x1, blocking collectives, exchange(): lax.all_to_all(rows[:, None], AXES, 0, 0, tiled=True).reshape(rows.shape)  10 us
    all_to_all x2, starting transfers between devices, exchange(): lax.all_to_all(rows[:, None], AXES, 0, 0, tiled=True).reshape(rows.shape)  7.54 us
    pallas_call x6, Pallas kernels, call(): pl.pallas_call(body, out_shape=tuple(outs), in_specs=in_specs or [VMEM] *...  6.94 us
    all_to_all x2, waiting for transfers between devices, exchange(): lax.all_to_all(rows[:, None], AXES, 0, 0, tiled=True).reshape(rows.shape)  5.3 us
    ppermute x2, starting transfers between devices, on_device(): lax.ppermute(x, 'gy', pairs)  3.16 us
    ppermute x1, starting transfers between devices, swap(): return [lax.ppermute(x, axis, pairs) for x, pairs in zip(sides, rounds)]  1.83 us
    ppermute x1, starting transfers between devices, trade(): lax.ppermute(x, 'gx', pairs)  1.83 us
    ppermute x2, waiting for transfers between devices, trade(): lax.ppermute(x, 'gy', pairs)  1.82 us
  transfers between devices with their start and end apart: 8, of which 4 were waited for; matrix products, arithmetic and copies ran while one was open for 1% of the time, Pallas kernels for 7%

profile of v9, /device:TPU:0, one launch (start us, length us, event | category | flops | bytes accessed | tf_op | source)
XLA Modules:
  0.0 42.2 jit_solution(15624062872931032834)
XLA Ops:
  0.6 1.0 %shard_map.104 = (f32[16,8,128]{2,1,0:T(8,128)S(1)}, bf16[16,8,128]{2,1,0:T(8,128)(2,1)S(1)}, f32[64,8,128]{2,1,0:T(8,128)S(1)}, f32[48,8,128]{2,1,0:T(8,128)S(1)}, f32[48,8,128]{2,1,0:T(8,128)S(1)}) custom-call(f32[6,16,8,128]{3,2,1,0:T(8,128)} %bitcast.47, f32[64,8,128]{2,1,0:T(8,128)} %bitcast.55), custom_call_target="tpu_custom_call" | custom-call | flops 16384 | bytes 1409024 | tf_op jit(solution)/shard_map/pallas_call | solution.py:37
  1.7 0.5 %collective-permute-start.4 = (f32[48,8,128]{2,1,0:T(8,128)S(1)}, f32[48,8,128]{2,1,0:T(8,128)S(1)}, u32[]{:S(2)}, u32[]{:S(2)}) collective-permute-start(f32[48,8,128]{2,1,0:T(8,128)S(1)} %get-tuple-element.100), channel_id=1, source_target_pairs={{0,4},{8,12},{4,0},{12,8},{1,5},{9,13},{5,1},{13,9},{2,6},{10,14},... | collective-permute-start | bytes 589832 | tf_op jit(solution)/shard_map/ppermute | solution.py:590
  2.2 2.6 %collective-permute-start.5 = (f32[48,8,128]{2,1,0:T(8,128)S(1)}, f32[48,8,128]{2,1,0:T(8,128)S(1)}, u32[]{:S(2)}, u32[]{:S(2)}) collective-permute-start(f32[48,8,128]{2,1,0:T(8,128)S(1)} %get-tuple-element.101), channel_id=1, source_target_pairs={{4,8},{12,0},{8,4},{0,12},{5,9},{13,1},{9,5},{1,13},{6,10},{14,2},... | collective-permute-start | bytes 589832 | tf_op jit(solution)/shard_map/ppermute | solution.py:590
  4.8 1.0 %shard_map.105 = f32[160,128]{1,0:T(8,128)} custom-call(f32[16,8,128]{2,1,0:T(8,128)S(1)} %get-tuple-element.107.vector, f32[64,8,128]{2,1,0:T(8,128)S(1)} %get-tuple-element.103.phi), custom_call_target="tpu_custom_call" | custom-call | flops 524288 | bytes 409600 | tf_op jit(solution)/shard_map/pallas_call | solution.py:37
  5.8 4.9 %all-to-all-start.1 = ((f32[160,1,128]{2,1,0:T(1,128)}), f32[160,1,128]{2,1,0:T(1,128)S(1)}, u32[]{:S(2)}, u32[]{:S(2)}) async-start(f32[160,1,128]{2,1,0:T(1,128)} %bitcast.17), calls=%async_computation.1 | async-start | bytes 163840 | tf_op jit(solution)/shard_map/all_to_all | solution.py:562
  10.7 0.0 collective-permute-done.4.rest_0_
  10.8 0.0 collective-permute-done.5.rest_1_
  10.8 0.0 copy-start.3
  10.8 4.6 %conditional.3 = (bf16[4,64,128]{2,1,0:T(8,128)(2,1)S(1)}, f32[88,128]{1,0:T(8,128)S(1)}, f32[16,8,128]{2,1,0:T(8,128)S(1)}, bf16[4,8,192,128]{3,2,1,0:T(8,128)(2,1)S(1)}, f32[16,8,128]{2,1,0:T(8,128)S(1)}) conditional(s32[]{:T(128)} %convert_element_type.14, () %tuple.36, (f32[48,8,128]{2,1,0:T(8,128)S(1)}, f32[48,8,128]{2,1,0:T(8,128)S(1)}, ...), branch_computations={%region_0.0_spmd, %region_1.2_spmd} | conditional | flops 10000286720 | bytes 5878173 | solution.py:641
  11.0 1.8 %collective-permute-start.3 = (bf16[4,4,2,6,128]{4,1,3,2,0:T(4,128)(2,1)S(1)}, bf16[4,4,2,6,128]{4,1,3,2,0:T(4,128)(2,1)S(1)}, u32[]{:S(2)}, u32[]{:S(2)}) collective-permute-start(bf16[4,4,2,6,128]{4,1,3,2,0:T(4,128)(2,1)S(1)} %slice_select_fusion), channel_id=1, source_target_pairs={{0,16},{16,0},{1,17},{17,1},{2,18},{18,2},{3,19},{19,3},{4,20},{20... | collective-permute-start | bytes 147464 | tf_op jit(solution)/shard_map/cond/branch_1_fun/ppermute | solution.py:549
  12.9 0.1 pad_maximum_fusion
  13.0 2.0 %branch_1_fun.1 = (f32[88,128]{1,0:T(8,128)S(1)}, f32[16,8,128]{2,1,0:T(8,128)S(1)}, bf16[4,8,192,128]{3,2,1,0:T(8,128)(2,1)S(1)}, f32[16,8,128]{2,1,0:T(8,128)S(1)}) custom-call(f32[64,8,128]{2,1,0:T(8,128)S(1)} %get-tuple-element.51.phi, f32[6,16,8,128]{3,2,1,0:T(8,128)} %get-tuple-element.52.basis, bf16[4,8,192,128]{3,2,1,0:T(8,128)(2,1)} %bitcast.60, ...), custom_call_target="tpu_custom_call" | custom-call | flops 10000000000 | bytes 4108288 | tf_op jit(solution)/shard_map/cond/branch_1_fun/pallas_call | solution.py:37
  15.0 0.2 collective-permute-done.3
  15.3 0.1 maximum_select_fusion
  15.4 0.0 copy-start.1
  15.4 0.0 copy-start.2
  15.4 0.0 copy-start.5
  15.4 3.1 %all-to-all-done.1 = f32[160,1,128]{2,1,0:T(1,128)S(1)} async-done(((f32[160,1,128]{2,1,0:T(1,128)}), f32[160,1,128]{2,1,0:T(1,128)S(1)}, u32[]{:S(2)}, u32[]{:S(2)}) %all-to-all-start.1) | async-done | bytes 81952 | tf_op jit(solution)/shard_map/all_to_all | solution.py:562
  18.5 0.0 copy-done.3
  18.5 0.0 copy-start
  18.5 0.0 copy-start.4
  18.5 1.5 %shard_map.106 = (f32[128,128]{1,0:T(8,128)}, f32[16,8,128]{2,1,0:T(8,128)S(1)}, f32[8,8,128]{2,1,0:T(8,128)S(1)}, f32[8,8,128]{2,1,0:T(8,128)S(1)}, f32[20,8,128]{2,1,0:T(8,128)S(1)}) custom-call(bf16[4,8,192,128]{3,2,1,0:T(8,128)(2,1)S(1)} %get-tuple-element.104.inv, bf16[4,64,128]{2,1,0:T(8,128)(2,1)S(1)} %get-tuple-element.105.cols, ...), custom_call_target="tpu_custom_call" | custom-call | flops 2097152 | bytes 2162688 | tf_op jit(solution)/shard_map/pallas_call | solution.py:37
  20.0 2.6 %all-to-all-start.2 = ((f32[128,1,128]{2,1,0:T(1,128)}), f32[128,1,128]{2,1,0:T(1,128)S(1)}, u32[]{:S(2)}, u32[]{:S(2)}) async-start(f32[128,1,128]{2,1,0:T(1,128)} %bitcast.22), calls=%async_computation.2 | async-start | bytes 131072 | tf_op jit(solution)/shard_map/all_to_all | solution.py:562
  22.6 5.3 %conditional.4 = ((f32[8,8,128]{2,1,0:T(8,128)S(1)}, f32[8,8,128]{2,1,0:T(8,128)S(1)}, f32[20,8,128]{2,1,0:T(8,128)S(1)})) conditional(s32[]{:T(128)} %convert_element_type.14, (f32[8,8,128]{2,1,0:T(8,128)S(1)}, f32[8,8,128]{2,1,0:T(8,128)S(1)}, f32[20,8,128]{2,1,0:T(8,128)S(1)}) %tuple.38, (f32[8,8,128]{2,1,0:T(8,128)S(1)}, ...), branch_computations={%region_2.3_spmd, %region_3.4_spmd} | conditional | bytes 884888 | solution.py:662
  22.6 1.8 %collective-permute-start.2 = (f32[20,8,128]{2,1,0:T(8,128)S(1)}, f32[20,8,128]{2,1,0:T(8,128)S(1)}, u32[]{:S(2)}, u32[]{:S(2)}) collective-permute-start(f32[20,8,128]{2,1,0:T(8,128)S(1)} %get-tuple-element.65), channel_id=1, source_target_pairs={{0,16},{16,0},{1,17},{17,1},{2,18},{18,2},{3,19},{19,3},{4,20},{20... | collective-permute-start | bytes 245768 | tf_op jit(solution)/shard_map/cond/branch_1_fun/ppermute | solution.py:655
  24.5 0.0 collective-permute-start
  24.5 1.6 %collective-permute-start.1 = (f32[8,8,128]{2,1,0:T(8,128)S(1)}, f32[8,8,128]{2,1,0:T(8,128)S(1)}, u32[]{:S(2)}, u32[]{:S(2)}) collective-permute-start(f32[8,8,128]{2,1,0:T(8,128)S(1)} %get-tuple-element.64), channel_id=1, source_target_pairs={{4,8},{12,0},{8,4},{0,12},{5,9},{13,1},{9,5},{1,13},{6,10},{14,2},... | collective-permute-start | bytes 98312 | tf_op jit(solution)/shard_map/cond/branch_1_fun/ppermute | solution.py:656
  26.0 0.0 collective-permute-done
  26.0 1.8 %collective-permute-done.1 = f32[8,8,128]{2,1,0:T(8,128)S(1)} collective-permute-done((f32[8,8,128]{2,1,0:T(8,128)S(1)}, f32[8,8,128]{2,1,0:T(8,128)S(1)}, u32[]{:S(2)}, u32[]{:S(2)}) %collective-permute-start.1) | collective-permute-done | bytes 32800 | tf_op jit(solution)/shard_map/cond/branch_1_fun/ppermute | solution.py:656
  27.9 0.0 collective-permute-done.2
  27.9 2.2 %all-to-all-done.2 = f32[128,1,128]{2,1,0:T(1,128)S(1)} async-done(((f32[128,1,128]{2,1,0:T(1,128)}), f32[128,1,128]{2,1,0:T(1,128)S(1)}, u32[]{:S(2)}, u32[]{:S(2)}) %all-to-all-start.2) | async-done | bytes 65568 | tf_op jit(solution)/shard_map/all_to_all | solution.py:562
  30.1 0.0 copy-done.1
  30.1 0.0 copy-done.2
  30.1 0.0 copy-done.5
  30.1 0.9 %shard_map.107 = (f32[16,8,128]{2,1,0:T(8,128)S(1)}, f32[16,8,128]{2,1,0:T(8,128)S(1)}, f32[32,128]{1,0:T(8,128)S(1)}) custom-call(f32[16,8,128]{2,1,0:T(8,128)S(1)} %get-tuple-element.109.loc, f32[64,8,128]{2,1,0:T(8,128)S(1)} %get-tuple-element.103.phi, f32[16,8,128]{2,1,0:T(8,128)S(1)} %bitcast.43, f32[24,8,128]{2,1,0:T(8,128)S(1)} %bitcast.42, ...), custom_call_target="tpu_custom_call" | custom-call | flops 1310720 | bytes 1765376 | tf_op jit(solution)/shard_map/pallas_call | solution.py:37
  31.0 10.0 %all_to_all.20 = f32[32,1,128]{2,1,0:T(1,128)S(1)} all-to-all(f32[32,1,128]{2,1,0:T(1,128)S(1)} %bitcast.46), channel_id=1, replica_groups=mesh['gx'=2,'gy'=4,'gz'=4] {'gx','gy','gz'}, dimensions={0} | all-to-all | bytes 32768 | tf_op jit(solution)/shard_map/all_to_all | solution.py:562
  41.0 0.0 copy-done
  41.0 0.0 copy-done.4
  41.0 0.5 %shard_map.108 = (f32[16,8,128]{2,1,0:T(8,128)S(1)}, f32[4,7]{1,0:T(4,128)S(1)}, s32[1]{0:T(128)S(4)}) custom-call(f32[32,128]{1,0:T(8,128)S(1)} %bitcast.44, f32[16,8,128]{2,1,0:T(8,128)S(1)} %get-tuple-element.119.image, f32[6,16,8,128]{3,2,1,0:T(8,128)S(1)} %bitcast.50, bf16[4,128,128]{2,1,0:T(8,128)(2,1)S(1)} %copy-done, f32[8,128]{1,0:T(8,128)S(1)} %copy-done.4), custom_call_target="tpu_custom_call" | custom-call | flops 262144 | bytes 675956 | tf_op jit(solution)/shard_map/pallas_call | solution.py:37
  41.5 0.0 copy-start.6
  41.5 0.0 copy-start.7
  41.6 0.6 %copy.83 = f32[4,4,4,2,128]{4,3,2,1,0:T(2,128)} copy(f32[4,4,4,2,128]{4,3,2,1,0:T(2,128)S(1)} %bitcast.37) | data formatting | bytes 131072
  42.2 0.0 copy-done.6
  42.2 0.0 copy-done.7
  (14 shorter events, 0.2 us)
Async XLA Ops:
  1.7 9.1 %collective-permute-start.4 = (f32[48,8,128]{2,1,0:T(8,128)S(1)}, f32[48,8,128]{2,1,0:T(8,128)S(1)}, u32[]{:S(2)}, u32[]{:S(2)}) collective-permute-start(f32[48,8,128]{2,1,0:T(8,128)S(1)} %get-tuple-element.100), channel_id=1, source_target_pairs={{0,4},{8,12},{4,0},{12,8},{1,5},{9,13},{5,1},{13,9},{2,6},{10,14},... | collective-permute-start | bytes 589832 | tf_op jit(solution)/shard_map/ppermute | solution.py:590
  2.2 8.6 %collective-permute-start.5 = (f32[48,8,128]{2,1,0:T(8,128)S(1)}, f32[48,8,128]{2,1,0:T(8,128)S(1)}, u32[]{:S(2)}, u32[]{:S(2)}) collective-permute-start(f32[48,8,128]{2,1,0:T(8,128)S(1)} %get-tuple-element.101), channel_id=1, source_target_pairs={{4,8},{12,0},{8,4},{0,12},{5,9},{13,1},{9,5},{1,13},{6,10},{14,2},... | collective-permute-start | bytes 589832 | tf_op jit(solution)/shard_map/ppermute | solution.py:590
  5.8 12.6 %all-to-all-start.1 = ((f32[160,1,128]{2,1,0:T(1,128)}), f32[160,1,128]{2,1,0:T(1,128)S(1)}, u32[]{:S(2)}, u32[]{:S(2)}) async-start(f32[160,1,128]{2,1,0:T(1,128)} %bitcast.17), calls=%async_computation.1 | async-start | bytes 163840 | tf_op jit(solution)/shard_map/all_to_all | solution.py:562
  10.8 7.7 %copy-start.3 = (f32[16,512]{1,0:T(8,128)S(1)}, f32[16,512]{1,0:T(8,128)}, u32[]{:S(2)}) copy-start(f32[16,512]{1,0:T(8,128)} %factor.1) | copy-start | bytes 98308
  11.0 4.3 %collective-permute-start.3 = (bf16[4,4,2,6,128]{4,1,3,2,0:T(4,128)(2,1)S(1)}, bf16[4,4,2,6,128]{4,1,3,2,0:T(4,128)(2,1)S(1)}, u32[]{:S(2)}, u32[]{:S(2)}) collective-permute-start(bf16[4,4,2,6,128]{4,1,3,2,0:T(4,128)(2,1)S(1)} %slice_select_fusion), channel_id=1, source_target_pairs={{0,16},{16,0},{1,17},{17,1},{2,18},{18,2},{3,19},{19,3},{4,20},{20... | collective-permute-start | bytes 147464 | tf_op jit(solution)/shard_map/cond/branch_1_fun/ppermute | solution.py:549
  15.4 14.8 %copy-start.1 = (f32[6,4,4,2,128]{4,3,2,1,0:T(2,128)S(1)}, f32[6,4,4,2,128]{4,3,2,1,0:T(2,128)}, u32[]{:S(2)}) copy-start(f32[6,4,4,2,128]{4,3,2,1,0:T(2,128)} %param.19) | copy-start | bytes 294916
  15.4 14.7 %copy-start.2 = (f32[4,4,4,2,128]{4,3,2,1,0:T(2,128)S(1)}, f32[4,4,4,2,128]{4,3,2,1,0:T(2,128)}, u32[]{:S(2)}) copy-start(f32[4,4,4,2,128]{4,3,2,1,0:T(2,128)} %param.18) | copy-start | bytes 196612
  15.4 14.7 %copy-start.5 = (f32[6,4,4,4,2,128]{5,4,3,2,1,0:T(2,128)S(1)}, f32[6,4,4,4,2,128]{5,4,3,2,1,0:T(2,128)}, u32[]{:S(2)}) copy-start(f32[6,4,4,4,2,128]{5,4,3,2,1,0:T(2,128)} %param.16) | copy-start | bytes 1179652
  18.5 22.6 %copy-start = (bf16[4,128,128]{2,1,0:T(8,128)(2,1)S(1)}, bf16[4,128,128]{2,1,0:T(8,128)(2,1)}, u32[]{:S(2)}) copy-start(bf16[4,128,128]{2,1,0:T(8,128)(2,1)} %constant.92.clone.maps) | copy-start | bytes 393220
  18.5 22.6 %copy-start.4 = (f32[8,128]{1,0:T(8,128)S(1)}, f32[8,128]{1,0:T(8,128)}, u32[]{:S(2)}) copy-start(f32[8,128]{1,0:T(8,128)} %constant.93.clone.fixed) | copy-start | bytes 12292
  20.0 10.1 %all-to-all-start.2 = ((f32[128,1,128]{2,1,0:T(1,128)}), f32[128,1,128]{2,1,0:T(1,128)S(1)}, u32[]{:S(2)}, u32[]{:S(2)}) async-start(f32[128,1,128]{2,1,0:T(1,128)} %bitcast.22), calls=%async_computation.2 | async-start | bytes 131072 | tf_op jit(solution)/shard_map/all_to_all | solution.py:562
  22.6 5.2 %collective-permute-start.2 = (f32[20,8,128]{2,1,0:T(8,128)S(1)}, f32[20,8,128]{2,1,0:T(8,128)S(1)}, u32[]{:S(2)}, u32[]{:S(2)}) collective-permute-start(f32[20,8,128]{2,1,0:T(8,128)S(1)} %get-tuple-element.65), channel_id=1, source_target_pairs={{0,16},{16,0},{1,17},{17,1},{2,18},{18,2},{3,19},{19,3},{4,20},{20... | collective-permute-start | bytes 245768 | tf_op jit(solution)/shard_map/cond/branch_1_fun/ppermute | solution.py:655
  24.5 1.6 %collective-permute-start = (f32[8,8,128]{2,1,0:T(8,128)S(1)}, f32[8,8,128]{2,1,0:T(8,128)S(1)}, u32[]{:S(2)}, u32[]{:S(2)}) collective-permute-start(f32[8,8,128]{2,1,0:T(8,128)S(1)} %get-tuple-element.63), channel_id=1, source_target_pairs={{0,4},{8,12},{4,0},{12,8},{1,5},{9,13},{5,1},{13,9},{2,6},{10,14},... | collective-permute-start | bytes 98312 | tf_op jit(solution)/shard_map/cond/branch_1_fun/ppermute | solution.py:656
  24.5 3.4 %collective-permute-start.1 = (f32[8,8,128]{2,1,0:T(8,128)S(1)}, f32[8,8,128]{2,1,0:T(8,128)S(1)}, u32[]{:S(2)}, u32[]{:S(2)}) collective-permute-start(f32[8,8,128]{2,1,0:T(8,128)S(1)} %get-tuple-element.64), channel_id=1, source_target_pairs={{4,8},{12,0},{8,4},{0,12},{5,9},{13,1},{9,5},{1,13},{6,10},{14,2},... | collective-permute-start | bytes 98312 | tf_op jit(solution)/shard_map/cond/branch_1_fun/ppermute | solution.py:656
  41.5 0.7 %copy-start.6 = (f32[4,7]{1,0:T(4,128)}, f32[4,7]{1,0:T(4,128)S(1)}, u32[]{:S(2)}) copy-start(f32[4,7]{1,0:T(4,128)S(1)} %get-tuple-element.160) | copy-start | bytes 340
  41.5 0.7 %copy-start.7 = (f32[16,8,128]{2,1,0:T(8,128)}, f32[16,8,128]{2,1,0:T(8,128)S(1)}, u32[]{:S(2)}) copy-start(f32[16,8,128]{2,1,0:T(8,128)S(1)} %get-tuple-element.125) | copy-start | bytes 196612

commit v10 on v9

--- a/solution.py
+++ b/solution.py
@@ -258,27 +258,28 @@
     n = factor.shape[1] // K
     stride = out.shape[0] // n
     sub, lane = iota(0), iota(1)
-    diag = (lane >> 4) == sub
+    mine = [(lane >> 4) == ((sub + s) & 7) for s in range(S)]
+    columns = []
+    for b in range(n // 8):
+        rows = factor[:, 128 * b : 128 * b + 128]
+        columns.append([rows] + [rolled(rows, K * s, 1) for s in range(1, S)])
     image = [jnp.zeros((K, 128), F32) for _ in range(S)]
     for b in range(n // 8):
         rhs = got[pl.ds(8 * GATHERED * b, 8, stride=GATHERED), :]
-        rows = factor[:, 128 * b : 128 * b + 128]
         rhs = pltpu.roll(rhs, 0, 1, stride=K, stride_axis=0)
         for s in range(S):
-            mine = jnp.where(diag, rolled(rhs, -K * s, 1) if s else rhs, 0.0)
-            image[s] = image[s] + rows * jnp.sum(mine, axis=0, keepdims=True)
+            row = jnp.sum(jnp.where(mine[s], rhs, 0.0), axis=0, keepdims=True)
+            image[s] = image[s] + columns[b][s] * row
     image = [jnp.sum(x, axis=1, keepdims=True) for x in image]
     shares = []
     for b in range(n // 8):
-        rows = factor[:, 128 * b : 128 * b + 128]
         block = jnp.zeros((8, 128), F32)
         for s in range(S):
-            part = jnp.sum(rows * image[s], axis=0, keepdims=True)
-            mine = jnp.where(diag, part, 0.0)
-            block = block + (rolled(mine, K * s, 1) if s else mine)
+            row = jnp.sum(columns[b][s] * image[s], axis=0, keepdims=True)
+            block = jnp.where(mine[s], row, block)
         for bit in (1, 2, 4):
             block = jnp.where((sub & bit) == 0, block, rolled(block, -K * bit, 1))
-        shares.append(block)
+        shares.append(jnp.where(lane < S * K, block, 0.0))
     shares = jnp.concatenate(shares, 0)
     nz = lax.axis_size("gz")
     plane = lax.axis_size("gy") * nz
@@ -391,14 +392,6 @@
     there = jnp.where(lower, below.astype(jnp.int32), above.astype(jnp.int32)) == 1
     columns = jnp.transpose(jnp.where(there, z, 0.0))
 
-    own = coefs("own")
-    p = [loc[i] for i in range(S * C)]
-    for s in range(S):
-        for k in range(K):
-            w = splat(own, s * K + k)
-            for c in range(C):
-                p[s * C + c] = p[s * C + c] + w * phi[k * C + c]
-
     odd_y = lax.axis_index("gy") % 2 == 1
     odd_x = lax.axis_index("gx") % 2 == 1
 
@@ -441,6 +434,14 @@
     else:
         x_first = x_side(faces[2], coefs("x"))
         x_second = x_first
+
+    own = coefs("own")
+    p = [loc[i] for i in range(S * C)]
+    for s in range(S):
+        for k in range(K):
+            w = splat(own, s * K + k)
+            for c in range(C):
+                p[s * C + c] = p[s * C + c] + w * phi[k * C + c]
 
     for s in range(S):
         sides = []

time: 42.5 us -> 42.3 us (level)
  no operation moved by 1% of the time
where the time goes in v10:
time: 42.3 us; the launch traced here: 42.1 us
  starting transfers between devices  15.9 us (38%)
  blocking collectives  10 us (24%)
  waiting for transfers between devices  7.36 us (17%)
  Pallas kernels  6.79 us (16%)
  local copies, waits for them, and re-layouts  0.83 us (2%)
  between operations  0.76 us (2%)
    all_to_all x1, blocking collectives, exchange(): lax.all_to_all(rows[:, None], AXES, 0, 0, tiled=True).reshape(rows.shape)  10 us
    all_to_all x2, starting transfers between devices, exchange(): lax.all_to_all(rows[:, None], AXES, 0, 0, tiled=True).reshape(rows.shape)  7.53 us
    pallas_call x6, Pallas kernels, call(): pl.pallas_call(body, out_shape=tuple(outs), in_specs=in_specs or [VMEM] *...  6.79 us
    all_to_all x2, waiting for transfers between devices, exchange(): lax.all_to_all(rows[:, None], AXES, 0, 0, tiled=True).reshape(rows.shape)  5.3 us
    ppermute x2, starting transfers between devices, on_device(): lax.ppermute(x, 'gy', pairs)  3.16 us
    ppermute x1, starting transfers between devices, swap(): return [lax.ppermute(x, axis, pairs) for x, pairs in zip(sides, rounds)]  1.83 us
    ppermute x1, starting transfers between devices, trade(): lax.ppermute(x, 'gx', pairs)  1.83 us
    ppermute x2, waiting for transfers between devices, trade(): lax.ppermute(x, 'gy', pairs)  1.82 us
  transfers between devices with their start and end apart: 8, of which 4 were waited for; matrix products, arithmetic and copies ran while one was open for 1% of the time, Pallas kernels for 7%

profile of v10, /device:TPU:0, one launch (start us, length us, event | category | flops | bytes accessed | tf_op | source)
XLA Modules:
  0.0 42.1 jit_solution(269756078928716468)
XLA Ops:
  0.6 1.0 %shard_map.104 = (f32[16,8,128]{2,1,0:T(8,128)S(1)}, bf16[16,8,128]{2,1,0:T(8,128)(2,1)S(1)}, f32[64,8,128]{2,1,0:T(8,128)S(1)}, f32[48,8,128]{2,1,0:T(8,128)S(1)}, f32[48,8,128]{2,1,0:T(8,128)S(1)}) custom-call(f32[6,16,8,128]{3,2,1,0:T(8,128)} %bitcast.47, f32[64,8,128]{2,1,0:T(8,128)} %bitcast.55), custom_call_target="tpu_custom_call" | custom-call | flops 16384 | bytes 1409024 | tf_op jit(solution)/shard_map/pallas_call | solution.py:37
  1.7 0.5 %collective-permute-start.4 = (f32[48,8,128]{2,1,0:T(8,128)S(1)}, f32[48,8,128]{2,1,0:T(8,128)S(1)}, u32[]{:S(2)}, u32[]{:S(2)}) collective-permute-start(f32[48,8,128]{2,1,0:T(8,128)S(1)} %get-tuple-element.100), channel_id=1, source_target_pairs={{0,4},{8,12},{4,0},{12,8},{1,5},{9,13},{5,1},{13,9},{2,6},{10,14},... | collective-permute-start | bytes 589832 | tf_op jit(solution)/shard_map/ppermute | solution.py:591
  2.2 2.6 %collective-permute-start.5 = (f32[48,8,128]{2,1,0:T(8,128)S(1)}, f32[48,8,128]{2,1,0:T(8,128)S(1)}, u32[]{:S(2)}, u32[]{:S(2)}) collective-permute-start(f32[48,8,128]{2,1,0:T(8,128)S(1)} %get-tuple-element.101), channel_id=1, source_target_pairs={{4,8},{12,0},{8,4},{0,12},{5,9},{13,1},{9,5},{1,13},{6,10},{14,2},... | collective-permute-start | bytes 589832 | tf_op jit(solution)/shard_map/ppermute | solution.py:591
  4.8 1.0 %shard_map.105 = f32[160,128]{1,0:T(8,128)} custom-call(f32[16,8,128]{2,1,0:T(8,128)S(1)} %get-tuple-element.107.vector, f32[64,8,128]{2,1,0:T(8,128)S(1)} %get-tuple-element.103.phi), custom_call_target="tpu_custom_call" | custom-call | flops 524288 | bytes 409600 | tf_op jit(solution)/shard_map/pallas_call | solution.py:37
  5.8 4.9 %all-to-all-start.1 = ((f32[160,1,128]{2,1,0:T(1,128)}), f32[160,1,128]{2,1,0:T(1,128)S(1)}, u32[]{:S(2)}, u32[]{:S(2)}) async-start(f32[160,1,128]{2,1,0:T(1,128)} %bitcast.17), calls=%async_computation.1 | async-start | bytes 163840 | tf_op jit(solution)/shard_map/all_to_all | solution.py:563
  10.7 0.0 collective-permute-done.4.rest_0_
  10.8 0.0 collective-permute-done.5.rest_1_
  10.8 0.0 copy-start.3
  10.8 4.6 %conditional.3 = (bf16[4,64,128]{2,1,0:T(8,128)(2,1)S(1)}, f32[88,128]{1,0:T(8,128)S(1)}, f32[16,8,128]{2,1,0:T(8,128)S(1)}, bf16[4,8,192,128]{3,2,1,0:T(8,128)(2,1)S(1)}, f32[16,8,128]{2,1,0:T(8,128)S(1)}) conditional(s32[]{:T(128)} %convert_element_type.14, () %tuple.36, (f32[48,8,128]{2,1,0:T(8,128)S(1)}, f32[48,8,128]{2,1,0:T(8,128)S(1)}, ...), branch_computations={%region_0.0_spmd, %region_1.2_spmd} | conditional | flops 10000286720 | bytes 5878173 | solution.py:642
  11.0 1.8 %collective-permute-start.3 = (bf16[4,4,2,6,128]{4,1,3,2,0:T(4,128)(2,1)S(1)}, bf16[4,4,2,6,128]{4,1,3,2,0:T(4,128)(2,1)S(1)}, u32[]{:S(2)}, u32[]{:S(2)}) collective-permute-start(bf16[4,4,2,6,128]{4,1,3,2,0:T(4,128)(2,1)S(1)} %slice_select_fusion), channel_id=1, source_target_pairs={{0,16},{16,0},{1,17},{17,1},{2,18},{18,2},{3,19},{19,3},{4,20},{20... | collective-permute-start | bytes 147464 | tf_op jit(solution)/shard_map/cond/branch_1_fun/ppermute | solution.py:550
  12.9 0.1 pad_maximum_fusion
  13.0 2.0 %branch_1_fun.1 = (f32[88,128]{1,0:T(8,128)S(1)}, f32[16,8,128]{2,1,0:T(8,128)S(1)}, bf16[4,8,192,128]{3,2,1,0:T(8,128)(2,1)S(1)}, f32[16,8,128]{2,1,0:T(8,128)S(1)}) custom-call(f32[64,8,128]{2,1,0:T(8,128)S(1)} %get-tuple-element.51.phi, f32[6,16,8,128]{3,2,1,0:T(8,128)} %get-tuple-element.52.basis, bf16[4,8,192,128]{3,2,1,0:T(8,128)(2,1)} %bitcast.60, ...), custom_call_target="tpu_custom_call" | custom-call | flops 10000000000 | bytes 4108288 | tf_op jit(solution)/shard_map/cond/branch_1_fun/pallas_call | solution.py:37
  15.0 0.2 collective-permute-done.3
  15.3 0.1 maximum_select_fusion
  15.4 0.0 copy-start.1
  15.4 0.0 copy-start.2
  15.4 0.0 copy-start.5
  15.4 3.1 %all-to-all-done.1 = f32[160,1,128]{2,1,0:T(1,128)S(1)} async-done(((f32[160,1,128]{2,1,0:T(1,128)}), f32[160,1,128]{2,1,0:T(1,128)S(1)}, u32[]{:S(2)}, u32[]{:S(2)}) %all-to-all-start.1) | async-done | bytes 81952 | tf_op jit(solution)/shard_map/all_to_all | solution.py:563
  18.5 0.0 copy-done.3
  18.5 0.0 copy-start
  18.5 0.0 copy-start.4
  18.5 1.4 %shard_map.106 = (f32[128,128]{1,0:T(8,128)}, f32[16,8,128]{2,1,0:T(8,128)S(1)}, f32[8,8,128]{2,1,0:T(8,128)S(1)}, f32[8,8,128]{2,1,0:T(8,128)S(1)}, f32[20,8,128]{2,1,0:T(8,128)S(1)}) custom-call(bf16[4,8,192,128]{3,2,1,0:T(8,128)(2,1)S(1)} %get-tuple-element.104.inv, bf16[4,64,128]{2,1,0:T(8,128)(2,1)S(1)} %get-tuple-element.105.cols, ...), custom_call_target="tpu_custom_call" | custom-call | flops 2097152 | bytes 2162688 | tf_op jit(solution)/shard_map/pallas_call | solution.py:37
  19.8 2.6 %all-to-all-start.2 = ((f32[128,1,128]{2,1,0:T(1,128)}), f32[128,1,128]{2,1,0:T(1,128)S(1)}, u32[]{:S(2)}, u32[]{:S(2)}) async-start(f32[128,1,128]{2,1,0:T(1,128)} %bitcast.22), calls=%async_computation.2 | async-start | bytes 131072 | tf_op jit(solution)/shard_map/all_to_all | solution.py:563
  22.5 5.3 %conditional.4 = ((f32[8,8,128]{2,1,0:T(8,128)S(1)}, f32[8,8,128]{2,1,0:T(8,128)S(1)}, f32[20,8,128]{2,1,0:T(8,128)S(1)})) conditional(s32[]{:T(128)} %convert_element_type.14, (f32[8,8,128]{2,1,0:T(8,128)S(1)}, f32[8,8,128]{2,1,0:T(8,128)S(1)}, f32[20,8,128]{2,1,0:T(8,128)S(1)}) %tuple.38, (f32[8,8,128]{2,1,0:T(8,128)S(1)}, ...), branch_computations={%region_2.3_spmd, %region_3.4_spmd} | conditional | bytes 884888 | solution.py:663
  22.5 1.8 %collective-permute-start.2 = (f32[20,8,128]{2,1,0:T(8,128)S(1)}, f32[20,8,128]{2,1,0:T(8,128)S(1)}, u32[]{:S(2)}, u32[]{:S(2)}) collective-permute-start(f32[20,8,128]{2,1,0:T(8,128)S(1)} %get-tuple-element.65), channel_id=1, source_target_pairs={{0,16},{16,0},{1,17},{17,1},{2,18},{18,2},{3,19},{19,3},{4,20},{20... | collective-permute-start | bytes 245768 | tf_op jit(solution)/shard_map/cond/branch_1_fun/ppermute | solution.py:656
  24.3 0.0 collective-permute-start
  24.3 1.6 %collective-permute-start.1 = (f32[8,8,128]{2,1,0:T(8,128)S(1)}, f32[8,8,128]{2,1,0:T(8,128)S(1)}, u32[]{:S(2)}, u32[]{:S(2)}) collective-permute-start(f32[8,8,128]{2,1,0:T(8,128)S(1)} %get-tuple-element.64), channel_id=1, source_target_pairs={{4,8},{12,0},{8,4},{0,12},{5,9},{13,1},{9,5},{1,13},{6,10},{14,2},... | collective-permute-start | bytes 98312 | tf_op jit(solution)/shard_map/cond/branch_1_fun/ppermute | solution.py:657
  25.9 0.0 collective-permute-done
  25.9 1.8 %collective-permute-done.1 = f32[8,8,128]{2,1,0:T(8,128)S(1)} collective-permute-done((f32[8,8,128]{2,1,0:T(8,128)S(1)}, f32[8,8,128]{2,1,0:T(8,128)S(1)}, u32[]{:S(2)}, u32[]{:S(2)}) %collective-permute-start.1) | collective-permute-done | bytes 32800 | tf_op jit(solution)/shard_map/cond/branch_1_fun/ppermute | solution.py:657
  27.7 0.0 collective-permute-done.2
  27.8 2.2 %all-to-all-done.2 = f32[128,1,128]{2,1,0:T(1,128)S(1)} async-done(((f32[128,1,128]{2,1,0:T(1,128)}), f32[128,1,128]{2,1,0:T(1,128)S(1)}, u32[]{:S(2)}, u32[]{:S(2)}) %all-to-all-start.2) | async-done | bytes 65568 | tf_op jit(solution)/shard_map/all_to_all | solution.py:563
  30.0 0.0 copy-done.1
  30.0 0.0 copy-done.2
  30.0 0.0 copy-done.5
  30.0 0.9 %shard_map.107 = (f32[16,8,128]{2,1,0:T(8,128)S(1)}, f32[16,8,128]{2,1,0:T(8,128)S(1)}, f32[32,128]{1,0:T(8,128)S(1)}) custom-call(f32[16,8,128]{2,1,0:T(8,128)S(1)} %get-tuple-element.109.loc, f32[64,8,128]{2,1,0:T(8,128)S(1)} %get-tuple-element.103.phi, f32[16,8,128]{2,1,0:T(8,128)S(1)} %bitcast.43, f32[24,8,128]{2,1,0:T(8,128)S(1)} %bitcast.42, ...), custom_call_target="tpu_custom_call" | custom-call | flops 1310720 | bytes 1765376 | tf_op jit(solution)/shard_map/pallas_call | solution.py:37
  30.9 10.0 %all_to_all.20 = f32[32,1,128]{2,1,0:T(1,128)S(1)} all-to-all(f32[32,1,128]{2,1,0:T(1,128)S(1)} %bitcast.46), channel_id=1, replica_groups=mesh['gx'=2,'gy'=4,'gz'=4] {'gx','gy','gz'}, dimensions={0} | all-to-all | bytes 32768 | tf_op jit(solution)/shard_map/all_to_all | solution.py:563
  40.9 0.0 copy-done
  40.9 0.0 copy-done.4
  40.9 0.5 %shard_map.108 = (f32[16,8,128]{2,1,0:T(8,128)S(1)}, f32[4,7]{1,0:T(4,128)S(1)}, s32[1]{0:T(128)S(4)}) custom-call(f32[32,128]{1,0:T(8,128)S(1)} %bitcast.44, f32[16,8,128]{2,1,0:T(8,128)S(1)} %get-tuple-element.119.image, f32[6,16,8,128]{3,2,1,0:T(8,128)S(1)} %bitcast.50, bf16[4,128,128]{2,1,0:T(8,128)(2,1)S(1)} %copy-done, f32[8,128]{1,0:T(8,128)S(1)} %copy-done.4), custom_call_target="tpu_custom_call" | custom-call | flops 262144 | bytes 675956 | tf_op jit(solution)/shard_map/pallas_call | solution.py:37
  41.4 0.0 copy-start.6
  41.4 0.0 copy-start.7
  41.4 0.6 %copy.83 = f32[4,4,4,2,128]{4,3,2,1,0:T(2,128)} copy(f32[4,4,4,2,128]{4,3,2,1,0:T(2,128)S(1)} %bitcast.37) | data formatting | bytes 131072
  42.0 0.0 copy-done.6
  42.0 0.0 copy-done.7
  (14 shorter events, 0.2 us)
Async XLA Ops:
  1.7 9.1 %collective-permute-start.4 = (f32[48,8,128]{2,1,0:T(8,128)S(1)}, f32[48,8,128]{2,1,0:T(8,128)S(1)}, u32[]{:S(2)}, u32[]{:S(2)}) collective-permute-start(f32[48,8,128]{2,1,0:T(8,128)S(1)} %get-tuple-element.100), channel_id=1, source_target_pairs={{0,4},{8,12},{4,0},{12,8},{1,5},{9,13},{5,1},{13,9},{2,6},{10,14},... | collective-permute-start | bytes 589832 | tf_op jit(solution)/shard_map/ppermute | solution.py:591
  2.2 8.6 %collective-permute-start.5 = (f32[48,8,128]{2,1,0:T(8,128)S(1)}, f32[48,8,128]{2,1,0:T(8,128)S(1)}, u32[]{:S(2)}, u32[]{:S(2)}) collective-permute-start(f32[48,8,128]{2,1,0:T(8,128)S(1)} %get-tuple-element.101), channel_id=1, source_target_pairs={{4,8},{12,0},{8,4},{0,12},{5,9},{13,1},{9,5},{1,13},{6,10},{14,2},... | collective-permute-start | bytes 589832 | tf_op jit(solution)/shard_map/ppermute | solution.py:591
  5.8 12.6 %all-to-all-start.1 = ((f32[160,1,128]{2,1,0:T(1,128)}), f32[160,1,128]{2,1,0:T(1,128)S(1)}, u32[]{:S(2)}, u32[]{:S(2)}) async-start(f32[160,1,128]{2,1,0:T(1,128)} %bitcast.17), calls=%async_computation.1 | async-start | bytes 163840 | tf_op jit(solution)/shard_map/all_to_all | solution.py:563
  10.8 7.7 %copy-start.3 = (f32[16,512]{1,0:T(8,128)S(1)}, f32[16,512]{1,0:T(8,128)}, u32[]{:S(2)}) copy-start(f32[16,512]{1,0:T(8,128)} %factor.1) | copy-start | bytes 98308
  11.0 4.3 %collective-permute-start.3 = (bf16[4,4,2,6,128]{4,1,3,2,0:T(4,128)(2,1)S(1)}, bf16[4,4,2,6,128]{4,1,3,2,0:T(4,128)(2,1)S(1)}, u32[]{:S(2)}, u32[]{:S(2)}) collective-permute-start(bf16[4,4,2,6,128]{4,1,3,2,0:T(4,128)(2,1)S(1)} %slice_select_fusion), channel_id=1, source_target_pairs={{0,16},{16,0},{1,17},{17,1},{2,18},{18,2},{3,19},{19,3},{4,20},{20... | collective-permute-start | bytes 147464 | tf_op jit(solution)/shard_map/cond/branch_1_fun/ppermute | solution.py:550
  15.4 14.6 %copy-start.1 = (f32[6,4,4,2,128]{4,3,2,1,0:T(2,128)S(1)}, f32[6,4,4,2,128]{4,3,2,1,0:T(2,128)}, u32[]{:S(2)}) copy-start(f32[6,4,4,2,128]{4,3,2,1,0:T(2,128)} %param.19) | copy-start | bytes 294916
  15.4 14.6 %copy-start.2 = (f32[4,4,4,2,128]{4,3,2,1,0:T(2,128)S(1)}, f32[4,4,4,2,128]{4,3,2,1,0:T(2,128)}, u32[]{:S(2)}) copy-start(f32[4,4,4,2,128]{4,3,2,1,0:T(2,128)} %param.18) | copy-start | bytes 196612
  15.4 14.6 %copy-start.5 = (f32[6,4,4,4,2,128]{5,4,3,2,1,0:T(2,128)S(1)}, f32[6,4,4,4,2,128]{5,4,3,2,1,0:T(2,128)}, u32[]{:S(2)}) copy-start(f32[6,4,4,4,2,128]{5,4,3,2,1,0:T(2,128)} %param.16) | copy-start | bytes 1179652
  18.5 22.4 %copy-start = (bf16[4,128,128]{2,1,0:T(8,128)(2,1)S(1)}, bf16[4,128,128]{2,1,0:T(8,128)(2,1)}, u32[]{:S(2)}) copy-start(bf16[4,128,128]{2,1,0:T(8,128)(2,1)} %constant.92.clone.maps) | copy-start | bytes 393220
  18.5 22.4 %copy-start.4 = (f32[8,128]{1,0:T(8,128)S(1)}, f32[8,128]{1,0:T(8,128)}, u32[]{:S(2)}) copy-start(f32[8,128]{1,0:T(8,128)} %constant.93.clone.fixed) | copy-start | bytes 12292
  19.8 10.1 %all-to-all-start.2 = ((f32[128,1,128]{2,1,0:T(1,128)}), f32[128,1,128]{2,1,0:T(1,128)S(1)}, u32[]{:S(2)}, u32[]{:S(2)}) async-start(f32[128,1,128]{2,1,0:T(1,128)} %bitcast.22), calls=%async_computation.2 | async-start | bytes 131072 | tf_op jit(solution)/shard_map/all_to_all | solution.py:563
  22.5 5.2 %collective-permute-start.2 = (f32[20,8,128]{2,1,0:T(8,128)S(1)}, f32[20,8,128]{2,1,0:T(8,128)S(1)}, u32[]{:S(2)}, u32[]{:S(2)}) collective-permute-start(f32[20,8,128]{2,1,0:T(8,128)S(1)} %get-tuple-element.65), channel_id=1, source_target_pairs={{0,16},{16,0},{1,17},{17,1},{2,18},{18,2},{3,19},{19,3},{4,20},{20... | collective-permute-start | bytes 245768 | tf_op jit(solution)/shard_map/cond/branch_1_fun/ppermute | solution.py:656
  24.3 1.6 %collective-permute-start = (f32[8,8,128]{2,1,0:T(8,128)S(1)}, f32[8,8,128]{2,1,0:T(8,128)S(1)}, u32[]{:S(2)}, u32[]{:S(2)}) collective-permute-start(f32[8,8,128]{2,1,0:T(8,128)S(1)} %get-tuple-element.63), channel_id=1, source_target_pairs={{0,4},{8,12},{4,0},{12,8},{1,5},{9,13},{5,1},{13,9},{2,6},{10,14},... | collective-permute-start | bytes 98312 | tf_op jit(solution)/shard_map/cond/branch_1_fun/ppermute | solution.py:657
  24.3 3.4 %collective-permute-start.1 = (f32[8,8,128]{2,1,0:T(8,128)S(1)}, f32[8,8,128]{2,1,0:T(8,128)S(1)}, u32[]{:S(2)}, u32[]{:S(2)}) collective-permute-start(f32[8,8,128]{2,1,0:T(8,128)S(1)} %get-tuple-element.64), channel_id=1, source_target_pairs={{4,8},{12,0},{8,4},{0,12},{5,9},{13,1},{9,5},{1,13},{6,10},{14,2},... | collective-permute-start | bytes 98312 | tf_op jit(solution)/shard_map/cond/branch_1_fun/ppermute | solution.py:657
  41.4 0.7 %copy-start.6 = (f32[4,7]{1,0:T(4,128)}, f32[4,7]{1,0:T(4,128)S(1)}, u32[]{:S(2)}) copy-start(f32[4,7]{1,0:T(4,128)S(1)} %get-tuple-element.160) | copy-start | bytes 340
  41.4 0.7 %copy-start.7 = (f32[16,8,128]{2,1,0:T(8,128)}, f32[16,8,128]{2,1,0:T(8,128)S(1)}, u32[]{:S(2)}) copy-start(f32[16,8,128]{2,1,0:T(8,128)S(1)} %get-tuple-element.125) | copy-start | bytes 196612

commit v11 on v10

--- a/solution.py
+++ b/solution.py
@@ -157,6 +157,7 @@
 
 
 def rhs_body(vector, phi, out):
+    faces = across(ends(), phi[...].reshape(K * C * XY, CZ))
     rows = []
     for s in range(S):
         v = [vector[s * C + c] for c in range(C)]
@@ -165,7 +166,6 @@
         rows.append(row_sums(prods[8:]))
     rows.append(jnp.zeros((64, 128), F32))
     rhs = across(jnp.ones((8, 128), F32), jnp.concatenate(rows, 0))
-    faces = across(ends(), phi[...].reshape(K * C * XY, CZ))
     n = out.shape[0] // GATHERED
     me, _, _ = place()
     later = lax.broadcasted_iota(jnp.int32, (n, 128), 0) > me

time: 42.3 us -> 42.3 us (level)
  no operation moved by 1% of the time
where the time goes in v11:
time: 42.3 us; the launch traced here: 42 us
  starting transfers between devices  15.9 us (38%)
  blocking collectives  10 us (24%)
  waiting for transfers between devices  7.36 us (17%)
  Pallas kernels  6.75 us (16%)
  local copies, waits for them, and re-layouts  0.83 us (2%)
  between operations  0.76 us (2%)
    all_to_all x1, blocking collectives, exchange(): lax.all_to_all(rows[:, None], AXES, 0, 0, tiled=True).reshape(rows.shape)  10 us
    all_to_all x2, starting transfers between devices, exchange(): lax.all_to_all(rows[:, None], AXES, 0, 0, tiled=True).reshape(rows.shape)  7.53 us
    pallas_call x6, Pallas kernels, call(): pl.pallas_call(body, out_shape=tuple(outs), in_specs=in_specs or [VMEM] *...  6.75 us
    all_to_all x2, waiting for transfers between devices, exchange(): lax.all_to_all(rows[:, None], AXES, 0, 0, tiled=True).reshape(rows.shape)  5.3 us
    ppermute x2, starting transfers between devices, on_device(): lax.ppermute(x, 'gy', pairs)  3.16 us
    ppermute x1, starting transfers between devices, swap(): return [lax.ppermute(x, axis, pairs) for x, pairs in zip(sides, rounds)]  1.83 us
    ppermute x1, starting transfers between devices, trade(): lax.ppermute(x, 'gx', pairs)  1.83 us
    ppermute x2, waiting for transfers between devices, trade(): lax.ppermute(x, 'gy', pairs)  1.82 us
  transfers between devices with their start and end apart: 8, of which 4 were waited for; matrix products, arithmetic and copies ran while one was open for 1% of the time, Pallas kernels for 7%

profile of v11, /device:TPU:0, one launch (start us, length us, event | category | flops | bytes accessed | tf_op | source)
XLA Modules:
  0.0 42.0 jit_solution(15238005197392293578)
XLA Ops:
  0.6 1.0 %shard_map.104 = (f32[16,8,128]{2,1,0:T(8,128)S(1)}, bf16[16,8,128]{2,1,0:T(8,128)(2,1)S(1)}, f32[64,8,128]{2,1,0:T(8,128)S(1)}, f32[48,8,128]{2,1,0:T(8,128)S(1)}, f32[48,8,128]{2,1,0:T(8,128)S(1)}) custom-call(f32[6,16,8,128]{3,2,1,0:T(8,128)} %bitcast.47, f32[64,8,128]{2,1,0:T(8,128)} %bitcast.55), custom_call_target="tpu_custom_call" | custom-call | flops 16384 | bytes 1409024 | tf_op jit(solution)/shard_map/pallas_call | solution.py:37
  1.7 0.5 %collective-permute-start.4 = (f32[48,8,128]{2,1,0:T(8,128)S(1)}, f32[48,8,128]{2,1,0:T(8,128)S(1)}, u32[]{:S(2)}, u32[]{:S(2)}) collective-permute-start(f32[48,8,128]{2,1,0:T(8,128)S(1)} %get-tuple-element.100), channel_id=1, source_target_pairs={{0,4},{8,12},{4,0},{12,8},{1,5},{9,13},{5,1},{13,9},{2,6},{10,14},... | collective-permute-start | bytes 589832 | tf_op jit(solution)/shard_map/ppermute | solution.py:591
  2.2 2.6 %collective-permute-start.5 = (f32[48,8,128]{2,1,0:T(8,128)S(1)}, f32[48,8,128]{2,1,0:T(8,128)S(1)}, u32[]{:S(2)}, u32[]{:S(2)}) collective-permute-start(f32[48,8,128]{2,1,0:T(8,128)S(1)} %get-tuple-element.101), channel_id=1, source_target_pairs={{4,8},{12,0},{8,4},{0,12},{5,9},{13,1},{9,5},{1,13},{6,10},{14,2},... | collective-permute-start | bytes 589832 | tf_op jit(solution)/shard_map/ppermute | solution.py:591
  4.8 1.0 %shard_map.105 = f32[160,128]{1,0:T(8,128)} custom-call(f32[16,8,128]{2,1,0:T(8,128)S(1)} %get-tuple-element.107.vector, f32[64,8,128]{2,1,0:T(8,128)S(1)} %get-tuple-element.103.phi), custom_call_target="tpu_custom_call" | custom-call | flops 524288 | bytes 409600 | tf_op jit(solution)/shard_map/pallas_call | solution.py:37
  5.8 4.9 %all-to-all-start.1 = ((f32[160,1,128]{2,1,0:T(1,128)}), f32[160,1,128]{2,1,0:T(1,128)S(1)}, u32[]{:S(2)}, u32[]{:S(2)}) async-start(f32[160,1,128]{2,1,0:T(1,128)} %bitcast.17), calls=%async_computation.1 | async-start | bytes 163840 | tf_op jit(solution)/shard_map/all_to_all | solution.py:563
  10.7 0.0 collective-permute-done.4.rest_0_
  10.7 0.0 collective-permute-done.5.rest_1_
  10.7 0.0 copy-start.3
  10.7 4.6 %conditional.3 = (bf16[4,64,128]{2,1,0:T(8,128)(2,1)S(1)}, f32[88,128]{1,0:T(8,128)S(1)}, f32[16,8,128]{2,1,0:T(8,128)S(1)}, bf16[4,8,192,128]{3,2,1,0:T(8,128)(2,1)S(1)}, f32[16,8,128]{2,1,0:T(8,128)S(1)}) conditional(s32[]{:T(128)} %convert_element_type.14, () %tuple.36, (f32[48,8,128]{2,1,0:T(8,128)S(1)}, f32[48,8,128]{2,1,0:T(8,128)S(1)}, ...), branch_computations={%region_0.0_spmd, %region_1.2_spmd} | conditional | flops 10000286720 | bytes 5878173 | solution.py:642
  10.9 1.8 %collective-permute-start.3 = (bf16[4,4,2,6,128]{4,1,3,2,0:T(4,128)(2,1)S(1)}, bf16[4,4,2,6,128]{4,1,3,2,0:T(4,128)(2,1)S(1)}, u32[]{:S(2)}, u32[]{:S(2)}) collective-permute-start(bf16[4,4,2,6,128]{4,1,3,2,0:T(4,128)(2,1)S(1)} %slice_select_fusion), channel_id=1, source_target_pairs={{0,16},{16,0},{1,17},{17,1},{2,18},{18,2},{3,19},{19,3},{4,20},{20... | collective-permute-start | bytes 147464 | tf_op jit(solution)/shard_map/cond/branch_1_fun/ppermute | solution.py:550
  12.8 0.1 pad_maximum_fusion
  13.0 2.0 %branch_1_fun.1 = (f32[88,128]{1,0:T(8,128)S(1)}, f32[16,8,128]{2,1,0:T(8,128)S(1)}, bf16[4,8,192,128]{3,2,1,0:T(8,128)(2,1)S(1)}, f32[16,8,128]{2,1,0:T(8,128)S(1)}) custom-call(f32[64,8,128]{2,1,0:T(8,128)S(1)} %get-tuple-element.51.phi, f32[6,16,8,128]{3,2,1,0:T(8,128)} %get-tuple-element.52.basis, bf16[4,8,192,128]{3,2,1,0:T(8,128)(2,1)} %bitcast.60, ...), custom_call_target="tpu_custom_call" | custom-call | flops 10000000000 | bytes 4108288 | tf_op jit(solution)/shard_map/cond/branch_1_fun/pallas_call | solution.py:37
  15.0 0.2 collective-permute-done.3
  15.2 0.1 maximum_select_fusion
  15.3 0.0 copy-start.1
  15.3 0.0 copy-start.2
  15.3 0.0 copy-start.5
  15.4 3.1 %all-to-all-done.1 = f32[160,1,128]{2,1,0:T(1,128)S(1)} async-done(((f32[160,1,128]{2,1,0:T(1,128)}), f32[160,1,128]{2,1,0:T(1,128)S(1)}, u32[]{:S(2)}, u32[]{:S(2)}) %all-to-all-start.1) | async-done | bytes 81952 | tf_op jit(solution)/shard_map/all_to_all | solution.py:563
  18.4 0.0 copy-done.3
  18.4 0.0 copy-start
  18.4 0.0 copy-start.4
  18.4 1.4 %shard_map.106 = (f32[128,128]{1,0:T(8,128)}, f32[16,8,128]{2,1,0:T(8,128)S(1)}, f32[8,8,128]{2,1,0:T(8,128)S(1)}, f32[8,8,128]{2,1,0:T(8,128)S(1)}, f32[20,8,128]{2,1,0:T(8,128)S(1)}) custom-call(bf16[4,8,192,128]{3,2,1,0:T(8,128)(2,1)S(1)} %get-tuple-element.104.inv, bf16[4,64,128]{2,1,0:T(8,128)(2,1)S(1)} %get-tuple-element.105.cols, ...), custom_call_target="tpu_custom_call" | custom-call | flops 2097152 | bytes 2162688 | tf_op jit(solution)/shard_map/pallas_call | solution.py:37
  19.8 2.6 %all-to-all-start.2 = ((f32[128,1,128]{2,1,0:T(1,128)}), f32[128,1,128]{2,1,0:T(1,128)S(1)}, u32[]{:S(2)}, u32[]{:S(2)}) async-start(f32[128,1,128]{2,1,0:T(1,128)} %bitcast.22), calls=%async_computation.2 | async-start | bytes 131072 | tf_op jit(solution)/shard_map/all_to_all | solution.py:563
  22.5 5.3 %conditional.4 = ((f32[8,8,128]{2,1,0:T(8,128)S(1)}, f32[8,8,128]{2,1,0:T(8,128)S(1)}, f32[20,8,128]{2,1,0:T(8,128)S(1)})) conditional(s32[]{:T(128)} %convert_element_type.14, (f32[8,8,128]{2,1,0:T(8,128)S(1)}, f32[8,8,128]{2,1,0:T(8,128)S(1)}, f32[20,8,128]{2,1,0:T(8,128)S(1)}) %tuple.38, (f32[8,8,128]{2,1,0:T(8,128)S(1)}, ...), branch_computations={%region_2.3_spmd, %region_3.4_spmd} | conditional | bytes 884888 | solution.py:663
  22.5 1.8 %collective-permute-start.2 = (f32[20,8,128]{2,1,0:T(8,128)S(1)}, f32[20,8,128]{2,1,0:T(8,128)S(1)}, u32[]{:S(2)}, u32[]{:S(2)}) collective-permute-start(f32[20,8,128]{2,1,0:T(8,128)S(1)} %get-tuple-element.65), channel_id=1, source_target_pairs={{0,16},{16,0},{1,17},{17,1},{2,18},{18,2},{3,19},{19,3},{4,20},{20... | collective-permute-start | bytes 245768 | tf_op jit(solution)/shard_map/cond/branch_1_fun/ppermute | solution.py:656
  24.3 0.0 collective-permute-start
  24.3 1.6 %collective-permute-start.1 = (f32[8,8,128]{2,1,0:T(8,128)S(1)}, f32[8,8,128]{2,1,0:T(8,128)S(1)}, u32[]{:S(2)}, u32[]{:S(2)}) collective-permute-start(f32[8,8,128]{2,1,0:T(8,128)S(1)} %get-tuple-element.64), channel_id=1, source_target_pairs={{4,8},{12,0},{8,4},{0,12},{5,9},{13,1},{9,5},{1,13},{6,10},{14,2},... | collective-permute-start | bytes 98312 | tf_op jit(solution)/shard_map/cond/branch_1_fun/ppermute | solution.py:657
  25.9 0.0 collective-permute-done
  25.9 1.8 %collective-permute-done.1 = f32[8,8,128]{2,1,0:T(8,128)S(1)} collective-permute-done((f32[8,8,128]{2,1,0:T(8,128)S(1)}, f32[8,8,128]{2,1,0:T(8,128)S(1)}, u32[]{:S(2)}, u32[]{:S(2)}) %collective-permute-start.1) | collective-permute-done | bytes 32800 | tf_op jit(solution)/shard_map/cond/branch_1_fun/ppermute | solution.py:657
  27.7 0.0 collective-permute-done.2
  27.7 2.2 %all-to-all-done.2 = f32[128,1,128]{2,1,0:T(1,128)S(1)} async-done(((f32[128,1,128]{2,1,0:T(1,128)}), f32[128,1,128]{2,1,0:T(1,128)S(1)}, u32[]{:S(2)}, u32[]{:S(2)}) %all-to-all-start.2) | async-done | bytes 65568 | tf_op jit(solution)/shard_map/all_to_all | solution.py:563
  29.9 0.0 copy-done.1
  30.0 0.0 copy-done.2
  30.0 0.0 copy-done.5
  30.0 0.9 %shard_map.107 = (f32[16,8,128]{2,1,0:T(8,128)S(1)}, f32[16,8,128]{2,1,0:T(8,128)S(1)}, f32[32,128]{1,0:T(8,128)S(1)}) custom-call(f32[16,8,128]{2,1,0:T(8,128)S(1)} %get-tuple-element.109.loc, f32[64,8,128]{2,1,0:T(8,128)S(1)} %get-tuple-element.103.phi, f32[16,8,128]{2,1,0:T(8,128)S(1)} %bitcast.43, f32[24,8,128]{2,1,0:T(8,128)S(1)} %bitcast.42, ...), custom_call_target="tpu_custom_call" | custom-call | flops 1310720 | bytes 1765376 | tf_op jit(solution)/shard_map/pallas_call | solution.py:37
  30.8 10.0 %all_to_all.20 = f32[32,1,128]{2,1,0:T(1,128)S(1)} all-to-all(f32[32,1,128]{2,1,0:T(1,128)S(1)} %bitcast.46), channel_id=1, replica_groups=mesh['gx'=2,'gy'=4,'gz'=4] {'gx','gy','gz'}, dimensions={0} | all-to-all | bytes 32768 | tf_op jit(solution)/shard_map/all_to_all | solution.py:563
  40.9 0.0 copy-done
  40.9 0.0 copy-done.4
  40.9 0.5 %shard_map.108 = (f32[16,8,128]{2,1,0:T(8,128)S(1)}, f32[4,7]{1,0:T(4,128)S(1)}, s32[1]{0:T(128)S(4)}) custom-call(f32[32,128]{1,0:T(8,128)S(1)} %bitcast.44, f32[16,8,128]{2,1,0:T(8,128)S(1)} %get-tuple-element.119.image, f32[6,16,8,128]{3,2,1,0:T(8,128)S(1)} %bitcast.50, bf16[4,128,128]{2,1,0:T(8,128)(2,1)S(1)} %copy-done, f32[8,128]{1,0:T(8,128)S(1)} %copy-done.4), custom_call_target="tpu_custom_call" | custom-call | flops 262144 | bytes 675956 | tf_op jit(solution)/shard_map/pallas_call | solution.py:37
  41.3 0.0 copy-start.6
  41.4 0.0 copy-start.7
  41.4 0.6 %copy.83 = f32[4,4,4,2,128]{4,3,2,1,0:T(2,128)} copy(f32[4,4,4,2,128]{4,3,2,1,0:T(2,128)S(1)} %bitcast.37) | data formatting | bytes 131072
  42.0 0.0 copy-done.6
  42.0 0.0 copy-done.7
  (14 shorter events, 0.2 us)
Async XLA Ops:
  1.7 9.0 %collective-permute-start.4 = (f32[48,8,128]{2,1,0:T(8,128)S(1)}, f32[48,8,128]{2,1,0:T(8,128)S(1)}, u32[]{:S(2)}, u32[]{:S(2)}) collective-permute-start(f32[48,8,128]{2,1,0:T(8,128)S(1)} %get-tuple-element.100), channel_id=1, source_target_pairs={{0,4},{8,12},{4,0},{12,8},{1,5},{9,13},{5,1},{13,9},{2,6},{10,14},... | collective-permute-start | bytes 589832 | tf_op jit(solution)/shard_map/ppermute | solution.py:591
  2.2 8.5 %collective-permute-start.5 = (f32[48,8,128]{2,1,0:T(8,128)S(1)}, f32[48,8,128]{2,1,0:T(8,128)S(1)}, u32[]{:S(2)}, u32[]{:S(2)}) collective-permute-start(f32[48,8,128]{2,1,0:T(8,128)S(1)} %get-tuple-element.101), channel_id=1, source_target_pairs={{4,8},{12,0},{8,4},{0,12},{5,9},{13,1},{9,5},{1,13},{6,10},{14,2},... | collective-permute-start | bytes 589832 | tf_op jit(solution)/shard_map/ppermute | solution.py:591
  5.8 12.6 %all-to-all-start.1 = ((f32[160,1,128]{2,1,0:T(1,128)}), f32[160,1,128]{2,1,0:T(1,128)S(1)}, u32[]{:S(2)}, u32[]{:S(2)}) async-start(f32[160,1,128]{2,1,0:T(1,128)} %bitcast.17), calls=%async_computation.1 | async-start | bytes 163840 | tf_op jit(solution)/shard_map/all_to_all | solution.py:563
  10.7 7.7 %copy-start.3 = (f32[16,512]{1,0:T(8,128)S(1)}, f32[16,512]{1,0:T(8,128)}, u32[]{:S(2)}) copy-start(f32[16,512]{1,0:T(8,128)} %factor.1) | copy-start | bytes 98308
  10.9 4.3 %collective-permute-start.3 = (bf16[4,4,2,6,128]{4,1,3,2,0:T(4,128)(2,1)S(1)}, bf16[4,4,2,6,128]{4,1,3,2,0:T(4,128)(2,1)S(1)}, u32[]{:S(2)}, u32[]{:S(2)}) collective-permute-start(bf16[4,4,2,6,128]{4,1,3,2,0:T(4,128)(2,1)S(1)} %slice_select_fusion), channel_id=1, source_target_pairs={{0,16},{16,0},{1,17},{17,1},{2,18},{18,2},{3,19},{19,3},{4,20},{20... | collective-permute-start | bytes 147464 | tf_op jit(solution)/shard_map/cond/branch_1_fun/ppermute | solution.py:550
  15.3 14.6 %copy-start.1 = (f32[6,4,4,2,128]{4,3,2,1,0:T(2,128)S(1)}, f32[6,4,4,2,128]{4,3,2,1,0:T(2,128)}, u32[]{:S(2)}) copy-start(f32[6,4,4,2,128]{4,3,2,1,0:T(2,128)} %param.19) | copy-start | bytes 294916
  15.3 14.6 %copy-start.2 = (f32[4,4,4,2,128]{4,3,2,1,0:T(2,128)S(1)}, f32[4,4,4,2,128]{4,3,2,1,0:T(2,128)}, u32[]{:S(2)}) copy-start(f32[4,4,4,2,128]{4,3,2,1,0:T(2,128)} %param.18) | copy-start | bytes 196612
  15.3 14.6 %copy-start.5 = (f32[6,4,4,4,2,128]{5,4,3,2,1,0:T(2,128)S(1)}, f32[6,4,4,4,2,128]{5,4,3,2,1,0:T(2,128)}, u32[]{:S(2)}) copy-start(f32[6,4,4,4,2,128]{5,4,3,2,1,0:T(2,128)} %param.16) | copy-start | bytes 1179652
  18.4 22.4 %copy-start = (bf16[4,128,128]{2,1,0:T(8,128)(2,1)S(1)}, bf16[4,128,128]{2,1,0:T(8,128)(2,1)}, u32[]{:S(2)}) copy-start(bf16[4,128,128]{2,1,0:T(8,128)(2,1)} %constant.92.clone.maps) | copy-start | bytes 393220
  18.4 22.4 %copy-start.4 = (f32[8,128]{1,0:T(8,128)S(1)}, f32[8,128]{1,0:T(8,128)}, u32[]{:S(2)}) copy-start(f32[8,128]{1,0:T(8,128)} %constant.93.clone.fixed) | copy-start | bytes 12292
  19.8 10.1 %all-to-all-start.2 = ((f32[128,1,128]{2,1,0:T(1,128)}), f32[128,1,128]{2,1,0:T(1,128)S(1)}, u32[]{:S(2)}, u32[]{:S(2)}) async-start(f32[128,1,128]{2,1,0:T(1,128)} %bitcast.22), calls=%async_computation.2 | async-start | bytes 131072 | tf_op jit(solution)/shard_map/all_to_all | solution.py:563
  22.5 5.2 %collective-permute-start.2 = (f32[20,8,128]{2,1,0:T(8,128)S(1)}, f32[20,8,128]{2,1,0:T(8,128)S(1)}, u32[]{:S(2)}, u32[]{:S(2)}) collective-permute-start(f32[20,8,128]{2,1,0:T(8,128)S(1)} %get-tuple-element.65), channel_id=1, source_target_pairs={{0,16},{16,0},{1,17},{17,1},{2,18},{18,2},{3,19},{19,3},{4,20},{20... | collective-permute-start | bytes 245768 | tf_op jit(solution)/shard_map/cond/branch_1_fun/ppermute | solution.py:656
  24.3 1.6 %collective-permute-start = (f32[8,8,128]{2,1,0:T(8,128)S(1)}, f32[8,8,128]{2,1,0:T(8,128)S(1)}, u32[]{:S(2)}, u32[]{:S(2)}) collective-permute-start(f32[8,8,128]{2,1,0:T(8,128)S(1)} %get-tuple-element.63), channel_id=1, source_target_pairs={{0,4},{8,12},{4,0},{12,8},{1,5},{9,13},{5,1},{13,9},{2,6},{10,14},... | collective-permute-start | bytes 98312 | tf_op jit(solution)/shard_map/cond/branch_1_fun/ppermute | solution.py:657
  24.3 3.4 %collective-permute-start.1 = (f32[8,8,128]{2,1,0:T(8,128)S(1)}, f32[8,8,128]{2,1,0:T(8,128)S(1)}, u32[]{:S(2)}, u32[]{:S(2)}) collective-permute-start(f32[8,8,128]{2,1,0:T(8,128)S(1)} %get-tuple-element.64), channel_id=1, source_target_pairs={{4,8},{12,0},{8,4},{0,12},{5,9},{13,1},{9,5},{1,13},{6,10},{14,2},... | collective-permute-start | bytes 98312 | tf_op jit(solution)/shard_map/cond/branch_1_fun/ppermute | solution.py:657
  41.3 0.7 %copy-start.6 = (f32[4,7]{1,0:T(4,128)}, f32[4,7]{1,0:T(4,128)S(1)}, u32[]{:S(2)}) copy-start(f32[4,7]{1,0:T(4,128)S(1)} %get-tuple-element.160) | copy-start | bytes 340
  41.4 0.7 %copy-start.7 = (f32[16,8,128]{2,1,0:T(8,128)}, f32[16,8,128]{2,1,0:T(8,128)S(1)}, u32[]{:S(2)}) copy-start(f32[16,8,128]{2,1,0:T(8,128)S(1)} %get-tuple-element.125) | copy-start | bytes 196612

commit v12 on v10

--- a/solution.py
+++ b/solution.py
@@ -320,8 +320,8 @@
     else:
         at = edge(lax.axis_index("gx") == 1)
         starts = [(EXTENT * c + at, SIDE * c) for c in range(C)]
+    factor_body(two_x, got, factor, out)
     solve(inv, cols, starts, done, unroll=True)
-    factor_body(two_x, got, factor, out)
     send_ends(two_x, across(ends(), loc[...].reshape(S * C * XY, CZ)), out)
     odd_y = lax.axis_index("gy") % 2 == 1
     for i in range(S * C // 2):

time: 42.3 us -> 42.3 us (level)
  no operation moved by 1% of the time
where the time goes in v12:
time: 42.3 us; the launch traced here: 42.1 us
  starting transfers between devices  15.9 us (38%)
  blocking collectives  10 us (24%)
  waiting for transfers between devices  7.36 us (17%)
  Pallas kernels  6.79 us (16%)
  local copies, waits for them, and re-layouts  0.83 us (2%)
  between operations  0.76 us (2%)
    all_to_all x1, blocking collectives, exchange(): lax.all_to_all(rows[:, None], AXES, 0, 0, tiled=True).reshape(rows.shape)  10 us
    all_to_all x2, starting transfers between devices, exchange(): lax.all_to_all(rows[:, None], AXES, 0, 0, tiled=True).reshape(rows.shape)  7.53 us
    pallas_call x6, Pallas kernels, call(): pl.pallas_call(body, out_shape=tuple(outs), in_specs=in_specs or [VMEM] *...  6.79 us
    all_to_all x2, waiting for transfers between devices, exchange(): lax.all_to_all(rows[:, None], AXES, 0, 0, tiled=True).reshape(rows.shape)  5.3 us
    ppermute x2, starting transfers between devices, on_device(): lax.ppermute(x, 'gy', pairs)  3.16 us
    ppermute x1, starting transfers between devices, swap(): return [lax.ppermute(x, axis, pairs) for x, pairs in zip(sides, rounds)]  1.83 us
    ppermute x1, starting transfers between devices, trade(): lax.ppermute(x, 'gx', pairs)  1.83 us
    ppermute x2, waiting for transfers between devices, trade(): lax.ppermute(x, 'gy', pairs)  1.82 us
  transfers between devices with their start and end apart: 8, of which 4 were waited for; matrix products, arithmetic and copies ran while one was open for 1% of the time, Pallas kernels for 7%

profile of v12, /device:TPU:0, one launch (start us, length us, event | category | flops | bytes accessed | tf_op | source)
XLA Modules:
  0.0 42.1 jit_solution(9301959086711830575)
XLA Ops:
  0.6 1.0 %shard_map.104 = (f32[16,8,128]{2,1,0:T(8,128)S(1)}, bf16[16,8,128]{2,1,0:T(8,128)(2,1)S(1)}, f32[64,8,128]{2,1,0:T(8,128)S(1)}, f32[48,8,128]{2,1,0:T(8,128)S(1)}, f32[48,8,128]{2,1,0:T(8,128)S(1)}) custom-call(f32[6,16,8,128]{3,2,1,0:T(8,128)} %bitcast.47, f32[64,8,128]{2,1,0:T(8,128)} %bitcast.55), custom_call_target="tpu_custom_call" | custom-call | flops 16384 | bytes 1409024 | tf_op jit(solution)/shard_map/pallas_call | solution.py:37
  1.7 0.5 %collective-permute-start.4 = (f32[48,8,128]{2,1,0:T(8,128)S(1)}, f32[48,8,128]{2,1,0:T(8,128)S(1)}, u32[]{:S(2)}, u32[]{:S(2)}) collective-permute-start(f32[48,8,128]{2,1,0:T(8,128)S(1)} %get-tuple-element.100), channel_id=1, source_target_pairs={{0,4},{8,12},{4,0},{12,8},{1,5},{9,13},{5,1},{13,9},{2,6},{10,14},... | collective-permute-start | bytes 589832 | tf_op jit(solution)/shard_map/ppermute | solution.py:591
  2.2 2.6 %collective-permute-start.5 = (f32[48,8,128]{2,1,0:T(8,128)S(1)}, f32[48,8,128]{2,1,0:T(8,128)S(1)}, u32[]{:S(2)}, u32[]{:S(2)}) collective-permute-start(f32[48,8,128]{2,1,0:T(8,128)S(1)} %get-tuple-element.101), channel_id=1, source_target_pairs={{4,8},{12,0},{8,4},{0,12},{5,9},{13,1},{9,5},{1,13},{6,10},{14,2},... | collective-permute-start | bytes 589832 | tf_op jit(solution)/shard_map/ppermute | solution.py:591
  4.8 1.0 %shard_map.105 = f32[160,128]{1,0:T(8,128)} custom-call(f32[16,8,128]{2,1,0:T(8,128)S(1)} %get-tuple-element.107.vector, f32[64,8,128]{2,1,0:T(8,128)S(1)} %get-tuple-element.103.phi), custom_call_target="tpu_custom_call" | custom-call | flops 524288 | bytes 409600 | tf_op jit(solution)/shard_map/pallas_call | solution.py:37
  5.8 4.9 %all-to-all-start.1 = ((f32[160,1,128]{2,1,0:T(1,128)}), f32[160,1,128]{2,1,0:T(1,128)S(1)}, u32[]{:S(2)}, u32[]{:S(2)}) async-start(f32[160,1,128]{2,1,0:T(1,128)} %bitcast.17), calls=%async_computation.1 | async-start | bytes 163840 | tf_op jit(solution)/shard_map/all_to_all | solution.py:563
  10.7 0.0 collective-permute-done.4.rest_0_
  10.8 0.0 collective-permute-done.5.rest_1_
  10.8 0.0 copy-start.3
  10.8 4.6 %conditional.3 = (bf16[4,64,128]{2,1,0:T(8,128)(2,1)S(1)}, f32[88,128]{1,0:T(8,128)S(1)}, f32[16,8,128]{2,1,0:T(8,128)S(1)}, bf16[4,8,192,128]{3,2,1,0:T(8,128)(2,1)S(1)}, f32[16,8,128]{2,1,0:T(8,128)S(1)}) conditional(s32[]{:T(128)} %convert_element_type.14, () %tuple.36, (f32[48,8,128]{2,1,0:T(8,128)S(1)}, f32[48,8,128]{2,1,0:T(8,128)S(1)}, ...), branch_computations={%region_0.0_spmd, %region_1.2_spmd} | conditional | flops 10000286720 | bytes 5878173 | solution.py:642
  11.0 1.8 %collective-permute-start.3 = (bf16[4,4,2,6,128]{4,1,3,2,0:T(4,128)(2,1)S(1)}, bf16[4,4,2,6,128]{4,1,3,2,0:T(4,128)(2,1)S(1)}, u32[]{:S(2)}, u32[]{:S(2)}) collective-permute-start(bf16[4,4,2,6,128]{4,1,3,2,0:T(4,128)(2,1)S(1)} %slice_select_fusion), channel_id=1, source_target_pairs={{0,16},{16,0},{1,17},{17,1},{2,18},{18,2},{3,19},{19,3},{4,20},{20... | collective-permute-start | bytes 147464 | tf_op jit(solution)/shard_map/cond/branch_1_fun/ppermute | solution.py:550
  12.9 0.1 pad_maximum_fusion
  13.0 2.0 %branch_1_fun.1 = (f32[88,128]{1,0:T(8,128)S(1)}, f32[16,8,128]{2,1,0:T(8,128)S(1)}, bf16[4,8,192,128]{3,2,1,0:T(8,128)(2,1)S(1)}, f32[16,8,128]{2,1,0:T(8,128)S(1)}) custom-call(f32[64,8,128]{2,1,0:T(8,128)S(1)} %get-tuple-element.51.phi, f32[6,16,8,128]{3,2,1,0:T(8,128)} %get-tuple-element.52.basis, bf16[4,8,192,128]{3,2,1,0:T(8,128)(2,1)} %bitcast.60, ...), custom_call_target="tpu_custom_call" | custom-call | flops 10000000000 | bytes 4108288 | tf_op jit(solution)/shard_map/cond/branch_1_fun/pallas_call | solution.py:37
  15.0 0.2 collective-permute-done.3
  15.3 0.1 maximum_select_fusion
  15.4 0.0 copy-start.1
  15.4 0.0 copy-start.2
  15.4 0.0 copy-start.5
  15.4 3.1 %all-to-all-done.1 = f32[160,1,128]{2,1,0:T(1,128)S(1)} async-done(((f32[160,1,128]{2,1,0:T(1,128)}), f32[160,1,128]{2,1,0:T(1,128)S(1)}, u32[]{:S(2)}, u32[]{:S(2)}) %all-to-all-start.1) | async-done | bytes 81952 | tf_op jit(solution)/shard_map/all_to_all | solution.py:563
  18.5 0.0 copy-done.3
  18.5 0.0 copy-start
  18.5 0.0 copy-start.4
  18.5 1.4 %shard_map.106 = (f32[128,128]{1,0:T(8,128)}, f32[16,8,128]{2,1,0:T(8,128)S(1)}, f32[8,8,128]{2,1,0:T(8,128)S(1)}, f32[8,8,128]{2,1,0:T(8,128)S(1)}, f32[20,8,128]{2,1,0:T(8,128)S(1)}) custom-call(bf16[4,8,192,128]{3,2,1,0:T(8,128)(2,1)S(1)} %get-tuple-element.104.inv, bf16[4,64,128]{2,1,0:T(8,128)(2,1)S(1)} %get-tuple-element.105.cols, ...), custom_call_target="tpu_custom_call" | custom-call | flops 2097152 | bytes 2162688 | tf_op jit(solution)/shard_map/pallas_call | solution.py:37
  19.8 2.6 %all-to-all-start.2 = ((f32[128,1,128]{2,1,0:T(1,128)}), f32[128,1,128]{2,1,0:T(1,128)S(1)}, u32[]{:S(2)}, u32[]{:S(2)}) async-start(f32[128,1,128]{2,1,0:T(1,128)} %bitcast.22), calls=%async_computation.2 | async-start | bytes 131072 | tf_op jit(solution)/shard_map/all_to_all | solution.py:563
  22.5 5.3 %conditional.4 = ((f32[8,8,128]{2,1,0:T(8,128)S(1)}, f32[8,8,128]{2,1,0:T(8,128)S(1)}, f32[20,8,128]{2,1,0:T(8,128)S(1)})) conditional(s32[]{:T(128)} %convert_element_type.14, (f32[8,8,128]{2,1,0:T(8,128)S(1)}, f32[8,8,128]{2,1,0:T(8,128)S(1)}, f32[20,8,128]{2,1,0:T(8,128)S(1)}) %tuple.38, (f32[8,8,128]{2,1,0:T(8,128)S(1)}, ...), branch_computations={%region_2.3_spmd, %region_3.4_spmd} | conditional | bytes 884888 | solution.py:663
  22.5 1.8 %collective-permute-start.2 = (f32[20,8,128]{2,1,0:T(8,128)S(1)}, f32[20,8,128]{2,1,0:T(8,128)S(1)}, u32[]{:S(2)}, u32[]{:S(2)}) collective-permute-start(f32[20,8,128]{2,1,0:T(8,128)S(1)} %get-tuple-element.65), channel_id=1, source_target_pairs={{0,16},{16,0},{1,17},{17,1},{2,18},{18,2},{3,19},{19,3},{4,20},{20... | collective-permute-start | bytes 245768 | tf_op jit(solution)/shard_map/cond/branch_1_fun/ppermute | solution.py:656
  24.3 0.0 collective-permute-start
  24.3 1.6 %collective-permute-start.1 = (f32[8,8,128]{2,1,0:T(8,128)S(1)}, f32[8,8,128]{2,1,0:T(8,128)S(1)}, u32[]{:S(2)}, u32[]{:S(2)}) collective-permute-start(f32[8,8,128]{2,1,0:T(8,128)S(1)} %get-tuple-element.64), channel_id=1, source_target_pairs={{4,8},{12,0},{8,4},{0,12},{5,9},{13,1},{9,5},{1,13},{6,10},{14,2},... | collective-permute-start | bytes 98312 | tf_op jit(solution)/shard_map/cond/branch_1_fun/ppermute | solution.py:657
  25.9 0.0 collective-permute-done
  25.9 1.8 %collective-permute-done.1 = f32[8,8,128]{2,1,0:T(8,128)S(1)} collective-permute-done((f32[8,8,128]{2,1,0:T(8,128)S(1)}, f32[8,8,128]{2,1,0:T(8,128)S(1)}, u32[]{:S(2)}, u32[]{:S(2)}) %collective-permute-start.1) | collective-permute-done | bytes 32800 | tf_op jit(solution)/shard_map/cond/branch_1_fun/ppermute | solution.py:657
  27.7 0.0 collective-permute-done.2
  27.8 2.2 %all-to-all-done.2 = f32[128,1,128]{2,1,0:T(1,128)S(1)} async-done(((f32[128,1,128]{2,1,0:T(1,128)}), f32[128,1,128]{2,1,0:T(1,128)S(1)}, u32[]{:S(2)}, u32[]{:S(2)}) %all-to-all-start.2) | async-done | bytes 65568 | tf_op jit(solution)/shard_map/all_to_all | solution.py:563
  30.0 0.0 copy-done.1
  30.0 0.0 copy-done.2
  30.0 0.0 copy-done.5
  30.0 0.9 %shard_map.107 = (f32[16,8,128]{2,1,0:T(8,128)S(1)}, f32[16,8,128]{2,1,0:T(8,128)S(1)}, f32[32,128]{1,0:T(8,128)S(1)}) custom-call(f32[16,8,128]{2,1,0:T(8,128)S(1)} %get-tuple-element.109.loc, f32[64,8,128]{2,1,0:T(8,128)S(1)} %get-tuple-element.103.phi, f32[16,8,128]{2,1,0:T(8,128)S(1)} %bitcast.43, f32[24,8,128]{2,1,0:T(8,128)S(1)} %bitcast.42, ...), custom_call_target="tpu_custom_call" | custom-call | flops 1310720 | bytes 1765376 | tf_op jit(solution)/shard_map/pallas_call | solution.py:37
  30.9 10.0 %all_to_all.20 = f32[32,1,128]{2,1,0:T(1,128)S(1)} all-to-all(f32[32,1,128]{2,1,0:T(1,128)S(1)} %bitcast.46), channel_id=1, replica_groups=mesh['gx'=2,'gy'=4,'gz'=4] {'gx','gy','gz'}, dimensions={0} | all-to-all | bytes 32768 | tf_op jit(solution)/shard_map/all_to_all | solution.py:563
  40.9 0.0 copy-done
  40.9 0.0 copy-done.4
  40.9 0.5 %shard_map.108 = (f32[16,8,128]{2,1,0:T(8,128)S(1)}, f32[4,7]{1,0:T(4,128)S(1)}, s32[1]{0:T(128)S(4)}) custom-call(f32[32,128]{1,0:T(8,128)S(1)} %bitcast.44, f32[16,8,128]{2,1,0:T(8,128)S(1)} %get-tuple-element.119.image, f32[6,16,8,128]{3,2,1,0:T(8,128)S(1)} %bitcast.50, bf16[4,128,128]{2,1,0:T(8,128)(2,1)S(1)} %copy-done, f32[8,128]{1,0:T(8,128)S(1)} %copy-done.4), custom_call_target="tpu_custom_call" | custom-call | flops 262144 | bytes 675956 | tf_op jit(solution)/shard_map/pallas_call | solution.py:37
  41.4 0.0 copy-start.6
  41.4 0.0 copy-start.7
  41.4 0.6 %copy.83 = f32[4,4,4,2,128]{4,3,2,1,0:T(2,128)} copy(f32[4,4,4,2,128]{4,3,2,1,0:T(2,128)S(1)} %bitcast.37) | data formatting | bytes 131072
  42.0 0.0 copy-done.6
  42.0 0.0 copy-done.7
  (14 shorter events, 0.2 us)
Async XLA Ops:
  1.7 9.1 %collective-permute-start.4 = (f32[48,8,128]{2,1,0:T(8,128)S(1)}, f32[48,8,128]{2,1,0:T(8,128)S(1)}, u32[]{:S(2)}, u32[]{:S(2)}) collective-permute-start(f32[48,8,128]{2,1,0:T(8,128)S(1)} %get-tuple-element.100), channel_id=1, source_target_pairs={{0,4},{8,12},{4,0},{12,8},{1,5},{9,13},{5,1},{13,9},{2,6},{10,14},... | collective-permute-start | bytes 589832 | tf_op jit(solution)/shard_map/ppermute | solution.py:591
  2.2 8.6 %collective-permute-start.5 = (f32[48,8,128]{2,1,0:T(8,128)S(1)}, f32[48,8,128]{2,1,0:T(8,128)S(1)}, u32[]{:S(2)}, u32[]{:S(2)}) collective-permute-start(f32[48,8,128]{2,1,0:T(8,128)S(1)} %get-tuple-element.101), channel_id=1, source_target_pairs={{4,8},{12,0},{8,4},{0,12},{5,9},{13,1},{9,5},{1,13},{6,10},{14,2},... | collective-permute-start | bytes 589832 | tf_op jit(solution)/shard_map/ppermute | solution.py:591
  5.8 12.6 %all-to-all-start.1 = ((f32[160,1,128]{2,1,0:T(1,128)}), f32[160,1,128]{2,1,0:T(1,128)S(1)}, u32[]{:S(2)}, u32[]{:S(2)}) async-start(f32[160,1,128]{2,1,0:T(1,128)} %bitcast.17), calls=%async_computation.1 | async-start | bytes 163840 | tf_op jit(solution)/shard_map/all_to_all | solution.py:563
  10.8 7.7 %copy-start.3 = (f32[16,512]{1,0:T(8,128)S(1)}, f32[16,512]{1,0:T(8,128)}, u32[]{:S(2)}) copy-start(f32[16,512]{1,0:T(8,128)} %factor.1) | copy-start | bytes 98308
  11.0 4.3 %collective-permute-start.3 = (bf16[4,4,2,6,128]{4,1,3,2,0:T(4,128)(2,1)S(1)}, bf16[4,4,2,6,128]{4,1,3,2,0:T(4,128)(2,1)S(1)}, u32[]{:S(2)}, u32[]{:S(2)}) collective-permute-start(bf16[4,4,2,6,128]{4,1,3,2,0:T(4,128)(2,1)S(1)} %slice_select_fusion), channel_id=1, source_target_pairs={{0,16},{16,0},{1,17},{17,1},{2,18},{18,2},{3,19},{19,3},{4,20},{20... | collective-permute-start | bytes 147464 | tf_op jit(solution)/shard_map/cond/branch_1_fun/ppermute | solution.py:550
  15.4 14.6 %copy-start.1 = (f32[6,4,4,2,128]{4,3,2,1,0:T(2,128)S(1)}, f32[6,4,4,2,128]{4,3,2,1,0:T(2,128)}, u32[]{:S(2)}) copy-start(f32[6,4,4,2,128]{4,3,2,1,0:T(2,128)} %param.19) | copy-start | bytes 294916
  15.4 14.6 %copy-start.2 = (f32[4,4,4,2,128]{4,3,2,1,0:T(2,128)S(1)}, f32[4,4,4,2,128]{4,3,2,1,0:T(2,128)}, u32[]{:S(2)}) copy-start(f32[4,4,4,2,128]{4,3,2,1,0:T(2,128)} %param.18) | copy-start | bytes 196612
  15.4 14.6 %copy-start.5 = (f32[6,4,4,4,2,128]{5,4,3,2,1,0:T(2,128)S(1)}, f32[6,4,4,4,2,128]{5,4,3,2,1,0:T(2,128)}, u32[]{:S(2)}) copy-start(f32[6,4,4,4,2,128]{5,4,3,2,1,0:T(2,128)} %param.16) | copy-start | bytes 1179652
  18.5 22.4 %copy-start = (bf16[4,128,128]{2,1,0:T(8,128)(2,1)S(1)}, bf16[4,128,128]{2,1,0:T(8,128)(2,1)}, u32[]{:S(2)}) copy-start(bf16[4,128,128]{2,1,0:T(8,128)(2,1)} %constant.92.clone.maps) | copy-start | bytes 393220
  18.5 22.4 %copy-start.4 = (f32[8,128]{1,0:T(8,128)S(1)}, f32[8,128]{1,0:T(8,128)}, u32[]{:S(2)}) copy-start(f32[8,128]{1,0:T(8,128)} %constant.93.clone.fixed) | copy-start | bytes 12292
  19.8 10.1 %all-to-all-start.2 = ((f32[128,1,128]{2,1,0:T(1,128)}), f32[128,1,128]{2,1,0:T(1,128)S(1)}, u32[]{:S(2)}, u32[]{:S(2)}) async-start(f32[128,1,128]{2,1,0:T(1,128)} %bitcast.22), calls=%async_computation.2 | async-start | bytes 131072 | tf_op jit(solution)/shard_map/all_to_all | solution.py:563
  22.5 5.2 %collective-permute-start.2 = (f32[20,8,128]{2,1,0:T(8,128)S(1)}, f32[20,8,128]{2,1,0:T(8,128)S(1)}, u32[]{:S(2)}, u32[]{:S(2)}) collective-permute-start(f32[20,8,128]{2,1,0:T(8,128)S(1)} %get-tuple-element.65), channel_id=1, source_target_pairs={{0,16},{16,0},{1,17},{17,1},{2,18},{18,2},{3,19},{19,3},{4,20},{20... | collective-permute-start | bytes 245768 | tf_op jit(solution)/shard_map/cond/branch_1_fun/ppermute | solution.py:656
  24.3 1.6 %collective-permute-start = (f32[8,8,128]{2,1,0:T(8,128)S(1)}, f32[8,8,128]{2,1,0:T(8,128)S(1)}, u32[]{:S(2)}, u32[]{:S(2)}) collective-permute-start(f32[8,8,128]{2,1,0:T(8,128)S(1)} %get-tuple-element.63), channel_id=1, source_target_pairs={{0,4},{8,12},{4,0},{12,8},{1,5},{9,13},{5,1},{13,9},{2,6},{10,14},... | collective-permute-start | bytes 98312 | tf_op jit(solution)/shard_map/cond/branch_1_fun/ppermute | solution.py:657
  24.3 3.4 %collective-permute-start.1 = (f32[8,8,128]{2,1,0:T(8,128)S(1)}, f32[8,8,128]{2,1,0:T(8,128)S(1)}, u32[]{:S(2)}, u32[]{:S(2)}) collective-permute-start(f32[8,8,128]{2,1,0:T(8,128)S(1)} %get-tuple-element.64), channel_id=1, source_target_pairs={{4,8},{12,0},{8,4},{0,12},{5,9},{13,1},{9,5},{1,13},{6,10},{14,2},... | collective-permute-start | bytes 98312 | tf_op jit(solution)/shard_map/cond/branch_1_fun/ppermute | solution.py:657
  41.4 0.7 %copy-start.6 = (f32[4,7]{1,0:T(4,128)}, f32[4,7]{1,0:T(4,128)S(1)}, u32[]{:S(2)}) copy-start(f32[4,7]{1,0:T(4,128)S(1)} %get-tuple-element.160) | copy-start | bytes 340
  41.4 0.7 %copy-start.7 = (f32[16,8,128]{2,1,0:T(8,128)}, f32[16,8,128]{2,1,0:T(8,128)S(1)}, u32[]{:S(2)}) copy-start(f32[16,8,128]{2,1,0:T(8,128)S(1)} %get-tuple-element.125) | copy-start | bytes 196612
